TPU v7x, 256 devices: a whole 4x4x8 slice. The times are simulated.
256 devices in a mesh: ctx: 32 (over z, x), tp: 4 (over y), dp: 2 (over core).
Axes of the slice: x: 4, y: 4, z: 8, core: 2. Of those that a mesh axis runs over, the one named last changes fastest.
Arguments:
- queries: bfloat16 [49152, 2048], P(('dp', 'ctx'), 'tp'), parts along dimension 0, may hold values from -6 to 6
- key_rows: bfloat16 [49152, 2048], P(('dp', 'ctx'), 'tp'), parts along dimension 0, may hold values from -6 to 6
- values: bfloat16 [49152, 2048], P(('dp', 'ctx'), 'tp'), parts along dimension 0, may hold values from -6 to 6
- doc_lengths: int32 [128], P('dp'), parts along dimension 0, may hold values from 1 to 2304, 24576 in all
- in_gate: bfloat16 [49152, 2048], P(('dp', 'ctx'), 'tp'), parts along dimension 0, may hold values from -6 to 6
- out_gate: bfloat16 [49152, 2048], P(('dp', 'ctx'), 'tp'), parts along dimension 0, may hold values from -6 to 6
- filter_taps: float32 [4096, 24576], P(('dp', 'tp'), 'ctx'), parts along dimension 0, may hold values from -0.078125 to 0.078125
Outputs:
- attn_out: bfloat16 [49152, 2048], P(('dp', 'ctx'), 'tp'), parts along dimension 0
- hyena_out: bfloat16 [49152, 2048], P(('dp', 'ctx'), 'tp'), parts along dimension 0
There are 2 independent parts, one for each index of `dp`. A program takes and returns all parts, laid end to end along the dimension named above; each array names one. Nothing has to cross between parts.
Inputs may be any that keep to these rules, and one draw needn't show every extreme that they name: `doc_lengths`: the lengths sum to 24576, and the longest is exactly 2304.
All inputs are finite; a program needn't handle non-finite values.
Results may differ from a plain program's by a relative error of at most 0.012.
Values may be sent and summed in bfloat16 or wider, within the bound.
No kernel may reach another device: no remote copies, remote signals or barrier semaphores. Data moves between devices by JAX's collectives and lax.ppermute only.
A program may use at most 192 MiB of HBM per device.

v0:
```python
import math

import jax
import jax.numpy as jnp
from jax import lax
from jax.sharding import PartitionSpec as P

HEAD_DIM = 128
KV_REACH = 3


masked_score = -1e30


def passed_along(x, axis, by):
    length = lax.axis_size(axis)
    pairs = [(i, i + by) for i in range(length) if 0 <= i + by < length]
    return lax.ppermute(x, axis, pairs)


def doc_of(positions, doc_lengths):
    order = jnp.arange(doc_lengths.shape[0], dtype=jnp.int32)
    before = order[:, None] < order[None, :]
    starts = jnp.sum(jnp.where(before, doc_lengths[:, None], 0), axis=0)
    inside = (starts[None, :] <= positions[:, None]).astype(jnp.int32)
    return jnp.sum(inside, axis=1) - 1


def attend_block(carried, pair, query_heads, allowed):
    running_max, running_sum, weighted = carried
    row_count = query_heads.shape[0]
    key_heads = pair[0].reshape(row_count, -1, HEAD_DIM)
    value_heads = pair[1].reshape(row_count, -1, HEAD_DIM)
    scores = jnp.einsum(
        "qhd,khd->hqk", query_heads, key_heads, preferred_element_type=jnp.float32
    ) / math.sqrt(HEAD_DIM)
    scores = jnp.where(allowed[None], scores, masked_score)
    new_max = jnp.maximum(running_max, jnp.max(scores, axis=2))
    rescale = jnp.exp(running_max - new_max)
    exp_scores = jnp.exp(scores - new_max[:, :, None])
    running_sum = running_sum * rescale + jnp.sum(exp_scores, axis=2)
    weighted = weighted * rescale[:, :, None] + jnp.einsum(
        "hqk,khd->hqd",
        exp_scores.astype(jnp.bfloat16),
        value_heads,
        preferred_element_type=jnp.float32,
    )
    return (new_max, running_sum, weighted)


def split_parts(source):
    high_part = lax.optimization_barrier(source.astype(jnp.bfloat16))
    low_part = (source - high_part.astype(jnp.float32)).astype(jnp.bfloat16)
    return (high_part, low_part)


def split_mul(form, left_parts, right_parts):
    first = jnp.einsum(form, left_parts[0], right_parts[0], preferred_element_type=jnp.float32)
    second = jnp.einsum(form, left_parts[0], right_parts[1], preferred_element_type=jnp.float32)
    third = jnp.einsum(form, left_parts[1], right_parts[0], preferred_element_type=jnp.float32)
    return first + (second + third)


def dft_tables(length):
    inner_len = math.gcd(length, 256)
    outer_len = 2 * length // inner_len
    freq_rows = jnp.arange(outer_len, dtype=jnp.int32)
    time_rows = jnp.arange(outer_len // 2, dtype=jnp.int32)
    inner_index = jnp.arange(inner_len, dtype=jnp.int32)
    angle_outer = (
        2.0
        * math.pi
        / outer_len
        * (freq_rows[:, None] * time_rows[None, :] % outer_len).astype(jnp.float32)
    )
    angle_twist = (
        2.0
        * math.pi
        / (2 * length)
        * (freq_rows[:, None] * inner_index[None, :] % (2 * length)).astype(jnp.float32)
    )
    angle_inner = (
        2.0
        * math.pi
        / inner_len
        * (inner_index[:, None] * inner_index[None, :] % inner_len).astype(jnp.float32)
    )
    return (
        split_parts(jnp.cos(angle_outer)),
        split_parts(-jnp.sin(angle_outer)),
        jnp.cos(angle_twist),
        -jnp.sin(angle_twist),
        split_parts(jnp.cos(angle_inner)),
        split_parts(-jnp.sin(angle_inner)),
    )


def right_mul(left_parts, table_parts):
    return split_mul("cin,nm->cim", left_parts, table_parts)


def forward_dft(samples, tables):
    outer_cos, outer_sin, twist_cos, twist_sin, inner_cos, inner_sin = tables
    item_count = samples.shape[0]
    shaped = split_parts(samples.reshape(item_count, outer_cos[0].shape[1], inner_cos[0].shape[0]))
    section_real = split_mul("ij,cjn->cin", outer_cos, shaped)
    section_imag = split_mul("ij,cjn->cin", outer_sin, shaped)
    turned_real = split_parts(section_real * twist_cos - section_imag * twist_sin)
    turned_imag = split_parts(section_real * twist_sin + section_imag * twist_cos)
    spec_real = right_mul(turned_real, inner_cos) - right_mul(turned_imag, inner_sin)
    spec_imag = right_mul(turned_real, inner_sin) + right_mul(turned_imag, inner_cos)
    return (spec_real, spec_imag)


def inverse_dft(prod_real, prod_imag, tables):
    outer_cos, outer_sin, twist_cos, twist_sin, inner_cos, inner_sin = tables
    item_count = prod_real.shape[0]
    half_len = outer_cos[0].shape[1]
    inner_len = inner_cos[0].shape[0]
    real_parts = split_parts(prod_real)
    imag_parts = split_parts(prod_imag)
    back_real = right_mul(real_parts, inner_cos) + right_mul(imag_parts, inner_sin)
    back_imag = right_mul(imag_parts, inner_cos) - right_mul(real_parts, inner_sin)
    unturn_real = split_parts(back_real * twist_cos + back_imag * twist_sin)
    unturn_imag = split_parts(back_imag * twist_cos - back_real * twist_sin)
    rows_out = split_mul("ij,cin->cjn", outer_cos, unturn_real) + split_mul(
        "ij,cin->cjn", outer_sin, unturn_imag
    )
    return (rows_out * (1.0 / (2 * half_len * inner_len))).reshape(item_count, half_len * inner_len)


def filter_apply(signal, filter_spec, tables):
    sig_real, sig_imag = forward_dft(signal, tables)
    tap_real, tap_imag = filter_spec
    prod_real = sig_real * tap_real - sig_imag * tap_imag
    prod_imag = sig_real * tap_imag + sig_imag * tap_real
    return inverse_dft(prod_real, prod_imag, tables)


def body(queries, key_rows, values, doc_lengths, in_gate, out_gate, filter_taps):
    row_count, channels = queries.shape
    head_count = channels // HEAD_DIM
    group_count = lax.axis_size("ctx")
    per_group = channels // group_count
    seq_len = row_count * group_count
    tables = dft_tables(seq_len)
    taps_grouped = filter_taps.reshape(group_count, per_group, row_count)
    query_pos = lax.axis_index("ctx") * row_count + jnp.arange(row_count, dtype=jnp.int32)
    query_doc = doc_of(query_pos, doc_lengths)
    query_heads = queries.reshape(row_count, head_count, HEAD_DIM)
    carried = (
        jnp.full((head_count, row_count), masked_score, jnp.float32),
        jnp.zeros((head_count, row_count), jnp.float32),
        jnp.zeros((head_count, row_count, HEAD_DIM), jnp.float32),
    )

    def visit(state_now, pair, distance):
        key_pos = query_pos - distance * row_count
        key_doc = doc_of(key_pos, doc_lengths)
        allowed = (key_doc[None, :] == query_doc[:, None]) & (
            key_pos[None, :] <= query_pos[:, None]
        )
        return attend_block(state_now, pair, query_heads, allowed)

    own_pair = jnp.stack((key_rows, values))
    carried = visit(carried, own_pair, 0)
    moving = own_pair
    for distance in range(1, KV_REACH + 1):
        moving = passed_along(moving, "ctx", 1)
        carried = visit(carried, moving, distance)
    running_max, running_sum, weighted = carried
    attended = (
        (weighted / running_sum[:, :, None])
        .transpose(1, 0, 2)
        .reshape(row_count, channels)
        .astype(jnp.bfloat16)
    )
    gated = (in_gate.astype(jnp.float32) * attended.astype(jnp.float32)).T
    gated_grouped = gated.reshape(group_count, per_group, row_count)
    pair = (
        lax.all_to_all(
            gated_grouped.astype(jnp.bfloat16), "ctx", split_axis=0, concat_axis=2, tiled=True
        ).astype(gated_grouped.dtype),
        lax.all_to_all(
            taps_grouped.astype(jnp.bfloat16), "ctx", split_axis=0, concat_axis=2, tiled=True
        ).astype(taps_grouped.dtype),
    )
    item_count = pair[0].shape[1]
    signal = pair[0].reshape(item_count, -1)
    taps = pair[1].reshape(item_count, -1)
    result = filter_apply(signal, forward_dft(taps, tables), tables)
    mixed = result.reshape(1, item_count, -1)
    returned = lax.all_to_all(
        mixed.astype(jnp.bfloat16), "ctx", split_axis=2, concat_axis=0, tiled=True
    ).astype(mixed.dtype)
    hyena_out = (out_gate.astype(jnp.float32) * returned.reshape(channels, row_count).T).astype(
        jnp.bfloat16
    )
    return (attended, hyena_out)


def solution(mesh):
    return jax.shard_map(
        body,
        mesh=mesh,
        in_specs=(
            P(("dp", "ctx"), "tp"),
            P(("dp", "ctx"), "tp"),
            P(("dp", "ctx"), "tp"),
            P("dp"),
            P(("dp", "ctx"), "tp"),
            P(("dp", "ctx"), "tp"),
            P(("dp", "tp"), "ctx"),
        ),
        out_specs=(P(("dp", "ctx"), "tp"), P(("dp", "ctx"), "tp")),
        check_vma=False,
    )
```

profile of v0, /device:TPU:16, one launch (start us, length us, event | category | flops | bytes accessed | tf_op | source)
XLA Modules:
  0.0 573.7 jit_solution(11655899679153076258)
XLA Ops:
  5.2 4.6 collective-permute-start
  10.7 9.9 %all-to-all-start.1 = ((bf16[32,16,768]{2,1,0:T(8,128)(2,1)}), bf16[32,16,768]{2,1,0:T(8,128)(2,1)S(1)}, u32[]{:S(2)}, u32[]{:S(2)}) async-start(bf16[32,16,768]{2,1,0:T(8,128)(2,1)} %bitcast.42), calls=%async_computation.1 | async-start | bytes 1572864 | tf_op jit(solution)/shard_map/all_to_all | solution.py:184
  23.3 27.1 %collective-permute-done = bf16[2,768,512]{1,2,0:T(8,128)(2,1)} collective-permute-done((bf16[2,768,512]{1,2,0:T(8,128)(2,1)}, bf16[2,768,512]{1,2,0:T(8,128)(2,1)}, u32[]{:S(2)}, u32[]{:S(2)}) %collective-permute-start) | collective-permute-done | bytes 1572896 | tf_op jit(solution)/shard_map/ppermute | solution.py:18
  50.4 5.6 collective-permute-start.1
  58.4 3.4 compare_and_fusion.3
  62.5 6.5 %fusion = (f32[4,768]{1,0:T(4,128)S(1)}, f32[4,768,768]{1,2,0:T(8,128)}) fusion(pred[768,768]{0,1:T(8,128)(4,1)S(1)} %get-tuple-element.53, bf16[768,512]{1,0:T(8,128)(2,1)} %param.8, bf16[768,512]{1,0:T(8,128)(2,1)S(1)} %copy-done), kind=kOutput, calls=%fused_computation.8 | convolution fusion | flops 611054592 | bytes 11612160 | tf_op jit(solution)/shard_map/qhd,khd->hqk/dot_general | solution.py:34
  69.1 3.0 all-to-all-done.1
  74.7 12.7 %collective-permute-done.1 = bf16[2,768,512]{1,2,0:T(8,128)(2,1)} collective-permute-done((bf16[2,768,512]{1,2,0:T(8,128)(2,1)}, bf16[2,768,512]{1,2,0:T(8,128)(2,1)}, u32[]{:S(2)}, u32[]{:S(2)}) %collective-permute-start.1) | collective-permute-done | bytes 1572896 | tf_op jit(solution)/shard_map/ppermute | solution.py:18
  87.3 4.7 collective-permute-start.2
  92.0 2.4 fusion.225
  94.4 5.7 fusion.9
  100.1 2.4 fusion.226
  104.5 18.9 %collective-permute-done.2 = bf16[2,768,512]{1,2,0:T(8,128)(2,1)S(1)} collective-permute-done((bf16[2,768,512]{1,2,0:T(8,128)(2,1)}, bf16[2,768,512]{1,2,0:T(8,128)(2,1)S(1)}, u32[]{:S(2)}, u32[]{:S(2)}) %collective-permute-start.2) | collective-permute-done | bytes 1572896 | tf_op jit(solution)/shard_map/ppermute | solution.py:18
  126.4 5.9 %fusion.7 = f32[4,768]{1,0:T(4,128)S(1)} fusion(f32[4,768,768]{1,2,0:T(8,128)} %get-tuple-element.64, f32[4,768]{1,0:T(4,128)S(1)} %get-tuple-element.52, pred[768,768]{0,1:T(8,128)(4,1)} %copy-done.17), kind=kLoop, calls=%fused_computation.15 | loop fusion | flops 9434112 | bytes 10051584 | tf_op jit(solution)/shard_map/reduce_sum | solution.py:41
  132.3 7.6 %fusion.12 = f32[4,768,128]{1,2,0:T(8,128)} fusion(bf16[768,4,128]{0,2,1:T(8,128)(2,1)S(1)} %bitcast.429, f32[4,768,768]{1,2,0:T(8,128)} %get-tuple-element.64, f32[4,768]{1,0:T(4,128)S(1)} %get-tuple-element.52, pred[768,768]{0,1:T(8,128)(4,1)S(1)} %copy-done.18), kind=kOutput, calls=%fused_computation.20 | convolution fusion | flops 613416960 | bytes 12398592 | tf_op jit(solution)/shard_map/hqk,khd->hqd/dot_general | solution.py:42
  139.9 6.2 %fusion.1 = f32[4,768]{1,0:T(4,128)S(1)} fusion(f32[4,768,768]{2,1,0:T(8,128)} %get-tuple-element.62, f32[4,768]{1,0:T(4,128)S(1)} %get-tuple-element.27, pred[768,768]{0,1:T(8,128)(4,1)S(1)} %copy-done.11), kind=kLoop, calls=%fused_computation.9 | loop fusion | flops 9434112 | bytes 10051584 | tf_op jit(solution)/shard_map/reduce_sum | solution.py:41
  146.1 7.5 %fusion.18 = f32[4,768,128]{1,2,0:T(8,128)} fusion(bf16[768,4,128]{0,2,1:T(8,128)(2,1)S(1)} %bitcast.432, f32[4,768,768]{2,1,0:T(8,128)} %get-tuple-element.62, f32[4,768]{1,0:T(4,128)S(1)} %get-tuple-element.27, pred[768,768]{0,1:T(8,128)(4,1)S(1)} %copy-done.11), kind=kOutput, calls=%fused_computation.23 | convolution fusion | flops 613416960 | bytes 12398592 | tf_op jit(solution)/shard_map/hqk,khd->hqd/dot_general | solution.py:42
  155.7 4.1 fusion.16
  162.3 3.3 fusion.32
  166.8 28.9 %all-to-all-start = ((bf16[32,16,768]{2,1,0:T(8,128)(2,1)}), bf16[32,16,768]{2,1,0:T(8,128)(2,1)S(1)}, u32[]{:S(2)}, u32[]{:S(2)}) async-start(bf16[32,16,768]{2,1,0:T(8,128)(2,1)} %bitcast.26), calls=%async_computation | async-start | bytes 1572864 | tf_op jit(solution)/shard_map/all_to_all | solution.py:181
  201.4 2.7 fusion.25
  204.2 13.0 %all-to-all-done = bf16[32,16,768]{2,1,0:T(8,128)(2,1)S(1)} async-done(((bf16[32,16,768]{2,1,0:T(8,128)(2,1)}), bf16[32,16,768]{2,1,0:T(8,128)(2,1)S(1)}, u32[]{:S(2)}, u32[]{:S(2)}) %all-to-all-start) | async-done | bytes 786464 | tf_op jit(solution)/shard_map/all_to_all | solution.py:181
  223.1 5.3 fusion.39
  230.6 3.3 fusion.215
  233.9 3.2 fusion.203
  241.5 3.2 fusion.217
  244.7 3.2 fusion.205
  250.1 3.1 subtract_convert_fusion.4
  258.2 3.3 fusion.199
  261.5 3.1 fusion.211
  267.5 2.3 fusion.88
  272.1 3.3 fusion.201
  275.3 3.2 fusion.213
  281.3 3.3 add_subtract_fusion.1
  284.7 7.7 %add_add_fusion.1 = f32[16,192,256]{2,1,0:T(8,128)} fusion(f32[16,192,256]{2,1,0:T(8,128)} %fusion.107, f32[16,192,256]{2,1,0:T(8,128)} %fusion.211, f32[16,192,256]{2,1,0:T(8,128)} %fusion.86, f32[16,192,256]{2,1,0:T(8,128)} %fusion.199, f32[16,192,256]{2,1,0:T(8,128)S(1)} %fusion.84, bf16[16,192,256]{2,1,0:T(8,128)(2,1)S(1)} %get-tuple-element.32, ...), kind=kOutput, calls=%fused_computation.48 | convolution fusion | flops 406585344 | bytes 20578304 | tf_op jit(solution)/shard_map/cin,nm->cim/dot_general | solution.py:60
  294.1 3.1 add_subtract_fusion.2
  297.2 8.4 %fusion.219 = (bf16[16,192,256]{2,1,0:T(8,128)(2,1)S(1)}, f32[16,192,256]{2,1,0:T(8,128)S(1)}, bf16[16,192,256]{2,1,0:T(8,128)(2,1)S(1)}, f32[16,192,256]{2,1,0:T(8,128)S(1)}) fusion(f32[16,192,256]{2,1,0:T(8,128)} %add_add_fusion.1, f32[16,192,256]{2,1,0:T(8,128)} %add_subtract_fusion.2, f32[16,192,256]{2,1,0:T(8,128)S(1)} %add_subtract_fusion.1, ...), kind=kOutput, calls=%fused_computation.282 | convolution fusion | flops 412876800 | bytes 36306944 | tf_op jit(solution)/shard_map/cin,nm->cim/dot_general | solution.py:60
  307.7 3.2 fusion.197
  315.2 3.2 fusion.207
  325.1 5.2 add_add_fusion
  330.3 5.1 fusion.41
  340.7 19.0 %copy.214 = bf16[1,16,24576]{1,0,2:T(2,128)(2,1)} copy(bf16[1,16,24576]{2,1,0:T(8,128)(2,1)S(1)} %convert_element_type.328) | data formatting | bytes 1572864 | tf_op jit(solution)/shard_map/convert_element_type | solution.py:194
  360.2 134.9 %reduce = bf16[24576,16]{1,0:T(8,128)(2,1)} reduce(bf16[24576,1,16]{2,1,0:T(2,128)(2,1)} %bitcast.419, bf16[]{:T(256)} %broadcast.405), dimensions={1}, to_apply=%bitcast.326.reduce_sub_computation | reduce | bytes 1572866
  495.1 9.9 %reshape.434 = bf16[32,2,6144]{2,1,0:T(2,128)(2,1)} reshape(bf16[24576,16]{1,0:T(8,128)(2,1)} %reduce) | data formatting | bytes 1572864
  505.0 4.9 all-to-all-start.2
  511.3 19.6 %all-to-all-done.2 = bf16[32,2,6144]{2,1,0:T(2,128)(2,1)S(1)} async-done(((bf16[32,2,6144]{2,1,0:T(2,128)(2,1)}), bf16[32,2,6144]{2,1,0:T(2,128)(2,1)S(1)}, u32[]{:S(2)}, u32[]{:S(2)}) %all-to-all-start.2) | async-done | bytes 786464 | tf_op jit(solution)/shard_map/all_to_all | solution.py:193
  530.9 17.2 %reshape.435 = bf16[24576,1,16]{2,1,0:T(2,128)(2,1)} reshape(bf16[32,2,6144]{2,1,0:T(2,128)(2,1)S(1)} %all-to-all-done.2) | data formatting | bytes 1572864
  548.0 22.6 %copy.215 = bf16[1,16,24576]{2,1,0:T(8,128)(2,1)S(1)} copy(bf16[1,16,24576]{1,0,2:T(2,128)(2,1)} %bitcast.418) | data formatting | bytes 1572864 | tf_op jit(solution)/shard_map/all_to_all | solution.py:193
  (132 shorter events, 82.6 us)
Async XLA Ops:
  0.6 61.9 %copy-start = (bf16[768,512]{1,0:T(8,128)(2,1)S(1)}, bf16[768,512]{1,0:T(8,128)(2,1)}, u32[]{:S(2)}) copy-start(bf16[768,512]{1,0:T(8,128)(2,1)} %param.7) | copy-start | bytes 2359300
  2.1 8.5 %copy-start.14 = (bf16[768,512]{0,1:T(8,128)(2,1)}, bf16[768,512]{0,1:T(8,128)(2,1)S(1)}, u32[]{:S(2)}) copy-start(bf16[768,512]{0,1:T(8,128)(2,1)S(1)} %copy.238) | copy-start | bytes 2359300
  3.8 5.9 %copy-start.19 = (f32[512,768]{1,0:T(8,128)S(1)}, f32[512,768]{1,0:T(8,128)}, u32[]{:S(2)}) copy-start(f32[512,768]{1,0:T(8,128)} %param.13) | copy-start | bytes 4718596
  3.8 17.1 %copy-start.25 = (s32[64]{0:T(128)S(1)}, s32[64]{0:T(128)}, u32[]{:S(2)}) copy-start(s32[64]{0:T(128)} %param.10) | copy-start | bytes 772
  3.9 52.5 %copy-start.20 = (bf16[768,512]{1,0:T(8,128)(2,1)S(1)}, bf16[768,512]{1,0:T(8,128)(2,1)}, u32[]{:S(2)}) copy-start(bf16[768,512]{1,0:T(8,128)(2,1)} %param.11) | copy-start | bytes 2359300
  5.2 45.2 %collective-permute-start = (bf16[2,768,512]{1,2,0:T(8,128)(2,1)}, bf16[2,768,512]{1,2,0:T(8,128)(2,1)}, u32[]{:S(2)}, u32[]{:S(2)}) collective-permute-start(bf16[2,768,512]{1,2,0:T(8,128)(2,1)} %pad_maximum_fusion), channel_id=1, source_target_pairs={{0,8},{8,16},{16,24},{24,32},{32,40},{40,48},{48,56},{56,64},{64,7... | collective-permute-start | bytes 4718600 | tf_op jit(solution)/shard_map/ppermute | solution.py:18
  10.7 61.4 %all-to-all-start.1 = ((bf16[32,16,768]{2,1,0:T(8,128)(2,1)}), bf16[32,16,768]{2,1,0:T(8,128)(2,1)S(1)}, u32[]{:S(2)}, u32[]{:S(2)}) async-start(bf16[32,16,768]{2,1,0:T(8,128)(2,1)} %bitcast.42), calls=%async_computation.1 | async-start | bytes 1572864 | tf_op jit(solution)/shard_map/all_to_all | solution.py:184
  50.4 36.9 %collective-permute-start.1 = (bf16[2,768,512]{1,2,0:T(8,128)(2,1)}, bf16[2,768,512]{1,2,0:T(8,128)(2,1)}, u32[]{:S(2)}, u32[]{:S(2)}) collective-permute-start(bf16[2,768,512]{1,2,0:T(8,128)(2,1)} %collective-permute-done), channel_id=1, source_target_pairs={{0,8},{8,16},{16,24},{24,32},{32,40},{40,48},{48,56},{56,64},{64,7... | collective-permute-start | bytes 4718600 | tf_op jit(solution)/shard_map/ppermute | solution.py:18
  61.7 0.8 copy-start.17
  74.7 19.8 %copy-start.11 = (pred[768,768]{0,1:T(8,128)(4,1)S(1)}, pred[768,768]{0,1:T(8,128)(4,1)}, u32[]{:S(2)}) copy-start(pred[768,768]{0,1:T(8,128)(4,1)} %get-tuple-element.56) | copy-start | bytes 1769476
  87.3 36.0 %collective-permute-start.2 = (bf16[2,768,512]{1,2,0:T(8,128)(2,1)}, bf16[2,768,512]{1,2,0:T(8,128)(2,1)S(1)}, u32[]{:S(2)}, u32[]{:S(2)}) collective-permute-start(bf16[2,768,512]{1,2,0:T(8,128)(2,1)} %collective-permute-done.1), channel_id=1, source_target_pairs={{0,8},{8,16},{16,24},{24,32},{32,40},{40,48},{48,56},{56,64},{64,7... | collective-permute-start | bytes 4718600 | tf_op jit(solution)/shard_map/ppermute | solution.py:18
  126.4 5.9 %copy-start.15 = (bf16[768,512]{0,1:T(8,128)(2,1)S(1)}, bf16[768,512]{0,1:T(8,128)(2,1)}, u32[]{:S(2)}) copy-start(bf16[768,512]{0,1:T(8,128)(2,1)} %copy-done.14) | copy-start | bytes 2359300
  126.4 5.9 %copy-start.18 = (pred[768,768]{0,1:T(8,128)(4,1)S(1)}, pred[768,768]{0,1:T(8,128)(4,1)}, u32[]{:S(2)}) copy-start(pred[768,768]{0,1:T(8,128)(4,1)} %copy-done.17) | copy-start | bytes 1769476
  139.9 6.2 %copy-start.23 = (bf16[1,768,512]{1,2,0:T(8,128)(2,1)S(1)}, bf16[1,768,512]{1,2,0:T(8,128)(2,1)}, u32[]{:S(2)}) copy-start(bf16[1,768,512]{1,2,0:T(8,128)(2,1)} %get-tuple-element.42) | copy-start | bytes 2359300
  153.6 2.1 copy-start.24
  159.7 2.1 copy-start.22
  159.7 2.1 copy-start.26
  159.7 2.1 copy-start.27
  159.7 2.6 copy-start.28
  162.3 3.3 copy-start.16
  165.7 1.2 copy-start.12
  166.8 50.4 %all-to-all-start = ((bf16[32,16,768]{2,1,0:T(8,128)(2,1)}), bf16[32,16,768]{2,1,0:T(8,128)(2,1)S(1)}, u32[]{:S(2)}, u32[]{:S(2)}) async-start(bf16[32,16,768]{2,1,0:T(8,128)(2,1)} %bitcast.26), calls=%async_computation | async-start | bytes 1572864 | tf_op jit(solution)/shard_map/all_to_all | solution.py:181
  221.3 1.9 copy-start.2
  272.0 8.7 %copy-start.10 = (f32[16,192,256]{2,1,0:T(8,128)S(1)}, f32[16,192,256]{2,1,0:T(8,128)}, u32[]{:S(2)}) copy-start(f32[16,192,256]{2,1,0:T(8,128)} %fusion.93) | copy-start | bytes 9437188
  275.3 5.5 copy-start.8
  275.3 5.5 copy-start.9
  278.5 2.8 copy-start.7
  284.6 7.7 %copy-start.3 = (f32[16,192,256]{2,1,0:T(8,128)S(1)}, f32[16,192,256]{2,1,0:T(8,128)}, u32[]{:S(2)}) copy-start(f32[16,192,256]{2,1,0:T(8,128)} %fusion.118) | copy-start | bytes 9437188
  284.6 7.7 %copy-start.4 = (f32[16,192,256]{2,1,0:T(8,128)S(1)}, f32[16,192,256]{2,1,0:T(8,128)}, u32[]{:S(2)}) copy-start(f32[16,192,256]{2,1,0:T(8,128)} %fusion.217) | copy-start | bytes 9437188
  284.7 8.1 %copy-start.5 = (f32[16,192,256]{2,1,0:T(8,128)S(1)}, f32[16,192,256]{2,1,0:T(8,128)}, u32[]{:S(2)}) copy-start(f32[16,192,256]{2,1,0:T(8,128)} %fusion.205) | copy-start | bytes 9437188
  284.7 9.4 %copy-start.6 = (f32[16,192,256]{2,1,0:T(8,128)S(1)}, f32[16,192,256]{2,1,0:T(8,128)}, u32[]{:S(2)}) copy-start(f32[16,192,256]{2,1,0:T(8,128)} %fusion.96) | copy-start | bytes 9437188
  495.1 14.8 %copy-start.21 = (bf16[768,512]{1,0:T(8,128)(2,1)S(1)}, bf16[768,512]{1,0:T(8,128)(2,1)}, u32[]{:S(2)}) copy-start(bf16[768,512]{1,0:T(8,128)(2,1)} %param.12) | copy-start | bytes 2359300
  505.0 5.2 copy-start.13
  505.0 25.9 %all-to-all-start.2 = ((bf16[32,2,6144]{2,1,0:T(2,128)(2,1)}), bf16[32,2,6144]{2,1,0:T(2,128)(2,1)S(1)}, u32[]{:S(2)}, u32[]{:S(2)}) async-start(bf16[32,2,6144]{2,1,0:T(2,128)(2,1)} %reshape.434), calls=%async_computation.2 | async-start | bytes 1572864 | tf_op jit(solution)/shard_map/all_to_all | solution.py:193
  571.0 2.3 copy-start.1
where the time goes:
time: 582 us; the launch traced here: 574 us
  other arithmetic  165 us (28%)
  matrix products  163 us (28%)
  waiting for transfers between devices  94.2 us (16%)
  local copies, waits for them, and re-layouts  91 us (16%)
  starting transfers between devices  58.4 us (10%)
    unnamed x1, other arithmetic  135 us
    ppermute x3, waiting for transfers between devices, passed_along(): return lax.ppermute(x, axis, pairs)  58.7 us
    dot_general x18, matrix products, split_mul(): jnp.einsum(form, left_parts[1], right_parts[0], preferred_element_type=jn...  54.5 us
    dot_general x18, matrix products, split_mul(): jnp.einsum(form, left_parts[0], right_parts[1], preferred_element_type=jn...  41.8 us
    unnamed x67, local copies, waits for them, and re-layouts  37.7 us
    all_to_all x1, starting transfers between devices, body(): lax.all_to_all(gated_grouped.astype(jnp.bfloat16), 'ctx', split_axis=0, c...  28.9 us
    dot_general x18, matrix products, split_mul(): jnp.einsum(form, left_parts[0], right_parts[0], preferred_element_type=jn...  28.2 us
    all_to_all x1, local copies, waits for them, and re-layouts, body(): lax.all_to_all(mixed.astype(jnp.bfloat16), 'ctx', split_axis=2, concat_ax...  22.6 us
  transfers between devices with their start and end apart: 6, of which 6 were waited for; matrix products, arithmetic and copies ran while one was open for 7% of the time, Pallas kernels for 0%

commit v1 on v0

v1 whole, which is shorter than its diff:
```python
import functools
import math

import jax
import jax.numpy as jnp
import ml_dtypes
import numpy as np
from jax import lax
from jax.experimental import pallas as pl
from jax.experimental.pallas import tpu as pltpu
from jax.sharding import PartitionSpec as P

HEAD_DIM = 128
KV_REACH = 3
X_SIZE = 4
Q_BLOCK = 256
K_BLOCK = 256
LANES = 128
masked_score = -1e30


def document_starts(positions, doc_lengths):
    order = jnp.arange(doc_lengths.shape[0], dtype=jnp.int32)
    before = order[:, None] < order[None, :]
    starts = jnp.sum(jnp.where(before, doc_lengths[:, None], 0), axis=0)
    inside = starts[None, :] <= positions[:, None]
    return jnp.max(jnp.where(inside, starts[None, :], 0), axis=1)


def attention_kernel(
    lo_ref, start_ref, q_ref, gate_ref, kp_ref, ko_ref, vp_ref, vo_ref, out_ref, gated_ref, keys, values_t
):
    step = pl.program_id(0)
    reach = kp_ref.shape[0]
    front = keys.shape[0] - reach - ko_ref.shape[0]

    @pl.when(step == 0)
    def _():
        if front:
            keys[0:front] = jnp.zeros((front, HEAD_DIM), jnp.bfloat16)
            values_t[0] = jnp.zeros(values_t.shape[1:], jnp.bfloat16)
        keys[front : front + reach] = kp_ref[...]
        keys[front + reach :] = ko_ref[...]
        for ref, base in ((vp_ref, front), (vo_ref, front + reach)):
            for row in range(0, ref.shape[0], 256):
                block, at = divmod(base + row, K_BLOCK)
                part = ref[row : row + 256].astype(jnp.float32).T
                values_t[block, :, at : at + 256] = part.astype(jnp.bfloat16)

    queries = q_ref[...]
    first = front + reach + step * Q_BLOCK
    start = start_ref[0]
    query_index = first + lax.broadcasted_iota(jnp.int32, (1, Q_BLOCK), 1)
    key_offset = lax.broadcasted_iota(jnp.int32, (K_BLOCK, 1), 0)
    factor = math.log2(math.e) / math.sqrt(HEAD_DIM)

    def visit(block, carried):
        top, total, weighted = carried
        key_rows = keys[pl.ds(pl.multiple_of(block * K_BLOCK, K_BLOCK), K_BLOCK)]
        scores = lax.dot_general(
            key_rows, queries, (((1,), (1,)), ((), ())), preferred_element_type=jnp.float32
        )
        index = block * K_BLOCK + key_offset
        kept = (index >= start) & (index <= query_index)
        scores = jnp.where(kept, scores * factor, masked_score)
        new_top = jnp.maximum(top, jnp.max(scores, axis=0, keepdims=True))
        rescale = jnp.exp2(top - new_top)
        weight = jnp.exp2(scores - new_top)
        total = total * rescale + jnp.sum(weight, axis=0, keepdims=True)
        weighted = weighted * rescale + jnp.dot(
            values_t[block], weight.astype(jnp.bfloat16), preferred_element_type=jnp.float32
        )
        return new_top, total, weighted

    last = (first + Q_BLOCK - 1) // K_BLOCK
    top, total, weighted = lax.fori_loop(
        lo_ref[step],
        last + 1,
        visit,
        (
            jnp.full((1, Q_BLOCK), masked_score, jnp.float32),
            jnp.zeros((1, Q_BLOCK), jnp.float32),
            jnp.zeros((HEAD_DIM, Q_BLOCK), jnp.float32),
        ),
    )
    attended = (weighted * (1.0 / total)).astype(jnp.bfloat16).astype(jnp.float32)
    out_ref[...] = attended.T.astype(jnp.bfloat16)
    gated_ref[...] = (attended * gate_ref[...].astype(jnp.float32).T).astype(jnp.bfloat16)


def attention(queries, gate, keys_before, keys_own, values_before, values_own, start):
    rows = queries.shape[0]
    reach = keys_before.shape[0]
    front = -reach % K_BLOCK
    steps = rows // Q_BLOCK
    start = start + front
    lo = start[::Q_BLOCK] // K_BLOCK
    whole = lambda i, lo: (0, 0)
    by_rows = lambda i, lo: (i, 0)
    key_total = front + reach + rows
    return pl.pallas_call(
        attention_kernel,
        name="attention",
        grid_spec=pltpu.PrefetchScalarGridSpec(
            num_scalar_prefetch=1,
            grid=(steps,),
            in_specs=[
                pl.BlockSpec((1, 1, Q_BLOCK), lambda i, lo: (i, 0, 0)),
                pl.BlockSpec((Q_BLOCK, HEAD_DIM), by_rows),
                pl.BlockSpec((Q_BLOCK, HEAD_DIM), by_rows),
                pl.BlockSpec((reach, HEAD_DIM), whole),
                pl.BlockSpec((rows, HEAD_DIM), whole),
                pl.BlockSpec((reach, HEAD_DIM), whole),
                pl.BlockSpec((rows, HEAD_DIM), whole),
            ],
            out_specs=[
                pl.BlockSpec((Q_BLOCK, HEAD_DIM), by_rows),
                pl.BlockSpec((HEAD_DIM, Q_BLOCK), lambda i, lo: (0, i)),
            ],
            scratch_shapes=[
                pltpu.VMEM((key_total, HEAD_DIM), jnp.bfloat16),
                pltpu.VMEM((key_total // K_BLOCK, HEAD_DIM, K_BLOCK), jnp.bfloat16),
            ],
        ),
        out_shape=[
            jax.ShapeDtypeStruct((rows, HEAD_DIM), jnp.bfloat16),
            jax.ShapeDtypeStruct((HEAD_DIM, rows), jnp.bfloat16),
        ],
        compiler_params=pltpu.CompilerParams(vmem_limit_bytes=40 * 2**20),
        cost_estimate=pl.CostEstimate(
            flops=4 * rows * 1536 * HEAD_DIM, bytes_accessed=10 * rows * HEAD_DIM, transcendentals=rows * 1536
        ),
    )(lo, start.reshape(steps, 1, Q_BLOCK), queries, gate, keys_before, keys_own, values_before, values_own)


def high_low(table):
    high = table.astype(np.float32).astype(ml_dtypes.bfloat16)
    low = (table - high.astype(np.float64)).astype(np.float32).astype(ml_dtypes.bfloat16)
    return np.stack((high, low))


def transform_tables(length, senders, tap_senders):
    outer = length // LANES
    k1 = np.arange(outer)
    per_sender = outer // senders
    a_signal = (np.arange(senders)[None, :] * per_sender + np.arange(per_sender)[:, None]).reshape(-1)
    per_tap = outer // tap_senders
    a_tap = (np.arange(tap_senders)[None, :] * per_tap + np.arange(per_tap)[:, None]).reshape(-1)
    b = np.arange(LANES)

    def angles(a):
        return 2.0 * np.pi * ((4 * k1[:, None] + 1) * a[None, :] % (4 * outer)) / (4 * outer)

    def forward(a):
        angle = angles(a)
        return high_low(np.concatenate((np.cos(angle), -np.sin(angle)), axis=0))

    twist = 2.0 * np.pi * ((4 * k1[:, None] + 1) * b[None, :] % (4 * length)) / (4 * length)
    inner = 2.0 * np.pi * (b[:, None] * b[None, :] % LANES) / LANES
    cos, sin = np.cos(inner), np.sin(inner)
    back = angles(a_tap).T
    return dict(
        signal=forward(a_signal),
        taps=forward(a_tap),
        twist=np.stack((np.cos(twist), -np.sin(twist))).astype(np.float32),
        inner=high_low(np.block([[cos, -sin], [sin, cos]])),
        inner_back=high_low(np.block([[cos, sin], [-sin, cos]])),
        back=high_low(np.concatenate((np.cos(back), -np.sin(back)), axis=1) / length),
    )


def table_dot(table_ref, right):
    return jnp.dot(table_ref[0], right, preferred_element_type=jnp.float32) + jnp.dot(
        table_ref[1], right, preferred_element_type=jnp.float32
    )


def dot_table(left, table_ref):
    return jnp.dot(left, table_ref[0], preferred_element_type=jnp.float32) + jnp.dot(
        left, table_ref[1], preferred_element_type=jnp.float32
    )


def spread(source_ref, spread_ref):
    rows = spread_ref.shape[1]
    for j in range(spread_ref.shape[0]):
        part = source_ref[:, :, j * LANES : (j + 1) * LANES]
        spread_ref[j] = part.reshape(rows, LANES).astype(jnp.float32)


def channel_rows(spread_ref, channel, channels):
    senders = spread_ref.shape[1] // channels
    parts = [spread_ref[j, pl.ds(channel, senders, stride=channels), :] for j in range(spread_ref.shape[0])]
    return jnp.concatenate(parts, axis=0).astype(jnp.bfloat16)


def spectrum(rows, outer_ref, twist_ref, inner_ref):
    outer = rows.shape[0]
    section = table_dot(outer_ref, rows)
    real, imag = section[:outer], section[outer:]
    turned_real = real * twist_ref[0] - imag * twist_ref[1]
    turned_imag = real * twist_ref[1] + imag * twist_ref[0]
    turned = jnp.concatenate((turned_real.astype(jnp.bfloat16), turned_imag.astype(jnp.bfloat16)), axis=1)
    return dot_table(turned, inner_ref)


def taps_kernel(taps_ref, outer_ref, twist_ref, inner_ref, out_ref, spread_ref):
    channels = taps_ref.shape[1]
    spread(taps_ref, spread_ref)
    for c in range(channels):
        out_ref[c] = spectrum(channel_rows(spread_ref, c, channels), outer_ref, twist_ref, inner_ref)


def conv_kernel(
    signal_ref, taps_ref, outer_ref, twist_ref, inner_ref, inner_back_ref, back_ref, out_ref, spread_ref, result_ref
):
    channels = signal_ref.shape[1]
    receivers = out_ref.shape[0]
    spread(signal_ref, spread_ref)
    for c in range(channels):
        signal = spectrum(channel_rows(spread_ref, c, channels), outer_ref, twist_ref, inner_ref)
        taps = taps_ref[c]
        sig_real, sig_imag = signal[:, :LANES], signal[:, LANES:]
        tap_real, tap_imag = taps[:, :LANES], taps[:, LANES:]
        prod_real = sig_real * tap_real - sig_imag * tap_imag
        prod_imag = sig_real * tap_imag + sig_imag * tap_real
        prod = jnp.concatenate((prod_real.astype(jnp.bfloat16), prod_imag.astype(jnp.bfloat16)), axis=1)
        turned = dot_table(prod, inner_back_ref)
        real, imag = turned[:, :LANES], turned[:, LANES:]
        back_real = real * twist_ref[0] + imag * twist_ref[1]
        back_imag = imag * twist_ref[0] - real * twist_ref[1]
        both = jnp.concatenate((back_real.astype(jnp.bfloat16), back_imag.astype(jnp.bfloat16)), axis=0)
        rows = table_dot(back_ref, both)
        for j in range(result_ref.shape[0]):
            result_ref[j, pl.ds(c, receivers, stride=channels), :] = rows[j * receivers : (j + 1) * receivers]
    for j in range(result_ref.shape[0]):
        part = result_ref[j].reshape(receivers, channels, LANES)
        out_ref[:, :, j * LANES : (j + 1) * LANES] = part.astype(jnp.bfloat16)


def finish_kernel(mixed_ref, gate_ref, attended_ref, attn_ref, hyena_ref):
    mixed = mixed_ref[...].reshape(HEAD_DIM, mixed_ref.shape[3]).astype(jnp.float32).T
    hyena_ref[...] = (gate_ref[...].astype(jnp.float32) * mixed).astype(jnp.bfloat16)
    attn_ref[...] = attended_ref[0]


def finish(returned, out_gate, attended):
    rows, channels = out_gate.shape
    z_size = returned.shape[0] // X_SIZE
    returned = returned.reshape(z_size, X_SIZE, returned.shape[1], rows)
    by_columns = pl.BlockSpec((rows, HEAD_DIM), lambda i: (0, i))
    return pl.pallas_call(
        finish_kernel,
        name="finish",
        grid=(channels // HEAD_DIM,),
        in_specs=[
            pl.BlockSpec((z_size, 1, returned.shape[2], rows), lambda i: (0, i, 0, 0)),
            by_columns,
            pl.BlockSpec((1, rows, HEAD_DIM), lambda i: (i, 0, 0)),
        ],
        out_specs=[by_columns, by_columns],
        out_shape=[jax.ShapeDtypeStruct((rows, channels), jnp.bfloat16)] * 2,
        compiler_params=pltpu.CompilerParams(vmem_limit_bytes=40 * 2**20),
    )(returned, out_gate, attended)


def body(queries, key_rows, values, doc_lengths, in_gate, out_gate, filter_taps):
    row_count, channels = queries.shape
    ctx = lax.axis_size("ctx")
    z_size = ctx // X_SIZE
    group_rows = X_SIZE * row_count
    reach = KV_REACH * row_count
    per_device = channels // ctx
    x_groups = [[z * X_SIZE + x for x in range(X_SIZE)] for z in range(z_size)]
    z_groups = [[z * X_SIZE + x for z in range(z_size)] for x in range(X_SIZE)]
    upward = [(i, i + X_SIZE) for i in range(ctx - X_SIZE)]
    tables = transform_tables(row_count * ctx, z_size, ctx)

    def to_heads(x):
        heads = x.reshape(row_count, X_SIZE, HEAD_DIM).transpose(1, 0, 2)
        moved = lax.all_to_all(heads, "ctx", split_axis=0, concat_axis=0, tiled=True, axis_index_groups=x_groups)
        return moved.reshape(group_rows, HEAD_DIM)

    def from_before(x):
        return lax.ppermute(x[group_rows - reach :], "ctx", upward)

    keys_own = to_heads(key_rows)
    keys_before = from_before(keys_own)
    values_own = to_heads(values)
    values_before = from_before(values_own)
    query_heads = to_heads(queries)
    gate_heads = to_heads(in_gate)

    taps = filter_taps.astype(jnp.bfloat16).reshape(X_SIZE, z_size, per_device, row_count)
    taps = taps.transpose(1, 0, 2, 3).reshape(ctx, per_device, row_count)
    taps = lax.all_to_all(taps, "ctx", split_axis=0, concat_axis=0, tiled=True)

    group_first = (lax.axis_index("ctx") // X_SIZE) * group_rows
    positions = group_first + jnp.arange(group_rows, dtype=jnp.int32)
    start = document_starts(positions, doc_lengths) - (group_first - reach)

    outer = row_count * ctx // LANES
    limit = pltpu.CompilerParams(vmem_limit_bytes=48 * 2**20)
    transform_flops = 2 * per_device * outer * LANES * (2 * outer + 4 * LANES) * 2
    taps_spectrum = pl.pallas_call(
        taps_kernel,
        name="taps_spectrum",
        out_shape=jax.ShapeDtypeStruct((per_device, outer, 2 * LANES), jnp.float32),
        scratch_shapes=[pltpu.VMEM((row_count // LANES, ctx * per_device, LANES), jnp.float32)],
        compiler_params=limit,
        cost_estimate=pl.CostEstimate(flops=transform_flops, bytes_accessed=4 * 2**20, transcendentals=0),
    )(taps, tables["taps"], tables["twist"], tables["inner"])

    attended, gated = attention(
        query_heads, gate_heads, keys_before, keys_own, values_before, values_own, start
    )
    attended = lax.all_to_all(
        attended.reshape(X_SIZE, row_count, HEAD_DIM),
        "ctx",
        split_axis=0,
        concat_axis=0,
        tiled=True,
        axis_index_groups=x_groups,
    )
    signal = lax.all_to_all(
        gated.reshape(z_size, per_device, group_rows),
        "ctx",
        split_axis=0,
        concat_axis=0,
        tiled=True,
        axis_index_groups=z_groups,
    )
    mixed = pl.pallas_call(
        conv_kernel,
        name="convolution",
        out_shape=jax.ShapeDtypeStruct((ctx, per_device, row_count), jnp.bfloat16),
        scratch_shapes=[
            pltpu.VMEM((group_rows // LANES, z_size * per_device, LANES), jnp.float32),
            pltpu.VMEM((row_count // LANES, ctx * per_device, LANES), jnp.float32),
        ],
        compiler_params=limit,
        cost_estimate=pl.CostEstimate(flops=2 * transform_flops, bytes_accessed=5 * 2**20, transcendentals=0),
    )(
        signal,
        taps_spectrum,
        tables["signal"],
        tables["twist"],
        tables["inner"],
        tables["inner_back"],
        tables["back"],
    )
    returned = lax.all_to_all(mixed, "ctx", split_axis=0, concat_axis=0, tiled=True)
    return finish(returned, out_gate, attended)


def solution(mesh):
    return jax.shard_map(
        body,
        mesh=mesh,
        in_specs=(
            P(("dp", "ctx"), "tp"),
            P(("dp", "ctx"), "tp"),
            P(("dp", "ctx"), "tp"),
            P("dp"),
            P(("dp", "ctx"), "tp"),
            P(("dp", "ctx"), "tp"),
            P(("dp", "tp"), "ctx"),
        ),
        out_specs=(P(("dp", "ctx"), "tp"), P(("dp", "ctx"), "tp")),
        check_vma=False,
    )
```

time: 582 us -> 220 us (0.38); the launches traced: 574 us -> 220 us
  other arithmetic: 165 us -> 1.81 us
  matrix products: 163 us -> 0 us
  local copies, waits for them, and re-layouts: 91 us -> 12.9 us
  blocking collectives: 0 us -> 66.9 us
  Pallas kernels: 0 us -> 36.2 us
  waiting for transfers between devices: 94.2 us -> 64 us
  starting transfers between devices: 58.4 us -> 37.5 us
    dot_general x62 -> x0, matrix products: 163 us -> none  [the longest x18 54.5 us: split_mul(): jnp.einsum(form, left_parts[1], right_parts[0], preferred_element_type=jn...]
    unnamed x1 -> x0, other arithmetic: 135 us -> none
    all_to_all x0 -> x2, blocking collectives: none -> 66.9 us  [the longest x1 42 us: body(): lax.all_to_all(gated.reshape(z_size, per_device, group_rows), 'ctx', spli...]
    pallas_call x0 -> x4, Pallas kernels: none -> 36.2 us  [the longest x1 16.5 us: attention(): pl.pallas_call(attention_kernel, name='attention', grid_spec=pltpu.Prefet...]
    unnamed x67 -> x30, local copies, waits for them, and re-layouts: 37.7 us -> 5 us
    ppermute x3 -> x2, waiting for transfers between devices: 58.7 us -> 27.4 us  [from_before(): return lax.ppermute(x[group_rows - reach:], 'ctx', upward)]
    all_to_all x5 -> x0, local copies, waits for them, and re-layouts: 25.8 us -> none  [the longest x1 22.6 us: body(): lax.all_to_all(mixed.astype(jnp.bfloat16), 'ctx', split_axis=2, concat_ax...]
    convert_element_type x2 -> x0, local copies, waits for them, and re-layouts: 19.3 us -> none  [body(): mixed.astype(jnp.bfloat16)]
  transfers between devices with their start and end apart: 6 -> 8, of which waited for: 6 -> 6; matrix products, arithmetic and copies ran while one was open for 7% -> 4% of each run, Pallas kernels for 0% -> 16%
where the time goes in v1:
time: 220 us
  blocking collectives  66.9 us (30%)
  waiting for transfers between devices  64 us (29%)
  starting transfers between devices  37.5 us (17%)
  Pallas kernels  36.2 us (16%)
  local copies, waits for them, and re-layouts  12.9 us (6%)
    all_to_all x1, blocking collectives, body(): lax.all_to_all(gated.reshape(z_size, per_device, group_rows), 'ctx', spli...  42 us
    all_to_all x4, waiting for transfers between devices, to_heads(): lax.all_to_all(heads, 'ctx', split_axis=0, concat_axis=0, tiled=True, axi...  36.6 us
    ppermute x2, waiting for transfers between devices, from_before(): return lax.ppermute(x[group_rows - reach:], 'ctx', upward)  27.4 us
    all_to_all x1, blocking collectives, body(): lax.all_to_all(mixed, 'ctx', split_axis=0, concat_axis=0, tiled=True)  24.9 us
    pallas_call x1, Pallas kernels, attention(): pl.pallas_call(attention_kernel, name='attention', grid_spec=pltpu.Prefet...  16.5 us
    all_to_all x4, starting transfers between devices, to_heads(): lax.all_to_all(heads, 'ctx', split_axis=0, concat_axis=0, tiled=True, axi...  15.5 us
    pallas_call x1, Pallas kernels, body(): pl.pallas_call(conv_kernel, name='convolution', out_shape=jax.ShapeDtypeS...  10.3 us
    all_to_all x1, starting transfers between devices, body(): taps = lax.all_to_all(taps, 'ctx', split_axis=0, concat_axis=0, tiled=True)  9.57 us
  transfers between devices with their start and end apart: 8, of which 6 were waited for; matrix products, arithmetic and copies ran while one was open for 4% of the time, Pallas kernels for 16%

profile of v1, /device:TPU:16, one launch (start us, length us, event | category | flops | bytes accessed | tf_op | source)
XLA Modules:
  0.0 220.2 jit_solution(5341223069785586387)
XLA Ops:
  0.6 0.0 copy-start
  0.6 0.0 copy-start.12
  0.7 0.0 copy-start.13
  0.7 1.1 copy-done
  1.8 1.0 bitcast_bitcast_fusion.3
  2.8 4.3 %all-to-all-start = ((bf16[4,768,128]{2,1,0:T(8,128)(2,1)}), bf16[4,768,128]{2,1,0:T(8,128)(2,1)S(1)}, u32[]{:S(2)}, u32[]{:S(2)}) async-start(bf16[4,768,128]{2,1,0:T(8,128)(2,1)} %bitcast_bitcast_fusion.3), calls=%async_computation | async-start | bytes 1572864 | tf_op jit(solution)/shard_map/all_to_all | solution.py:281
  7.1 0.0 copy-done.12
  7.1 1.0 bitcast_bitcast_fusion.1
  8.1 11.3 %all-to-all-done = bf16[4,768,128]{2,1,0:T(8,128)(2,1)S(1)} async-done(((bf16[4,768,128]{2,1,0:T(8,128)(2,1)}), bf16[4,768,128]{2,1,0:T(8,128)(2,1)S(1)}, u32[]{:S(2)}, u32[]{:S(2)}) %all-to-all-start) | async-done | bytes 786464 | tf_op jit(solution)/shard_map/all_to_all | solution.py:281
  19.4 3.5 %all-to-all-start.2 = ((bf16[4,768,128]{2,1,0:T(8,128)(2,1)}), bf16[4,768,128]{2,1,0:T(8,128)(2,1)S(1)}, u32[]{:S(2)}, u32[]{:S(2)}) async-start(bf16[4,768,128]{2,1,0:T(8,128)(2,1)} %bitcast_bitcast_fusion.1), calls=%async_computation.2 | async-start | bytes 1572864 | tf_op jit(solution)/shard_map/all_to_all | solution.py:281
  22.9 0.0 copy-done.13
  22.9 1.0 bitcast_bitcast_fusion
  23.9 10.3 %all-to-all-done.2 = bf16[4,768,128]{2,1,0:T(8,128)(2,1)S(1)} async-done(((bf16[4,768,128]{2,1,0:T(8,128)(2,1)}), bf16[4,768,128]{2,1,0:T(8,128)(2,1)S(1)}, u32[]{:S(2)}, u32[]{:S(2)}) %all-to-all-start.2) | async-done | bytes 786464 | tf_op jit(solution)/shard_map/all_to_all | solution.py:281
  34.2 3.5 %all-to-all-start.3 = ((bf16[4,768,128]{2,1,0:T(8,128)(2,1)}), bf16[4,768,128]{2,1,0:T(8,128)(2,1)S(1)}, u32[]{:S(2)}, u32[]{:S(2)}) async-start(bf16[4,768,128]{2,1,0:T(8,128)(2,1)} %bitcast_bitcast_fusion), calls=%async_computation.3 | async-start | bytes 1572864 | tf_op jit(solution)/shard_map/all_to_all | solution.py:281
  37.7 2.1 bitcast_bitcast_fusion.2
  39.9 8.0 %all-to-all-done.3 = bf16[4,768,128]{2,1,0:T(8,128)(2,1)S(1)} async-done(((bf16[4,768,128]{2,1,0:T(8,128)(2,1)}), bf16[4,768,128]{2,1,0:T(8,128)(2,1)S(1)}, u32[]{:S(2)}, u32[]{:S(2)}) %all-to-all-start.3) | async-done | bytes 786464 | tf_op jit(solution)/shard_map/all_to_all | solution.py:281
  47.8 4.2 %all-to-all-start.1 = ((bf16[4,768,128]{2,1,0:T(8,128)(2,1)}), bf16[4,768,128]{2,1,0:T(8,128)(2,1)}, u32[]{:S(2)}, u32[]{:S(2)}) async-start(bf16[4,768,128]{2,1,0:T(8,128)(2,1)} %bitcast_bitcast_fusion.2), calls=%async_computation.1 | async-start | bytes 1572864 | tf_op jit(solution)/shard_map/all_to_all | solution.py:281
  52.0 0.0 copy-start.14
  52.1 1.5 convert_element_type.3
  53.5 1.0 copy.24
  54.5 7.1 %all-to-all-done.1 = bf16[4,768,128]{2,1,0:T(8,128)(2,1)} async-done(((bf16[4,768,128]{2,1,0:T(8,128)(2,1)}), bf16[4,768,128]{2,1,0:T(8,128)(2,1)}, u32[]{:S(2)}, u32[]{:S(2)}) %all-to-all-start.1) | async-done | bytes 786464 | tf_op jit(solution)/shard_map/all_to_all | solution.py:281
  61.6 9.6 %all-to-all-start.5 = ((bf16[32,16,768]{2,1,0:T(8,128)(2,1)}), bf16[32,16,768]{2,1,0:T(8,128)(2,1)}, u32[]{:S(2)}, u32[]{:S(2)}) async-start(bf16[32,16,768]{2,1,0:T(8,128)(2,1)} %bitcast.49), calls=%async_computation.5 | async-start | bytes 1572864 | tf_op jit(solution)/shard_map/all_to_all | solution.py:296
  71.2 0.0 copy-done.14
  71.2 0.1 select_reduce_fusion.1
  71.3 0.9 slice.20
  72.1 4.4 %collective-permute-start = (bf16[2304,128]{1,0:T(8,128)(2,1)}, bf16[2304,128]{1,0:T(8,128)(2,1)}, u32[]{:S(2)}, u32[]{:S(2)}) collective-permute-start(bf16[2304,128]{1,0:T(8,128)(2,1)} %bitcast.6), channel_id=1, source_target_pairs={{0,32},{8,40},{16,48},{24,56},{32,64},{40,72},{48,80},{56,88},{64,... | collective-permute-start | bytes 1769480 | tf_op jit(solution)/shard_map/ppermute | solution.py:285
  76.6 0.8 slice.21
  77.4 3.4 %collective-permute-start.1 = (bf16[2304,128]{1,0:T(8,128)(2,1)}, bf16[2304,128]{1,0:T(8,128)(2,1)}, u32[]{:S(2)}, u32[]{:S(2)}) collective-permute-start(bf16[2304,128]{1,0:T(8,128)(2,1)} %bitcast.9), channel_id=1, source_target_pairs={{0,32},{8,40},{16,48},{24,56},{32,64},{40,72},{48,80},{56,88},{64,... | collective-permute-start | bytes 1769480 | tf_op jit(solution)/shard_map/ppermute | solution.py:285
  80.8 0.2 select_reduce_fusion
  81.0 0.1 slice.15
  81.1 18.9 %collective-permute-done.kp_ref = bf16[2304,128]{1,0:T(8,128)(2,1)} collective-permute-done((bf16[2304,128]{1,0:T(8,128)(2,1)}, bf16[2304,128]{1,0:T(8,128)(2,1)}, u32[]{:S(2)}, u32[]{:S(2)}) %collective-permute-start) | collective-permute-done | bytes 589856 | tf_op jit(solution)/shard_map/ppermute | solution.py:285
  100.0 8.5 %collective-permute-done.1.vp_ref = bf16[2304,128]{1,0:T(8,128)(2,1)} collective-permute-done((bf16[2304,128]{1,0:T(8,128)(2,1)}, bf16[2304,128]{1,0:T(8,128)(2,1)}, u32[]{:S(2)}, u32[]{:S(2)}) %collective-permute-start.1) | collective-permute-done | bytes 589856 | tf_op jit(solution)/shard_map/ppermute | solution.py:285
  108.5 16.5 %attention.1 = (bf16[3072,128]{1,0:T(8,128)(2,1)S(1)}, bf16[128,3072]{1,0:T(8,128)(2,1)S(1)}) custom-call(s32[12]{0:T(128)S(1)} %and_select_fusion.lo_ref, s32[12,1,256]{2,1,0:T(1,128)S(1)} %bitcast.48, bf16[3072,128]{1,0:T(8,128)(2,1)S(1)} %bitcast.45, bf16[3072,128]{1,0:T(8,128)(2,1)} %bitcast.4.gate_ref, bf16[2304,128]{1,0:T(8,128)(2,1)} %collective-permute-done.kp_ref, ...), custom_call_target="tpu_custom_call" | custom-call | flops 2415919104 | bytes 3932160 | tf_op jit(solution)/shard_map/attention/pallas_call | solution.py:101
  125.0 0.0 copy-start.1
  125.0 0.9 copy-done.1
  125.9 0.9 copy-done.2
  126.8 0.0 all-to-all-done.5.taps_ref
  126.8 42.0 %all_to_all.40.signal_ref = bf16[8,16,3072]{2,1,0:T(8,128)(2,1)} all-to-all(bf16[8,16,3072]{2,1,0:T(8,128)(2,1)} %bitcast.47), channel_id=1, replica_groups={{0,32,64,96,128,160,192,224},{8,40,72,104,136,168,200,232},{16,48,80,11..., dimensions={0} | all-to-all | bytes 1572864 | tf_op jit(solution)/shard_map/all_to_all | solution.py:325
  168.8 4.6 %all-to-all-start.7 = ((bf16[4,768,128]{2,1,0:T(8,128)(2,1)}), bf16[4,768,128]{2,1,0:T(8,128)(2,1)S(1)}, u32[]{:S(2)}, u32[]{:S(2)}) async-start(bf16[4,768,128]{2,1,0:T(8,128)(2,1)} %bitcast.46), calls=%async_computation.7 | async-start | bytes 1572864 | tf_op jit(solution)/shard_map/all_to_all | solution.py:317
  173.4 0.0 copy-done.6
  173.4 0.0 copy-start.11
  173.4 0.9 copy-done.11
  174.3 7.5 %taps_spectrum.1.taps_ref = f32[16,192,256]{2,1,0:T(8,128)S(1)} custom-call(bf16[32,16,768]{2,1,0:T(8,128)(2,1)} %all-to-all-done.5.taps_ref, bf16[2,384,192]{2,1,0:T(8,128)(2,1)S(1)} %copy-done.6, f32[2,192,128]{2,1,0:T(8,128)S(1)} %copy-done.11, bf16[2,256,256]{2,1,0:T(8,128)(2,1)S(1)} %copy-done.8), custom_call_target="tpu_custom_call" | custom-call | flops 1409286144 | bytes 4194304 | tf_op jit(solution)/shard_map/taps_spectrum/pallas_call | solution.py:305
  181.9 10.3 %convolution.1 = bf16[32,16,768]{2,1,0:T(8,128)(2,1)S(1)} custom-call(bf16[8,16,3072]{2,1,0:T(8,128)(2,1)S(1)} %copy-done.3, f32[16,192,256]{2,1,0:T(8,128)S(1)} %taps_spectrum.1.taps_ref, bf16[2,384,192]{2,1,0:T(8,128)(2,1)S(1)} %copy-done.5, f32[2,192,128]{2,1,0:T(8,128)S(1)} %copy-done.11, bf16[2,256,256]{2,1,0:T(8,128)(2,1)S(1)} %copy-done.9, ...), custom_call_target="tpu_custom_call" | custom-call | flops 2818572288 | bytes 5242880 | tf_op jit(solution)/shard_map/convolution/pallas_call | solution.py:333
  192.2 0.0 all-to-all-done.7.attended_ref
  192.2 24.9 %all_to_all.41 = bf16[32,16,768]{2,1,0:T(8,128)(2,1)S(1)} all-to-all(bf16[32,16,768]{2,1,0:T(8,128)(2,1)S(1)} %convolution.1), channel_id=1, replica_groups=mesh['ctx'=32,'tp'=4,'dp'=2] {'ctx'}, dimensions={0} | all-to-all | bytes 1572864 | tf_op jit(solution)/shard_map/all_to_all | solution.py:352
  217.1 1.1 copy-done.4
  218.2 2.0 finish.1
  (18 shorter events, 0.0 us)
Async XLA Ops:
  0.6 1.1 copy-start
  0.6 6.4 %copy-start.12 = (bf16[768,512]{1,0:T(8,128)(2,1)S(1)}, bf16[768,512]{1,0:T(8,128)(2,1)}, u32[]{:S(2)}) copy-start(bf16[768,512]{1,0:T(8,128)(2,1)} %param.14) | copy-start | bytes 2359300
  0.7 22.2 %copy-start.13 = (bf16[768,512]{1,0:T(8,128)(2,1)S(1)}, bf16[768,512]{1,0:T(8,128)(2,1)}, u32[]{:S(2)}) copy-start(bf16[768,512]{1,0:T(8,128)(2,1)} %param.15) | copy-start | bytes 2359300
  2.8 16.6 %all-to-all-start = ((bf16[4,768,128]{2,1,0:T(8,128)(2,1)}), bf16[4,768,128]{2,1,0:T(8,128)(2,1)S(1)}, u32[]{:S(2)}, u32[]{:S(2)}) async-start(bf16[4,768,128]{2,1,0:T(8,128)(2,1)} %bitcast_bitcast_fusion.3), calls=%async_computation | async-start | bytes 1572864 | tf_op jit(solution)/shard_map/all_to_all | solution.py:281
  19.4 14.8 %all-to-all-start.2 = ((bf16[4,768,128]{2,1,0:T(8,128)(2,1)}), bf16[4,768,128]{2,1,0:T(8,128)(2,1)S(1)}, u32[]{:S(2)}, u32[]{:S(2)}) async-start(bf16[4,768,128]{2,1,0:T(8,128)(2,1)} %bitcast_bitcast_fusion.1), calls=%async_computation.2 | async-start | bytes 1572864 | tf_op jit(solution)/shard_map/all_to_all | solution.py:281
  34.2 13.6 %all-to-all-start.3 = ((bf16[4,768,128]{2,1,0:T(8,128)(2,1)}), bf16[4,768,128]{2,1,0:T(8,128)(2,1)S(1)}, u32[]{:S(2)}, u32[]{:S(2)}) async-start(bf16[4,768,128]{2,1,0:T(8,128)(2,1)} %bitcast_bitcast_fusion), calls=%async_computation.3 | async-start | bytes 1572864 | tf_op jit(solution)/shard_map/all_to_all | solution.py:281
  47.8 13.7 %all-to-all-start.1 = ((bf16[4,768,128]{2,1,0:T(8,128)(2,1)}), bf16[4,768,128]{2,1,0:T(8,128)(2,1)}, u32[]{:S(2)}, u32[]{:S(2)}) async-start(bf16[4,768,128]{2,1,0:T(8,128)(2,1)} %bitcast_bitcast_fusion.2), calls=%async_computation.1 | async-start | bytes 1572864 | tf_op jit(solution)/shard_map/all_to_all | solution.py:281
  52.0 19.1 %copy-start.14 = (s32[64]{0:T(128)S(1)}, s32[64]{0:T(128)}, u32[]{:S(2)}) copy-start(s32[64]{0:T(128)} %param.16) | copy-start | bytes 772
  61.6 65.2 %all-to-all-start.5 = ((bf16[32,16,768]{2,1,0:T(8,128)(2,1)}), bf16[32,16,768]{2,1,0:T(8,128)(2,1)}, u32[]{:S(2)}, u32[]{:S(2)}) async-start(bf16[32,16,768]{2,1,0:T(8,128)(2,1)} %bitcast.49), calls=%async_computation.5 | async-start | bytes 1572864 | tf_op jit(solution)/shard_map/all_to_all | solution.py:296
  72.1 27.9 %collective-permute-start = (bf16[2304,128]{1,0:T(8,128)(2,1)}, bf16[2304,128]{1,0:T(8,128)(2,1)}, u32[]{:S(2)}, u32[]{:S(2)}) collective-permute-start(bf16[2304,128]{1,0:T(8,128)(2,1)} %bitcast.6), channel_id=1, source_target_pairs={{0,32},{8,40},{16,48},{24,56},{32,64},{40,72},{48,80},{56,88},{64,... | collective-permute-start | bytes 1769480 | tf_op jit(solution)/shard_map/ppermute | solution.py:285
  77.4 31.1 %collective-permute-start.1 = (bf16[2304,128]{1,0:T(8,128)(2,1)}, bf16[2304,128]{1,0:T(8,128)(2,1)}, u32[]{:S(2)}, u32[]{:S(2)}) collective-permute-start(bf16[2304,128]{1,0:T(8,128)(2,1)} %bitcast.9), channel_id=1, source_target_pairs={{0,32},{8,40},{16,48},{24,56},{32,64},{40,72},{48,80},{56,88},{64,... | collective-permute-start | bytes 1769480 | tf_op jit(solution)/shard_map/ppermute | solution.py:285
  125.0 0.9 copy-start.1
  125.9 0.9 copy-start.2
  126.8 46.6 %copy-start.6 = (bf16[2,384,192]{2,1,0:T(8,128)(2,1)S(1)}, bf16[2,384,192]{2,1,0:T(8,128)(2,1)}, u32[]{:S(2)}) copy-start(bf16[2,384,192]{2,1,0:T(8,128)(2,1)} %constant.55.clone.outer_ref) | copy-start | bytes 884740
  126.8 46.6 %copy-start.8 = (bf16[2,256,256]{2,1,0:T(8,128)(2,1)S(1)}, bf16[2,256,256]{2,1,0:T(8,128)(2,1)}, u32[]{:S(2)}) copy-start(bf16[2,256,256]{2,1,0:T(8,128)(2,1)} %constant.57.clone.inner_ref) | copy-start | bytes 786436
  168.8 13.0 %copy-start.5 = (bf16[2,384,192]{2,1,0:T(8,128)(2,1)S(1)}, bf16[2,384,192]{2,1,0:T(8,128)(2,1)}, u32[]{:S(2)}) copy-start(bf16[2,384,192]{2,1,0:T(8,128)(2,1)} %constant.58.clone.outer_ref) | copy-start | bytes 884740
  168.8 23.4 %all-to-all-start.7 = ((bf16[4,768,128]{2,1,0:T(8,128)(2,1)}), bf16[4,768,128]{2,1,0:T(8,128)(2,1)S(1)}, u32[]{:S(2)}, u32[]{:S(2)}) async-start(bf16[4,768,128]{2,1,0:T(8,128)(2,1)} %bitcast.46), calls=%async_computation.7 | async-start | bytes 1572864 | tf_op jit(solution)/shard_map/all_to_all | solution.py:317
  173.4 0.9 copy-start.11
  174.3 7.5 %copy-start.3 = (bf16[8,16,3072]{2,1,0:T(8,128)(2,1)S(1)}, bf16[8,16,3072]{2,1,0:T(8,128)(2,1)}, u32[]{:S(2)}) copy-start(bf16[8,16,3072]{2,1,0:T(8,128)(2,1)} %all_to_all.40.signal_ref) | copy-start | bytes 2359300
  174.3 7.5 %copy-start.7 = (bf16[2,192,384]{2,1,0:T(8,128)(2,1)S(1)}, bf16[2,192,384]{2,1,0:T(8,128)(2,1)}, u32[]{:S(2)}) copy-start(bf16[2,192,384]{2,1,0:T(8,128)(2,1)} %constant.60.clone.back_ref) | copy-start | bytes 884740
  174.3 7.5 %copy-start.9 = (bf16[2,256,256]{2,1,0:T(8,128)(2,1)S(1)}, bf16[2,256,256]{2,1,0:T(8,128)(2,1)}, u32[]{:S(2)}) copy-start(bf16[2,256,256]{2,1,0:T(8,128)(2,1)} %constant.57.clone.inner_ref) | copy-start | bytes 786436
  174.3 7.5 %copy-start.10 = (bf16[2,256,256]{2,1,0:T(8,128)(2,1)S(1)}, bf16[2,256,256]{2,1,0:T(8,128)(2,1)}, u32[]{:S(2)}) copy-start(bf16[2,256,256]{2,1,0:T(8,128)(2,1)} %constant.59.clone.inner_back_ref) | copy-start | bytes 786436
  217.1 1.1 copy-start.4

commit v2 on v1

--- a/solution.py
+++ b/solution.py
@@ -13,8 +13,8 @@
 HEAD_DIM = 128
 KV_REACH = 3
 X_SIZE = 4
-Q_BLOCK = 256
-K_BLOCK = 256
+Q_BLOCK = 768
+K_BLOCK = 384
 LANES = 128
 masked_score = -1e30
 
@@ -42,12 +42,12 @@
         keys[front : front + reach] = kp_ref[...]
         keys[front + reach :] = ko_ref[...]
         for ref, base in ((vp_ref, front), (vo_ref, front + reach)):
-            for row in range(0, ref.shape[0], 256):
+            for row in range(0, ref.shape[0], LANES):
                 block, at = divmod(base + row, K_BLOCK)
-                part = ref[row : row + 256].astype(jnp.float32).T
-                values_t[block, :, at : at + 256] = part.astype(jnp.bfloat16)
-
-    queries = q_ref[...]
+                part = ref[row : row + LANES].astype(jnp.float32).T
+                values_t[block, :, at : at + LANES] = part.astype(jnp.bfloat16)
+
+    queries = q_ref[0, 0]
     first = front + reach + step * Q_BLOCK
     start = start_ref[0]
     query_index = first + lax.broadcasted_iota(jnp.int32, (1, Q_BLOCK), 1)
@@ -85,11 +85,12 @@
     )
     attended = (weighted * (1.0 / total)).astype(jnp.bfloat16).astype(jnp.float32)
     out_ref[...] = attended.T.astype(jnp.bfloat16)
-    gated_ref[...] = (attended * gate_ref[...].astype(jnp.float32).T).astype(jnp.bfloat16)
-
-
-def attention(queries, gate, keys_before, keys_own, values_before, values_own, start):
-    rows = queries.shape[0]
+    gated_ref[...] = (attended * gate_ref[0, 0].astype(jnp.float32).T).astype(jnp.bfloat16)
+
+
+def attention(queries_gate, keys_before, keys_own, values_before, values_own, start):
+    rows = keys_own.shape[0]
+    per_block = queries_gate.shape[2] // Q_BLOCK
     reach = keys_before.shape[0]
     front = -reach % K_BLOCK
     steps = rows // Q_BLOCK
@@ -106,8 +107,8 @@
             grid=(steps,),
             in_specs=[
                 pl.BlockSpec((1, 1, Q_BLOCK), lambda i, lo: (i, 0, 0)),
-                pl.BlockSpec((Q_BLOCK, HEAD_DIM), by_rows),
-                pl.BlockSpec((Q_BLOCK, HEAD_DIM), by_rows),
+                pl.BlockSpec((1, 1, Q_BLOCK, HEAD_DIM), lambda i, lo: (i // per_block, 0, i % per_block, 0)),
+                pl.BlockSpec((1, 1, Q_BLOCK, HEAD_DIM), lambda i, lo: (i // per_block, 1, i % per_block, 0)),
                 pl.BlockSpec((reach, HEAD_DIM), whole),
                 pl.BlockSpec((rows, HEAD_DIM), whole),
                 pl.BlockSpec((reach, HEAD_DIM), whole),
@@ -128,9 +129,9 @@
         ],
         compiler_params=pltpu.CompilerParams(vmem_limit_bytes=40 * 2**20),
         cost_estimate=pl.CostEstimate(
-            flops=4 * rows * 1536 * HEAD_DIM, bytes_accessed=10 * rows * HEAD_DIM, transcendentals=rows * 1536
+            flops=16 * 10**9, bytes_accessed=10 * rows * HEAD_DIM, transcendentals=rows * 1536
         ),
-    )(lo, start.reshape(steps, 1, Q_BLOCK), queries, gate, keys_before, keys_own, values_before, values_own)
+    )(lo, start.reshape(steps, 1, Q_BLOCK), queries_gate, queries_gate, keys_before, keys_own, values_before, values_own)
 
 
 def high_low(table):
@@ -276,24 +277,30 @@
     upward = [(i, i + X_SIZE) for i in range(ctx - X_SIZE)]
     tables = transform_tables(row_count * ctx, z_size, ctx)
 
-    def to_heads(x):
-        heads = x.reshape(row_count, X_SIZE, HEAD_DIM).transpose(1, 0, 2)
-        moved = lax.all_to_all(heads, "ctx", split_axis=0, concat_axis=0, tiled=True, axis_index_groups=x_groups)
-        return moved.reshape(group_rows, HEAD_DIM)
+    def by_head(x):
+        return x.reshape(row_count, X_SIZE, HEAD_DIM).transpose(1, 0, 2)
+
+    def exchanged(x, groups=None):
+        return lax.all_to_all(x, "ctx", split_axis=0, concat_axis=0, tiled=True, axis_index_groups=groups)
 
     def from_before(x):
-        return lax.ppermute(x[group_rows - reach :], "ctx", upward)
-
-    keys_own = to_heads(key_rows)
-    keys_before = from_before(keys_own)
-    values_own = to_heads(values)
-    values_before = from_before(values_own)
-    query_heads = to_heads(queries)
-    gate_heads = to_heads(in_gate)
+        return lax.ppermute(x.reshape(group_rows, HEAD_DIM)[group_rows - reach :], "ctx", upward)
 
     taps = filter_taps.astype(jnp.bfloat16).reshape(X_SIZE, z_size, per_device, row_count)
     taps = taps.transpose(1, 0, 2, 3).reshape(ctx, per_device, row_count)
-    taps = lax.all_to_all(taps, "ctx", split_axis=0, concat_axis=0, tiled=True)
+
+    keys_own = exchanged(by_head(key_rows), x_groups)
+    keys_own, value_heads = lax.optimization_barrier((keys_own, by_head(values)))
+    keys_before = from_before(keys_own)
+    values_own = exchanged(value_heads, x_groups)
+    queries_gate = jnp.stack((by_head(queries), by_head(in_gate)), axis=1)
+    values_own, keys_before, queries_gate = lax.optimization_barrier((values_own, keys_before, queries_gate))
+    values_before = from_before(values_own)
+    queries_gate = exchanged(queries_gate, x_groups)
+    queries_gate, values_before, taps = lax.optimization_barrier((queries_gate, values_before, taps))
+    taps = exchanged(taps)
+    keys_own = keys_own.reshape(group_rows, HEAD_DIM)
+    values_own = values_own.reshape(group_rows, HEAD_DIM)
 
     group_first = (lax.axis_index("ctx") // X_SIZE) * group_rows
     positions = group_first + jnp.arange(group_rows, dtype=jnp.int32)
@@ -301,35 +308,19 @@
 
     outer = row_count * ctx // LANES
     limit = pltpu.CompilerParams(vmem_limit_bytes=48 * 2**20)
-    transform_flops = 2 * per_device * outer * LANES * (2 * outer + 4 * LANES) * 2
+    attended, gated = attention(queries_gate, keys_before, keys_own, values_before, values_own, start)
+    gated, taps = lax.optimization_barrier((gated, taps))
     taps_spectrum = pl.pallas_call(
         taps_kernel,
         name="taps_spectrum",
         out_shape=jax.ShapeDtypeStruct((per_device, outer, 2 * LANES), jnp.float32),
         scratch_shapes=[pltpu.VMEM((row_count // LANES, ctx * per_device, LANES), jnp.float32)],
         compiler_params=limit,
-        cost_estimate=pl.CostEstimate(flops=transform_flops, bytes_accessed=4 * 2**20, transcendentals=0),
+        cost_estimate=pl.CostEstimate(flops=6 * 10**9, bytes_accessed=4 * 2**20, transcendentals=0),
     )(taps, tables["taps"], tables["twist"], tables["inner"])
-
-    attended, gated = attention(
-        query_heads, gate_heads, keys_before, keys_own, values_before, values_own, start
-    )
-    attended = lax.all_to_all(
-        attended.reshape(X_SIZE, row_count, HEAD_DIM),
-        "ctx",
-        split_axis=0,
-        concat_axis=0,
-        tiled=True,
-        axis_index_groups=x_groups,
-    )
-    signal = lax.all_to_all(
-        gated.reshape(z_size, per_device, group_rows),
-        "ctx",
-        split_axis=0,
-        concat_axis=0,
-        tiled=True,
-        axis_index_groups=z_groups,
-    )
+    signal = exchanged(gated.reshape(z_size, per_device, group_rows), z_groups)
+    signal, attended = lax.optimization_barrier((signal, attended.reshape(X_SIZE, row_count, HEAD_DIM)))
+    attended = exchanged(attended, x_groups)
     mixed = pl.pallas_call(
         conv_kernel,
         name="convolution",
@@ -339,7 +330,7 @@
             pltpu.VMEM((row_count // LANES, ctx * per_device, LANES), jnp.float32),
         ],
         compiler_params=limit,
-        cost_estimate=pl.CostEstimate(flops=2 * transform_flops, bytes_accessed=5 * 2**20, transcendentals=0),
+        cost_estimate=pl.CostEstimate(flops=9 * 10**9, bytes_accessed=5 * 2**20, transcendentals=0),
     )(
         signal,
         taps_spectrum,
@@ -349,7 +340,8 @@
         tables["inner_back"],
         tables["back"],
     )
-    returned = lax.all_to_all(mixed, "ctx", split_axis=0, concat_axis=0, tiled=True)
+    mixed, attended = lax.optimization_barrier((mixed, attended))
+    returned = exchanged(mixed)
     return finish(returned, out_gate, attended)
 
 

time: 220 us -> 170 us (0.77); the launches traced: 220 us -> 167 us
  blocking collectives: 66.9 us -> 21.8 us
  waiting for transfers between devices: 64 us -> 32.5 us
  local copies, waits for them, and re-layouts: 12.9 us -> 26.2 us
  starting transfers between devices: 37.5 us -> 48.5 us
  Pallas kernels: 36.2 us -> 32.9 us
  other arithmetic: 1.81 us -> 4.49 us
    all_to_all x2 -> x1, blocking collectives: 66.9 us -> 21.8 us  [exchanged(): lax.all_to_all(x, 'ctx', split_axis=0, concat_axis=0, tiled=True, axis_in...]
    ppermute x2, waiting for transfers between devices: 27.4 us -> 8.12 us  [from_before(): lax.ppermute(x.reshape(group_rows, HEAD_DIM)[group_rows - reach:], 'ctx',...]
    unnamed x30 -> x40, local copies, waits for them, and re-layouts: 5 us -> 17.7 us
    all_to_all x6, waiting for transfers between devices: 36.6 us -> 24.4 us  [exchanged(): lax.all_to_all(x, 'ctx', split_axis=0, concat_axis=0, tiled=True, axis_in...]
    all_to_all x6, starting transfers between devices: 29.6 us -> 40.8 us  [exchanged(): lax.all_to_all(x, 'ctx', split_axis=0, concat_axis=0, tiled=True, axis_in...]
    reshape x0 -> x2, local copies, waits for them, and re-layouts: none -> 4.58 us  [by_head(): return x.reshape(row_count, X_SIZE, HEAD_DIM).transpose(1, 0, 2)]
    transpose x4 -> x2, local copies, waits for them, and re-layouts: 5.2 us -> 2.06 us  [by_head(): return x.reshape(row_count, X_SIZE, HEAD_DIM).transpose(1, 0, 2)]
    another operation x0 -> x1, other arithmetic: none -> 2.69 us  [body(): queries_gate = jnp.stack((by_head(queries), by_head(in_gate)), axis=1)]
  transfers between devices with their start and end apart: 8 -> 8, of which waited for: 6 -> 5; matrix products, arithmetic and copies ran while one was open for 4% -> 10% of each run, Pallas kernels for 16% -> 18%
where the time goes in v2:
time: 170 us; the launch traced here: 167 us
  starting transfers between devices  48.5 us (29%)
  Pallas kernels  32.9 us (19%)
  waiting for transfers between devices  32.5 us (19%)
  local copies, waits for them, and re-layouts  26.2 us (15%)
  blocking collectives  21.8 us (13%)
  other arithmetic  4.49 us (3%)
    all_to_all x6, starting transfers between devices, exchanged(): lax.all_to_all(x, 'ctx', split_axis=0, concat_axis=0, tiled=True, axis_in...  40.8 us
    all_to_all x6, waiting for transfers between devices, exchanged(): lax.all_to_all(x, 'ctx', split_axis=0, concat_axis=0, tiled=True, axis_in...  24.4 us
    all_to_all x1, blocking collectives, exchanged(): lax.all_to_all(x, 'ctx', split_axis=0, concat_axis=0, tiled=True, axis_in...  21.8 us
    unnamed x40, local copies, waits for them, and re-layouts  17.7 us
    pallas_call x1, Pallas kernels, attention(): pl.pallas_call(attention_kernel, name='attention', grid_spec=pltpu.Prefet...  14.4 us
    pallas_call x1, Pallas kernels, body(): pl.pallas_call(conv_kernel, name='convolution', out_shape=jax.ShapeDtypeS...  10.3 us
    ppermute x2, waiting for transfers between devices, from_before(): lax.ppermute(x.reshape(group_rows, HEAD_DIM)[group_rows - reach:], 'ctx',...  8.12 us
    ppermute x2, starting transfers between devices, from_before(): lax.ppermute(x.reshape(group_rows, HEAD_DIM)[group_rows - reach:], 'ctx',...  7.67 us
  transfers between devices with their start and end apart: 8, of which 5 were waited for; matrix products, arithmetic and copies ran while one was open for 10% of the time, Pallas kernels for 18%

profile of v2, /device:TPU:16, one launch (start us, length us, event | category | flops | bytes accessed | tf_op | source)
XLA Modules:
  0.0 167.2 jit_solution(2418715468708729699)
XLA Ops:
  0.6 0.0 copy-start
  0.7 1.1 copy-done
  1.8 1.0 bitcast_bitcast_fusion.1
  2.8 4.3 %all-to-all-start = ((bf16[4,768,128]{2,1,0:T(8,128)(2,1)}), bf16[4,768,128]{2,1,0:T(8,128)(2,1)S(1)}, u32[]{:S(2)}, u32[]{:S(2)}) async-start(bf16[4,768,128]{2,1,0:T(8,128)(2,1)} %bitcast_bitcast_fusion.1), calls=%async_computation | async-start | bytes 1572864 | tf_op jit(solution)/shard_map/all_to_all | solution.py:284
  7.1 1.0 bitcast_bitcast_fusion
  8.1 11.2 %all-to-all-done = bf16[4,768,128]{2,1,0:T(8,128)(2,1)S(1)} async-done(((bf16[4,768,128]{2,1,0:T(8,128)(2,1)}), bf16[4,768,128]{2,1,0:T(8,128)(2,1)S(1)}, u32[]{:S(2)}, u32[]{:S(2)}) %all-to-all-start) | async-done | bytes 786464 | tf_op jit(solution)/shard_map/all_to_all | solution.py:284
  19.4 3.5 %all-to-all-start.1 = ((bf16[4,768,128]{2,1,0:T(8,128)(2,1)}), bf16[4,768,128]{2,1,0:T(8,128)(2,1)S(1)}, u32[]{:S(2)}, u32[]{:S(2)}) async-start(bf16[4,768,128]{2,1,0:T(8,128)(2,1)} %bitcast_bitcast_fusion), calls=%async_computation.1 | async-start | bytes 1572864 | tf_op jit(solution)/shard_map/all_to_all | solution.py:284
  22.9 3.9 %collective-permute-start = (bf16[2304,128]{1,0:T(8,128)(2,1)S(1)}, bf16[2304,128]{1,0:T(8,128)(2,1)S(1)}, u32[]{:S(2)}, u32[]{:S(2)}) collective-permute-start(bf16[2304,128]{1,0:T(8,128)(2,1)S(1)} %bitcast.45), channel_id=1, source_target_pairs={{0,32},{8,40},{16,48},{24,56},{32,64},{40,72},{48,80},{56,88},{64,... | collective-permute-start | bytes 1769480 | tf_op jit(solution)/shard_map/ppermute | solution.py:287
  26.8 2.3 %copy.27 = bf16[768,512]{0,1:T(8,128)(2,1)} copy(bf16[768,512]{1,0:T(8,128)(2,1)} %param.13) | data formatting | bytes 1572864 | tf_op args[0]
  29.1 2.3 %copy.28 = bf16[768,4,128]{2,0,1:T(8,128)(2,1)} copy(bf16[768,4,128]{0,2,1:T(8,128)(2,1)} %bitcast.40) | data formatting | bytes 1572864 | tf_op jit(solution)/shard_map/reshape | solution.py:281
  31.4 2.3 %copy.29 = bf16[768,512]{0,1:T(8,128)(2,1)} copy(bf16[768,512]{1,0:T(8,128)(2,1)} %param.17) | data formatting | bytes 1572864 | tf_op args[4]
  33.7 2.3 %copy.30 = bf16[768,4,128]{2,0,1:T(8,128)(2,1)} copy(bf16[768,4,128]{0,2,1:T(8,128)(2,1)} %bitcast.41) | data formatting | bytes 1572864 | tf_op jit(solution)/shard_map/reshape | solution.py:281
  35.9 2.7 %pad_maximum_fusion = bf16[4,2,768,128]{3,2,1,0:T(8,128)(2,1)} fusion(bf16[4,1,768,128]{3,2,1,0:T(8,128)(2,1)} %bitcast.43, bf16[4,1,768,128]{3,2,1,0:T(8,128)(2,1)} %bitcast.42), kind=kLoop, calls=%fused_computation | loop fusion | flops 786432 | bytes 3145728 | tf_op jit(solution)/shard_map/stack | solution.py:296
  38.6 0.0 copy-start.3
  38.7 0.8 copy-done.3
  39.5 4.8 %all-to-all-start.2 = ((bf16[4,2,768,128]{3,2,1,0:T(8,128)(2,1)}), bf16[4,2,768,128]{3,2,1,0:T(8,128)(2,1)}, u32[]{:S(2)}, u32[]{:S(2)}) async-start(bf16[4,2,768,128]{3,2,1,0:T(8,128)(2,1)} %pad_maximum_fusion), calls=%async_computation.2 | async-start | bytes 3145728 | tf_op jit(solution)/shard_map/all_to_all | solution.py:284
  44.2 0.9 slice.18
  45.1 3.8 %collective-permute-start.1 = (bf16[2304,128]{1,0:T(8,128)(2,1)}, bf16[2304,128]{1,0:T(8,128)(2,1)S(1)}, u32[]{:S(2)}, u32[]{:S(2)}) collective-permute-start(bf16[2304,128]{1,0:T(8,128)(2,1)} %bitcast.10), channel_id=1, source_target_pairs={{0,32},{8,40},{16,48},{24,56},{32,64},{40,72},{48,80},{56,88},{64,... | collective-permute-start | bytes 1769480 | tf_op jit(solution)/shard_map/ppermute | solution.py:287
  48.9 0.1 select_reduce_fusion.1
  49.0 0.2 select_reduce_fusion
  49.2 0.1 slice.15
  49.3 1.5 convert_element_type.3
  50.8 1.0 copy.31
  51.8 8.1 %collective-permute-done.1.vp_ref = bf16[2304,128]{1,0:T(8,128)(2,1)S(1)} collective-permute-done((bf16[2304,128]{1,0:T(8,128)(2,1)}, bf16[2304,128]{1,0:T(8,128)(2,1)S(1)}, u32[]{:S(2)}, u32[]{:S(2)}) %collective-permute-start.1) | collective-permute-done | bytes 589856 | tf_op jit(solution)/shard_map/ppermute | solution.py:287
  59.9 0.8 copy-done.5
  60.7 2.7 %all-to-all-done.2.q_ref.gate_ref = bf16[4,2,768,128]{3,2,1,0:T(8,128)(2,1)} async-done(((bf16[4,2,768,128]{3,2,1,0:T(8,128)(2,1)}), bf16[4,2,768,128]{3,2,1,0:T(8,128)(2,1)}, u32[]{:S(2)}, u32[]{:S(2)}) %all-to-all-start.2) | async-done | bytes 1572896 | tf_op jit(solution)/shard_map/all_to_all | solution.py:284
  63.4 11.1 %all-to-all-start.3 = ((bf16[32,16,768]{2,1,0:T(8,128)(2,1)}), bf16[32,16,768]{2,1,0:T(8,128)(2,1)S(1)}, u32[]{:S(2)}, u32[]{:S(2)}) async-start(bf16[32,16,768]{2,1,0:T(8,128)(2,1)} %bitcast.39), calls=%async_computation.3 | async-start | bytes 1572864 | tf_op jit(solution)/shard_map/all_to_all | solution.py:284
  74.6 0.0 copy-start.4
  74.6 1.1 copy-done.4
  75.6 1.1 copy-done.6
  76.7 14.4 %attention.1 = (bf16[3072,128]{1,0:T(8,128)(2,1)}, bf16[128,3072]{1,0:T(8,128)(2,1)S(1)}) custom-call(s32[4]{0:T(128)S(1)} %and_select_fusion.lo_ref, s32[4,1,768]{2,1,0:T(1,128)S(1)} %bitcast.38, bf16[4,2,768,128]{3,2,1,0:T(8,128)(2,1)} %all-to-all-done.2.q_ref.gate_ref, bf16[4,2,768,128]{3,2,1,0:T(8,128)(2,1)} %all-to-all-done.2.q_ref.gate_ref, ...), custom_call_target="tpu_custom_call" | custom-call | flops 16000000000 | bytes 3932160 | tf_op jit(solution)/shard_map/attention/pallas_call | solution.py:102
  91.1 0.9 copy-done.1
  91.9 2.2 %all-to-all-done.3.taps_ref = bf16[32,16,768]{2,1,0:T(8,128)(2,1)S(1)} async-done(((bf16[32,16,768]{2,1,0:T(8,128)(2,1)}), bf16[32,16,768]{2,1,0:T(8,128)(2,1)S(1)}, u32[]{:S(2)}, u32[]{:S(2)}) %all-to-all-start.3) | async-done | bytes 786464 | tf_op jit(solution)/shard_map/all_to_all | solution.py:284
  94.1 12.9 %all-to-all-start.4 = ((bf16[8,16,3072]{2,1,0:T(8,128)(2,1)}), bf16[8,16,3072]{2,1,0:T(8,128)(2,1)S(1)}, u32[]{:S(2)}, u32[]{:S(2)}) async-start(bf16[8,16,3072]{2,1,0:T(8,128)(2,1)} %bitcast.37), calls=%async_computation.4 | async-start | bytes 1572864 | tf_op jit(solution)/shard_map/all_to_all | solution.py:284
  107.1 6.2 %taps_spectrum.1.taps_ref = f32[16,192,256]{2,1,0:T(8,128)S(1)} custom-call(bf16[32,16,768]{2,1,0:T(8,128)(2,1)S(1)} %all-to-all-done.3.taps_ref, bf16[2,384,192]{2,1,0:T(8,128)(2,1)S(1)} %copy-done.8, f32[2,192,128]{2,1,0:T(8,128)S(1)} %copy-done.13, bf16[2,256,256]{2,1,0:T(8,128)(2,1)S(1)} %copy-done.10), custom_call_target="tpu_custom_call" | custom-call | flops 6000000000 | bytes 4194304 | tf_op jit(solution)/shard_map/taps_spectrum/pallas_call | solution.py:313
  113.3 1.6 copy-done.15
  115.0 8.2 %all-to-all-done.4.signal_ref = bf16[8,16,3072]{2,1,0:T(8,128)(2,1)S(1)} async-done(((bf16[8,16,3072]{2,1,0:T(8,128)(2,1)}), bf16[8,16,3072]{2,1,0:T(8,128)(2,1)S(1)}, u32[]{:S(2)}, u32[]{:S(2)}) %all-to-all-start.4) | async-done | bytes 786464 | tf_op jit(solution)/shard_map/all_to_all | solution.py:284
  123.2 4.3 %all-to-all-start.5 = ((bf16[4,768,128]{2,1,0:T(8,128)(2,1)}), bf16[4,768,128]{2,1,0:T(8,128)(2,1)S(1)}, u32[]{:S(2)}, u32[]{:S(2)}) async-start(bf16[4,768,128]{2,1,0:T(8,128)(2,1)} %bitcast.17), calls=%async_computation.5 | async-start | bytes 1572864 | tf_op jit(solution)/shard_map/all_to_all | solution.py:284
  127.5 1.0 copy-done.9
  128.4 0.9 copy-done.11
  129.4 0.9 copy-done.12
  130.3 0.9 copy-done.14
  131.3 1.9 %copy-done.16 = f32[16,192,256]{2,1,0:T(8,128)S(1)} copy-done((f32[16,192,256]{2,1,0:T(8,128)S(1)}, f32[16,192,256]{2,1,0:T(8,128)}, u32[]{:S(2)}) %copy-start.16) | copy-done | bytes 3145752
  133.1 10.3 %convolution.1 = bf16[32,16,768]{2,1,0:T(8,128)(2,1)S(1)} custom-call(bf16[8,16,3072]{2,1,0:T(8,128)(2,1)S(1)} %all-to-all-done.4.signal_ref, f32[16,192,256]{2,1,0:T(8,128)S(1)} %copy-done.16, bf16[2,384,192]{2,1,0:T(8,128)(2,1)S(1)} %copy-done.7, f32[2,192,128]{2,1,0:T(8,128)S(1)} %copy-done.14, bf16[2,256,256]{2,1,0:T(8,128)(2,1)S(1)} %copy-done.11, ...), custom_call_target="tpu_custom_call" | custom-call | flops 8999999488 | bytes 5242880 | tf_op jit(solution)/shard_map/convolution/pallas_call | solution.py:324
  143.5 0.0 all-to-all-done.5.attended_ref
  143.5 0.0 copy-start.2
  143.5 21.8 %all_to_all.35 = bf16[32,16,768]{2,1,0:T(8,128)(2,1)S(1)} all-to-all(bf16[32,16,768]{2,1,0:T(8,128)(2,1)S(1)} %convolution.1), channel_id=1, replica_groups=mesh['ctx'=32,'tp'=4,'dp'=2] {'ctx'}, dimensions={0} | all-to-all | bytes 1572864 | tf_op jit(solution)/shard_map/all_to_all | solution.py:284
  165.3 2.0 %finish.1 = (bf16[768,512]{1,0:T(8,128)(2,1)}, bf16[768,512]{1,0:T(8,128)(2,1)}) custom-call(bf16[8,4,16,768]{3,2,1,0:T(8,128)(2,1)S(1)} %bitcast.34, bf16[768,512]{1,0:T(8,128)(2,1)S(1)} %copy-done.2, bf16[4,768,128]{2,1,0:T(8,128)(2,1)S(1)} %all-to-all-done.5.attended_ref), custom_call_target="tpu_custom_call" | custom-call | tf_op jit(solution)/shard_map/finish/pallas_call | solution.py:253
  (28 shorter events, 0.1 us)
Async XLA Ops:
  0.6 1.1 copy-start
  0.6 6.4 %copy-start.17 = (bf16[768,512]{1,0:T(8,128)(2,1)S(1)}, bf16[768,512]{1,0:T(8,128)(2,1)}, u32[]{:S(2)}) copy-start(bf16[768,512]{1,0:T(8,128)(2,1)} %param.15) | copy-start | bytes 2359300
  2.8 16.6 %all-to-all-start = ((bf16[4,768,128]{2,1,0:T(8,128)(2,1)}), bf16[4,768,128]{2,1,0:T(8,128)(2,1)S(1)}, u32[]{:S(2)}, u32[]{:S(2)}) async-start(bf16[4,768,128]{2,1,0:T(8,128)(2,1)} %bitcast_bitcast_fusion.1), calls=%async_computation | async-start | bytes 1572864 | tf_op jit(solution)/shard_map/all_to_all | solution.py:284
  19.4 19.3 %all-to-all-start.1 = ((bf16[4,768,128]{2,1,0:T(8,128)(2,1)}), bf16[4,768,128]{2,1,0:T(8,128)(2,1)S(1)}, u32[]{:S(2)}, u32[]{:S(2)}) async-start(bf16[4,768,128]{2,1,0:T(8,128)(2,1)} %bitcast_bitcast_fusion), calls=%async_computation.1 | async-start | bytes 1572864 | tf_op jit(solution)/shard_map/all_to_all | solution.py:284
  22.9 15.7 %collective-permute-start = (bf16[2304,128]{1,0:T(8,128)(2,1)S(1)}, bf16[2304,128]{1,0:T(8,128)(2,1)S(1)}, u32[]{:S(2)}, u32[]{:S(2)}) collective-permute-start(bf16[2304,128]{1,0:T(8,128)(2,1)S(1)} %bitcast.45), channel_id=1, source_target_pairs={{0,32},{8,40},{16,48},{24,56},{32,64},{40,72},{48,80},{56,88},{64,... | collective-permute-start | bytes 1769480 | tf_op jit(solution)/shard_map/ppermute | solution.py:287
  38.6 10.3 %copy-start.18 = (s32[64]{0:T(128)S(1)}, s32[64]{0:T(128)}, u32[]{:S(2)}) copy-start(s32[64]{0:T(128)} %param.16) | copy-start | bytes 772
  38.6 0.8 copy-start.3
  39.5 24.0 %all-to-all-start.2 = ((bf16[4,2,768,128]{3,2,1,0:T(8,128)(2,1)}), bf16[4,2,768,128]{3,2,1,0:T(8,128)(2,1)}, u32[]{:S(2)}, u32[]{:S(2)}) async-start(bf16[4,2,768,128]{3,2,1,0:T(8,128)(2,1)} %pad_maximum_fusion), calls=%async_computation.2 | async-start | bytes 3145728 | tf_op jit(solution)/shard_map/all_to_all | solution.py:284
  45.1 14.8 %collective-permute-start.1 = (bf16[2304,128]{1,0:T(8,128)(2,1)}, bf16[2304,128]{1,0:T(8,128)(2,1)S(1)}, u32[]{:S(2)}, u32[]{:S(2)}) collective-permute-start(bf16[2304,128]{1,0:T(8,128)(2,1)} %bitcast.10), channel_id=1, source_target_pairs={{0,32},{8,40},{16,48},{24,56},{32,64},{40,72},{48,80},{56,88},{64,... | collective-permute-start | bytes 1769480 | tf_op jit(solution)/shard_map/ppermute | solution.py:287
  59.9 0.8 copy-start.5
  63.4 30.7 %all-to-all-start.3 = ((bf16[32,16,768]{2,1,0:T(8,128)(2,1)}), bf16[32,16,768]{2,1,0:T(8,128)(2,1)S(1)}, u32[]{:S(2)}, u32[]{:S(2)}) async-start(bf16[32,16,768]{2,1,0:T(8,128)(2,1)} %bitcast.39), calls=%async_computation.3 | async-start | bytes 1572864 | tf_op jit(solution)/shard_map/all_to_all | solution.py:284
  74.6 1.1 copy-start.4
  75.6 1.1 copy-start.6
  91.1 0.9 copy-start.1
  91.9 15.1 %copy-start.8 = (bf16[2,384,192]{2,1,0:T(8,128)(2,1)S(1)}, bf16[2,384,192]{2,1,0:T(8,128)(2,1)}, u32[]{:S(2)}) copy-start(bf16[2,384,192]{2,1,0:T(8,128)(2,1)} %constant.50.clone.outer_ref) | copy-start | bytes 884740
  91.9 15.1 %copy-start.10 = (bf16[2,256,256]{2,1,0:T(8,128)(2,1)S(1)}, bf16[2,256,256]{2,1,0:T(8,128)(2,1)}, u32[]{:S(2)}) copy-start(bf16[2,256,256]{2,1,0:T(8,128)(2,1)} %constant.52.clone.inner_ref) | copy-start | bytes 786436
  91.9 15.1 %copy-start.13 = (f32[2,192,128]{2,1,0:T(8,128)S(1)}, f32[2,192,128]{2,1,0:T(8,128)}, u32[]{:S(2)}) copy-start(f32[2,192,128]{2,1,0:T(8,128)} %constant.51.clone.twist_ref) | copy-start | bytes 589828
  94.1 29.1 %all-to-all-start.4 = ((bf16[8,16,3072]{2,1,0:T(8,128)(2,1)}), bf16[8,16,3072]{2,1,0:T(8,128)(2,1)S(1)}, u32[]{:S(2)}, u32[]{:S(2)}) async-start(bf16[8,16,3072]{2,1,0:T(8,128)(2,1)} %bitcast.37), calls=%async_computation.4 | async-start | bytes 1572864 | tf_op jit(solution)/shard_map/all_to_all | solution.py:284
  113.3 1.6 copy-start.15
  115.0 12.5 %copy-start.7 = (bf16[2,384,192]{2,1,0:T(8,128)(2,1)S(1)}, bf16[2,384,192]{2,1,0:T(8,128)(2,1)}, u32[]{:S(2)}) copy-start(bf16[2,384,192]{2,1,0:T(8,128)(2,1)} %constant.53.clone.outer_ref) | copy-start | bytes 884740
  123.2 20.3 %all-to-all-start.5 = ((bf16[4,768,128]{2,1,0:T(8,128)(2,1)}), bf16[4,768,128]{2,1,0:T(8,128)(2,1)S(1)}, u32[]{:S(2)}, u32[]{:S(2)}) async-start(bf16[4,768,128]{2,1,0:T(8,128)(2,1)} %bitcast.17), calls=%async_computation.5 | async-start | bytes 1572864 | tf_op jit(solution)/shard_map/all_to_all | solution.py:284
  127.5 1.0 copy-start.9
  128.4 0.9 copy-start.11
  129.4 0.9 copy-start.12
  130.3 0.9 copy-start.14
  131.3 1.9 %copy-start.16 = (f32[16,192,256]{2,1,0:T(8,128)S(1)}, f32[16,192,256]{2,1,0:T(8,128)}, u32[]{:S(2)}) copy-start(f32[16,192,256]{2,1,0:T(8,128)} %copy-done.15) | copy-start | bytes 9437188
  143.5 21.8 %copy-start.2 = (bf16[768,512]{1,0:T(8,128)(2,1)S(1)}, bf16[768,512]{1,0:T(8,128)(2,1)}, u32[]{:S(2)}) copy-start(bf16[768,512]{1,0:T(8,128)(2,1)} %gate_ref.1) | copy-start | bytes 2359300

commit v3 on v2

v3 whole, which is shorter than its diff:
```python
import functools
import math

import jax
import jax.numpy as jnp
import ml_dtypes
import numpy as np
from jax import lax
from jax.experimental import pallas as pl
from jax.experimental.pallas import tpu as pltpu
from jax.sharding import PartitionSpec as P

HEAD_DIM = 128
X_SIZE = 4
Q_BLOCK = 768
K_BLOCK = 384
LANES = 128
VMEM_LIMIT = 62 * 2**20
PAIRS = 4
masked_score = -1e30


def document_starts(positions, doc_lengths):
    order = jnp.arange(doc_lengths.shape[0], dtype=jnp.int32)
    before = order[:, None] < order[None, :]
    starts = jnp.sum(jnp.where(before, doc_lengths[:, None], 0), axis=0)
    inside = starts[None, :] <= positions[:, None]
    return jnp.max(jnp.where(inside, starts[None, :], 0), axis=1)


def identity(size):
    row = lax.broadcasted_iota(jnp.int32, (size, size), 0)
    column = lax.broadcasted_iota(jnp.int32, (size, size), 1)
    return jnp.where(row == column, 1.0, 0.0).astype(jnp.bfloat16)


def transposed(x, eye):
    return lax.dot_general(eye, x, (((1,), (1,)), ((), ())), preferred_element_type=jnp.float32)


def pieces_kernel(x_ref, first_ref, second_ref, *rest):
    outs, sems = rest[:X_SIZE], rest[X_SIZE]
    copies = []
    for k, out in enumerate(outs):
        column = pl.multiple_of(lax.rem(x_ref[0] + k, X_SIZE) * HEAD_DIM, HEAD_DIM)
        for which, ref in enumerate((first_ref, second_ref)):
            copy = pltpu.make_async_copy(ref.at[:, pl.ds(column, HEAD_DIM)], out.at[which], sems.at[k, which])
            copy.start()
            copies.append(copy)
    for copy in copies:
        copy.wait()


def pieces_of(x_index, first, second):
    anywhere = pl.BlockSpec(memory_space=pl.ANY)
    return pl.pallas_call(
        pieces_kernel,
        name="pieces",
        in_specs=[pl.BlockSpec(memory_space=pltpu.SMEM), anywhere, anywhere],
        out_specs=[anywhere] * X_SIZE,
        out_shape=[jax.ShapeDtypeStruct((2, first.shape[0], HEAD_DIM), jnp.bfloat16)] * X_SIZE,
        scratch_shapes=[pltpu.SemaphoreType.DMA((X_SIZE, 2))],
    )(x_index, first, second)


def attention_kernel(lo_ref, mid_ref, x_ref, start_ref, *rest):
    own, before, asked = rest[:X_SIZE], rest[X_SIZE : 2 * X_SIZE], rest[2 * X_SIZE : 3 * X_SIZE]
    out_ref, gated_ref, keys, values, values_t, queries_all, gate_all, sems = rest[3 * X_SIZE :]
    step = pl.program_id(0)
    group = queries_all.shape[0]
    piece = group // X_SIZE
    eye = identity(HEAD_DIM)

    @pl.when(step == 0)
    def _():
        copies = []
        for k in range(X_SIZE):
            at = pl.multiple_of(lax.rem(x_ref[0] + X_SIZE - k, X_SIZE) * piece, piece)
            early, late = pl.ds(at, piece), pl.ds(at + group, piece)
            for n, (source, target) in enumerate(
                (
                    (own[k].at[0], keys.at[late]),
                    (own[k].at[1], values.at[late]),
                    (before[k].at[0], keys.at[early]),
                    (before[k].at[1], values.at[early]),
                    (asked[k].at[0], queries_all.at[early]),
                    (asked[k].at[1], gate_all.at[early]),
                )
            ):
                copy = pltpu.make_async_copy(source, target, sems.at[k, n])
                copy.start()
                copies.append(copy)
        for copy in copies:
            copy.wait()

        def turn(block, _):
            rows = values[pl.ds(pl.multiple_of(block * K_BLOCK, K_BLOCK), K_BLOCK)]
            values_t[block] = transposed(rows, eye).astype(jnp.bfloat16)
            return 0

        lax.fori_loop(lo_ref[0], values_t.shape[0], turn, 0)

    here = pl.ds(pl.multiple_of(step * Q_BLOCK, Q_BLOCK), Q_BLOCK)
    queries = transposed(queries_all[here], eye).astype(jnp.bfloat16)
    first = group + step * Q_BLOCK
    start = start_ref[0]
    query_index = first + lax.broadcasted_iota(jnp.int32, (1, Q_BLOCK), 1)
    key_offset = lax.broadcasted_iota(jnp.int32, (K_BLOCK, 1), 0)
    factor = math.log2(math.e) / math.sqrt(HEAD_DIM)

    def visit(masked, block, carried):
        top, total, weighted = carried
        key_rows = keys[pl.ds(pl.multiple_of(block * K_BLOCK, K_BLOCK), K_BLOCK)]
        scores = jnp.dot(key_rows, queries, preferred_element_type=jnp.float32) * factor
        if masked:
            index = block * K_BLOCK + key_offset
            scores = jnp.where((index >= start) & (index <= query_index), scores, masked_score)
        new_top = jnp.maximum(top, jnp.max(scores, axis=0, keepdims=True))
        rescale = jnp.exp2(top - new_top)
        weight = jnp.exp2(scores - new_top)
        total = total * rescale + jnp.sum(weight, axis=0, keepdims=True)
        weighted = weighted * rescale + jnp.dot(
            values_t[block], weight.astype(jnp.bfloat16), preferred_element_type=jnp.float32
        )
        return new_top, total, weighted

    diagonal = first // K_BLOCK
    last = (first + Q_BLOCK - 1) // K_BLOCK
    middle = jnp.minimum(mid_ref[step], diagonal)
    carried = (
        jnp.full((1, Q_BLOCK), masked_score, jnp.float32),
        jnp.zeros((1, Q_BLOCK), jnp.float32),
        jnp.zeros((HEAD_DIM, Q_BLOCK), jnp.float32),
    )
    edge, inside = functools.partial(visit, True), functools.partial(visit, False)
    carried = lax.fori_loop(lo_ref[step], middle, edge, carried)
    carried = lax.fori_loop(middle, diagonal, inside, carried)
    top, total, weighted = lax.fori_loop(diagonal, last + 1, edge, carried)
    rounded = (weighted * (1.0 / total)).astype(jnp.bfloat16)
    wide = identity(2 * LANES)
    for at in range(0, Q_BLOCK, 2 * LANES):
        part = transposed(rounded[:, at : at + 2 * LANES], wide)
        out_ref[at : at + 2 * LANES] = part.astype(jnp.bfloat16)
    gated_ref[...] = (rounded.astype(jnp.float32) * transposed(gate_all[here], eye)).astype(jnp.bfloat16)


def attention(x_index, own, before, asked, start):
    rows = X_SIZE * own[0].shape[1]
    steps = rows // Q_BLOCK
    lo = start[::Q_BLOCK] // K_BLOCK
    middle = start[Q_BLOCK - 1 :: Q_BLOCK] // K_BLOCK + 1
    anywhere = pl.BlockSpec(memory_space=pl.ANY)
    return pl.pallas_call(
        attention_kernel,
        name="attention",
        grid_spec=pltpu.PrefetchScalarGridSpec(
            num_scalar_prefetch=3,
            grid=(steps,),
            in_specs=[pl.BlockSpec((1, 1, Q_BLOCK), lambda i, *_: (i, 0, 0))] + [anywhere] * (3 * X_SIZE),
            out_specs=[
                pl.BlockSpec((Q_BLOCK, HEAD_DIM), lambda i, *_: (i, 0)),
                pl.BlockSpec((HEAD_DIM, Q_BLOCK), lambda i, *_: (0, i)),
            ],
            scratch_shapes=[
                pltpu.VMEM((2 * rows, HEAD_DIM), jnp.bfloat16),
                pltpu.VMEM((2 * rows, HEAD_DIM), jnp.bfloat16),
                pltpu.VMEM((2 * rows // K_BLOCK, HEAD_DIM, K_BLOCK), jnp.bfloat16),
                pltpu.VMEM((rows, HEAD_DIM), jnp.bfloat16),
                pltpu.VMEM((rows, HEAD_DIM), jnp.bfloat16),
                pltpu.SemaphoreType.DMA((X_SIZE, 6)),
            ],
        ),
        out_shape=[
            jax.ShapeDtypeStruct((rows, HEAD_DIM), jnp.bfloat16),
            jax.ShapeDtypeStruct((HEAD_DIM, rows), jnp.bfloat16),
        ],
        compiler_params=pltpu.CompilerParams(vmem_limit_bytes=VMEM_LIMIT),
        cost_estimate=pl.CostEstimate(
            flops=16 * 10**9, bytes_accessed=10 * rows * HEAD_DIM, transcendentals=rows * 1536
        ),
    )(lo, middle, x_index, start.reshape(steps, 1, Q_BLOCK), *own, *before, *asked)


def high_low(table):
    high = table.astype(np.float32).astype(ml_dtypes.bfloat16)
    low = (table - high.astype(np.float64)).astype(np.float32).astype(ml_dtypes.bfloat16)
    return high, low


def transform_tables(length, senders, tap_senders):
    outer = length // LANES
    k1 = np.arange(outer)
    per_sender = outer // senders
    a_signal = (np.arange(senders)[None, :] * per_sender + np.arange(per_sender)[:, None]).reshape(-1)
    per_tap = outer // tap_senders
    a_tap = (np.arange(tap_senders)[None, :] * per_tap + np.arange(per_tap)[:, None]).reshape(-1)
    b = np.arange(LANES)

    def angles(a):
        return 2.0 * np.pi * ((4 * k1[:, None] + 1) * a[None, :] % (4 * outer)) / (4 * outer)

    def left(table):
        return np.concatenate(high_low(table), axis=1)

    def right(table):
        return np.concatenate(high_low(table), axis=0)

    def forward(a):
        angle = angles(a)
        return left(np.concatenate((np.cos(angle), -np.sin(angle)), axis=0))

    twist = 2.0 * np.pi * ((4 * k1[:, None] + 1) * b[None, :] % (4 * length)) / (4 * length)
    inner = 2.0 * np.pi * (b[:, None] * b[None, :] % LANES) / LANES
    cos, sin = np.cos(inner), np.sin(inner)
    back = angles(a_tap).T
    return dict(
        signal=forward(a_signal),
        taps=forward(a_tap),
        twist=np.stack((np.cos(twist), -np.sin(twist))).astype(np.float32),
        inner=right(np.block([[cos, -sin], [sin, cos]])),
        inner_back=right(np.block([[cos, sin], [-sin, cos]])),
        back=left(np.concatenate((np.cos(back), -np.sin(back)), axis=1) / length),
    )


def table_dot(table_ref, right):
    return jnp.dot(table_ref[...], jnp.concatenate((right, right), axis=0), preferred_element_type=jnp.float32)


def dot_table(left, table_ref):
    return jnp.dot(jnp.concatenate((left, left), axis=1), table_ref[...], preferred_element_type=jnp.float32)


def spread(source_ref, spread_ref):
    rows = spread_ref.shape[1]
    for j in range(spread_ref.shape[0]):
        part = source_ref[:, :, j * LANES : (j + 1) * LANES]
        spread_ref[j] = part.reshape(rows, LANES).astype(jnp.float32)


def channel_rows(spread_ref, channel, channels):
    senders = spread_ref.shape[1] // channels
    pair = []
    for c in (channel, channel + 1):
        parts = [spread_ref[j, pl.ds(c, senders, stride=channels), :] for j in range(spread_ref.shape[0])]
        pair.append(jnp.concatenate(parts, axis=0).astype(jnp.bfloat16))
    return jnp.concatenate(pair, axis=1)


def spectrum(rows, outer_ref, twist_ref, inner_ref):
    outer = rows.shape[0]
    section = table_dot(outer_ref, rows)
    turned = []
    for lane in (0, LANES):
        real, imag = section[:outer, lane : lane + LANES], section[outer:, lane : lane + LANES]
        turned_real = real * twist_ref[0] - imag * twist_ref[1]
        turned_imag = real * twist_ref[1] + imag * twist_ref[0]
        turned.append(jnp.concatenate((turned_real.astype(jnp.bfloat16), turned_imag.astype(jnp.bfloat16)), axis=1))
    return dot_table(jnp.concatenate(turned, axis=0), inner_ref)


def taps_kernel(taps_ref, outer_ref, twist_ref, inner_ref, out_ref, spread_ref):
    step = pl.program_id(0)
    channels = taps_ref.shape[1]

    @pl.when(step == 0)
    def _():
        spread(taps_ref, spread_ref)

    for pair in range(out_ref.shape[0]):
        channel = step * 2 * out_ref.shape[0] + 2 * pair
        out_ref[pair] = spectrum(channel_rows(spread_ref, channel, channels), outer_ref, twist_ref, inner_ref)


def conv_kernel(
    signal_ref, taps_ref, outer_ref, twist_ref, inner_ref, inner_back_ref, back_ref, out_ref, spread_ref, result_ref
):
    step = pl.program_id(0)
    channels = signal_ref.shape[1]
    receivers = out_ref.shape[0]
    outer = twist_ref.shape[1]

    @pl.when(step == 0)
    def _():
        spread(signal_ref, spread_ref)

    for pair in range(taps_ref.shape[0]):
        channel = step * 2 * taps_ref.shape[0] + 2 * pair
        signal = spectrum(channel_rows(spread_ref, channel, channels), outer_ref, twist_ref, inner_ref)
        taps = taps_ref[pair]
        sig_real, sig_imag = signal[:, :LANES], signal[:, LANES:]
        tap_real, tap_imag = taps[:, :LANES], taps[:, LANES:]
        prod_real = sig_real * tap_real - sig_imag * tap_imag
        prod_imag = sig_real * tap_imag + sig_imag * tap_real
        prod = jnp.concatenate((prod_real.astype(jnp.bfloat16), prod_imag.astype(jnp.bfloat16)), axis=1)
        turned = dot_table(prod, inner_back_ref)
        both = []
        for row in (0, outer):
            real, imag = turned[row : row + outer, :LANES], turned[row : row + outer, LANES:]
            back_real = real * twist_ref[0] + imag * twist_ref[1]
            back_imag = imag * twist_ref[0] - real * twist_ref[1]
            both.append(jnp.concatenate((back_real.astype(jnp.bfloat16), back_imag.astype(jnp.bfloat16)), axis=0))
        rows = table_dot(back_ref, jnp.concatenate(both, axis=1))
        for n in range(2):
            for j in range(result_ref.shape[0]):
                part = rows[j * receivers : (j + 1) * receivers, n * LANES : (n + 1) * LANES]
                result_ref[j, pl.ds(channel + n, receivers, stride=channels), :] = part

    @pl.when(step == pl.num_programs(0) - 1)
    def _():
        for j in range(result_ref.shape[0]):
            part = result_ref[j].reshape(receivers, channels, LANES)
            out_ref[:, :, j * LANES : (j + 1) * LANES] = part.astype(jnp.bfloat16)


def whole(array):
    return pl.BlockSpec(array.shape, lambda i: (0,) * array.ndim)


def transform_taps(taps, tables):
    senders, channels, rows = taps.shape
    outer = tables["twist"].shape[1]
    operands = (taps, tables["taps"], tables["twist"], tables["inner"])
    return pl.pallas_call(
        taps_kernel,
        name="taps_spectrum",
        grid=(channels // (2 * PAIRS),),
        in_specs=[whole(x) for x in operands],
        out_specs=pl.BlockSpec((PAIRS, 2 * outer, 2 * LANES), lambda i: (i, 0, 0)),
        out_shape=jax.ShapeDtypeStruct((channels // 2, 2 * outer, 2 * LANES), jnp.float32),
        scratch_shapes=[pltpu.VMEM((rows // LANES, senders * channels, LANES), jnp.float32)],
        compiler_params=pltpu.CompilerParams(vmem_limit_bytes=VMEM_LIMIT),
        cost_estimate=pl.CostEstimate(flops=5 * 10**9, bytes_accessed=4 * 2**20, transcendentals=0),
    )(*operands)


def convolve(signal, spectra, tables, receivers):
    senders, channels, rows = signal.shape
    out_rows = senders * rows // receivers
    operands = [tables[n] for n in ("signal", "twist", "inner", "inner_back", "back")]
    return pl.pallas_call(
        conv_kernel,
        name="convolution",
        grid=(channels // (2 * PAIRS),),
        in_specs=[whole(signal), pl.BlockSpec((PAIRS,) + spectra.shape[1:], lambda i: (i, 0, 0))]
        + [whole(x) for x in operands],
        out_specs=pl.BlockSpec((receivers, channels, out_rows), lambda i: (0, 0, 0)),
        out_shape=jax.ShapeDtypeStruct((receivers, channels, out_rows), jnp.bfloat16),
        scratch_shapes=[
            pltpu.VMEM((rows // LANES, senders * channels, LANES), jnp.float32),
            pltpu.VMEM((out_rows // LANES, receivers * channels, LANES), jnp.float32),
        ],
        compiler_params=pltpu.CompilerParams(vmem_limit_bytes=VMEM_LIMIT),
        cost_estimate=pl.CostEstimate(flops=7 * 10**9, bytes_accessed=5 * 2**20, transcendentals=0),
    )(signal, spectra, *operands)


def finish_kernel(mixed_ref, gate_ref, attended_ref, attn_ref, hyena_ref):
    mixed = mixed_ref[...].reshape(HEAD_DIM, mixed_ref.shape[3]).astype(jnp.float32).T
    hyena_ref[...] = (gate_ref[...].astype(jnp.float32) * mixed).astype(jnp.bfloat16)
    attn_ref[...] = attended_ref[0]


def finish(returned, out_gate, attended):
    rows, channels = out_gate.shape
    z_size = returned.shape[0] // X_SIZE
    returned = returned.reshape(z_size, X_SIZE, returned.shape[1], rows)
    by_columns = pl.BlockSpec((rows, HEAD_DIM), lambda i: (0, i))
    return pl.pallas_call(
        finish_kernel,
        name="finish",
        grid=(channels // HEAD_DIM,),
        in_specs=[
            pl.BlockSpec((z_size, 1, returned.shape[2], rows), lambda i: (0, i, 0, 0)),
            by_columns,
            pl.BlockSpec((1, rows, HEAD_DIM), lambda i: (i, 0, 0)),
        ],
        out_specs=[by_columns, by_columns],
        out_shape=[jax.ShapeDtypeStruct((rows, channels), jnp.bfloat16)] * 2,
        compiler_params=pltpu.CompilerParams(vmem_limit_bytes=VMEM_LIMIT),
    )(returned, out_gate, attended)


def body(queries, key_rows, values, doc_lengths, in_gate, out_gate, filter_taps):
    row_count, channels = queries.shape
    ctx = lax.axis_size("ctx")
    z_size = ctx // X_SIZE
    group_rows = X_SIZE * row_count
    per_device = channels // ctx
    x_groups = [[z * X_SIZE + x for x in range(X_SIZE)] for z in range(z_size)]
    z_groups = [[z * X_SIZE + x for z in range(z_size)] for x in range(X_SIZE)]
    tables = transform_tables(row_count * ctx, z_size, ctx)
    me = lax.axis_index("ctx").astype(jnp.int32)
    x_index = lax.rem(me, X_SIZE).reshape(1)

    def exchanged(x, groups=None):
        return lax.all_to_all(x, "ctx", split_axis=0, concat_axis=0, tiled=True, axis_index_groups=groups)

    def along_x(piece, k):
        pairs = [(z * X_SIZE + x, z * X_SIZE + (x + k) % X_SIZE) for z in range(z_size) for x in range(X_SIZE)]
        return lax.ppermute(piece, "ctx", pairs)

    def along_z(piece, k):
        pairs = [(i, i + X_SIZE) for i in range(ctx - X_SIZE) if i % X_SIZE != k]
        return lax.ppermute(piece, "ctx", pairs)

    def arrived(pieces):
        return [pieces[0]] + [along_x(pieces[k], k) for k in range(1, X_SIZE)]

    taps = filter_taps.astype(jnp.bfloat16).reshape(X_SIZE, z_size, per_device, row_count)
    taps = taps.transpose(1, 0, 2, 3).reshape(ctx, per_device, row_count)
    own = arrived(pieces_of(x_index, key_rows, values))
    taps = exchanged(taps)
    before = [along_z(own[k], k) for k in range(X_SIZE)]
    taps, queries, in_gate = lax.optimization_barrier((taps, queries, in_gate))
    asked = arrived(pieces_of(x_index, queries, in_gate))

    group_first = (me // X_SIZE) * group_rows
    positions = group_first + jnp.arange(group_rows, dtype=jnp.int32)
    start = document_starts(positions, doc_lengths) - (group_first - group_rows)

    attended, gated = attention(x_index, own, before, asked, start)
    gated, taps = lax.optimization_barrier((gated, taps))
    signal = exchanged(gated.reshape(z_size, per_device, group_rows), z_groups)
    spectra = transform_taps(taps, tables)
    signal, attended = lax.optimization_barrier((signal, attended.reshape(X_SIZE, row_count, HEAD_DIM)))
    attended = exchanged(attended, x_groups)
    mixed = convolve(signal, spectra, tables, ctx)
    mixed, attended = lax.optimization_barrier((mixed, attended))
    returned = exchanged(mixed)
    return finish(returned, out_gate, attended)


def solution(mesh):
    return jax.shard_map(
        body,
        mesh=mesh,
        in_specs=(
            P(("dp", "ctx"), "tp"),
            P(("dp", "ctx"), "tp"),
            P(("dp", "ctx"), "tp"),
            P("dp"),
            P(("dp", "ctx"), "tp"),
            P(("dp", "ctx"), "tp"),
            P(("dp", "tp"), "ctx"),
        ),
        out_specs=(P(("dp", "ctx"), "tp"), P(("dp", "ctx"), "tp")),
        check_vma=False,
    )
```

time: 170 us -> 260 us (1.53); the launches traced: 167 us -> 260 us
  Pallas kernels: 32.9 us -> 137 us
  local copies, waits for them, and re-layouts: 26.2 us -> 1.17 us
  waiting for transfers between devices: 32.5 us -> 43.8 us
  blocking collectives: 21.8 us -> 26.7 us
    pallas_call x2 -> x4, Pallas kernels: 16.5 us -> 114 us  [the longest x2 97.6 us: pieces_of(): pl.pallas_call(pieces_kernel, name='pieces', in_specs=[pl.BlockSpec(memor...]
    ppermute x2 -> x10, waiting for transfers between devices: 8.12 us -> 26.2 us  [the longest x6 26.2 us: along_x(): return lax.ppermute(piece, 'ctx', pairs)]
    unnamed x40 -> x22, local copies, waits for them, and re-layouts: 17.7 us -> 0.04 us
    ppermute x2 -> x10, starting transfers between devices: 7.67 us -> 21 us  [the longest x4 11.7 us: along_z(): return lax.ppermute(piece, 'ctx', pairs)]
    all_to_all x6 -> x3, starting transfers between devices: 40.8 us -> 27.7 us  [exchanged(): lax.all_to_all(x, 'ctx', split_axis=0, concat_axis=0, tiled=True, axis_in...]
    all_to_all x6 -> x3, waiting for transfers between devices: 24.4 us -> 17.6 us  [exchanged(): lax.all_to_all(x, 'ctx', split_axis=0, concat_axis=0, tiled=True, axis_in...]
    all_to_all x1, blocking collectives: 21.8 us -> 26.7 us  [exchanged(): lax.all_to_all(x, 'ctx', split_axis=0, concat_axis=0, tiled=True, axis_in...]
    reshape x2 -> x0, local copies, waits for them, and re-layouts: 4.58 us -> none  [by_head(): return x.reshape(row_count, X_SIZE, HEAD_DIM).transpose(1, 0, 2)]
  transfers between devices with their start and end apart: 8 -> 13, of which waited for: 5 -> 6; matrix products, arithmetic and copies ran while one was open for 10% -> 0% of each run, Pallas kernels for 18% -> 44%
where the time goes in v3:
time: 260 us
  Pallas kernels  137 us (53%)
  starting transfers between devices  48.7 us (19%)
  waiting for transfers between devices  43.8 us (17%)
  blocking collectives  26.7 us (10%)
    pallas_call x2, Pallas kernels, pieces_of(): pl.pallas_call(pieces_kernel, name='pieces', in_specs=[pl.BlockSpec(memor...  97.6 us
    all_to_all x3, starting transfers between devices, exchanged(): lax.all_to_all(x, 'ctx', split_axis=0, concat_axis=0, tiled=True, axis_in...  27.7 us
    all_to_all x1, blocking collectives, exchanged(): lax.all_to_all(x, 'ctx', split_axis=0, concat_axis=0, tiled=True, axis_in...  26.7 us
    ppermute x6, waiting for transfers between devices, along_x(): return lax.ppermute(piece, 'ctx', pairs)  26.2 us
    pallas_call x1, Pallas kernels, attention(): pl.pallas_call(attention_kernel, name='attention', grid_spec=pltpu.Prefet...  18.6 us
    all_to_all x3, waiting for transfers between devices, exchanged(): lax.all_to_all(x, 'ctx', split_axis=0, concat_axis=0, tiled=True, axis_in...  17.6 us
    ppermute x4, starting transfers between devices, along_z(): return lax.ppermute(piece, 'ctx', pairs)  11.7 us
    pallas_call x1, Pallas kernels, convolve(): pl.pallas_call(conv_kernel, name='convolution', grid=(channels // (2 * PA...  11.4 us
  transfers between devices with their start and end apart: 13, of which 6 were waited for; matrix products, arithmetic and copies ran while one was open for 0% of the time, Pallas kernels for 44%

profile of v3, /device:TPU:16, one launch (start us, length us, event | category | flops | bytes accessed | tf_op | source)
XLA Modules:
  0.0 260.5 jit_solution(685234682695297291)
XLA Ops:
  0.6 0.0 copy-start.10
  0.6 1.5 convert_element_type.3
  2.1 1.0 copy.16
  3.1 11.3 %all-to-all-start = ((bf16[32,16,768]{2,1,0:T(8,128)(2,1)}), bf16[32,16,768]{2,1,0:T(8,128)(2,1)S(1)}, u32[]{:S(2)}, u32[]{:S(2)}) async-start(bf16[32,16,768]{2,1,0:T(8,128)(2,1)} %bitcast.4), calls=%async_computation | async-start | bytes 1572864 | tf_op jit(solution)/shard_map/all_to_all | solution.py:397
  14.4 48.8 %pieces.2 = (bf16[2,768,128]{2,1,0:T(8,128)(2,1)}, bf16[2,768,128]{2,1,0:T(8,128)(2,1)}, bf16[2,768,128]{2,1,0:T(8,128)(2,1)}, bf16[2,768,128]{2,1,0:T(8,128)(2,1)}) custom-call(s32[1]{0:T(128)} %bitcast.x_ref, bf16[768,512]{1,0:T(8,128)(2,1)} %first_ref.1, bf16[768,512]{1,0:T(8,128)(2,1)} %second_ref.1), custom_call_target="tpu_custom_call" | custom-call | tf_op jit(solution)/shard_map/pieces/pallas_call | solution.py:56
  63.3 1.9 collective-permute-start
  65.1 2.7 %collective-permute-start.1 = (bf16[2,768,128]{2,1,0:T(8,128)(2,1)}, bf16[2,768,128]{2,1,0:T(8,128)(2,1)S(1)}, u32[]{:S(2)}, u32[]{:S(2)}) collective-permute-start(bf16[2,768,128]{2,1,0:T(8,128)(2,1)} %get-tuple-element.23), channel_id=1, source_target_pairs={{0,16},{8,24},{16,0},{24,8},{32,48},{40,56},{48,32},{56,40},{64,80... | collective-permute-start | bytes 1179656 | tf_op jit(solution)/shard_map/ppermute | solution.py:401
  67.8 1.5 collective-permute-start.2
  69.3 0.7 collective-permute-start.3
  69.9 6.2 %collective-permute-done.rest_1_ = bf16[2,768,128]{2,1,0:T(8,128)(2,1)S(1)} collective-permute-done((bf16[2,768,128]{2,1,0:T(8,128)(2,1)}, bf16[2,768,128]{2,1,0:T(8,128)(2,1)S(1)}, u32[]{:S(2)}, u32[]{:S(2)}) %collective-permute-start) | collective-permute-done | bytes 393248 | tf_op jit(solution)/shard_map/ppermute | solution.py:401
  76.1 3.5 %collective-permute-start.4 = (bf16[2,768,128]{2,1,0:T(8,128)(2,1)S(1)}, bf16[2,768,128]{2,1,0:T(8,128)(2,1)S(1)}, u32[]{:S(2)}, u32[]{:S(2)}) collective-permute-start(bf16[2,768,128]{2,1,0:T(8,128)(2,1)S(1)} %collective-permute-done.rest_1_), channel_id=1, source_target_pairs={{0,32},{16,48},{24,56},{32,64},{48,80},{56,88},{64,96},{80,112},{8... | collective-permute-start | bytes 1179656 | tf_op jit(solution)/shard_map/ppermute | solution.py:405
  79.6 0.0 copy-done.10
  79.7 0.1 select_reduce_fusion.1
  79.8 0.2 select_reduce_fusion
  80.0 4.7 %collective-permute-done.1.rest_2_ = bf16[2,768,128]{2,1,0:T(8,128)(2,1)S(1)} collective-permute-done((bf16[2,768,128]{2,1,0:T(8,128)(2,1)}, bf16[2,768,128]{2,1,0:T(8,128)(2,1)S(1)}, u32[]{:S(2)}, u32[]{:S(2)}) %collective-permute-start.1) | collective-permute-done | bytes 393248 | tf_op jit(solution)/shard_map/ppermute | solution.py:401
  84.7 3.4 %collective-permute-start.5 = (bf16[2,768,128]{2,1,0:T(8,128)(2,1)S(1)}, bf16[2,768,128]{2,1,0:T(8,128)(2,1)S(1)}, u32[]{:S(2)}, u32[]{:S(2)}) collective-permute-start(bf16[2,768,128]{2,1,0:T(8,128)(2,1)S(1)} %collective-permute-done.1.rest_2_), channel_id=1, source_target_pairs={{0,32},{8,40},{24,56},{32,64},{40,72},{56,88},{64,96},{72,104},{88... | collective-permute-start | bytes 1179656 | tf_op jit(solution)/shard_map/ppermute | solution.py:405
  88.1 0.0 collective-permute-done.2.rest_3_
  88.1 0.0 copy-start.6
  88.1 4.1 %collective-permute-start.6 = (bf16[2,768,128]{2,1,0:T(8,128)(2,1)S(1)}, bf16[2,768,128]{2,1,0:T(8,128)(2,1)}, u32[]{:S(2)}, u32[]{:S(2)}) collective-permute-start(bf16[2,768,128]{2,1,0:T(8,128)(2,1)S(1)} %collective-permute-done.2.rest_3_), channel_id=1, source_target_pairs={{0,32},{8,40},{16,48},{32,64},{40,72},{48,80},{64,96},{72,104},{80... | collective-permute-start | bytes 1179656 | tf_op jit(solution)/shard_map/ppermute | solution.py:405
  92.2 0.0 all-to-all-done.taps_ref
  92.3 48.8 %pieces.3 = (bf16[2,768,128]{2,1,0:T(8,128)(2,1)}, bf16[2,768,128]{2,1,0:T(8,128)(2,1)}, bf16[2,768,128]{2,1,0:T(8,128)(2,1)}, bf16[2,768,128]{2,1,0:T(8,128)(2,1)}) custom-call(s32[1]{0:T(128)} %bitcast.x_ref, bf16[768,512]{1,0:T(8,128)(2,1)} %first_ref.2, bf16[768,512]{1,0:T(8,128)(2,1)} %second_ref.2), custom_call_target="tpu_custom_call" | custom-call | tf_op jit(solution)/shard_map/pieces/pallas_call | solution.py:56
  141.1 0.1 collective-permute-start.7
  141.2 0.0 collective-permute-done.3.rest_4_
  141.2 0.0 copy-start.7
  141.2 0.1 collective-permute-start.8
  141.3 0.0 collective-permute-done.4.rest_5_
  141.3 3.2 %collective-permute-start.9 = (bf16[2,768,128]{2,1,0:T(8,128)(2,1)}, bf16[2,768,128]{2,1,0:T(8,128)(2,1)}, u32[]{:S(2)}, u32[]{:S(2)}) collective-permute-start(bf16[2,768,128]{2,1,0:T(8,128)(2,1)} %get-tuple-element.30), channel_id=1, source_target_pairs={{0,24},{8,0},{16,8},{24,16},{32,56},{40,32},{48,40},{56,48},{64,88... | collective-permute-start | bytes 1179656 | tf_op jit(solution)/shard_map/ppermute | solution.py:401
  144.5 0.1 slice.7
  144.6 0.1 slice.6
  144.7 0.6 and_select_fusion.1
  145.3 0.0 collective-permute-done.5.rest_6_
  145.3 0.0 collective-permute-done.6.rest_7_
  145.3 14.6 %collective-permute-done.7.rest_9_ = bf16[2,768,128]{2,1,0:T(8,128)(2,1)} collective-permute-done((bf16[2,768,128]{2,1,0:T(8,128)(2,1)}, bf16[2,768,128]{2,1,0:T(8,128)(2,1)}, u32[]{:S(2)}, u32[]{:S(2)}) %collective-permute-start.7) | collective-permute-done | bytes 393248 | tf_op jit(solution)/shard_map/ppermute | solution.py:401
  159.9 0.0 copy-done.8
  159.9 0.0 collective-permute-done.8.rest_10_
  159.9 0.6 collective-permute-done.9.rest_11_
  160.5 0.0 copy-done.4
  160.6 18.6 %attention.1 = (bf16[3072,128]{1,0:T(8,128)(2,1)}, bf16[128,3072]{1,0:T(8,128)(2,1)}) custom-call(s32[4]{0:T(128)} %get-tuple-element.40.lo_ref, s32[4]{0:T(128)} %get-tuple-element.41.mid_ref, s32[1]{0:T(128)} %bitcast.x_ref, s32[4,1,768]{2,1,0:T(1,128)} %bitcast.12, bf16[2,768,128]{2,1,0:T(8,128)(2,1)} %get-tuple-element.21.rest_0_, ...), custom_call_target="tpu_custom_call" | custom-call | flops 16000000000 | bytes 3932160 | tf_op jit(solution)/shard_map/attention/pallas_call | solution.py:153
  179.2 0.0 copy-done.1
  179.2 11.4 %all-to-all-start.1 = ((bf16[8,16,3072]{2,1,0:T(8,128)(2,1)}), bf16[8,16,3072]{2,1,0:T(8,128)(2,1)S(1)}, u32[]{:S(2)}, u32[]{:S(2)}) async-start(bf16[8,16,3072]{2,1,0:T(8,128)(2,1)} %bitcast.11), calls=%async_computation.1 | async-start | bytes 1572864 | tf_op jit(solution)/shard_map/all_to_all | solution.py:397
  190.6 5.4 %taps_spectrum.1.taps_ref = f32[8,384,256]{2,1,0:T(8,128)} custom-call(bf16[32,16,768]{2,1,0:T(8,128)(2,1)} %copy-done.1, bf16[384,384]{1,0:T(8,128)(2,1)} %constant.53.clone.outer_ref, f32[2,192,128]{2,1,0:T(8,128)} %constant.54.clone.twist_ref, bf16[512,256]{1,0:T(8,128)(2,1)} %constant.55.clone.inner_ref), custom_call_target="tpu_custom_call" | custom-call | flops 5000000000 | bytes 4194304 | tf_op jit(solution)/shard_map/taps_spectrum/pallas_call | solution.py:324
  196.0 16.5 %all-to-all-done.1.signal_ref = bf16[8,16,3072]{2,1,0:T(8,128)(2,1)S(1)} async-done(((bf16[8,16,3072]{2,1,0:T(8,128)(2,1)}), bf16[8,16,3072]{2,1,0:T(8,128)(2,1)S(1)}, u32[]{:S(2)}, u32[]{:S(2)}) %all-to-all-start.1) | async-done | bytes 786464 | tf_op jit(solution)/shard_map/all_to_all | solution.py:397
  212.5 5.0 %all-to-all-start.2 = ((bf16[4,768,128]{2,1,0:T(8,128)(2,1)}), bf16[4,768,128]{2,1,0:T(8,128)(2,1)S(1)}, u32[]{:S(2)}, u32[]{:S(2)}) async-start(bf16[4,768,128]{2,1,0:T(8,128)(2,1)} %bitcast.6), calls=%async_computation.2 | async-start | bytes 1572864 | tf_op jit(solution)/shard_map/all_to_all | solution.py:397
  217.5 11.4 %convolution.1 = bf16[32,16,768]{2,1,0:T(8,128)(2,1)} custom-call(bf16[8,16,3072]{2,1,0:T(8,128)(2,1)} %copy-done.2, f32[8,384,256]{2,1,0:T(8,128)} %taps_spectrum.1.taps_ref, bf16[384,384]{1,0:T(8,128)(2,1)} %constant.56.clone.outer_ref, f32[2,192,128]{2,1,0:T(8,128)} %constant.54.clone.twist_ref, bf16[512,256]{1,0:T(8,128)(2,1)} %constant.55.clone.inner_ref, ...), custom_call_target="tpu_custom_call" | custom-call | flops 7000000000 | bytes 5242880 | tf_op jit(solution)/shard_map/convolution/pallas_call | solution.py:341
  228.8 1.1 all-to-all-done.2.attended_ref
  229.9 26.7 %all_to_all.20 = bf16[32,16,768]{2,1,0:T(8,128)(2,1)} all-to-all(bf16[32,16,768]{2,1,0:T(8,128)(2,1)} %convolution.1), channel_id=1, replica_groups=mesh['ctx'=32,'tp'=4,'dp'=2] {'ctx'}, dimensions={0} | all-to-all | bytes 1572864 | tf_op jit(solution)/shard_map/all_to_all | solution.py:397
  256.6 0.0 copy-done
  256.6 3.9 %finish.1 = (bf16[768,512]{1,0:T(8,128)(2,1)}, bf16[768,512]{1,0:T(8,128)(2,1)}) custom-call(bf16[8,4,16,768]{3,2,1,0:T(8,128)(2,1)} %bitcast.9, bf16[768,512]{1,0:T(8,128)(2,1)} %gate_ref.1, bf16[4,768,128]{2,1,0:T(8,128)(2,1)} %copy-done), custom_call_target="tpu_custom_call" | custom-call | tf_op jit(solution)/shard_map/finish/pallas_call | solution.py:369
  (16 shorter events, 0.0 us)
Async XLA Ops:
  0.6 79.0 %copy-start.10 = (s32[64]{0:T(128)S(1)}, s32[64]{0:T(128)}, u32[]{:S(2)}) copy-start(s32[64]{0:T(128)} %param.16) | copy-start | bytes 772
  3.1 89.2 %all-to-all-start = ((bf16[32,16,768]{2,1,0:T(8,128)(2,1)}), bf16[32,16,768]{2,1,0:T(8,128)(2,1)S(1)}, u32[]{:S(2)}, u32[]{:S(2)}) async-start(bf16[32,16,768]{2,1,0:T(8,128)(2,1)} %bitcast.4), calls=%async_computation | async-start | bytes 1572864 | tf_op jit(solution)/shard_map/all_to_all | solution.py:397
  63.3 12.9 %collective-permute-start = (bf16[2,768,128]{2,1,0:T(8,128)(2,1)}, bf16[2,768,128]{2,1,0:T(8,128)(2,1)S(1)}, u32[]{:S(2)}, u32[]{:S(2)}) collective-permute-start(bf16[2,768,128]{2,1,0:T(8,128)(2,1)} %get-tuple-element.22), channel_id=1, source_target_pairs={{0,8},{8,16},{16,24},{24,0},{32,40},{40,48},{48,56},{56,32},{64,72... | collective-permute-start | bytes 1179656 | tf_op jit(solution)/shard_map/ppermute | solution.py:401
  65.1 19.6 %collective-permute-start.1 = (bf16[2,768,128]{2,1,0:T(8,128)(2,1)}, bf16[2,768,128]{2,1,0:T(8,128)(2,1)S(1)}, u32[]{:S(2)}, u32[]{:S(2)}) collective-permute-start(bf16[2,768,128]{2,1,0:T(8,128)(2,1)} %get-tuple-element.23), channel_id=1, source_target_pairs={{0,16},{8,24},{16,0},{24,8},{32,48},{40,56},{48,32},{56,40},{64,80... | collective-permute-start | bytes 1179656 | tf_op jit(solution)/shard_map/ppermute | solution.py:401
  67.8 20.3 %collective-permute-start.2 = (bf16[2,768,128]{2,1,0:T(8,128)(2,1)}, bf16[2,768,128]{2,1,0:T(8,128)(2,1)S(1)}, u32[]{:S(2)}, u32[]{:S(2)}) collective-permute-start(bf16[2,768,128]{2,1,0:T(8,128)(2,1)} %get-tuple-element.24), channel_id=1, source_target_pairs={{0,24},{8,0},{16,8},{24,16},{32,56},{40,32},{48,40},{56,48},{64,88... | collective-permute-start | bytes 1179656 | tf_op jit(solution)/shard_map/ppermute | solution.py:401
  69.3 71.9 %collective-permute-start.3 = (bf16[2,768,128]{2,1,0:T(8,128)(2,1)}, bf16[2,768,128]{2,1,0:T(8,128)(2,1)S(1)}, u32[]{:S(2)}, u32[]{:S(2)}) collective-permute-start(bf16[2,768,128]{2,1,0:T(8,128)(2,1)} %get-tuple-element.21.rest_0_), channel_id=1, source_target_pairs={{8,40},{16,48},{24,56},{40,72},{48,80},{56,88},{72,104},{80,112},{... | collective-permute-start | bytes 1179656 | tf_op jit(solution)/shard_map/ppermute | solution.py:405
  76.1 84.4 %copy-start.4 = (bf16[2,768,128]{2,1,0:T(8,128)(2,1)}, bf16[2,768,128]{2,1,0:T(8,128)(2,1)S(1)}, u32[]{:S(2)}) copy-start(bf16[2,768,128]{2,1,0:T(8,128)(2,1)S(1)} %collective-permute-done.rest_1_) | copy-start | bytes 1179652
  76.1 65.2 %collective-permute-start.4 = (bf16[2,768,128]{2,1,0:T(8,128)(2,1)S(1)}, bf16[2,768,128]{2,1,0:T(8,128)(2,1)S(1)}, u32[]{:S(2)}, u32[]{:S(2)}) collective-permute-start(bf16[2,768,128]{2,1,0:T(8,128)(2,1)S(1)} %collective-permute-done.rest_1_), channel_id=1, source_target_pairs={{0,32},{16,48},{24,56},{32,64},{48,80},{56,88},{64,96},{80,112},{8... | collective-permute-start | bytes 1179656 | tf_op jit(solution)/shard_map/ppermute | solution.py:405
  84.7 75.9 %copy-start.5 = (bf16[2,768,128]{2,1,0:T(8,128)(2,1)}, bf16[2,768,128]{2,1,0:T(8,128)(2,1)S(1)}, u32[]{:S(2)}) copy-start(bf16[2,768,128]{2,1,0:T(8,128)(2,1)S(1)} %collective-permute-done.1.rest_2_) | copy-start | bytes 1179652
  84.7 60.6 %collective-permute-start.5 = (bf16[2,768,128]{2,1,0:T(8,128)(2,1)S(1)}, bf16[2,768,128]{2,1,0:T(8,128)(2,1)S(1)}, u32[]{:S(2)}, u32[]{:S(2)}) collective-permute-start(bf16[2,768,128]{2,1,0:T(8,128)(2,1)S(1)} %collective-permute-done.1.rest_2_), channel_id=1, source_target_pairs={{0,32},{8,40},{24,56},{32,64},{40,72},{56,88},{64,96},{72,104},{88... | collective-permute-start | bytes 1179656 | tf_op jit(solution)/shard_map/ppermute | solution.py:405
  88.1 72.5 %copy-start.6 = (bf16[2,768,128]{2,1,0:T(8,128)(2,1)}, bf16[2,768,128]{2,1,0:T(8,128)(2,1)S(1)}, u32[]{:S(2)}) copy-start(bf16[2,768,128]{2,1,0:T(8,128)(2,1)S(1)} %collective-permute-done.2.rest_3_) | copy-start | bytes 1179652
  88.1 57.2 %collective-permute-start.6 = (bf16[2,768,128]{2,1,0:T(8,128)(2,1)S(1)}, bf16[2,768,128]{2,1,0:T(8,128)(2,1)}, u32[]{:S(2)}, u32[]{:S(2)}) collective-permute-start(bf16[2,768,128]{2,1,0:T(8,128)(2,1)S(1)} %collective-permute-done.2.rest_3_), channel_id=1, source_target_pairs={{0,32},{8,40},{16,48},{32,64},{40,72},{48,80},{64,96},{72,104},{80... | collective-permute-start | bytes 1179656 | tf_op jit(solution)/shard_map/ppermute | solution.py:405
  92.3 87.0 %copy-start.1 = (bf16[32,16,768]{2,1,0:T(8,128)(2,1)}, bf16[32,16,768]{2,1,0:T(8,128)(2,1)S(1)}, u32[]{:S(2)}) copy-start(bf16[32,16,768]{2,1,0:T(8,128)(2,1)S(1)} %all-to-all-done.taps_ref) | copy-start | bytes 2359300
  141.1 18.8 %collective-permute-start.7 = (bf16[2,768,128]{2,1,0:T(8,128)(2,1)}, bf16[2,768,128]{2,1,0:T(8,128)(2,1)}, u32[]{:S(2)}, u32[]{:S(2)}) collective-permute-start(bf16[2,768,128]{2,1,0:T(8,128)(2,1)} %get-tuple-element.28), channel_id=1, source_target_pairs={{0,8},{8,16},{16,24},{24,0},{32,40},{40,48},{48,56},{56,32},{64,72... | collective-permute-start | bytes 1179656 | tf_op jit(solution)/shard_map/ppermute | solution.py:401
  141.2 4.1 %copy-start.7 = (bf16[2,768,128]{2,1,0:T(8,128)(2,1)}, bf16[2,768,128]{2,1,0:T(8,128)(2,1)S(1)}, u32[]{:S(2)}) copy-start(bf16[2,768,128]{2,1,0:T(8,128)(2,1)S(1)} %collective-permute-done.3.rest_4_) | copy-start | bytes 1179652
  141.2 18.7 %collective-permute-start.8 = (bf16[2,768,128]{2,1,0:T(8,128)(2,1)}, bf16[2,768,128]{2,1,0:T(8,128)(2,1)}, u32[]{:S(2)}, u32[]{:S(2)}) collective-permute-start(bf16[2,768,128]{2,1,0:T(8,128)(2,1)} %get-tuple-element.29), channel_id=1, source_target_pairs={{0,16},{8,24},{16,0},{24,8},{32,48},{40,56},{48,32},{56,40},{64,80... | collective-permute-start | bytes 1179656 | tf_op jit(solution)/shard_map/ppermute | solution.py:401
  141.3 18.6 %copy-start.8 = (bf16[2,768,128]{2,1,0:T(8,128)(2,1)}, bf16[2,768,128]{2,1,0:T(8,128)(2,1)S(1)}, u32[]{:S(2)}) copy-start(bf16[2,768,128]{2,1,0:T(8,128)(2,1)S(1)} %collective-permute-done.4.rest_5_) | copy-start | bytes 1179652
  141.3 19.2 %collective-permute-start.9 = (bf16[2,768,128]{2,1,0:T(8,128)(2,1)}, bf16[2,768,128]{2,1,0:T(8,128)(2,1)}, u32[]{:S(2)}, u32[]{:S(2)}) collective-permute-start(bf16[2,768,128]{2,1,0:T(8,128)(2,1)} %get-tuple-element.30), channel_id=1, source_target_pairs={{0,24},{8,0},{16,8},{24,16},{32,56},{40,32},{48,40},{56,48},{64,88... | collective-permute-start | bytes 1179656 | tf_op jit(solution)/shard_map/ppermute | solution.py:401
  144.5 16.1 %copy-start.3 = (s32[3072]{0:T(1024)}, s32[3072]{0:T(1024)S(1)}, u32[]{:S(2)}) copy-start(s32[3072]{0:T(1024)S(1)} %broadcast_subtract_fusion) | copy-start | bytes 36868
  145.3 14.6 %copy-start.9 = (bf16[2,768,128]{2,1,0:T(8,128)(2,1)}, bf16[2,768,128]{2,1,0:T(8,128)(2,1)S(1)}, u32[]{:S(2)}) copy-start(bf16[2,768,128]{2,1,0:T(8,128)(2,1)S(1)} %collective-permute-done.5.rest_6_) | copy-start | bytes 1179652
  179.2 33.3 %all-to-all-start.1 = ((bf16[8,16,3072]{2,1,0:T(8,128)(2,1)}), bf16[8,16,3072]{2,1,0:T(8,128)(2,1)S(1)}, u32[]{:S(2)}, u32[]{:S(2)}) async-start(bf16[8,16,3072]{2,1,0:T(8,128)(2,1)} %bitcast.11), calls=%async_computation.1 | async-start | bytes 1572864 | tf_op jit(solution)/shard_map/all_to_all | solution.py:397
  212.5 5.0 %copy-start.2 = (bf16[8,16,3072]{2,1,0:T(8,128)(2,1)}, bf16[8,16,3072]{2,1,0:T(8,128)(2,1)S(1)}, u32[]{:S(2)}) copy-start(bf16[8,16,3072]{2,1,0:T(8,128)(2,1)S(1)} %all-to-all-done.1.signal_ref) | copy-start | bytes 2359300
  212.5 17.4 %all-to-all-start.2 = ((bf16[4,768,128]{2,1,0:T(8,128)(2,1)}), bf16[4,768,128]{2,1,0:T(8,128)(2,1)S(1)}, u32[]{:S(2)}, u32[]{:S(2)}) async-start(bf16[4,768,128]{2,1,0:T(8,128)(2,1)} %bitcast.6), calls=%async_computation.2 | async-start | bytes 1572864 | tf_op jit(solution)/shard_map/all_to_all | solution.py:397
  229.9 26.7 %copy-start = (bf16[4,768,128]{2,1,0:T(8,128)(2,1)}, bf16[4,768,128]{2,1,0:T(8,128)(2,1)S(1)}, u32[]{:S(2)}) copy-start(bf16[4,768,128]{2,1,0:T(8,128)(2,1)S(1)} %all-to-all-done.2.attended_ref) | copy-start | bytes 2359300

commit v4 on v3

--- a/solution.py
+++ b/solution.py
@@ -14,6 +14,7 @@
 X_SIZE = 4
 Q_BLOCK = 768
 K_BLOCK = 384
+Q_SUB = 768
 LANES = 128
 VMEM_LIMIT = 62 * 2**20
 PAIRS = 4
@@ -28,38 +29,38 @@
     return jnp.max(jnp.where(inside, starts[None, :], 0), axis=1)
 
 
-def identity(size):
-    row = lax.broadcasted_iota(jnp.int32, (size, size), 0)
-    column = lax.broadcasted_iota(jnp.int32, (size, size), 1)
-    return jnp.where(row == column, 1.0, 0.0).astype(jnp.bfloat16)
-
-
-def transposed(x, eye):
-    return lax.dot_general(eye, x, (((1,), (1,)), ((), ())), preferred_element_type=jnp.float32)
-
-
 def pieces_kernel(x_ref, first_ref, second_ref, *rest):
-    outs, sems = rest[:X_SIZE], rest[X_SIZE]
-    copies = []
-    for k, out in enumerate(outs):
+    outs, (held, in_sems, out_sems) = rest[:X_SIZE], rest[X_SIZE:]
+    arriving, leaving = [], []
+    for k in range(X_SIZE):
         column = pl.multiple_of(lax.rem(x_ref[0] + k, X_SIZE) * HEAD_DIM, HEAD_DIM)
         for which, ref in enumerate((first_ref, second_ref)):
-            copy = pltpu.make_async_copy(ref.at[:, pl.ds(column, HEAD_DIM)], out.at[which], sems.at[k, which])
+            copy = pltpu.make_async_copy(ref.at[:, pl.ds(column, HEAD_DIM)], held.at[k, which], in_sems.at[k, which])
             copy.start()
-            copies.append(copy)
-    for copy in copies:
+            arriving.append((k, which, copy))
+    for k, which, copy in arriving:
         copy.wait()
+        out = pltpu.make_async_copy(held.at[k, which], outs[k].at[which], out_sems.at[k, which])
+        out.start()
+        leaving.append(out)
+    for out in leaving:
+        out.wait()
 
 
 def pieces_of(x_index, first, second):
+    rows = first.shape[0]
     anywhere = pl.BlockSpec(memory_space=pl.ANY)
     return pl.pallas_call(
         pieces_kernel,
         name="pieces",
         in_specs=[pl.BlockSpec(memory_space=pltpu.SMEM), anywhere, anywhere],
         out_specs=[anywhere] * X_SIZE,
-        out_shape=[jax.ShapeDtypeStruct((2, first.shape[0], HEAD_DIM), jnp.bfloat16)] * X_SIZE,
-        scratch_shapes=[pltpu.SemaphoreType.DMA((X_SIZE, 2))],
+        out_shape=[jax.ShapeDtypeStruct((2, rows, HEAD_DIM), jnp.bfloat16)] * X_SIZE,
+        scratch_shapes=[
+            pltpu.VMEM((X_SIZE, 2, rows, HEAD_DIM), jnp.bfloat16),
+            pltpu.SemaphoreType.DMA((X_SIZE, 2)),
+            pltpu.SemaphoreType.DMA((X_SIZE, 2)),
+        ],
     )(x_index, first, second)
 
 
@@ -69,79 +70,100 @@
     step = pl.program_id(0)
     group = queries_all.shape[0]
     piece = group // X_SIZE
-    eye = identity(HEAD_DIM)
+    group_blocks = group // K_BLOCK
+    piece_blocks = piece // K_BLOCK
+
+    def copies_of(k, chosen, sources):
+        at = pl.multiple_of(lax.rem(x_ref[0] + X_SIZE - k, X_SIZE) * piece, piece)
+        early, late = pl.ds(at, piece), pl.ds(at + group, piece)
+        targets = (keys.at[early], values.at[early], keys.at[late], values.at[late], queries_all.at[early], gate_all.at[early])
+        return [pltpu.make_async_copy(sources[n // 2].at[n % 2], targets[n], sems.at[k, n]) for n in chosen]
+
+    def reached(k):
+        position = lax.rem(x_ref[0] + X_SIZE - k, X_SIZE)
+        return jnp.logical_and(position > 0, (position + 1) * piece_blocks > lo_ref[0])
+
+    def turn(block, _):
+        rows = values[pl.ds(pl.multiple_of(block * K_BLOCK, K_BLOCK), K_BLOCK)]
+        values_t[block] = rows.T
+        return 0
 
     @pl.when(step == 0)
     def _():
-        copies = []
         for k in range(X_SIZE):
-            at = pl.multiple_of(lax.rem(x_ref[0] + X_SIZE - k, X_SIZE) * piece, piece)
-            early, late = pl.ds(at, piece), pl.ds(at + group, piece)
-            for n, (source, target) in enumerate(
-                (
-                    (own[k].at[0], keys.at[late]),
-                    (own[k].at[1], values.at[late]),
-                    (before[k].at[0], keys.at[early]),
-                    (before[k].at[1], values.at[early]),
-                    (asked[k].at[0], queries_all.at[early]),
-                    (asked[k].at[1], gate_all.at[early]),
-                )
-            ):
-                copy = pltpu.make_async_copy(source, target, sems.at[k, n])
+            sources = (before[k], own[k], asked[k])
+
+            @pl.when(reached(k))
+            def _():
+                for copy in copies_of(k, (0, 1), sources):
+                    copy.start()
+
+            for copy in copies_of(k, (2, 3, 4, 5), sources):
                 copy.start()
-                copies.append(copy)
-        for copy in copies:
-            copy.wait()
-
-        def turn(block, _):
-            rows = values[pl.ds(pl.multiple_of(block * K_BLOCK, K_BLOCK), K_BLOCK)]
-            values_t[block] = transposed(rows, eye).astype(jnp.bfloat16)
-            return 0
-
-        lax.fori_loop(lo_ref[0], values_t.shape[0], turn, 0)
+        for k in range(X_SIZE):
+
+            @pl.when(reached(k))
+            def _():
+                for copy in copies_of(k, (0, 1), (before[k], own[k], asked[k])):
+                    copy.wait()
+
+        lax.fori_loop(lo_ref[0], group_blocks, turn, 0)
+
+    now = lax.rem(x_ref[0] + X_SIZE - step, X_SIZE)
+    for copy in copies_of(now, (2, 3, 4, 5), (before[0], own[0], asked[0])):
+        copy.wait()
+    first = group + step * Q_BLOCK
+    diagonal = first // K_BLOCK
+    last = (first + Q_BLOCK - 1) // K_BLOCK
+    lax.fori_loop(diagonal, last + 1, turn, 0)
 
     here = pl.ds(pl.multiple_of(step * Q_BLOCK, Q_BLOCK), Q_BLOCK)
-    queries = transposed(queries_all[here], eye).astype(jnp.bfloat16)
-    first = group + step * Q_BLOCK
+    queries = queries_all[here].T
     start = start_ref[0]
     query_index = first + lax.broadcasted_iota(jnp.int32, (1, Q_BLOCK), 1)
     key_offset = lax.broadcasted_iota(jnp.int32, (K_BLOCK, 1), 0)
     factor = math.log2(math.e) / math.sqrt(HEAD_DIM)
-
-    def visit(masked, block, carried):
-        top, total, weighted = carried
+    subs = [slice(at, at + Q_SUB) for at in range(0, Q_BLOCK, Q_SUB)]
+
+    def visit(kind, block, carried):
         key_rows = keys[pl.ds(pl.multiple_of(block * K_BLOCK, K_BLOCK), K_BLOCK)]
-        scores = jnp.dot(key_rows, queries, preferred_element_type=jnp.float32) * factor
-        if masked:
-            index = block * K_BLOCK + key_offset
-            scores = jnp.where((index >= start) & (index <= query_index), scores, masked_score)
-        new_top = jnp.maximum(top, jnp.max(scores, axis=0, keepdims=True))
-        rescale = jnp.exp2(top - new_top)
-        weight = jnp.exp2(scores - new_top)
-        total = total * rescale + jnp.sum(weight, axis=0, keepdims=True)
-        weighted = weighted * rescale + jnp.dot(
-            values_t[block], weight.astype(jnp.bfloat16), preferred_element_type=jnp.float32
+        block_values = values_t[block]
+        index = block * K_BLOCK + key_offset
+        result = []
+        for sub, (top, total, weighted) in zip(subs, carried):
+            scores = jnp.dot(key_rows, queries[:, sub], preferred_element_type=jnp.float32) * factor
+            if kind == "before":
+                scores = jnp.where(index >= start[:, sub], scores, masked_score)
+            if kind == "diagonal":
+                kept = (index >= start[:, sub]) & (index <= query_index[:, sub])
+                scores = jnp.where(kept, scores, masked_score)
+            new_top = jnp.maximum(top, jnp.max(scores, axis=0, keepdims=True))
+            rescale = jnp.exp2(top - new_top)
+            weight = jnp.exp2(scores - new_top)
+            total = total * rescale + jnp.sum(weight, axis=0, keepdims=True)
+            weighted = weighted * rescale + jnp.dot(
+                block_values, weight.astype(jnp.bfloat16), preferred_element_type=jnp.float32
+            )
+            result.append((new_top, total, weighted))
+        return tuple(result)
+
+    middle = jnp.minimum(mid_ref[step], diagonal)
+    carried = tuple(
+        (
+            jnp.full((1, Q_SUB), masked_score, jnp.float32),
+            jnp.zeros((1, Q_SUB), jnp.float32),
+            jnp.zeros((HEAD_DIM, Q_SUB), jnp.float32),
         )
-        return new_top, total, weighted
-
-    diagonal = first // K_BLOCK
-    last = (first + Q_BLOCK - 1) // K_BLOCK
-    middle = jnp.minimum(mid_ref[step], diagonal)
-    carried = (
-        jnp.full((1, Q_BLOCK), masked_score, jnp.float32),
-        jnp.zeros((1, Q_BLOCK), jnp.float32),
-        jnp.zeros((HEAD_DIM, Q_BLOCK), jnp.float32),
+        for _ in subs
     )
-    edge, inside = functools.partial(visit, True), functools.partial(visit, False)
-    carried = lax.fori_loop(lo_ref[step], middle, edge, carried)
-    carried = lax.fori_loop(middle, diagonal, inside, carried)
-    top, total, weighted = lax.fori_loop(diagonal, last + 1, edge, carried)
-    rounded = (weighted * (1.0 / total)).astype(jnp.bfloat16)
-    wide = identity(2 * LANES)
-    for at in range(0, Q_BLOCK, 2 * LANES):
-        part = transposed(rounded[:, at : at + 2 * LANES], wide)
-        out_ref[at : at + 2 * LANES] = part.astype(jnp.bfloat16)
-    gated_ref[...] = (rounded.astype(jnp.float32) * transposed(gate_all[here], eye)).astype(jnp.bfloat16)
+    carried = lax.fori_loop(lo_ref[step], middle, functools.partial(visit, "before"), carried)
+    carried = lax.fori_loop(middle, diagonal, functools.partial(visit, "inside"), carried)
+    carried = lax.fori_loop(diagonal, last + 1, functools.partial(visit, "diagonal"), carried)
+    gate = gate_all[here].T
+    for sub, (top, total, weighted) in zip(subs, carried):
+        rounded = (weighted * (1.0 / total)).astype(jnp.bfloat16)
+        out_ref[0, sub] = rounded.T
+        gated_ref[:, sub] = (rounded.astype(jnp.float32) * gate[:, sub].astype(jnp.float32)).astype(jnp.bfloat16)
 
 
 def attention(x_index, own, before, asked, start):
@@ -158,7 +180,7 @@
             grid=(steps,),
             in_specs=[pl.BlockSpec((1, 1, Q_BLOCK), lambda i, *_: (i, 0, 0))] + [anywhere] * (3 * X_SIZE),
             out_specs=[
-                pl.BlockSpec((Q_BLOCK, HEAD_DIM), lambda i, *_: (i, 0)),
+                pl.BlockSpec((1, Q_BLOCK, HEAD_DIM), lambda i, lo, mid, x: (lax.rem(i - x[0] + X_SIZE, X_SIZE), 0, 0)),
                 pl.BlockSpec((HEAD_DIM, Q_BLOCK), lambda i, *_: (0, i)),
             ],
             scratch_shapes=[
@@ -171,7 +193,7 @@
             ],
         ),
         out_shape=[
-            jax.ShapeDtypeStruct((rows, HEAD_DIM), jnp.bfloat16),
+            jax.ShapeDtypeStruct((X_SIZE, rows // X_SIZE, HEAD_DIM), jnp.bfloat16),
             jax.ShapeDtypeStruct((HEAD_DIM, rows), jnp.bfloat16),
         ],
         compiler_params=pltpu.CompilerParams(vmem_limit_bytes=VMEM_LIMIT),
@@ -355,13 +377,46 @@
     )(signal, spectra, *operands)
 
 
-def finish_kernel(mixed_ref, gate_ref, attended_ref, attn_ref, hyena_ref):
-    mixed = mixed_ref[...].reshape(HEAD_DIM, mixed_ref.shape[3]).astype(jnp.float32).T
-    hyena_ref[...] = (gate_ref[...].astype(jnp.float32) * mixed).astype(jnp.bfloat16)
-    attn_ref[...] = attended_ref[0]
-
-
-def finish(returned, out_gate, attended):
+def assemble_kernel(x_ref, *rest):
+    pieces, (out, held, in_sems, out_sems) = rest[:X_SIZE], rest[X_SIZE:]
+    arriving = [pltpu.make_async_copy(pieces[k], held.at[k], in_sems.at[k]) for k in range(X_SIZE)]
+    for copy in arriving:
+        copy.start()
+    leaving = []
+    for k, copy in enumerate(arriving):
+        column = pl.multiple_of(lax.rem(x_ref[0] + X_SIZE - k, X_SIZE) * HEAD_DIM, HEAD_DIM)
+        copy.wait()
+        out_copy = pltpu.make_async_copy(held.at[k], out.at[:, pl.ds(column, HEAD_DIM)], out_sems.at[k])
+        out_copy.start()
+        leaving.append(out_copy)
+    for copy in leaving:
+        copy.wait()
+
+
+def assembled(x_index, pieces):
+    rows = pieces[0].shape[0]
+    anywhere = pl.BlockSpec(memory_space=pl.ANY)
+    return pl.pallas_call(
+        assemble_kernel,
+        name="assemble",
+        in_specs=[pl.BlockSpec(memory_space=pltpu.SMEM)] + [anywhere] * X_SIZE,
+        out_specs=anywhere,
+        out_shape=jax.ShapeDtypeStruct((rows, X_SIZE * HEAD_DIM), jnp.bfloat16),
+        scratch_shapes=[
+            pltpu.VMEM((X_SIZE, rows, HEAD_DIM), jnp.bfloat16),
+            pltpu.SemaphoreType.DMA((X_SIZE,)),
+            pltpu.SemaphoreType.DMA((X_SIZE,)),
+        ],
+        cost_estimate=pl.CostEstimate(flops=2 * 10**9, bytes_accessed=2**20, transcendentals=0),
+    )(x_index, *pieces)
+
+
+def finish_kernel(mixed_ref, gate_ref, hyena_ref):
+    mixed = mixed_ref[...].reshape(HEAD_DIM, mixed_ref.shape[3]).T
+    hyena_ref[...] = (gate_ref[...].astype(jnp.float32) * mixed.astype(jnp.float32)).astype(jnp.bfloat16)
+
+
+def finish(returned, out_gate):
     rows, channels = out_gate.shape
     z_size = returned.shape[0] // X_SIZE
     returned = returned.reshape(z_size, X_SIZE, returned.shape[1], rows)
@@ -370,15 +425,11 @@
         finish_kernel,
         name="finish",
         grid=(channels // HEAD_DIM,),
-        in_specs=[
-            pl.BlockSpec((z_size, 1, returned.shape[2], rows), lambda i: (0, i, 0, 0)),
-            by_columns,
-            pl.BlockSpec((1, rows, HEAD_DIM), lambda i: (i, 0, 0)),
-        ],
-        out_specs=[by_columns, by_columns],
-        out_shape=[jax.ShapeDtypeStruct((rows, channels), jnp.bfloat16)] * 2,
-        compiler_params=pltpu.CompilerParams(vmem_limit_bytes=VMEM_LIMIT),
-    )(returned, out_gate, attended)
+        in_specs=[pl.BlockSpec((z_size, 1, returned.shape[2], rows), lambda i: (0, i, 0, 0)), by_columns],
+        out_specs=by_columns,
+        out_shape=jax.ShapeDtypeStruct((rows, channels), jnp.bfloat16),
+        compiler_params=pltpu.CompilerParams(vmem_limit_bytes=16 * 2**20),
+    )(returned, out_gate)
 
 
 def body(queries, key_rows, values, doc_lengths, in_gate, out_gate, filter_taps):
@@ -387,7 +438,6 @@
     z_size = ctx // X_SIZE
     group_rows = X_SIZE * row_count
     per_device = channels // ctx
-    x_groups = [[z * X_SIZE + x for x in range(X_SIZE)] for z in range(z_size)]
     z_groups = [[z * X_SIZE + x for z in range(z_size)] for x in range(X_SIZE)]
     tables = transform_tables(row_count * ctx, z_size, ctx)
     me = lax.axis_index("ctx").astype(jnp.int32)
@@ -409,10 +459,12 @@
 
     taps = filter_taps.astype(jnp.bfloat16).reshape(X_SIZE, z_size, per_device, row_count)
     taps = taps.transpose(1, 0, 2, 3).reshape(ctx, per_device, row_count)
-    own = arrived(pieces_of(x_index, key_rows, values))
+    pieces = pieces_of(x_index, key_rows, values)
+    own = arrived(pieces)
+    taps, _ = lax.optimization_barrier((taps, pieces[0]))
     taps = exchanged(taps)
     before = [along_z(own[k], k) for k in range(X_SIZE)]
-    taps, queries, in_gate = lax.optimization_barrier((taps, queries, in_gate))
+    own[1], queries, in_gate = lax.optimization_barrier((own[1], queries, in_gate))
     asked = arrived(pieces_of(x_index, queries, in_gate))
 
     group_first = (me // X_SIZE) * group_rows
@@ -423,12 +475,12 @@
     gated, taps = lax.optimization_barrier((gated, taps))
     signal = exchanged(gated.reshape(z_size, per_device, group_rows), z_groups)
     spectra = transform_taps(taps, tables)
-    signal, attended = lax.optimization_barrier((signal, attended.reshape(X_SIZE, row_count, HEAD_DIM)))
-    attended = exchanged(attended, x_groups)
+    spectra, attended = lax.optimization_barrier((spectra, attended))
+    attended = arrived([attended[k] for k in range(X_SIZE)])
     mixed = convolve(signal, spectra, tables, ctx)
-    mixed, attended = lax.optimization_barrier((mixed, attended))
+    mixed, *attended = lax.optimization_barrier((mixed, *attended))
     returned = exchanged(mixed)
-    return finish(returned, out_gate, attended)
+    return assembled(x_index, attended), finish(returned, out_gate)
 
 
 def solution(mesh):

time: 260 us -> 163 us (0.63); the launches traced: 260 us -> 160 us
  Pallas kernels: 137 us -> 40 us
  blocking collectives: 26.7 us -> 0 us
  starting transfers between devices: 48.7 us -> 60.6 us
  waiting for transfers between devices: 43.8 us -> 53.6 us
  local copies, waits for them, and re-layouts: 1.17 us -> 4.04 us
    pallas_call x2, Pallas kernels: 97.6 us -> 4.87 us  [pieces_of(): pl.pallas_call(pieces_kernel, name='pieces', in_specs=[pl.BlockSpec(memor...]
    all_to_all x1 -> x0, blocking collectives: 26.7 us -> none  [exchanged(): lax.all_to_all(x, 'ctx', split_axis=0, concat_axis=0, tiled=True, axis_in...]
    ppermute x4, waiting for transfers between devices: 0.01 us -> 12.9 us  [along_z(): return lax.ppermute(piece, 'ctx', pairs)]
    ppermute x6 -> x9, waiting for transfers between devices: 26.2 us -> 13.4 us  [along_x(): return lax.ppermute(piece, 'ctx', pairs)]
    all_to_all x3, waiting for transfers between devices: 17.6 us -> 27.3 us  [exchanged(): lax.all_to_all(x, 'ctx', split_axis=0, concat_axis=0, tiled=True, axis_in...]
    ppermute x6 -> x9, starting transfers between devices: 9.37 us -> 18.2 us  [along_x(): return lax.ppermute(piece, 'ctx', pairs)]
    pallas_call x1, Pallas kernels: 18.6 us -> 14.5 us  [attention(): pl.pallas_call(attention_kernel, name='attention', grid_spec=pltpu.Prefet...]
    all_to_all x3, starting transfers between devices: 27.7 us -> 30.8 us  [exchanged(): lax.all_to_all(x, 'ctx', split_axis=0, concat_axis=0, tiled=True, axis_in...]
  transfers between devices with their start and end apart: 13 -> 16, of which waited for: 6 -> 7; matrix products, arithmetic and copies ran while one was open for 0% -> 3% of each run, Pallas kernels for 44% -> 22%
where the time goes in v4:
time: 163 us; the launch traced here: 160 us
  starting transfers between devices  60.6 us (37%)
  waiting for transfers between devices  53.6 us (33%)
  Pallas kernels  40 us (25%)
  local copies, waits for them, and re-layouts  4.04 us (2%)
    all_to_all x3, starting transfers between devices, exchanged(): lax.all_to_all(x, 'ctx', split_axis=0, concat_axis=0, tiled=True, axis_in...  30.8 us
    all_to_all x3, waiting for transfers between devices, exchanged(): lax.all_to_all(x, 'ctx', split_axis=0, concat_axis=0, tiled=True, axis_in...  27.3 us
    ppermute x9, starting transfers between devices, along_x(): return lax.ppermute(piece, 'ctx', pairs)  18.2 us
    pallas_call x1, Pallas kernels, attention(): pl.pallas_call(attention_kernel, name='attention', grid_spec=pltpu.Prefet...  14.5 us
    ppermute x9, waiting for transfers between devices, along_x(): return lax.ppermute(piece, 'ctx', pairs)  13.4 us
    ppermute x4, waiting for transfers between devices, along_z(): return lax.ppermute(piece, 'ctx', pairs)  12.9 us
    ppermute x4, starting transfers between devices, along_z(): return lax.ppermute(piece, 'ctx', pairs)  11.6 us
    pallas_call x1, Pallas kernels, convolve(): pl.pallas_call(conv_kernel, name='convolution', grid=(channels // (2 * PA...  11.3 us
  transfers between devices with their start and end apart: 16, of which 7 were waited for; matrix products, arithmetic and copies ran while one was open for 3% of the time, Pallas kernels for 22%

profile of v4, /device:TPU:16, one launch (start us, length us, event | category | flops | bytes accessed | tf_op | source)
XLA Modules:
  0.0 160.0 jit_solution(8959166350974127851)
XLA Ops:
  0.6 2.4 %pieces.2 = (bf16[2,768,128]{2,1,0:T(8,128)(2,1)}, bf16[2,768,128]{2,1,0:T(8,128)(2,1)}, bf16[2,768,128]{2,1,0:T(8,128)(2,1)}, bf16[2,768,128]{2,1,0:T(8,128)(2,1)}) custom-call(s32[1]{0:T(128)} %bitcast.x_ref, bf16[768,512]{1,0:T(8,128)(2,1)} %first_ref.1, bf16[768,512]{1,0:T(8,128)(2,1)} %second_ref.1), custom_call_target="tpu_custom_call" | custom-call | tf_op jit(solution)/shard_map/pieces/pallas_call | solution.py:53
  3.1 1.6 collective-permute-start
  4.6 0.7 collective-permute-start.3
  5.3 6.0 %collective-permute-start.1 = (bf16[2,768,128]{2,1,0:T(8,128)(2,1)}, bf16[2,768,128]{2,1,0:T(8,128)(2,1)S(1)}, u32[]{:S(2)}, u32[]{:S(2)}) collective-permute-start(bf16[2,768,128]{2,1,0:T(8,128)(2,1)} %get-tuple-element.28), channel_id=1, source_target_pairs={{0,16},{8,24},{16,0},{24,8},{32,48},{40,56},{48,32},{56,40},{64,80... | collective-permute-start | bytes 1179656 | tf_op jit(solution)/shard_map/ppermute | solution.py:451
  11.3 1.4 collective-permute-start.2
  12.7 2.9 %collective-permute-done.rest_1_ = bf16[2,768,128]{2,1,0:T(8,128)(2,1)S(1)} collective-permute-done((bf16[2,768,128]{2,1,0:T(8,128)(2,1)}, bf16[2,768,128]{2,1,0:T(8,128)(2,1)S(1)}, u32[]{:S(2)}, u32[]{:S(2)}) %collective-permute-start) | collective-permute-done | bytes 393248 | tf_op jit(solution)/shard_map/ppermute | solution.py:451
  15.6 2.5 %pieces.3 = (bf16[2,768,128]{2,1,0:T(8,128)(2,1)}, bf16[2,768,128]{2,1,0:T(8,128)(2,1)}, bf16[2,768,128]{2,1,0:T(8,128)(2,1)}, bf16[2,768,128]{2,1,0:T(8,128)(2,1)}) custom-call(s32[1]{0:T(128)} %bitcast.x_ref, bf16[768,512]{1,0:T(8,128)(2,1)} %first_ref.2, bf16[768,512]{1,0:T(8,128)(2,1)} %second_ref.2), custom_call_target="tpu_custom_call" | custom-call | tf_op jit(solution)/shard_map/pieces/pallas_call | solution.py:53
  18.1 0.0 copy-start.14
  18.1 1.3 collective-permute-start.7
  19.4 0.1 convert_element_type.3
  19.5 1.0 copy.16
  20.5 11.0 %all-to-all-start = ((bf16[32,16,768]{2,1,0:T(8,128)(2,1)}), bf16[32,16,768]{2,1,0:T(8,128)(2,1)S(1)}, u32[]{:S(2)}, u32[]{:S(2)}) async-start(bf16[32,16,768]{2,1,0:T(8,128)(2,1)} %bitcast.4), calls=%async_computation | async-start | bytes 1572864 | tf_op jit(solution)/shard_map/all_to_all | solution.py:447
  31.6 0.1 select_reduce_fusion.1
  31.7 0.2 select_reduce_fusion
  31.9 3.4 %collective-permute-start.8 = (bf16[2,768,128]{2,1,0:T(8,128)(2,1)S(1)}, bf16[2,768,128]{2,1,0:T(8,128)(2,1)S(1)}, u32[]{:S(2)}, u32[]{:S(2)}) collective-permute-start(bf16[2,768,128]{2,1,0:T(8,128)(2,1)S(1)} %copy-done.9), channel_id=1, source_target_pairs={{0,16},{8,24},{16,0},{24,8},{32,48},{40,56},{48,32},{56,40},{64,80... | collective-permute-start | bytes 1179656 | tf_op jit(solution)/shard_map/ppermute | solution.py:451
  35.3 0.0 collective-permute-done.3.rest_4_
  35.3 1.2 collective-permute-start.9
  36.5 0.0 collective-permute-done.1.rest_2_
  36.5 4.1 %collective-permute-start.4 = (bf16[2,768,128]{2,1,0:T(8,128)(2,1)S(1)}, bf16[2,768,128]{2,1,0:T(8,128)(2,1)}, u32[]{:S(2)}, u32[]{:S(2)}) collective-permute-start(bf16[2,768,128]{2,1,0:T(8,128)(2,1)S(1)} %collective-permute-done.rest_1_), channel_id=1, source_target_pairs={{0,32},{16,48},{24,56},{32,64},{48,80},{56,88},{64,96},{80,112},{8... | collective-permute-start | bytes 1179656 | tf_op jit(solution)/shard_map/ppermute | solution.py:455
  40.6 0.0 collective-permute-done.2.rest_3_
  40.6 3.4 %collective-permute-start.5 = (bf16[2,768,128]{2,1,0:T(8,128)(2,1)S(1)}, bf16[2,768,128]{2,1,0:T(8,128)(2,1)}, u32[]{:S(2)}, u32[]{:S(2)}) collective-permute-start(bf16[2,768,128]{2,1,0:T(8,128)(2,1)S(1)} %collective-permute-done.1.rest_2_), channel_id=1, source_target_pairs={{0,32},{8,40},{24,56},{32,64},{40,72},{56,88},{64,96},{72,104},{88... | collective-permute-start | bytes 1179656 | tf_op jit(solution)/shard_map/ppermute | solution.py:455
  44.0 0.0 collective-permute-done.7.rest_9_
  44.0 3.4 %collective-permute-start.6 = (bf16[2,768,128]{2,1,0:T(8,128)(2,1)}, bf16[2,768,128]{2,1,0:T(8,128)(2,1)}, u32[]{:S(2)}, u32[]{:S(2)}) collective-permute-start(bf16[2,768,128]{2,1,0:T(8,128)(2,1)} %collective-permute-done.2.rest_3_), channel_id=1, source_target_pairs={{0,32},{8,40},{16,48},{32,64},{40,72},{48,80},{64,96},{72,104},{80... | collective-permute-start | bytes 1179656 | tf_op jit(solution)/shard_map/ppermute | solution.py:455
  47.4 0.1 slice.18
  47.5 0.1 slice.19
  47.6 0.6 and_select_fusion.1
  48.2 2.3 %collective-permute-done.8.rest_10_ = bf16[2,768,128]{2,1,0:T(8,128)(2,1)S(1)} collective-permute-done((bf16[2,768,128]{2,1,0:T(8,128)(2,1)S(1)}, bf16[2,768,128]{2,1,0:T(8,128)(2,1)S(1)}, u32[]{:S(2)}, u32[]{:S(2)}) %collective-permute-start.8) | collective-permute-done | bytes 393248 | tf_op jit(solution)/shard_map/ppermute | solution.py:451
  50.5 8.2 %collective-permute-done.9.rest_11_ = bf16[2,768,128]{2,1,0:T(8,128)(2,1)} collective-permute-done((bf16[2,768,128]{2,1,0:T(8,128)(2,1)S(1)}, bf16[2,768,128]{2,1,0:T(8,128)(2,1)}, u32[]{:S(2)}, u32[]{:S(2)}) %collective-permute-start.9) | collective-permute-done | bytes 393248 | tf_op jit(solution)/shard_map/ppermute | solution.py:451
  58.7 0.0 collective-permute-done.4.rest_5_
  58.7 7.0 %collective-permute-done.5.rest_6_ = bf16[2,768,128]{2,1,0:T(8,128)(2,1)} collective-permute-done((bf16[2,768,128]{2,1,0:T(8,128)(2,1)S(1)}, bf16[2,768,128]{2,1,0:T(8,128)(2,1)}, u32[]{:S(2)}, u32[]{:S(2)}) %collective-permute-start.5) | collective-permute-done | bytes 393248 | tf_op jit(solution)/shard_map/ppermute | solution.py:455
  65.8 5.9 %collective-permute-done.6.rest_7_ = bf16[2,768,128]{2,1,0:T(8,128)(2,1)} collective-permute-done((bf16[2,768,128]{2,1,0:T(8,128)(2,1)}, bf16[2,768,128]{2,1,0:T(8,128)(2,1)}, u32[]{:S(2)}, u32[]{:S(2)}) %collective-permute-start.6) | collective-permute-done | bytes 393248 | tf_op jit(solution)/shard_map/ppermute | solution.py:455
  71.6 14.5 %attention.1 = (bf16[4,768,128]{2,1,0:T(8,128)(2,1)}, bf16[128,3072]{1,0:T(8,128)(2,1)}) custom-call(s32[4]{0:T(128)} %get-tuple-element.52.lo_ref, s32[4]{0:T(128)} %get-tuple-element.53.mid_ref, s32[1]{0:T(128)} %bitcast.x_ref, s32[4,1,768]{2,1,0:T(1,128)} %bitcast.19, bf16[2,768,128]{2,1,0:T(8,128)(2,1)} %get-tuple-element.25.rest_0_, ...), custom_call_target="tpu_custom_call" | custom-call | flops 16000000000 | bytes 3932160 | tf_op jit(solution)/shard_map/attention/pallas_call | solution.py:175
  86.2 15.8 %all-to-all-start.1 = ((bf16[8,16,3072]{2,1,0:T(8,128)(2,1)}), bf16[8,16,3072]{2,1,0:T(8,128)(2,1)S(1)}, u32[]{:S(2)}, u32[]{:S(2)}) async-start(bf16[8,16,3072]{2,1,0:T(8,128)(2,1)} %bitcast.18), calls=%async_computation.1 | async-start | bytes 1572864 | tf_op jit(solution)/shard_map/all_to_all | solution.py:447
  102.0 5.4 %taps_spectrum.1.taps_ref = f32[8,384,256]{2,1,0:T(8,128)} custom-call(bf16[32,16,768]{2,1,0:T(8,128)(2,1)} %copy-done.2, bf16[384,384]{1,0:T(8,128)(2,1)} %constant.53.clone.outer_ref, f32[2,192,128]{2,1,0:T(8,128)} %constant.54.clone.twist_ref, bf16[512,256]{1,0:T(8,128)(2,1)} %constant.55.clone.inner_ref), custom_call_target="tpu_custom_call" | custom-call | flops 5000000000 | bytes 4194304 | tf_op jit(solution)/shard_map/taps_spectrum/pallas_call | solution.py:346
  107.4 1.9 %slice_bitcast_fusion = (bf16[768,128]{1,0:T(8,128)(2,1)S(1)}, bf16[768,128]{1,0:T(8,128)(2,1)S(1)}, bf16[768,128]{1,0:T(8,128)(2,1)S(1)}, bf16[768,128]{1,0:T(8,128)(2,1)}) fusion(bf16[4,768,128]{2,1,0:T(8,128)(2,1)} %get-tuple-element.42), kind=kLoop, calls=%fused_computation.1 | loop fusion | bytes 1572864 | tf_op jit(solution)/shard_map/squeeze | solution.py:479
  109.3 0.0 collective-permute-start.11
  109.3 3.2 %collective-permute-start.12 = (bf16[768,128]{1,0:T(8,128)(2,1)S(1)}, bf16[768,128]{1,0:T(8,128)(2,1)S(1)}, u32[]{:S(2)}, u32[]{:S(2)}) collective-permute-start(bf16[768,128]{1,0:T(8,128)(2,1)S(1)} %get-tuple-element.48), channel_id=1, source_target_pairs={{0,24},{8,0},{16,8},{24,16},{32,56},{40,32},{48,40},{56,48},{64,88... | collective-permute-start | bytes 589832 | tf_op jit(solution)/shard_map/ppermute | solution.py:451
  112.6 9.7 %all-to-all-done.1.signal_ref = bf16[8,16,3072]{2,1,0:T(8,128)(2,1)S(1)} async-done(((bf16[8,16,3072]{2,1,0:T(8,128)(2,1)}), bf16[8,16,3072]{2,1,0:T(8,128)(2,1)S(1)}, u32[]{:S(2)}, u32[]{:S(2)}) %all-to-all-start.1) | async-done | bytes 786464 | tf_op jit(solution)/shard_map/all_to_all | solution.py:447
  122.2 0.9 copy-done.3
  123.1 11.3 %convolution.1 = bf16[32,16,768]{2,1,0:T(8,128)(2,1)} custom-call(bf16[8,16,3072]{2,1,0:T(8,128)(2,1)} %copy-done.3, f32[8,384,256]{2,1,0:T(8,128)} %taps_spectrum.1.taps_ref, bf16[384,384]{1,0:T(8,128)(2,1)} %constant.56.clone.outer_ref, f32[2,192,128]{2,1,0:T(8,128)} %constant.54.clone.twist_ref, bf16[512,256]{1,0:T(8,128)(2,1)} %constant.55.clone.inner_ref, ...), custom_call_target="tpu_custom_call" | custom-call | flops 7000000000 | bytes 5242880 | tf_op jit(solution)/shard_map/convolution/pallas_call | solution.py:363
  134.5 0.0 collective-permute-done.10.rest_1_
  134.5 0.0 collective-permute-done.11.rest_2_
  134.5 0.0 collective-permute-done.12.rest_3_
  134.5 3.9 %all-to-all-start.2 = ((bf16[32,16,768]{2,1,0:T(8,128)(2,1)}), bf16[32,16,768]{2,1,0:T(8,128)(2,1)S(1)}, u32[]{:S(2)}, u32[]{:S(2)}) async-start(bf16[32,16,768]{2,1,0:T(8,128)(2,1)} %convolution.1), calls=%async_computation.2 | async-start | bytes 1572864 | tf_op jit(solution)/shard_map/all_to_all | solution.py:447
  138.5 0.0 copy-start
  138.5 2.0 %assemble.1 = bf16[768,512]{1,0:T(8,128)(2,1)} custom-call(s32[1]{0:T(128)} %bitcast.x_ref, bf16[768,128]{1,0:T(8,128)(2,1)} %get-tuple-element.43.rest_0_, bf16[768,128]{1,0:T(8,128)(2,1)} %copy-done.11, bf16[768,128]{1,0:T(8,128)(2,1)} %copy-done.12, bf16[768,128]{1,0:T(8,128)(2,1)} %copy-done.13), custom_call_target="tpu_custom_call" | custom-call | flops 2000000000 | bytes 1048576 | tf_op jit(solution)/shard_map/assemble/pallas_call | solution.py:399
  140.5 17.7 %all-to-all-done.2 = bf16[32,16,768]{2,1,0:T(8,128)(2,1)S(1)} async-done(((bf16[32,16,768]{2,1,0:T(8,128)(2,1)}), bf16[32,16,768]{2,1,0:T(8,128)(2,1)S(1)}, u32[]{:S(2)}, u32[]{:S(2)}) %all-to-all-start.2) | async-done | bytes 786464 | tf_op jit(solution)/shard_map/all_to_all | solution.py:447
  158.2 1.9 %finish.1 = bf16[768,512]{1,0:T(8,128)(2,1)} custom-call(bf16[8,4,16,768]{3,2,1,0:T(8,128)(2,1)S(1)} %bitcast.16, bf16[768,512]{1,0:T(8,128)(2,1)S(1)} %copy-done), custom_call_target="tpu_custom_call" | custom-call | tf_op jit(solution)/shard_map/finish/pallas_call | solution.py:424
  (31 shorter events, 0.1 us)
Async XLA Ops:
  0.6 18.8 %copy-start.1 = (f32[512,768]{1,0:T(8,128)S(1)}, f32[512,768]{1,0:T(8,128)}, u32[]{:S(2)}) copy-start(f32[512,768]{1,0:T(8,128)} %param.19) | copy-start | bytes 4718596
  3.1 12.5 %collective-permute-start = (bf16[2,768,128]{2,1,0:T(8,128)(2,1)}, bf16[2,768,128]{2,1,0:T(8,128)(2,1)S(1)}, u32[]{:S(2)}, u32[]{:S(2)}) collective-permute-start(bf16[2,768,128]{2,1,0:T(8,128)(2,1)} %get-tuple-element.26), channel_id=1, source_target_pairs={{0,8},{8,16},{16,24},{24,0},{32,40},{40,48},{48,56},{56,32},{64,72... | collective-permute-start | bytes 1179656 | tf_op jit(solution)/shard_map/ppermute | solution.py:451
  4.6 30.6 %collective-permute-start.3 = (bf16[2,768,128]{2,1,0:T(8,128)(2,1)}, bf16[2,768,128]{2,1,0:T(8,128)(2,1)S(1)}, u32[]{:S(2)}, u32[]{:S(2)}) collective-permute-start(bf16[2,768,128]{2,1,0:T(8,128)(2,1)} %get-tuple-element.25.rest_0_), channel_id=1, source_target_pairs={{8,40},{16,48},{24,56},{40,72},{48,80},{56,88},{72,104},{80,112},{... | collective-permute-start | bytes 1179656 | tf_op jit(solution)/shard_map/ppermute | solution.py:455
  5.3 31.2 %collective-permute-start.1 = (bf16[2,768,128]{2,1,0:T(8,128)(2,1)}, bf16[2,768,128]{2,1,0:T(8,128)(2,1)S(1)}, u32[]{:S(2)}, u32[]{:S(2)}) collective-permute-start(bf16[2,768,128]{2,1,0:T(8,128)(2,1)} %get-tuple-element.28), channel_id=1, source_target_pairs={{0,16},{8,24},{16,0},{24,8},{32,48},{40,56},{48,32},{56,40},{64,80... | collective-permute-start | bytes 1179656 | tf_op jit(solution)/shard_map/ppermute | solution.py:451
  11.3 29.3 %collective-permute-start.2 = (bf16[2,768,128]{2,1,0:T(8,128)(2,1)}, bf16[2,768,128]{2,1,0:T(8,128)(2,1)}, u32[]{:S(2)}, u32[]{:S(2)}) collective-permute-start(bf16[2,768,128]{2,1,0:T(8,128)(2,1)} %get-tuple-element.29), channel_id=1, source_target_pairs={{0,24},{8,0},{16,8},{24,16},{32,56},{40,32},{48,40},{56,48},{64,88... | collective-permute-start | bytes 1179656 | tf_op jit(solution)/shard_map/ppermute | solution.py:451
  15.6 20.9 %copy-start.5 = (bf16[2,768,128]{2,1,0:T(8,128)(2,1)}, bf16[2,768,128]{2,1,0:T(8,128)(2,1)S(1)}, u32[]{:S(2)}) copy-start(bf16[2,768,128]{2,1,0:T(8,128)(2,1)S(1)} %collective-permute-done.rest_1_) | copy-start | bytes 1179652
  18.1 13.5 %copy-start.14 = (s32[64]{0:T(128)S(1)}, s32[64]{0:T(128)}, u32[]{:S(2)}) copy-start(s32[64]{0:T(128)} %param.16) | copy-start | bytes 772
  18.1 26.0 %collective-permute-start.7 = (bf16[2,768,128]{2,1,0:T(8,128)(2,1)}, bf16[2,768,128]{2,1,0:T(8,128)(2,1)}, u32[]{:S(2)}, u32[]{:S(2)}) collective-permute-start(bf16[2,768,128]{2,1,0:T(8,128)(2,1)} %get-tuple-element.33), channel_id=1, source_target_pairs={{0,8},{8,16},{16,24},{24,0},{32,40},{40,48},{48,56},{56,32},{64,72... | collective-permute-start | bytes 1179656 | tf_op jit(solution)/shard_map/ppermute | solution.py:451
  19.5 12.4 %copy-start.9 = (bf16[2,768,128]{2,1,0:T(8,128)(2,1)S(1)}, bf16[2,768,128]{2,1,0:T(8,128)(2,1)}, u32[]{:S(2)}) copy-start(bf16[2,768,128]{2,1,0:T(8,128)(2,1)} %get-tuple-element.34) | copy-start | bytes 1179652
  19.5 15.8 %copy-start.8 = (bf16[2,768,128]{2,1,0:T(8,128)(2,1)S(1)}, bf16[2,768,128]{2,1,0:T(8,128)(2,1)}, u32[]{:S(2)}) copy-start(bf16[2,768,128]{2,1,0:T(8,128)(2,1)} %get-tuple-element.35) | copy-start | bytes 1179652
  20.5 65.7 %all-to-all-start = ((bf16[32,16,768]{2,1,0:T(8,128)(2,1)}), bf16[32,16,768]{2,1,0:T(8,128)(2,1)S(1)}, u32[]{:S(2)}, u32[]{:S(2)}) async-start(bf16[32,16,768]{2,1,0:T(8,128)(2,1)} %bitcast.4), calls=%async_computation | async-start | bytes 1572864 | tf_op jit(solution)/shard_map/all_to_all | solution.py:447
  31.9 18.6 %collective-permute-start.8 = (bf16[2,768,128]{2,1,0:T(8,128)(2,1)S(1)}, bf16[2,768,128]{2,1,0:T(8,128)(2,1)S(1)}, u32[]{:S(2)}, u32[]{:S(2)}) collective-permute-start(bf16[2,768,128]{2,1,0:T(8,128)(2,1)S(1)} %copy-done.9), channel_id=1, source_target_pairs={{0,16},{8,24},{16,0},{24,8},{32,48},{40,56},{48,32},{56,40},{64,80... | collective-permute-start | bytes 1179656 | tf_op jit(solution)/shard_map/ppermute | solution.py:451
  35.3 36.4 %copy-start.6 = (bf16[2,768,128]{2,1,0:T(8,128)(2,1)}, bf16[2,768,128]{2,1,0:T(8,128)(2,1)S(1)}, u32[]{:S(2)}) copy-start(bf16[2,768,128]{2,1,0:T(8,128)(2,1)S(1)} %collective-permute-done.3.rest_4_) | copy-start | bytes 1179652
  35.3 23.5 %collective-permute-start.9 = (bf16[2,768,128]{2,1,0:T(8,128)(2,1)S(1)}, bf16[2,768,128]{2,1,0:T(8,128)(2,1)}, u32[]{:S(2)}, u32[]{:S(2)}) collective-permute-start(bf16[2,768,128]{2,1,0:T(8,128)(2,1)S(1)} %copy-done.8), channel_id=1, source_target_pairs={{0,24},{8,0},{16,8},{24,16},{32,56},{40,32},{48,40},{56,48},{64,88... | collective-permute-start | bytes 1179656 | tf_op jit(solution)/shard_map/ppermute | solution.py:451
  36.5 35.1 %copy-start.7 = (bf16[2,768,128]{2,1,0:T(8,128)(2,1)}, bf16[2,768,128]{2,1,0:T(8,128)(2,1)S(1)}, u32[]{:S(2)}) copy-start(bf16[2,768,128]{2,1,0:T(8,128)(2,1)S(1)} %collective-permute-done.1.rest_2_) | copy-start | bytes 1179652
  36.5 22.2 %collective-permute-start.4 = (bf16[2,768,128]{2,1,0:T(8,128)(2,1)S(1)}, bf16[2,768,128]{2,1,0:T(8,128)(2,1)}, u32[]{:S(2)}, u32[]{:S(2)}) collective-permute-start(bf16[2,768,128]{2,1,0:T(8,128)(2,1)S(1)} %collective-permute-done.rest_1_), channel_id=1, source_target_pairs={{0,32},{16,48},{24,56},{32,64},{48,80},{56,88},{64,96},{80,112},{8... | collective-permute-start | bytes 1179656 | tf_op jit(solution)/shard_map/ppermute | solution.py:455
  40.6 25.1 %collective-permute-start.5 = (bf16[2,768,128]{2,1,0:T(8,128)(2,1)S(1)}, bf16[2,768,128]{2,1,0:T(8,128)(2,1)}, u32[]{:S(2)}, u32[]{:S(2)}) collective-permute-start(bf16[2,768,128]{2,1,0:T(8,128)(2,1)S(1)} %collective-permute-done.1.rest_2_), channel_id=1, source_target_pairs={{0,32},{8,40},{24,56},{32,64},{40,72},{56,88},{64,96},{72,104},{88... | collective-permute-start | bytes 1179656 | tf_op jit(solution)/shard_map/ppermute | solution.py:455
  44.0 27.6 %collective-permute-start.6 = (bf16[2,768,128]{2,1,0:T(8,128)(2,1)}, bf16[2,768,128]{2,1,0:T(8,128)(2,1)}, u32[]{:S(2)}, u32[]{:S(2)}) collective-permute-start(bf16[2,768,128]{2,1,0:T(8,128)(2,1)} %collective-permute-done.2.rest_3_), channel_id=1, source_target_pairs={{0,32},{8,40},{16,48},{32,64},{40,72},{48,80},{64,96},{72,104},{80... | collective-permute-start | bytes 1179656 | tf_op jit(solution)/shard_map/ppermute | solution.py:455
  47.4 24.2 %copy-start.4 = (s32[3072]{0:T(1024)}, s32[3072]{0:T(1024)S(1)}, u32[]{:S(2)}) copy-start(s32[3072]{0:T(1024)S(1)} %broadcast_subtract_fusion) | copy-start | bytes 36868
  50.5 15.2 %copy-start.10 = (bf16[2,768,128]{2,1,0:T(8,128)(2,1)}, bf16[2,768,128]{2,1,0:T(8,128)(2,1)S(1)}, u32[]{:S(2)}) copy-start(bf16[2,768,128]{2,1,0:T(8,128)(2,1)S(1)} %collective-permute-done.8.rest_10_) | copy-start | bytes 1179652
  86.2 15.9 %copy-start.2 = (bf16[32,16,768]{2,1,0:T(8,128)(2,1)}, bf16[32,16,768]{2,1,0:T(8,128)(2,1)S(1)}, u32[]{:S(2)}) copy-start(bf16[32,16,768]{2,1,0:T(8,128)(2,1)S(1)} %all-to-all-done.taps_ref) | copy-start | bytes 2359300
  86.2 36.0 %all-to-all-start.1 = ((bf16[8,16,3072]{2,1,0:T(8,128)(2,1)}), bf16[8,16,3072]{2,1,0:T(8,128)(2,1)S(1)}, u32[]{:S(2)}, u32[]{:S(2)}) async-start(bf16[8,16,3072]{2,1,0:T(8,128)(2,1)} %bitcast.18), calls=%async_computation.1 | async-start | bytes 1572864 | tf_op jit(solution)/shard_map/all_to_all | solution.py:447
  109.3 25.1 %collective-permute-start.10 = (bf16[768,128]{1,0:T(8,128)(2,1)S(1)}, bf16[768,128]{1,0:T(8,128)(2,1)S(1)}, u32[]{:S(2)}, u32[]{:S(2)}) collective-permute-start(bf16[768,128]{1,0:T(8,128)(2,1)S(1)} %get-tuple-element.50), channel_id=1, source_target_pairs={{0,8},{8,16},{16,24},{24,0},{32,40},{40,48},{48,56},{56,32},{64,72... | collective-permute-start | bytes 589832 | tf_op jit(solution)/shard_map/ppermute | solution.py:451
  109.3 25.1 %collective-permute-start.11 = (bf16[768,128]{1,0:T(8,128)(2,1)S(1)}, bf16[768,128]{1,0:T(8,128)(2,1)S(1)}, u32[]{:S(2)}, u32[]{:S(2)}) collective-permute-start(bf16[768,128]{1,0:T(8,128)(2,1)S(1)} %get-tuple-element.49), channel_id=1, source_target_pairs={{0,16},{8,24},{16,0},{24,8},{32,48},{40,56},{48,32},{56,40},{64,80... | collective-permute-start | bytes 589832 | tf_op jit(solution)/shard_map/ppermute | solution.py:451
  109.3 25.2 %collective-permute-start.12 = (bf16[768,128]{1,0:T(8,128)(2,1)S(1)}, bf16[768,128]{1,0:T(8,128)(2,1)S(1)}, u32[]{:S(2)}, u32[]{:S(2)}) collective-permute-start(bf16[768,128]{1,0:T(8,128)(2,1)S(1)} %get-tuple-element.48), channel_id=1, source_target_pairs={{0,24},{8,0},{16,8},{24,16},{32,56},{40,32},{48,40},{56,48},{64,88... | collective-permute-start | bytes 589832 | tf_op jit(solution)/shard_map/ppermute | solution.py:451
  122.2 0.9 copy-start.3
  134.5 4.0 %copy-start.11 = (bf16[768,128]{1,0:T(8,128)(2,1)}, bf16[768,128]{1,0:T(8,128)(2,1)S(1)}, u32[]{:S(2)}) copy-start(bf16[768,128]{1,0:T(8,128)(2,1)S(1)} %collective-permute-done.10.rest_1_) | copy-start | bytes 589828
  134.5 4.0 %copy-start.12 = (bf16[768,128]{1,0:T(8,128)(2,1)}, bf16[768,128]{1,0:T(8,128)(2,1)S(1)}, u32[]{:S(2)}) copy-start(bf16[768,128]{1,0:T(8,128)(2,1)S(1)} %collective-permute-done.11.rest_2_) | copy-start | bytes 589828
  134.5 4.0 %copy-start.13 = (bf16[768,128]{1,0:T(8,128)(2,1)}, bf16[768,128]{1,0:T(8,128)(2,1)S(1)}, u32[]{:S(2)}) copy-start(bf16[768,128]{1,0:T(8,128)(2,1)S(1)} %collective-permute-done.12.rest_3_) | copy-start | bytes 589828
  134.5 23.7 %all-to-all-start.2 = ((bf16[32,16,768]{2,1,0:T(8,128)(2,1)}), bf16[32,16,768]{2,1,0:T(8,128)(2,1)S(1)}, u32[]{:S(2)}, u32[]{:S(2)}) async-start(bf16[32,16,768]{2,1,0:T(8,128)(2,1)} %convolution.1), calls=%async_computation.2 | async-start | bytes 1572864 | tf_op jit(solution)/shard_map/all_to_all | solution.py:447
  138.5 19.7 %copy-start = (bf16[768,512]{1,0:T(8,128)(2,1)S(1)}, bf16[768,512]{1,0:T(8,128)(2,1)}, u32[]{:S(2)}) copy-start(bf16[768,512]{1,0:T(8,128)(2,1)} %gate_ref.1) | copy-start | bytes 2359300

commit v5 on v4

--- a/solution.py
+++ b/solution.py
@@ -459,13 +459,13 @@
 
     taps = filter_taps.astype(jnp.bfloat16).reshape(X_SIZE, z_size, per_device, row_count)
     taps = taps.transpose(1, 0, 2, 3).reshape(ctx, per_device, row_count)
-    pieces = pieces_of(x_index, key_rows, values)
-    own = arrived(pieces)
-    taps, _ = lax.optimization_barrier((taps, pieces[0]))
-    taps = exchanged(taps)
+    own = arrived(pieces_of(x_index, key_rows, values))
     before = [along_z(own[k], k) for k in range(X_SIZE)]
     own[1], queries, in_gate = lax.optimization_barrier((own[1], queries, in_gate))
-    asked = arrived(pieces_of(x_index, queries, in_gate))
+    asked = pieces_of(x_index, queries, in_gate)
+    taps, *_ = lax.optimization_barrier((taps, *own, *asked))
+    asked = arrived(asked)
+    taps = exchanged(taps)
 
     group_first = (me // X_SIZE) * group_rows
     positions = group_first + jnp.arange(group_rows, dtype=jnp.int32)

time: 163 us -> 143 us (0.88); the launches traced: 160 us -> 142 us
  waiting for transfers between devices: 53.6 us -> 42.7 us
  starting transfers between devices: 60.6 us -> 49.8 us
  Pallas kernels: 40 us -> 42.8 us
    all_to_all x3, starting transfers between devices: 30.8 us -> 21.3 us  [exchanged(): lax.all_to_all(x, 'ctx', split_axis=0, concat_axis=0, tiled=True, axis_in...]
    ppermute x9, waiting for transfers between devices: 13.4 us -> 7.38 us  [along_x(): return lax.ppermute(piece, 'ctx', pairs)]
    pallas_call x1, Pallas kernels: 14.5 us -> 17.5 us  [attention(): pl.pallas_call(attention_kernel, name='attention', grid_spec=pltpu.Prefet...]
    ppermute x4, waiting for transfers between devices: 12.9 us -> 9.97 us  [along_z(): return lax.ppermute(piece, 'ctx', pairs)]
    ppermute x9, starting transfers between devices: 18.2 us -> 15.6 us  [along_x(): return lax.ppermute(piece, 'ctx', pairs)]
    all_to_all x3, waiting for transfers between devices: 27.3 us -> 25.4 us  [exchanged(): lax.all_to_all(x, 'ctx', split_axis=0, concat_axis=0, tiled=True, axis_in...]
  transfers between devices with their start and end apart: 16 -> 16, of which waited for: 7 -> 5; matrix products, arithmetic and copies ran while one was open for 3% -> 3% of each run, Pallas kernels for 22% -> 27%
where the time goes in v5:
time: 143 us; the launch traced here: 142 us
  starting transfers between devices  49.8 us (35%)
  Pallas kernels  42.8 us (30%)
  waiting for transfers between devices  42.7 us (30%)
  local copies, waits for them, and re-layouts  4.03 us (3%)
  other arithmetic  1.62 us (1%)
    all_to_all x3, waiting for transfers between devices, exchanged(): lax.all_to_all(x, 'ctx', split_axis=0, concat_axis=0, tiled=True, axis_in...  25.4 us
    all_to_all x3, starting transfers between devices, exchanged(): lax.all_to_all(x, 'ctx', split_axis=0, concat_axis=0, tiled=True, axis_in...  21.3 us
    pallas_call x1, Pallas kernels, attention(): pl.pallas_call(attention_kernel, name='attention', grid_spec=pltpu.Prefet...  17.5 us
    ppermute x9, starting transfers between devices, along_x(): return lax.ppermute(piece, 'ctx', pairs)  15.6 us
    ppermute x4, starting transfers between devices, along_z(): return lax.ppermute(piece, 'ctx', pairs)  12.9 us
    pallas_call x1, Pallas kernels, convolve(): pl.pallas_call(conv_kernel, name='convolution', grid=(channels // (2 * PA...  11.3 us
    ppermute x4, waiting for transfers between devices, along_z(): return lax.ppermute(piece, 'ctx', pairs)  9.97 us
    ppermute x9, waiting for transfers between devices, along_x(): return lax.ppermute(piece, 'ctx', pairs)  7.38 us
  transfers between devices with their start and end apart: 16, of which 5 were waited for; matrix products, arithmetic and copies ran while one was open for 3% of the time, Pallas kernels for 27%

profile of v5, /device:TPU:16, one launch (start us, length us, event | category | flops | bytes accessed | tf_op | source)
XLA Modules:
  0.0 141.9 jit_solution(9304106352096889730)
XLA Ops:
  0.6 2.4 %pieces.2 = (bf16[2,768,128]{2,1,0:T(8,128)(2,1)}, bf16[2,768,128]{2,1,0:T(8,128)(2,1)}, bf16[2,768,128]{2,1,0:T(8,128)(2,1)}, bf16[2,768,128]{2,1,0:T(8,128)(2,1)}) custom-call(s32[1]{0:T(128)} %bitcast.x_ref, bf16[768,512]{1,0:T(8,128)(2,1)} %first_ref.1, bf16[768,512]{1,0:T(8,128)(2,1)} %second_ref.1), custom_call_target="tpu_custom_call" | custom-call | tf_op jit(solution)/shard_map/pieces/pallas_call | solution.py:53
  3.1 1.6 %collective-permute-start = (bf16[2,768,128]{2,1,0:T(8,128)(2,1)}, bf16[2,768,128]{2,1,0:T(8,128)(2,1)S(1)}, u32[]{:S(2)}, u32[]{:S(2)}) collective-permute-start(bf16[2,768,128]{2,1,0:T(8,128)(2,1)} %get-tuple-element.26), channel_id=1, source_target_pairs={{0,8},{8,16},{16,24},{24,0},{32,40},{40,48},{48,56},{56,32},{64,72... | collective-permute-start | bytes 1179656 | tf_op jit(solution)/shard_map/ppermute | solution.py:451
  4.6 2.7 %collective-permute-start.1 = (bf16[2,768,128]{2,1,0:T(8,128)(2,1)}, bf16[2,768,128]{2,1,0:T(8,128)(2,1)S(1)}, u32[]{:S(2)}, u32[]{:S(2)}) collective-permute-start(bf16[2,768,128]{2,1,0:T(8,128)(2,1)} %get-tuple-element.28), channel_id=1, source_target_pairs={{0,16},{8,24},{16,0},{24,8},{32,48},{40,56},{48,32},{56,40},{64,80... | collective-permute-start | bytes 1179656 | tf_op jit(solution)/shard_map/ppermute | solution.py:451
  7.4 1.4 %collective-permute-start.2 = (bf16[2,768,128]{2,1,0:T(8,128)(2,1)}, bf16[2,768,128]{2,1,0:T(8,128)(2,1)S(1)}, u32[]{:S(2)}, u32[]{:S(2)}) collective-permute-start(bf16[2,768,128]{2,1,0:T(8,128)(2,1)} %get-tuple-element.29), channel_id=1, source_target_pairs={{0,24},{8,0},{16,8},{24,16},{32,56},{40,32},{48,40},{56,48},{64,88... | collective-permute-start | bytes 1179656 | tf_op jit(solution)/shard_map/ppermute | solution.py:451
  8.8 0.7 collective-permute-start.3
  9.5 6.1 %collective-permute-done.rest_1_ = bf16[2,768,128]{2,1,0:T(8,128)(2,1)S(1)} collective-permute-done((bf16[2,768,128]{2,1,0:T(8,128)(2,1)}, bf16[2,768,128]{2,1,0:T(8,128)(2,1)S(1)}, u32[]{:S(2)}, u32[]{:S(2)}) %collective-permute-start) | collective-permute-done | bytes 393248 | tf_op jit(solution)/shard_map/ppermute | solution.py:451
  15.6 4.6 %collective-permute-start.4 = (bf16[2,768,128]{2,1,0:T(8,128)(2,1)S(1)}, bf16[2,768,128]{2,1,0:T(8,128)(2,1)}, u32[]{:S(2)}, u32[]{:S(2)}) collective-permute-start(bf16[2,768,128]{2,1,0:T(8,128)(2,1)S(1)} %collective-permute-done.rest_1_), channel_id=1, source_target_pairs={{0,32},{16,48},{24,56},{32,64},{48,80},{56,88},{64,96},{80,112},{8... | collective-permute-start | bytes 1179656 | tf_op jit(solution)/shard_map/ppermute | solution.py:455
  20.2 0.7 select_reduce_fusion.1
  20.9 0.2 select_reduce_fusion
  21.2 2.3 %pieces.3 = (bf16[2,768,128]{2,1,0:T(8,128)(2,1)}, bf16[2,768,128]{2,1,0:T(8,128)(2,1)}, bf16[2,768,128]{2,1,0:T(8,128)(2,1)}, bf16[2,768,128]{2,1,0:T(8,128)(2,1)}) custom-call(s32[1]{0:T(128)} %bitcast.x_ref, bf16[768,512]{1,0:T(8,128)(2,1)} %first_ref.2, bf16[768,512]{1,0:T(8,128)(2,1)} %second_ref.2), custom_call_target="tpu_custom_call" | custom-call | tf_op jit(solution)/shard_map/pieces/pallas_call | solution.py:53
  23.5 0.1 collective-permute-start.7
  23.6 1.3 collective-permute-done.1.rest_2_
  24.8 2.7 %collective-permute-start.8 = (bf16[2,768,128]{2,1,0:T(8,128)(2,1)}, bf16[2,768,128]{2,1,0:T(8,128)(2,1)}, u32[]{:S(2)}, u32[]{:S(2)}) collective-permute-start(bf16[2,768,128]{2,1,0:T(8,128)(2,1)} %get-tuple-element.34), channel_id=1, source_target_pairs={{0,16},{8,24},{16,0},{24,8},{32,48},{40,56},{48,32},{56,40},{64,80... | collective-permute-start | bytes 1179656 | tf_op jit(solution)/shard_map/ppermute | solution.py:451
  27.6 1.4 %collective-permute-start.9 = (bf16[2,768,128]{2,1,0:T(8,128)(2,1)}, bf16[2,768,128]{2,1,0:T(8,128)(2,1)}, u32[]{:S(2)}, u32[]{:S(2)}) collective-permute-start(bf16[2,768,128]{2,1,0:T(8,128)(2,1)} %get-tuple-element.35), channel_id=1, source_target_pairs={{0,24},{8,0},{16,8},{24,16},{32,56},{40,32},{48,40},{56,48},{64,88... | collective-permute-start | bytes 1179656 | tf_op jit(solution)/shard_map/ppermute | solution.py:451
  29.0 0.0 collective-permute-done.3.rest_4_
  29.0 3.9 %collective-permute-start.5 = (bf16[2,768,128]{2,1,0:T(8,128)(2,1)S(1)}, bf16[2,768,128]{2,1,0:T(8,128)(2,1)}, u32[]{:S(2)}, u32[]{:S(2)}) collective-permute-start(bf16[2,768,128]{2,1,0:T(8,128)(2,1)S(1)} %collective-permute-done.1.rest_2_), channel_id=1, source_target_pairs={{0,32},{8,40},{24,56},{32,64},{40,72},{56,88},{64,96},{72,104},{88... | collective-permute-start | bytes 1179656 | tf_op jit(solution)/shard_map/ppermute | solution.py:455
  32.9 0.0 collective-permute-done.4.rest_5_
  32.9 3.8 %collective-permute-start.6 = (bf16[2,768,128]{2,1,0:T(8,128)(2,1)S(1)}, bf16[2,768,128]{2,1,0:T(8,128)(2,1)}, u32[]{:S(2)}, u32[]{:S(2)}) collective-permute-start(bf16[2,768,128]{2,1,0:T(8,128)(2,1)S(1)} %collective-permute-done.2.rest_3_), channel_id=1, source_target_pairs={{0,32},{8,40},{16,48},{32,64},{40,72},{48,80},{64,96},{72,104},{80... | collective-permute-start | bytes 1179656 | tf_op jit(solution)/shard_map/ppermute | solution.py:455
  36.7 0.1 slice.19
  36.8 0.1 slice.18
  36.9 0.1 convert_element_type.3
  37.0 1.0 copy.16
  37.9 5.9 %all-to-all-start = ((bf16[32,16,768]{2,1,0:T(8,128)(2,1)}), bf16[32,16,768]{2,1,0:T(8,128)(2,1)S(1)}, u32[]{:S(2)}, u32[]{:S(2)}) async-start(bf16[32,16,768]{2,1,0:T(8,128)(2,1)} %bitcast.4), calls=%async_computation | async-start | bytes 1572864 | tf_op jit(solution)/shard_map/all_to_all | solution.py:447
  43.8 0.6 and_select_fusion.1
  44.4 0.0 collective-permute-done.5.rest_6_
  44.4 10.0 %collective-permute-done.6.rest_7_ = bf16[2,768,128]{2,1,0:T(8,128)(2,1)} collective-permute-done((bf16[2,768,128]{2,1,0:T(8,128)(2,1)S(1)}, bf16[2,768,128]{2,1,0:T(8,128)(2,1)}, u32[]{:S(2)}, u32[]{:S(2)}) %collective-permute-start.6) | collective-permute-done | bytes 393248 | tf_op jit(solution)/shard_map/ppermute | solution.py:455
  54.4 0.0 collective-permute-done.7.rest_9_
  54.4 0.0 collective-permute-done.8.rest_10_
  54.4 0.0 collective-permute-done.9.rest_11_
  54.4 17.5 %attention.1 = (bf16[4,768,128]{2,1,0:T(8,128)(2,1)}, bf16[128,3072]{1,0:T(8,128)(2,1)}) custom-call(s32[4]{0:T(128)} %get-tuple-element.52.lo_ref, s32[4]{0:T(128)} %get-tuple-element.53.mid_ref, s32[1]{0:T(128)} %bitcast.x_ref, s32[4,1,768]{2,1,0:T(1,128)} %bitcast.19, bf16[2,768,128]{2,1,0:T(8,128)(2,1)} %get-tuple-element.25.rest_0_, ...), custom_call_target="tpu_custom_call" | custom-call | flops 16000000000 | bytes 3932160 | tf_op jit(solution)/shard_map/attention/pallas_call | solution.py:175
  71.9 0.0 all-to-all-done.taps_ref
  72.0 11.5 %all-to-all-start.1 = ((bf16[8,16,3072]{2,1,0:T(8,128)(2,1)}), bf16[8,16,3072]{2,1,0:T(8,128)(2,1)S(1)}, u32[]{:S(2)}, u32[]{:S(2)}) async-start(bf16[8,16,3072]{2,1,0:T(8,128)(2,1)} %bitcast.18), calls=%async_computation.1 | async-start | bytes 1572864 | tf_op jit(solution)/shard_map/all_to_all | solution.py:447
  83.5 5.4 %taps_spectrum.1.taps_ref = f32[8,384,256]{2,1,0:T(8,128)} custom-call(bf16[32,16,768]{2,1,0:T(8,128)(2,1)} %copy-done.2, bf16[384,384]{1,0:T(8,128)(2,1)} %constant.53.clone.outer_ref, f32[2,192,128]{2,1,0:T(8,128)} %constant.54.clone.twist_ref, bf16[512,256]{1,0:T(8,128)(2,1)} %constant.55.clone.inner_ref), custom_call_target="tpu_custom_call" | custom-call | flops 5000000000 | bytes 4194304 | tf_op jit(solution)/shard_map/taps_spectrum/pallas_call | solution.py:346
  88.8 1.9 %slice_bitcast_fusion = (bf16[768,128]{1,0:T(8,128)(2,1)S(1)}, bf16[768,128]{1,0:T(8,128)(2,1)S(1)}, bf16[768,128]{1,0:T(8,128)(2,1)S(1)}, bf16[768,128]{1,0:T(8,128)(2,1)}) fusion(bf16[4,768,128]{2,1,0:T(8,128)(2,1)} %get-tuple-element.42), kind=kLoop, calls=%fused_computation.1 | loop fusion | bytes 1572864 | tf_op jit(solution)/shard_map/squeeze | solution.py:479
  90.8 0.0 collective-permute-start.12
  90.8 5.6 %collective-permute-start.11 = (bf16[768,128]{1,0:T(8,128)(2,1)S(1)}, bf16[768,128]{1,0:T(8,128)(2,1)S(1)}, u32[]{:S(2)}, u32[]{:S(2)}) collective-permute-start(bf16[768,128]{1,0:T(8,128)(2,1)S(1)} %get-tuple-element.49), channel_id=1, source_target_pairs={{0,16},{8,24},{16,0},{24,8},{32,48},{40,56},{48,32},{56,40},{64,80... | collective-permute-start | bytes 589832 | tf_op jit(solution)/shard_map/ppermute | solution.py:451
  96.4 0.0 collective-permute-start.10
  96.4 7.5 %all-to-all-done.1.signal_ref = bf16[8,16,3072]{2,1,0:T(8,128)(2,1)S(1)} async-done(((bf16[8,16,3072]{2,1,0:T(8,128)(2,1)}), bf16[8,16,3072]{2,1,0:T(8,128)(2,1)S(1)}, u32[]{:S(2)}, u32[]{:S(2)}) %all-to-all-start.1) | async-done | bytes 786464 | tf_op jit(solution)/shard_map/all_to_all | solution.py:447
  103.9 0.9 copy-done.3
  104.8 11.3 %convolution.1 = bf16[32,16,768]{2,1,0:T(8,128)(2,1)} custom-call(bf16[8,16,3072]{2,1,0:T(8,128)(2,1)} %copy-done.3, f32[8,384,256]{2,1,0:T(8,128)} %taps_spectrum.1.taps_ref, bf16[384,384]{1,0:T(8,128)(2,1)} %constant.56.clone.outer_ref, f32[2,192,128]{2,1,0:T(8,128)} %constant.54.clone.twist_ref, bf16[512,256]{1,0:T(8,128)(2,1)} %constant.55.clone.inner_ref, ...), custom_call_target="tpu_custom_call" | custom-call | flops 7000000000 | bytes 5242880 | tf_op jit(solution)/shard_map/convolution/pallas_call | solution.py:363
  116.1 0.0 collective-permute-done.12.rest_3_
  116.2 0.0 collective-permute-done.10.rest_1_
  116.2 0.0 copy-start.11
  116.2 3.9 %all-to-all-start.2 = ((bf16[32,16,768]{2,1,0:T(8,128)(2,1)}), bf16[32,16,768]{2,1,0:T(8,128)(2,1)S(1)}, u32[]{:S(2)}, u32[]{:S(2)}) async-start(bf16[32,16,768]{2,1,0:T(8,128)(2,1)} %convolution.1), calls=%async_computation.2 | async-start | bytes 1572864 | tf_op jit(solution)/shard_map/all_to_all | solution.py:447
  120.1 0.0 copy-start
  120.1 2.0 %assemble.1 = bf16[768,512]{1,0:T(8,128)(2,1)} custom-call(s32[1]{0:T(128)} %bitcast.x_ref, bf16[768,128]{1,0:T(8,128)(2,1)} %get-tuple-element.43.rest_0_, bf16[768,128]{1,0:T(8,128)(2,1)} %copy-done.11, bf16[768,128]{1,0:T(8,128)(2,1)} %copy-done.10, bf16[768,128]{1,0:T(8,128)(2,1)} %copy-done.9), custom_call_target="tpu_custom_call" | custom-call | flops 2000000000 | bytes 1048576 | tf_op jit(solution)/shard_map/assemble/pallas_call | solution.py:399
  122.2 17.9 %all-to-all-done.2 = bf16[32,16,768]{2,1,0:T(8,128)(2,1)S(1)} async-done(((bf16[32,16,768]{2,1,0:T(8,128)(2,1)}), bf16[32,16,768]{2,1,0:T(8,128)(2,1)S(1)}, u32[]{:S(2)}, u32[]{:S(2)}) %all-to-all-start.2) | async-done | bytes 786464 | tf_op jit(solution)/shard_map/all_to_all | solution.py:447
  140.0 1.9 %finish.1 = bf16[768,512]{1,0:T(8,128)(2,1)} custom-call(bf16[8,4,16,768]{3,2,1,0:T(8,128)(2,1)S(1)} %bitcast.16, bf16[768,512]{1,0:T(8,128)(2,1)S(1)} %copy-done), custom_call_target="tpu_custom_call" | custom-call | tf_op jit(solution)/shard_map/finish/pallas_call | solution.py:424
  (25 shorter events, 0.1 us)
Async XLA Ops:
  0.6 36.2 %copy-start.1 = (f32[512,768]{1,0:T(8,128)S(1)}, f32[512,768]{1,0:T(8,128)}, u32[]{:S(2)}) copy-start(f32[512,768]{1,0:T(8,128)} %param.19) | copy-start | bytes 4718596
  3.1 12.5 %collective-permute-start = (bf16[2,768,128]{2,1,0:T(8,128)(2,1)}, bf16[2,768,128]{2,1,0:T(8,128)(2,1)S(1)}, u32[]{:S(2)}, u32[]{:S(2)}) collective-permute-start(bf16[2,768,128]{2,1,0:T(8,128)(2,1)} %get-tuple-element.26), channel_id=1, source_target_pairs={{0,8},{8,16},{16,24},{24,0},{32,40},{40,48},{48,56},{56,32},{64,72... | collective-permute-start | bytes 1179656 | tf_op jit(solution)/shard_map/ppermute | solution.py:451
  4.6 20.2 %collective-permute-start.1 = (bf16[2,768,128]{2,1,0:T(8,128)(2,1)}, bf16[2,768,128]{2,1,0:T(8,128)(2,1)S(1)}, u32[]{:S(2)}, u32[]{:S(2)}) collective-permute-start(bf16[2,768,128]{2,1,0:T(8,128)(2,1)} %get-tuple-element.28), channel_id=1, source_target_pairs={{0,16},{8,24},{16,0},{24,8},{32,48},{40,56},{48,32},{56,40},{64,80... | collective-permute-start | bytes 1179656 | tf_op jit(solution)/shard_map/ppermute | solution.py:451
  7.4 20.2 %collective-permute-start.2 = (bf16[2,768,128]{2,1,0:T(8,128)(2,1)}, bf16[2,768,128]{2,1,0:T(8,128)(2,1)S(1)}, u32[]{:S(2)}, u32[]{:S(2)}) collective-permute-start(bf16[2,768,128]{2,1,0:T(8,128)(2,1)} %get-tuple-element.29), channel_id=1, source_target_pairs={{0,24},{8,0},{16,8},{24,16},{32,56},{40,32},{48,40},{56,48},{64,88... | collective-permute-start | bytes 1179656 | tf_op jit(solution)/shard_map/ppermute | solution.py:451
  8.8 20.2 %collective-permute-start.3 = (bf16[2,768,128]{2,1,0:T(8,128)(2,1)}, bf16[2,768,128]{2,1,0:T(8,128)(2,1)S(1)}, u32[]{:S(2)}, u32[]{:S(2)}) collective-permute-start(bf16[2,768,128]{2,1,0:T(8,128)(2,1)} %get-tuple-element.25.rest_0_), channel_id=1, source_target_pairs={{8,40},{16,48},{24,56},{40,72},{48,80},{56,88},{72,104},{80,112},{... | collective-permute-start | bytes 1179656 | tf_op jit(solution)/shard_map/ppermute | solution.py:455
  15.6 22.3 %copy-start.5 = (bf16[2,768,128]{2,1,0:T(8,128)(2,1)}, bf16[2,768,128]{2,1,0:T(8,128)(2,1)S(1)}, u32[]{:S(2)}) copy-start(bf16[2,768,128]{2,1,0:T(8,128)(2,1)S(1)} %collective-permute-done.rest_1_) | copy-start | bytes 1179652
  15.6 17.3 %collective-permute-start.4 = (bf16[2,768,128]{2,1,0:T(8,128)(2,1)S(1)}, bf16[2,768,128]{2,1,0:T(8,128)(2,1)}, u32[]{:S(2)}, u32[]{:S(2)}) collective-permute-start(bf16[2,768,128]{2,1,0:T(8,128)(2,1)S(1)} %collective-permute-done.rest_1_), channel_id=1, source_target_pairs={{0,32},{16,48},{24,56},{32,64},{48,80},{56,88},{64,96},{80,112},{8... | collective-permute-start | bytes 1179656 | tf_op jit(solution)/shard_map/ppermute | solution.py:455
  23.5 30.9 %collective-permute-start.7 = (bf16[2,768,128]{2,1,0:T(8,128)(2,1)}, bf16[2,768,128]{2,1,0:T(8,128)(2,1)}, u32[]{:S(2)}, u32[]{:S(2)}) collective-permute-start(bf16[2,768,128]{2,1,0:T(8,128)(2,1)} %get-tuple-element.33), channel_id=1, source_target_pairs={{0,8},{8,16},{16,24},{24,0},{32,40},{40,48},{48,56},{56,32},{64,72... | collective-permute-start | bytes 1179656 | tf_op jit(solution)/shard_map/ppermute | solution.py:451
  24.8 29.6 %copy-start.6 = (bf16[2,768,128]{2,1,0:T(8,128)(2,1)}, bf16[2,768,128]{2,1,0:T(8,128)(2,1)S(1)}, u32[]{:S(2)}) copy-start(bf16[2,768,128]{2,1,0:T(8,128)(2,1)S(1)} %collective-permute-done.1.rest_2_) | copy-start | bytes 1179652
  24.8 29.5 %collective-permute-start.8 = (bf16[2,768,128]{2,1,0:T(8,128)(2,1)}, bf16[2,768,128]{2,1,0:T(8,128)(2,1)}, u32[]{:S(2)}, u32[]{:S(2)}) collective-permute-start(bf16[2,768,128]{2,1,0:T(8,128)(2,1)} %get-tuple-element.34), channel_id=1, source_target_pairs={{0,16},{8,24},{16,0},{24,8},{32,48},{40,56},{48,32},{56,40},{64,80... | collective-permute-start | bytes 1179656 | tf_op jit(solution)/shard_map/ppermute | solution.py:451
  27.6 26.8 %copy-start.7 = (bf16[2,768,128]{2,1,0:T(8,128)(2,1)}, bf16[2,768,128]{2,1,0:T(8,128)(2,1)S(1)}, u32[]{:S(2)}) copy-start(bf16[2,768,128]{2,1,0:T(8,128)(2,1)S(1)} %collective-permute-done.2.rest_3_) | copy-start | bytes 1179652
  27.6 26.8 %collective-permute-start.9 = (bf16[2,768,128]{2,1,0:T(8,128)(2,1)}, bf16[2,768,128]{2,1,0:T(8,128)(2,1)}, u32[]{:S(2)}, u32[]{:S(2)}) collective-permute-start(bf16[2,768,128]{2,1,0:T(8,128)(2,1)} %get-tuple-element.35), channel_id=1, source_target_pairs={{0,24},{8,0},{16,8},{24,16},{32,56},{40,32},{48,40},{56,48},{64,88... | collective-permute-start | bytes 1179656 | tf_op jit(solution)/shard_map/ppermute | solution.py:451
  29.0 8.9 %copy-start.8 = (bf16[2,768,128]{2,1,0:T(8,128)(2,1)}, bf16[2,768,128]{2,1,0:T(8,128)(2,1)S(1)}, u32[]{:S(2)}) copy-start(bf16[2,768,128]{2,1,0:T(8,128)(2,1)S(1)} %collective-permute-done.3.rest_4_) | copy-start | bytes 1179652
  29.0 15.4 %collective-permute-start.5 = (bf16[2,768,128]{2,1,0:T(8,128)(2,1)S(1)}, bf16[2,768,128]{2,1,0:T(8,128)(2,1)}, u32[]{:S(2)}, u32[]{:S(2)}) collective-permute-start(bf16[2,768,128]{2,1,0:T(8,128)(2,1)S(1)} %collective-permute-done.1.rest_2_), channel_id=1, source_target_pairs={{0,32},{8,40},{24,56},{32,64},{40,72},{56,88},{64,96},{72,104},{88... | collective-permute-start | bytes 1179656 | tf_op jit(solution)/shard_map/ppermute | solution.py:455
  32.9 21.5 %collective-permute-start.6 = (bf16[2,768,128]{2,1,0:T(8,128)(2,1)S(1)}, bf16[2,768,128]{2,1,0:T(8,128)(2,1)}, u32[]{:S(2)}, u32[]{:S(2)}) collective-permute-start(bf16[2,768,128]{2,1,0:T(8,128)(2,1)S(1)} %collective-permute-done.2.rest_3_), channel_id=1, source_target_pairs={{0,32},{8,40},{16,48},{32,64},{40,72},{48,80},{64,96},{72,104},{80... | collective-permute-start | bytes 1179656 | tf_op jit(solution)/shard_map/ppermute | solution.py:455
  36.7 17.7 %copy-start.4 = (s32[3072]{0:T(1024)}, s32[3072]{0:T(1024)S(1)}, u32[]{:S(2)}) copy-start(s32[3072]{0:T(1024)S(1)} %broadcast_subtract_fusion) | copy-start | bytes 36868
  37.9 34.0 %all-to-all-start = ((bf16[32,16,768]{2,1,0:T(8,128)(2,1)}), bf16[32,16,768]{2,1,0:T(8,128)(2,1)S(1)}, u32[]{:S(2)}, u32[]{:S(2)}) async-start(bf16[32,16,768]{2,1,0:T(8,128)(2,1)} %bitcast.4), calls=%async_computation | async-start | bytes 1572864 | tf_op jit(solution)/shard_map/all_to_all | solution.py:447
  71.9 11.5 %copy-start.2 = (bf16[32,16,768]{2,1,0:T(8,128)(2,1)}, bf16[32,16,768]{2,1,0:T(8,128)(2,1)S(1)}, u32[]{:S(2)}) copy-start(bf16[32,16,768]{2,1,0:T(8,128)(2,1)S(1)} %all-to-all-done.taps_ref) | copy-start | bytes 2359300
  72.0 31.9 %all-to-all-start.1 = ((bf16[8,16,3072]{2,1,0:T(8,128)(2,1)}), bf16[8,16,3072]{2,1,0:T(8,128)(2,1)S(1)}, u32[]{:S(2)}, u32[]{:S(2)}) async-start(bf16[8,16,3072]{2,1,0:T(8,128)(2,1)} %bitcast.18), calls=%async_computation.1 | async-start | bytes 1572864 | tf_op jit(solution)/shard_map/all_to_all | solution.py:447
  90.8 25.3 %collective-permute-start.12 = (bf16[768,128]{1,0:T(8,128)(2,1)S(1)}, bf16[768,128]{1,0:T(8,128)(2,1)S(1)}, u32[]{:S(2)}, u32[]{:S(2)}) collective-permute-start(bf16[768,128]{1,0:T(8,128)(2,1)S(1)} %get-tuple-element.48), channel_id=1, source_target_pairs={{0,24},{8,0},{16,8},{24,16},{32,56},{40,32},{48,40},{56,48},{64,88... | collective-permute-start | bytes 589832 | tf_op jit(solution)/shard_map/ppermute | solution.py:451
  90.8 25.4 %collective-permute-start.11 = (bf16[768,128]{1,0:T(8,128)(2,1)S(1)}, bf16[768,128]{1,0:T(8,128)(2,1)S(1)}, u32[]{:S(2)}, u32[]{:S(2)}) collective-permute-start(bf16[768,128]{1,0:T(8,128)(2,1)S(1)} %get-tuple-element.49), channel_id=1, source_target_pairs={{0,16},{8,24},{16,0},{24,8},{32,48},{40,56},{48,32},{56,40},{64,80... | collective-permute-start | bytes 589832 | tf_op jit(solution)/shard_map/ppermute | solution.py:451
  96.4 19.8 %collective-permute-start.10 = (bf16[768,128]{1,0:T(8,128)(2,1)S(1)}, bf16[768,128]{1,0:T(8,128)(2,1)S(1)}, u32[]{:S(2)}, u32[]{:S(2)}) collective-permute-start(bf16[768,128]{1,0:T(8,128)(2,1)S(1)} %get-tuple-element.50), channel_id=1, source_target_pairs={{0,8},{8,16},{16,24},{24,0},{32,40},{40,48},{48,56},{56,32},{64,72... | collective-permute-start | bytes 589832 | tf_op jit(solution)/shard_map/ppermute | solution.py:451
  103.9 0.9 copy-start.3
  116.1 4.0 %copy-start.9 = (bf16[768,128]{1,0:T(8,128)(2,1)}, bf16[768,128]{1,0:T(8,128)(2,1)S(1)}, u32[]{:S(2)}) copy-start(bf16[768,128]{1,0:T(8,128)(2,1)S(1)} %collective-permute-done.12.rest_3_) | copy-start | bytes 589828
  116.1 4.0 %copy-start.10 = (bf16[768,128]{1,0:T(8,128)(2,1)}, bf16[768,128]{1,0:T(8,128)(2,1)S(1)}, u32[]{:S(2)}) copy-start(bf16[768,128]{1,0:T(8,128)(2,1)S(1)} %collective-permute-done.11.rest_2_) | copy-start | bytes 589828
  116.2 4.0 %copy-start.11 = (bf16[768,128]{1,0:T(8,128)(2,1)}, bf16[768,128]{1,0:T(8,128)(2,1)S(1)}, u32[]{:S(2)}) copy-start(bf16[768,128]{1,0:T(8,128)(2,1)S(1)} %collective-permute-done.10.rest_1_) | copy-start | bytes 589828
  116.2 23.9 %all-to-all-start.2 = ((bf16[32,16,768]{2,1,0:T(8,128)(2,1)}), bf16[32,16,768]{2,1,0:T(8,128)(2,1)S(1)}, u32[]{:S(2)}, u32[]{:S(2)}) async-start(bf16[32,16,768]{2,1,0:T(8,128)(2,1)} %convolution.1), calls=%async_computation.2 | async-start | bytes 1572864 | tf_op jit(solution)/shard_map/all_to_all | solution.py:447
  120.1 19.9 %copy-start = (bf16[768,512]{1,0:T(8,128)(2,1)S(1)}, bf16[768,512]{1,0:T(8,128)(2,1)}, u32[]{:S(2)}) copy-start(bf16[768,512]{1,0:T(8,128)(2,1)} %gate_ref.1) | copy-start | bytes 2359300

commit v6 on v5

--- a/solution.py
+++ b/solution.py
@@ -12,11 +12,11 @@
 
 HEAD_DIM = 128
 X_SIZE = 4
+NEAR_FIRST = (0, 1, 3, 2)
 Q_BLOCK = 768
 K_BLOCK = 384
-Q_SUB = 768
 LANES = 128
-VMEM_LIMIT = 62 * 2**20
+VMEM_LIMIT = 63 * 2**20
 PAIRS = 4
 masked_score = -1e30
 
@@ -66,7 +66,7 @@
 
 def attention_kernel(lo_ref, mid_ref, x_ref, start_ref, *rest):
     own, before, asked = rest[:X_SIZE], rest[X_SIZE : 2 * X_SIZE], rest[2 * X_SIZE : 3 * X_SIZE]
-    out_ref, gated_ref, keys, values, values_t, queries_all, gate_all, sems = rest[3 * X_SIZE :]
+    out_ref, gated_ref, keys, values, values_t, queries_all, gate_all, weighted_ref, sems = rest[3 * X_SIZE :]
     step = pl.program_id(0)
     group = queries_all.shape[0]
     piece = group // X_SIZE
@@ -123,47 +123,38 @@
     query_index = first + lax.broadcasted_iota(jnp.int32, (1, Q_BLOCK), 1)
     key_offset = lax.broadcasted_iota(jnp.int32, (K_BLOCK, 1), 0)
     factor = math.log2(math.e) / math.sqrt(HEAD_DIM)
-    subs = [slice(at, at + Q_SUB) for at in range(0, Q_BLOCK, Q_SUB)]
+    weighted_ref[...] = jnp.zeros_like(weighted_ref)
 
     def visit(kind, block, carried):
+        top, total = carried
         key_rows = keys[pl.ds(pl.multiple_of(block * K_BLOCK, K_BLOCK), K_BLOCK)]
-        block_values = values_t[block]
+        scores = jnp.dot(key_rows, queries, preferred_element_type=jnp.float32) * factor
         index = block * K_BLOCK + key_offset
-        result = []
-        for sub, (top, total, weighted) in zip(subs, carried):
-            scores = jnp.dot(key_rows, queries[:, sub], preferred_element_type=jnp.float32) * factor
-            if kind == "before":
-                scores = jnp.where(index >= start[:, sub], scores, masked_score)
-            if kind == "diagonal":
-                kept = (index >= start[:, sub]) & (index <= query_index[:, sub])
-                scores = jnp.where(kept, scores, masked_score)
-            new_top = jnp.maximum(top, jnp.max(scores, axis=0, keepdims=True))
-            rescale = jnp.exp2(top - new_top)
-            weight = jnp.exp2(scores - new_top)
-            total = total * rescale + jnp.sum(weight, axis=0, keepdims=True)
-            weighted = weighted * rescale + jnp.dot(
-                block_values, weight.astype(jnp.bfloat16), preferred_element_type=jnp.float32
-            )
-            result.append((new_top, total, weighted))
-        return tuple(result)
+        if kind == "before":
+            scores = jnp.where(index >= start, scores, masked_score)
+        if kind == "diagonal":
+            scores = jnp.where((index >= start) & (index <= query_index), scores, masked_score)
+        new_top = jnp.maximum(top, jnp.max(scores, axis=0, keepdims=True))
+        rescale = jnp.exp2(top - new_top)
+        weight = jnp.exp2(scores - new_top)
+        total = total * rescale + jnp.sum(weight, axis=0, keepdims=True)
+        weighted_ref[...] = weighted_ref[...] * rescale + jnp.dot(
+            values_t[block], weight.astype(jnp.bfloat16), preferred_element_type=jnp.float32
+        )
+        return new_top, total
 
     middle = jnp.minimum(mid_ref[step], diagonal)
-    carried = tuple(
-        (
-            jnp.full((1, Q_SUB), masked_score, jnp.float32),
-            jnp.zeros((1, Q_SUB), jnp.float32),
-            jnp.zeros((HEAD_DIM, Q_SUB), jnp.float32),
-        )
-        for _ in subs
+    carried = (
+        jnp.full((1, Q_BLOCK), masked_score, jnp.float32),
+        jnp.zeros((1, Q_BLOCK), jnp.float32),
     )
     carried = lax.fori_loop(lo_ref[step], middle, functools.partial(visit, "before"), carried)
     carried = lax.fori_loop(middle, diagonal, functools.partial(visit, "inside"), carried)
-    carried = lax.fori_loop(diagonal, last + 1, functools.partial(visit, "diagonal"), carried)
-    gate = gate_all[here].T
-    for sub, (top, total, weighted) in zip(subs, carried):
-        rounded = (weighted * (1.0 / total)).astype(jnp.bfloat16)
-        out_ref[0, sub] = rounded.T
-        gated_ref[:, sub] = (rounded.astype(jnp.float32) * gate[:, sub].astype(jnp.float32)).astype(jnp.bfloat16)
+    _, total = lax.fori_loop(diagonal, last + 1, functools.partial(visit, "diagonal"), carried)
+    rounded = (weighted_ref[...] * (1.0 / total)).astype(jnp.bfloat16)
+    out_ref[0] = rounded.T
+    gated = rounded.astype(jnp.float32) * gate_all[here].T.astype(jnp.float32)
+    gated_ref[...] = gated.astype(jnp.bfloat16)
 
 
 def attention(x_index, own, before, asked, start):
@@ -189,6 +180,7 @@
                 pltpu.VMEM((2 * rows // K_BLOCK, HEAD_DIM, K_BLOCK), jnp.bfloat16),
                 pltpu.VMEM((rows, HEAD_DIM), jnp.bfloat16),
                 pltpu.VMEM((rows, HEAD_DIM), jnp.bfloat16),
+                pltpu.VMEM((HEAD_DIM, Q_BLOCK), jnp.float32),
                 pltpu.SemaphoreType.DMA((X_SIZE, 6)),
             ],
         ),
@@ -206,7 +198,7 @@
 def high_low(table):
     high = table.astype(np.float32).astype(ml_dtypes.bfloat16)
     low = (table - high.astype(np.float64)).astype(np.float32).astype(ml_dtypes.bfloat16)
-    return high, low
+    return np.stack((high, low))
 
 
 def transform_tables(length, senders, tap_senders):
@@ -221,15 +213,9 @@
     def angles(a):
         return 2.0 * np.pi * ((4 * k1[:, None] + 1) * a[None, :] % (4 * outer)) / (4 * outer)
 
-    def left(table):
-        return np.concatenate(high_low(table), axis=1)
-
-    def right(table):
-        return np.concatenate(high_low(table), axis=0)
-
     def forward(a):
         angle = angles(a)
-        return left(np.concatenate((np.cos(angle), -np.sin(angle)), axis=0))
+        return high_low(np.concatenate((np.cos(angle), -np.sin(angle)), axis=0))
 
     twist = 2.0 * np.pi * ((4 * k1[:, None] + 1) * b[None, :] % (4 * length)) / (4 * length)
     inner = 2.0 * np.pi * (b[:, None] * b[None, :] % LANES) / LANES
@@ -239,18 +225,22 @@
         signal=forward(a_signal),
         taps=forward(a_tap),
         twist=np.stack((np.cos(twist), -np.sin(twist))).astype(np.float32),
-        inner=right(np.block([[cos, -sin], [sin, cos]])),
-        inner_back=right(np.block([[cos, sin], [-sin, cos]])),
-        back=left(np.concatenate((np.cos(back), -np.sin(back)), axis=1) / length),
+        inner=high_low(np.block([[cos, -sin], [sin, cos]])),
+        inner_back=high_low(np.block([[cos, sin], [-sin, cos]])),
+        back=high_low(np.concatenate((np.cos(back), -np.sin(back)), axis=1) / length),
     )
 
 
 def table_dot(table_ref, right):
-    return jnp.dot(table_ref[...], jnp.concatenate((right, right), axis=0), preferred_element_type=jnp.float32)
+    return jnp.dot(table_ref[0], right, preferred_element_type=jnp.float32) + jnp.dot(
+        table_ref[1], right, preferred_element_type=jnp.float32
+    )
 
 
 def dot_table(left, table_ref):
-    return jnp.dot(jnp.concatenate((left, left), axis=1), table_ref[...], preferred_element_type=jnp.float32)
+    return jnp.dot(left, table_ref[0], preferred_element_type=jnp.float32) + jnp.dot(
+        left, table_ref[1], preferred_element_type=jnp.float32
+    )
 
 
 def spread(source_ref, spread_ref):
@@ -269,15 +259,16 @@
     return jnp.concatenate(pair, axis=1)
 
 
-def spectrum(rows, outer_ref, twist_ref, inner_ref):
-    outer = rows.shape[0]
-    section = table_dot(outer_ref, rows)
+def spectra_of(pairs, outer_ref, twist_ref, inner_ref):
+    outer = twist_ref.shape[1]
     turned = []
-    for lane in (0, LANES):
-        real, imag = section[:outer, lane : lane + LANES], section[outer:, lane : lane + LANES]
-        turned_real = real * twist_ref[0] - imag * twist_ref[1]
-        turned_imag = real * twist_ref[1] + imag * twist_ref[0]
-        turned.append(jnp.concatenate((turned_real.astype(jnp.bfloat16), turned_imag.astype(jnp.bfloat16)), axis=1))
+    for rows in pairs:
+        section = table_dot(outer_ref, rows)
+        for lane in (0, LANES):
+            real, imag = section[:outer, lane : lane + LANES], section[outer:, lane : lane + LANES]
+            turned_real = real * twist_ref[0] - imag * twist_ref[1]
+            turned_imag = real * twist_ref[1] + imag * twist_ref[0]
+            turned.append(jnp.concatenate((turned_real.astype(jnp.bfloat16), turned_imag.astype(jnp.bfloat16)), axis=1))
     return dot_table(jnp.concatenate(turned, axis=0), inner_ref)
 
 
@@ -289,9 +280,9 @@
     def _():
         spread(taps_ref, spread_ref)
 
-    for pair in range(out_ref.shape[0]):
-        channel = step * 2 * out_ref.shape[0] + 2 * pair
-        out_ref[pair] = spectrum(channel_rows(spread_ref, channel, channels), outer_ref, twist_ref, inner_ref)
+    first = step * 2 * PAIRS
+    pairs = [channel_rows(spread_ref, first + 2 * pair, channels) for pair in range(PAIRS)]
+    out_ref[...] = spectra_of(pairs, outer_ref, twist_ref, inner_ref)
 
 
 def conv_kernel(
@@ -306,18 +297,19 @@
     def _():
         spread(signal_ref, spread_ref)
 
-    for pair in range(taps_ref.shape[0]):
-        channel = step * 2 * taps_ref.shape[0] + 2 * pair
-        signal = spectrum(channel_rows(spread_ref, channel, channels), outer_ref, twist_ref, inner_ref)
-        taps = taps_ref[pair]
-        sig_real, sig_imag = signal[:, :LANES], signal[:, LANES:]
-        tap_real, tap_imag = taps[:, :LANES], taps[:, LANES:]
-        prod_real = sig_real * tap_real - sig_imag * tap_imag
-        prod_imag = sig_real * tap_imag + sig_imag * tap_real
-        prod = jnp.concatenate((prod_real.astype(jnp.bfloat16), prod_imag.astype(jnp.bfloat16)), axis=1)
-        turned = dot_table(prod, inner_back_ref)
+    first = step * 2 * PAIRS
+    pairs = [channel_rows(spread_ref, first + 2 * pair, channels) for pair in range(PAIRS)]
+    signal = spectra_of(pairs, outer_ref, twist_ref, inner_ref)
+    sig_real, sig_imag = signal[:, :LANES], signal[:, LANES:]
+    tap_real, tap_imag = taps_ref[:, :LANES], taps_ref[:, LANES:]
+    prod_real = sig_real * tap_real - sig_imag * tap_imag
+    prod_imag = sig_real * tap_imag + sig_imag * tap_real
+    prod = jnp.concatenate((prod_real.astype(jnp.bfloat16), prod_imag.astype(jnp.bfloat16)), axis=1)
+    turned = dot_table(prod, inner_back_ref)
+    for pair in range(PAIRS):
+        channel = first + 2 * pair
         both = []
-        for row in (0, outer):
+        for row in (2 * pair * outer, (2 * pair + 1) * outer):
             real, imag = turned[row : row + outer, :LANES], turned[row : row + outer, LANES:]
             back_real = real * twist_ref[0] + imag * twist_ref[1]
             back_imag = imag * twist_ref[0] - real * twist_ref[1]
@@ -348,8 +340,8 @@
         name="taps_spectrum",
         grid=(channels // (2 * PAIRS),),
         in_specs=[whole(x) for x in operands],
-        out_specs=pl.BlockSpec((PAIRS, 2 * outer, 2 * LANES), lambda i: (i, 0, 0)),
-        out_shape=jax.ShapeDtypeStruct((channels // 2, 2 * outer, 2 * LANES), jnp.float32),
+        out_specs=pl.BlockSpec((PAIRS * 2 * outer, 2 * LANES), lambda i: (i, 0)),
+        out_shape=jax.ShapeDtypeStruct((channels * outer, 2 * LANES), jnp.float32),
         scratch_shapes=[pltpu.VMEM((rows // LANES, senders * channels, LANES), jnp.float32)],
         compiler_params=pltpu.CompilerParams(vmem_limit_bytes=VMEM_LIMIT),
         cost_estimate=pl.CostEstimate(flops=5 * 10**9, bytes_accessed=4 * 2**20, transcendentals=0),
@@ -359,12 +351,13 @@
 def convolve(signal, spectra, tables, receivers):
     senders, channels, rows = signal.shape
     out_rows = senders * rows // receivers
+    outer = tables["twist"].shape[1]
     operands = [tables[n] for n in ("signal", "twist", "inner", "inner_back", "back")]
     return pl.pallas_call(
         conv_kernel,
         name="convolution",
         grid=(channels // (2 * PAIRS),),
-        in_specs=[whole(signal), pl.BlockSpec((PAIRS,) + spectra.shape[1:], lambda i: (i, 0, 0))]
+        in_specs=[whole(signal), pl.BlockSpec((PAIRS * 2 * outer, 2 * LANES), lambda i: (i, 0))]
         + [whole(x) for x in operands],
         out_specs=pl.BlockSpec((receivers, channels, out_rows), lambda i: (0, 0, 0)),
         out_shape=jax.ShapeDtypeStruct((receivers, channels, out_rows), jnp.bfloat16),
@@ -455,15 +448,20 @@
         return lax.ppermute(piece, "ctx", pairs)
 
     def arrived(pieces):
-        return [pieces[0]] + [along_x(pieces[k], k) for k in range(1, X_SIZE)]
+        moved = {k: along_x(pieces[k], k) for k in NEAR_FIRST[1:]}
+        return [pieces[0]] + [moved[k] for k in range(1, X_SIZE)]
 
     taps = filter_taps.astype(jnp.bfloat16).reshape(X_SIZE, z_size, per_device, row_count)
     taps = taps.transpose(1, 0, 2, 3).reshape(ctx, per_device, row_count)
-    own = arrived(pieces_of(x_index, key_rows, values))
-    before = [along_z(own[k], k) for k in range(X_SIZE)]
-    own[1], queries, in_gate = lax.optimization_barrier((own[1], queries, in_gate))
+    pieces = pieces_of(x_index, key_rows, values)
+    own = arrived(pieces)
+    moved = {k: along_z(own[k], k) for k in NEAR_FIRST}
+    before = [moved[k] for k in range(X_SIZE)]
+    _, queries, in_gate = lax.optimization_barrier((pieces[0], queries, in_gate))
     asked = pieces_of(x_index, queries, in_gate)
-    taps, *_ = lax.optimization_barrier((taps, *own, *asked))
+    both = lax.optimization_barrier((*own, *asked))
+    own, asked = list(both[:X_SIZE]), list(both[X_SIZE:])
+    taps, asked[0] = lax.optimization_barrier((taps, asked[0]))
     asked = arrived(asked)
     taps = exchanged(taps)
 

time: 143 us -> 137 us (0.958)
  Pallas kernels: 42.8 us -> 37.9 us
  starting transfers between devices: 49.8 us -> 52.1 us
  waiting for transfers between devices: 42.7 us -> 40.5 us
    all_to_all x3, starting transfers between devices: 21.3 us -> 26.1 us  [exchanged(): lax.all_to_all(x, 'ctx', split_axis=0, concat_axis=0, tiled=True, axis_in...]
    all_to_all x3, waiting for transfers between devices: 25.4 us -> 21.2 us  [exchanged(): lax.all_to_all(x, 'ctx', split_axis=0, concat_axis=0, tiled=True, axis_in...]
    pallas_call x1, Pallas kernels: 11.3 us -> 7.9 us  [convolve(): pl.pallas_call(conv_kernel, name='convolution', grid=(channels // (2 * PA...]
    ppermute x9, starting transfers between devices: 15.6 us -> 13.2 us  [along_x(): return lax.ppermute(piece, 'ctx', pairs)]
    ppermute x9, waiting for transfers between devices: 7.38 us -> 8.85 us  [along_x(): return lax.ppermute(piece, 'ctx', pairs)]
  transfers between devices with their start and end apart: 16 -> 16, of which waited for: 5 -> 5; matrix products, arithmetic and copies ran while one was open for 3% -> 3% of each run, Pallas kernels for 27% -> 25%
where the time goes in v6:
time: 137 us; the launch traced here: 135 us
  starting transfers between devices  52.1 us (38%)
  waiting for transfers between devices  40.5 us (30%)
  Pallas kernels  37.9 us (28%)
  local copies, waits for them, and re-layouts  3.13 us (2%)
    all_to_all x3, starting transfers between devices, exchanged(): lax.all_to_all(x, 'ctx', split_axis=0, concat_axis=0, tiled=True, axis_in...  26.1 us
    all_to_all x3, waiting for transfers between devices, exchanged(): lax.all_to_all(x, 'ctx', split_axis=0, concat_axis=0, tiled=True, axis_in...  21.2 us
    pallas_call x1, Pallas kernels, attention(): pl.pallas_call(attention_kernel, name='attention', grid_spec=pltpu.Prefet...  16.4 us
    ppermute x9, starting transfers between devices, along_x(): return lax.ppermute(piece, 'ctx', pairs)  13.2 us
    ppermute x4, starting transfers between devices, along_z(): return lax.ppermute(piece, 'ctx', pairs)  12.9 us
    ppermute x4, waiting for transfers between devices, along_z(): return lax.ppermute(piece, 'ctx', pairs)  10.4 us
    ppermute x9, waiting for transfers between devices, along_x(): return lax.ppermute(piece, 'ctx', pairs)  8.85 us
    pallas_call x1, Pallas kernels, convolve(): pl.pallas_call(conv_kernel, name='convolution', grid=(channels // (2 * PA...  7.9 us
  transfers between devices with their start and end apart: 16, of which 5 were waited for; matrix products, arithmetic and copies ran while one was open for 3% of the time, Pallas kernels for 25%

profile of v6, /device:TPU:16, one launch (start us, length us, event | category | flops | bytes accessed | tf_op | source)
XLA Modules:
  0.0 135.5 jit_solution(2932349919743532555)
XLA Ops:
  0.7 2.4 %pieces.2 = (bf16[2,768,128]{2,1,0:T(8,128)(2,1)}, bf16[2,768,128]{2,1,0:T(8,128)(2,1)}, bf16[2,768,128]{2,1,0:T(8,128)(2,1)}, bf16[2,768,128]{2,1,0:T(8,128)(2,1)}) custom-call(s32[1]{0:T(128)} %bitcast.x_ref, bf16[768,512]{1,0:T(8,128)(2,1)} %first_ref.1, bf16[768,512]{1,0:T(8,128)(2,1)} %second_ref.1), custom_call_target="tpu_custom_call" | custom-call | tf_op jit(solution)/shard_map/pieces/pallas_call | solution.py:53
  3.1 1.6 %collective-permute-start = (bf16[2,768,128]{2,1,0:T(8,128)(2,1)}, bf16[2,768,128]{2,1,0:T(8,128)(2,1)S(1)}, u32[]{:S(2)}, u32[]{:S(2)}) collective-permute-start(bf16[2,768,128]{2,1,0:T(8,128)(2,1)} %get-tuple-element.34), channel_id=1, source_target_pairs={{0,8},{8,16},{16,24},{24,0},{32,40},{40,48},{48,56},{56,32},{64,72... | collective-permute-start | bytes 1179656 | tf_op jit(solution)/shard_map/ppermute | solution.py:444
  4.7 2.7 %collective-permute-start.1 = (bf16[2,768,128]{2,1,0:T(8,128)(2,1)}, bf16[2,768,128]{2,1,0:T(8,128)(2,1)S(1)}, u32[]{:S(2)}, u32[]{:S(2)}) collective-permute-start(bf16[2,768,128]{2,1,0:T(8,128)(2,1)} %get-tuple-element.35), channel_id=1, source_target_pairs={{0,16},{8,24},{16,0},{24,8},{32,48},{40,56},{48,32},{56,40},{64,80... | collective-permute-start | bytes 1179656 | tf_op jit(solution)/shard_map/ppermute | solution.py:444
  7.4 1.4 %collective-permute-start.2 = (bf16[2,768,128]{2,1,0:T(8,128)(2,1)}, bf16[2,768,128]{2,1,0:T(8,128)(2,1)}, u32[]{:S(2)}, u32[]{:S(2)}) collective-permute-start(bf16[2,768,128]{2,1,0:T(8,128)(2,1)} %get-tuple-element.36), channel_id=1, source_target_pairs={{0,24},{8,0},{16,8},{24,16},{32,56},{40,32},{48,40},{56,48},{64,88... | collective-permute-start | bytes 1179656 | tf_op jit(solution)/shard_map/ppermute | solution.py:444
  8.8 0.7 collective-permute-start.3
  9.5 6.1 %collective-permute-done.rest_1_ = bf16[2,768,128]{2,1,0:T(8,128)(2,1)S(1)} collective-permute-done((bf16[2,768,128]{2,1,0:T(8,128)(2,1)}, bf16[2,768,128]{2,1,0:T(8,128)(2,1)S(1)}, u32[]{:S(2)}, u32[]{:S(2)}) %collective-permute-start) | collective-permute-done | bytes 393248 | tf_op jit(solution)/shard_map/ppermute | solution.py:444
  15.6 3.8 %collective-permute-start.4 = (bf16[2,768,128]{2,1,0:T(8,128)(2,1)S(1)}, bf16[2,768,128]{2,1,0:T(8,128)(2,1)S(1)}, u32[]{:S(2)}, u32[]{:S(2)}) collective-permute-start(bf16[2,768,128]{2,1,0:T(8,128)(2,1)S(1)} %collective-permute-done.rest_1_), channel_id=1, source_target_pairs={{0,32},{16,48},{24,56},{32,64},{48,80},{56,88},{64,96},{80,112},{8... | collective-permute-start | bytes 1179656 | tf_op jit(solution)/shard_map/ppermute | solution.py:448
  19.5 2.3 %pieces.3 = (bf16[2,768,128]{2,1,0:T(8,128)(2,1)}, bf16[2,768,128]{2,1,0:T(8,128)(2,1)}, bf16[2,768,128]{2,1,0:T(8,128)(2,1)}, bf16[2,768,128]{2,1,0:T(8,128)(2,1)}) custom-call(s32[1]{0:T(128)} %bitcast.x_ref, bf16[768,512]{1,0:T(8,128)(2,1)} %first_ref.2, bf16[768,512]{1,0:T(8,128)(2,1)} %second_ref.2), custom_call_target="tpu_custom_call" | custom-call | tf_op jit(solution)/shard_map/pieces/pallas_call | solution.py:53
  21.8 0.1 select_reduce_fusion.1
  21.9 0.2 select_reduce_fusion
  22.1 2.7 %collective-permute-done.1.rest_2_ = bf16[2,768,128]{2,1,0:T(8,128)(2,1)S(1)} collective-permute-done((bf16[2,768,128]{2,1,0:T(8,128)(2,1)}, bf16[2,768,128]{2,1,0:T(8,128)(2,1)S(1)}, u32[]{:S(2)}, u32[]{:S(2)}) %collective-permute-start.1) | collective-permute-done | bytes 393248 | tf_op jit(solution)/shard_map/ppermute | solution.py:444
  24.9 0.0 collective-permute-done.2.rest_3_
  24.9 1.4 %collective-permute-start.7 = (bf16[2,768,128]{2,1,0:T(8,128)(2,1)}, bf16[2,768,128]{2,1,0:T(8,128)(2,1)}, u32[]{:S(2)}, u32[]{:S(2)}) collective-permute-start(bf16[2,768,128]{2,1,0:T(8,128)(2,1)} %get-tuple-element.49), channel_id=1, source_target_pairs={{0,8},{8,16},{16,24},{24,0},{32,40},{40,48},{48,56},{56,32},{64,72... | collective-permute-start | bytes 1179656 | tf_op jit(solution)/shard_map/ppermute | solution.py:444
  26.3 2.4 %collective-permute-start.8 = (bf16[2,768,128]{2,1,0:T(8,128)(2,1)}, bf16[2,768,128]{2,1,0:T(8,128)(2,1)}, u32[]{:S(2)}, u32[]{:S(2)}) collective-permute-start(bf16[2,768,128]{2,1,0:T(8,128)(2,1)} %get-tuple-element.50), channel_id=1, source_target_pairs={{0,16},{8,24},{16,0},{24,8},{32,48},{40,56},{48,32},{56,40},{64,80... | collective-permute-start | bytes 1179656 | tf_op jit(solution)/shard_map/ppermute | solution.py:444
  28.7 1.6 %collective-permute-start.9 = (bf16[2,768,128]{2,1,0:T(8,128)(2,1)}, bf16[2,768,128]{2,1,0:T(8,128)(2,1)}, u32[]{:S(2)}, u32[]{:S(2)}) collective-permute-start(bf16[2,768,128]{2,1,0:T(8,128)(2,1)} %get-tuple-element.51), channel_id=1, source_target_pairs={{0,24},{8,0},{16,8},{24,16},{32,56},{40,32},{48,40},{56,48},{64,88... | collective-permute-start | bytes 1179656 | tf_op jit(solution)/shard_map/ppermute | solution.py:444
  30.2 0.0 collective-permute-done.3.rest_4_
  30.3 4.6 %collective-permute-start.5 = (bf16[2,768,128]{2,1,0:T(8,128)(2,1)S(1)}, bf16[2,768,128]{2,1,0:T(8,128)(2,1)}, u32[]{:S(2)}, u32[]{:S(2)}) collective-permute-start(bf16[2,768,128]{2,1,0:T(8,128)(2,1)S(1)} %collective-permute-done.1.rest_2_), channel_id=1, source_target_pairs={{0,32},{8,40},{24,56},{32,64},{40,72},{56,88},{64,96},{72,104},{88... | collective-permute-start | bytes 1179656 | tf_op jit(solution)/shard_map/ppermute | solution.py:448
  34.8 0.0 collective-permute-done.4.rest_5_
  34.8 3.9 %collective-permute-start.6 = (bf16[2,768,128]{2,1,0:T(8,128)(2,1)}, bf16[2,768,128]{2,1,0:T(8,128)(2,1)}, u32[]{:S(2)}, u32[]{:S(2)}) collective-permute-start(bf16[2,768,128]{2,1,0:T(8,128)(2,1)} %collective-permute-done.2.rest_3_), channel_id=1, source_target_pairs={{0,32},{8,40},{16,48},{32,64},{40,72},{48,80},{64,96},{72,104},{80... | collective-permute-start | bytes 1179656 | tf_op jit(solution)/shard_map/ppermute | solution.py:448
  38.7 0.1 slice.19
  38.8 0.1 slice.18
  38.9 0.1 convert_element_type.3
  39.0 1.0 copy.16
  39.9 6.3 %all-to-all-start = ((bf16[32,16,768]{2,1,0:T(8,128)(2,1)}), bf16[32,16,768]{2,1,0:T(8,128)(2,1)S(1)}, u32[]{:S(2)}, u32[]{:S(2)}) async-start(bf16[32,16,768]{2,1,0:T(8,128)(2,1)} %bitcast.4), calls=%async_computation | async-start | bytes 1572864 | tf_op jit(solution)/shard_map/all_to_all | solution.py:440
  46.3 0.6 and_select_fusion.1
  46.9 0.0 collective-permute-done.5.rest_6_
  46.9 10.4 %collective-permute-done.6.rest_7_ = bf16[2,768,128]{2,1,0:T(8,128)(2,1)} collective-permute-done((bf16[2,768,128]{2,1,0:T(8,128)(2,1)}, bf16[2,768,128]{2,1,0:T(8,128)(2,1)}, u32[]{:S(2)}, u32[]{:S(2)}) %collective-permute-start.6) | collective-permute-done | bytes 393248 | tf_op jit(solution)/shard_map/ppermute | solution.py:448
  57.3 0.0 collective-permute-done.7.rest_9_
  57.3 0.0 collective-permute-done.8.rest_10_
  57.3 0.0 collective-permute-done.9.rest_11_
  57.3 16.4 %attention.1 = (bf16[4,768,128]{2,1,0:T(8,128)(2,1)}, bf16[128,3072]{1,0:T(8,128)(2,1)}) custom-call(s32[4]{0:T(128)} %get-tuple-element.68.lo_ref, s32[4]{0:T(128)} %get-tuple-element.69.mid_ref, s32[1]{0:T(128)} %bitcast.x_ref, s32[4,1,768]{2,1,0:T(1,128)} %bitcast.19, bf16[2,768,128]{2,1,0:T(8,128)(2,1)} %get-tuple-element.43.rest_0_, ...), custom_call_target="tpu_custom_call" | custom-call | flops 16000000000 | bytes 3932160 | tf_op jit(solution)/shard_map/attention/pallas_call | solution.py:166
  73.7 0.0 all-to-all-done.taps_ref
  73.7 15.8 %all-to-all-start.1 = ((bf16[8,16,3072]{2,1,0:T(8,128)(2,1)}), bf16[8,16,3072]{2,1,0:T(8,128)(2,1)}, u32[]{:S(2)}, u32[]{:S(2)}) async-start(bf16[8,16,3072]{2,1,0:T(8,128)(2,1)} %bitcast.18), calls=%async_computation.1 | async-start | bytes 1572864 | tf_op jit(solution)/shard_map/all_to_all | solution.py:440
  89.5 5.0 %taps_spectrum.1.taps_ref = f32[3072,256]{1,0:T(8,128)} custom-call(bf16[32,16,768]{2,1,0:T(8,128)(2,1)} %copy-done.2, bf16[2,384,192]{2,1,0:T(8,128)(2,1)} %constant.53.clone.outer_ref, f32[2,192,128]{2,1,0:T(8,128)} %constant.54.clone.twist_ref, bf16[2,256,256]{2,1,0:T(8,128)(2,1)} %constant.55.clone.inner_ref), custom_call_target="tpu_custom_call" | custom-call | flops 5000000000 | bytes 4194304 | tf_op jit(solution)/shard_map/taps_spectrum/pallas_call | solution.py:338
  94.5 1.9 %slice_bitcast_fusion = (bf16[768,128]{1,0:T(8,128)(2,1)S(1)}, bf16[768,128]{1,0:T(8,128)(2,1)S(1)}, bf16[768,128]{1,0:T(8,128)(2,1)S(1)}, bf16[768,128]{1,0:T(8,128)(2,1)}) fusion(bf16[4,768,128]{2,1,0:T(8,128)(2,1)} %get-tuple-element.58), kind=kLoop, calls=%fused_computation.1 | loop fusion | bytes 1572864 | tf_op jit(solution)/shard_map/squeeze | solution.py:477
  96.4 0.0 collective-permute-start.12
  96.4 0.5 collective-permute-start.11
  97.0 1.5 %collective-permute-start.10 = (bf16[768,128]{1,0:T(8,128)(2,1)S(1)}, bf16[768,128]{1,0:T(8,128)(2,1)}, u32[]{:S(2)}, u32[]{:S(2)}) collective-permute-start(bf16[768,128]{1,0:T(8,128)(2,1)S(1)} %get-tuple-element.66), channel_id=1, source_target_pairs={{0,8},{8,16},{16,24},{24,0},{32,40},{40,48},{48,56},{56,32},{64,72... | collective-permute-start | bytes 589832 | tf_op jit(solution)/shard_map/ppermute | solution.py:444
  98.5 7.3 %all-to-all-done.1.signal_ref = bf16[8,16,3072]{2,1,0:T(8,128)(2,1)} async-done(((bf16[8,16,3072]{2,1,0:T(8,128)(2,1)}), bf16[8,16,3072]{2,1,0:T(8,128)(2,1)}, u32[]{:S(2)}, u32[]{:S(2)}) %all-to-all-start.1) | async-done | bytes 786464 | tf_op jit(solution)/shard_map/all_to_all | solution.py:440
  105.8 7.9 %convolution.1 = bf16[32,16,768]{2,1,0:T(8,128)(2,1)} custom-call(bf16[8,16,3072]{2,1,0:T(8,128)(2,1)} %all-to-all-done.1.signal_ref, f32[3072,256]{1,0:T(8,128)} %taps_spectrum.1.taps_ref, bf16[2,384,192]{2,1,0:T(8,128)(2,1)} %constant.56.clone.outer_ref, f32[2,192,128]{2,1,0:T(8,128)} %constant.54.clone.twist_ref, ...), custom_call_target="tpu_custom_call" | custom-call | flops 7000000000 | bytes 5242880 | tf_op jit(solution)/shard_map/convolution/pallas_call | solution.py:356
  113.7 0.0 collective-permute-done.12.rest_3_
  113.7 0.0 collective-permute-done.11.rest_2_
  113.7 0.0 collective-permute-done.10.rest_1_
  113.7 3.9 %all-to-all-start.2 = ((bf16[32,16,768]{2,1,0:T(8,128)(2,1)}), bf16[32,16,768]{2,1,0:T(8,128)(2,1)S(1)}, u32[]{:S(2)}, u32[]{:S(2)}) async-start(bf16[32,16,768]{2,1,0:T(8,128)(2,1)} %convolution.1), calls=%async_computation.2 | async-start | bytes 1572864 | tf_op jit(solution)/shard_map/all_to_all | solution.py:440
  117.6 0.0 copy-start
  117.7 2.0 %assemble.1 = bf16[768,512]{1,0:T(8,128)(2,1)} custom-call(s32[1]{0:T(128)} %bitcast.x_ref, bf16[768,128]{1,0:T(8,128)(2,1)} %get-tuple-element.59.rest_0_, bf16[768,128]{1,0:T(8,128)(2,1)} %collective-permute-done.10.rest_1_, bf16[768,128]{1,0:T(8,128)(2,1)} %copy-done.9, bf16[768,128]{1,0:T(8,128)(2,1)} %copy-done.8), custom_call_target="tpu_custom_call" | custom-call | flops 2000000000 | bytes 1048576 | tf_op jit(solution)/shard_map/assemble/pallas_call | solution.py:392
  119.7 13.9 %all-to-all-done.2 = bf16[32,16,768]{2,1,0:T(8,128)(2,1)S(1)} async-done(((bf16[32,16,768]{2,1,0:T(8,128)(2,1)}), bf16[32,16,768]{2,1,0:T(8,128)(2,1)S(1)}, u32[]{:S(2)}, u32[]{:S(2)}) %all-to-all-start.2) | async-done | bytes 786464 | tf_op jit(solution)/shard_map/all_to_all | solution.py:440
  133.6 1.9 %finish.1 = bf16[768,512]{1,0:T(8,128)(2,1)} custom-call(bf16[8,4,16,768]{3,2,1,0:T(8,128)(2,1)S(1)} %bitcast.16, bf16[768,512]{1,0:T(8,128)(2,1)S(1)} %copy-done), custom_call_target="tpu_custom_call" | custom-call | tf_op jit(solution)/shard_map/finish/pallas_call | solution.py:417
  (23 shorter events, 0.1 us)
Async XLA Ops:
  0.6 21.2 %copy-start.10 = (s32[64]{0:T(128)S(1)}, s32[64]{0:T(128)}, u32[]{:S(2)}) copy-start(s32[64]{0:T(128)} %param.16) | copy-start | bytes 772
  0.6 38.2 %copy-start.1 = (f32[512,768]{1,0:T(8,128)S(1)}, f32[512,768]{1,0:T(8,128)}, u32[]{:S(2)}) copy-start(f32[512,768]{1,0:T(8,128)} %param.19) | copy-start | bytes 4718596
  3.1 12.5 %collective-permute-start = (bf16[2,768,128]{2,1,0:T(8,128)(2,1)}, bf16[2,768,128]{2,1,0:T(8,128)(2,1)S(1)}, u32[]{:S(2)}, u32[]{:S(2)}) collective-permute-start(bf16[2,768,128]{2,1,0:T(8,128)(2,1)} %get-tuple-element.34), channel_id=1, source_target_pairs={{0,8},{8,16},{16,24},{24,0},{32,40},{40,48},{48,56},{56,32},{64,72... | collective-permute-start | bytes 1179656 | tf_op jit(solution)/shard_map/ppermute | solution.py:444
  4.7 20.2 %collective-permute-start.1 = (bf16[2,768,128]{2,1,0:T(8,128)(2,1)}, bf16[2,768,128]{2,1,0:T(8,128)(2,1)S(1)}, u32[]{:S(2)}, u32[]{:S(2)}) collective-permute-start(bf16[2,768,128]{2,1,0:T(8,128)(2,1)} %get-tuple-element.35), channel_id=1, source_target_pairs={{0,16},{8,24},{16,0},{24,8},{32,48},{40,56},{48,32},{56,40},{64,80... | collective-permute-start | bytes 1179656 | tf_op jit(solution)/shard_map/ppermute | solution.py:444
  7.4 17.5 %collective-permute-start.2 = (bf16[2,768,128]{2,1,0:T(8,128)(2,1)}, bf16[2,768,128]{2,1,0:T(8,128)(2,1)}, u32[]{:S(2)}, u32[]{:S(2)}) collective-permute-start(bf16[2,768,128]{2,1,0:T(8,128)(2,1)} %get-tuple-element.36), channel_id=1, source_target_pairs={{0,24},{8,0},{16,8},{24,16},{32,56},{40,32},{48,40},{56,48},{64,88... | collective-permute-start | bytes 1179656 | tf_op jit(solution)/shard_map/ppermute | solution.py:444
  8.8 21.4 %collective-permute-start.3 = (bf16[2,768,128]{2,1,0:T(8,128)(2,1)}, bf16[2,768,128]{2,1,0:T(8,128)(2,1)S(1)}, u32[]{:S(2)}, u32[]{:S(2)}) collective-permute-start(bf16[2,768,128]{2,1,0:T(8,128)(2,1)} %get-tuple-element.43.rest_0_), channel_id=1, source_target_pairs={{8,40},{16,48},{24,56},{40,72},{48,80},{56,88},{72,104},{80,112},{... | collective-permute-start | bytes 1179656 | tf_op jit(solution)/shard_map/ppermute | solution.py:448
  15.6 23.1 %copy-start.4 = (bf16[2,768,128]{2,1,0:T(8,128)(2,1)}, bf16[2,768,128]{2,1,0:T(8,128)(2,1)S(1)}, u32[]{:S(2)}) copy-start(bf16[2,768,128]{2,1,0:T(8,128)(2,1)S(1)} %collective-permute-done.rest_1_) | copy-start | bytes 1179652
  15.6 19.2 %collective-permute-start.4 = (bf16[2,768,128]{2,1,0:T(8,128)(2,1)S(1)}, bf16[2,768,128]{2,1,0:T(8,128)(2,1)S(1)}, u32[]{:S(2)}, u32[]{:S(2)}) collective-permute-start(bf16[2,768,128]{2,1,0:T(8,128)(2,1)S(1)} %collective-permute-done.rest_1_), channel_id=1, source_target_pairs={{0,32},{16,48},{24,56},{32,64},{48,80},{56,88},{64,96},{80,112},{8... | collective-permute-start | bytes 1179656 | tf_op jit(solution)/shard_map/ppermute | solution.py:448
  24.8 22.0 %copy-start.5 = (bf16[2,768,128]{2,1,0:T(8,128)(2,1)}, bf16[2,768,128]{2,1,0:T(8,128)(2,1)S(1)}, u32[]{:S(2)}) copy-start(bf16[2,768,128]{2,1,0:T(8,128)(2,1)S(1)} %collective-permute-done.1.rest_2_) | copy-start | bytes 1179652
  24.9 32.4 %collective-permute-start.7 = (bf16[2,768,128]{2,1,0:T(8,128)(2,1)}, bf16[2,768,128]{2,1,0:T(8,128)(2,1)}, u32[]{:S(2)}, u32[]{:S(2)}) collective-permute-start(bf16[2,768,128]{2,1,0:T(8,128)(2,1)} %get-tuple-element.49), channel_id=1, source_target_pairs={{0,8},{8,16},{16,24},{24,0},{32,40},{40,48},{48,56},{56,32},{64,72... | collective-permute-start | bytes 1179656 | tf_op jit(solution)/shard_map/ppermute | solution.py:444
  26.3 31.0 %collective-permute-start.8 = (bf16[2,768,128]{2,1,0:T(8,128)(2,1)}, bf16[2,768,128]{2,1,0:T(8,128)(2,1)}, u32[]{:S(2)}, u32[]{:S(2)}) collective-permute-start(bf16[2,768,128]{2,1,0:T(8,128)(2,1)} %get-tuple-element.50), channel_id=1, source_target_pairs={{0,16},{8,24},{16,0},{24,8},{32,48},{40,56},{48,32},{56,40},{64,80... | collective-permute-start | bytes 1179656 | tf_op jit(solution)/shard_map/ppermute | solution.py:444
  28.7 28.6 %collective-permute-start.9 = (bf16[2,768,128]{2,1,0:T(8,128)(2,1)}, bf16[2,768,128]{2,1,0:T(8,128)(2,1)}, u32[]{:S(2)}, u32[]{:S(2)}) collective-permute-start(bf16[2,768,128]{2,1,0:T(8,128)(2,1)} %get-tuple-element.51), channel_id=1, source_target_pairs={{0,24},{8,0},{16,8},{24,16},{32,56},{40,32},{48,40},{56,48},{64,88... | collective-permute-start | bytes 1179656 | tf_op jit(solution)/shard_map/ppermute | solution.py:444
  30.3 9.7 %copy-start.6 = (bf16[2,768,128]{2,1,0:T(8,128)(2,1)}, bf16[2,768,128]{2,1,0:T(8,128)(2,1)S(1)}, u32[]{:S(2)}) copy-start(bf16[2,768,128]{2,1,0:T(8,128)(2,1)S(1)} %collective-permute-done.3.rest_4_) | copy-start | bytes 1179652
  30.3 16.6 %collective-permute-start.5 = (bf16[2,768,128]{2,1,0:T(8,128)(2,1)S(1)}, bf16[2,768,128]{2,1,0:T(8,128)(2,1)}, u32[]{:S(2)}, u32[]{:S(2)}) collective-permute-start(bf16[2,768,128]{2,1,0:T(8,128)(2,1)S(1)} %collective-permute-done.1.rest_2_), channel_id=1, source_target_pairs={{0,32},{8,40},{24,56},{32,64},{40,72},{56,88},{64,96},{72,104},{88... | collective-permute-start | bytes 1179656 | tf_op jit(solution)/shard_map/ppermute | solution.py:448
  34.8 5.1 %copy-start.7 = (bf16[2,768,128]{2,1,0:T(8,128)(2,1)}, bf16[2,768,128]{2,1,0:T(8,128)(2,1)S(1)}, u32[]{:S(2)}) copy-start(bf16[2,768,128]{2,1,0:T(8,128)(2,1)S(1)} %collective-permute-done.4.rest_5_) | copy-start | bytes 1179652
  34.8 22.5 %collective-permute-start.6 = (bf16[2,768,128]{2,1,0:T(8,128)(2,1)}, bf16[2,768,128]{2,1,0:T(8,128)(2,1)}, u32[]{:S(2)}, u32[]{:S(2)}) collective-permute-start(bf16[2,768,128]{2,1,0:T(8,128)(2,1)} %collective-permute-done.2.rest_3_), channel_id=1, source_target_pairs={{0,32},{8,40},{16,48},{32,64},{40,72},{48,80},{64,96},{72,104},{80... | collective-permute-start | bytes 1179656 | tf_op jit(solution)/shard_map/ppermute | solution.py:448
  38.7 18.6 %copy-start.3 = (s32[3072]{0:T(1024)}, s32[3072]{0:T(1024)S(1)}, u32[]{:S(2)}) copy-start(s32[3072]{0:T(1024)S(1)} %broadcast_subtract_fusion) | copy-start | bytes 36868
  39.9 33.7 %all-to-all-start = ((bf16[32,16,768]{2,1,0:T(8,128)(2,1)}), bf16[32,16,768]{2,1,0:T(8,128)(2,1)S(1)}, u32[]{:S(2)}, u32[]{:S(2)}) async-start(bf16[32,16,768]{2,1,0:T(8,128)(2,1)} %bitcast.4), calls=%async_computation | async-start | bytes 1572864 | tf_op jit(solution)/shard_map/all_to_all | solution.py:440
  73.7 15.8 %copy-start.2 = (bf16[32,16,768]{2,1,0:T(8,128)(2,1)}, bf16[32,16,768]{2,1,0:T(8,128)(2,1)S(1)}, u32[]{:S(2)}) copy-start(bf16[32,16,768]{2,1,0:T(8,128)(2,1)S(1)} %all-to-all-done.taps_ref) | copy-start | bytes 2359300
  73.7 32.1 %all-to-all-start.1 = ((bf16[8,16,3072]{2,1,0:T(8,128)(2,1)}), bf16[8,16,3072]{2,1,0:T(8,128)(2,1)}, u32[]{:S(2)}, u32[]{:S(2)}) async-start(bf16[8,16,3072]{2,1,0:T(8,128)(2,1)} %bitcast.18), calls=%async_computation.1 | async-start | bytes 1572864 | tf_op jit(solution)/shard_map/all_to_all | solution.py:440
  96.4 17.2 %collective-permute-start.12 = (bf16[768,128]{1,0:T(8,128)(2,1)S(1)}, bf16[768,128]{1,0:T(8,128)(2,1)S(1)}, u32[]{:S(2)}, u32[]{:S(2)}) collective-permute-start(bf16[768,128]{1,0:T(8,128)(2,1)S(1)} %get-tuple-element.64), channel_id=1, source_target_pairs={{0,24},{8,0},{16,8},{24,16},{32,56},{40,32},{48,40},{56,48},{64,88... | collective-permute-start | bytes 589832 | tf_op jit(solution)/shard_map/ppermute | solution.py:444
  96.4 17.2 %collective-permute-start.11 = (bf16[768,128]{1,0:T(8,128)(2,1)S(1)}, bf16[768,128]{1,0:T(8,128)(2,1)S(1)}, u32[]{:S(2)}, u32[]{:S(2)}) collective-permute-start(bf16[768,128]{1,0:T(8,128)(2,1)S(1)} %get-tuple-element.65), channel_id=1, source_target_pairs={{0,16},{8,24},{16,0},{24,8},{32,48},{40,56},{48,32},{56,40},{64,80... | collective-permute-start | bytes 589832 | tf_op jit(solution)/shard_map/ppermute | solution.py:444
  97.0 16.7 %collective-permute-start.10 = (bf16[768,128]{1,0:T(8,128)(2,1)S(1)}, bf16[768,128]{1,0:T(8,128)(2,1)}, u32[]{:S(2)}, u32[]{:S(2)}) collective-permute-start(bf16[768,128]{1,0:T(8,128)(2,1)S(1)} %get-tuple-element.66), channel_id=1, source_target_pairs={{0,8},{8,16},{16,24},{24,0},{32,40},{40,48},{48,56},{56,32},{64,72... | collective-permute-start | bytes 589832 | tf_op jit(solution)/shard_map/ppermute | solution.py:444
  113.7 4.0 %copy-start.8 = (bf16[768,128]{1,0:T(8,128)(2,1)}, bf16[768,128]{1,0:T(8,128)(2,1)S(1)}, u32[]{:S(2)}) copy-start(bf16[768,128]{1,0:T(8,128)(2,1)S(1)} %collective-permute-done.12.rest_3_) | copy-start | bytes 589828
  113.7 4.0 %copy-start.9 = (bf16[768,128]{1,0:T(8,128)(2,1)}, bf16[768,128]{1,0:T(8,128)(2,1)S(1)}, u32[]{:S(2)}) copy-start(bf16[768,128]{1,0:T(8,128)(2,1)S(1)} %collective-permute-done.11.rest_2_) | copy-start | bytes 589828
  113.7 19.9 %all-to-all-start.2 = ((bf16[32,16,768]{2,1,0:T(8,128)(2,1)}), bf16[32,16,768]{2,1,0:T(8,128)(2,1)S(1)}, u32[]{:S(2)}, u32[]{:S(2)}) async-start(bf16[32,16,768]{2,1,0:T(8,128)(2,1)} %convolution.1), calls=%async_computation.2 | async-start | bytes 1572864 | tf_op jit(solution)/shard_map/all_to_all | solution.py:440
  117.6 16.0 %copy-start = (bf16[768,512]{1,0:T(8,128)(2,1)S(1)}, bf16[768,512]{1,0:T(8,128)(2,1)}, u32[]{:S(2)}) copy-start(bf16[768,512]{1,0:T(8,128)(2,1)} %gate_ref.1) | copy-start | bytes 2359300

commit v7 on v6

--- a/solution.py
+++ b/solution.py
@@ -459,8 +459,9 @@
     before = [moved[k] for k in range(X_SIZE)]
     _, queries, in_gate = lax.optimization_barrier((pieces[0], queries, in_gate))
     asked = pieces_of(x_index, queries, in_gate)
-    both = lax.optimization_barrier((*own, *asked))
-    own, asked = list(both[:X_SIZE]), list(both[X_SIZE:])
+    both = lax.optimization_barrier((*own, *asked, before[0], before[1]))
+    own, asked = list(both[:X_SIZE]), list(both[X_SIZE : 2 * X_SIZE])
+    before[0], before[1] = both[2 * X_SIZE :]
     taps, asked[0] = lax.optimization_barrier((taps, asked[0]))
     asked = arrived(asked)
     taps = exchanged(taps)

time: 137 us -> 145 us (1.058); the launches traced: 135 us -> 147 us
  waiting for transfers between devices: 40.5 us -> 53.9 us
  Pallas kernels: 37.9 us -> 35 us
    ppermute x9, waiting for transfers between devices: 8.85 us -> 21 us  [along_x(): return lax.ppermute(piece, 'ctx', pairs)]
    all_to_all x3, waiting for transfers between devices: 21.2 us -> 32.9 us  [exchanged(): lax.all_to_all(x, 'ctx', split_axis=0, concat_axis=0, tiled=True, axis_in...]
    ppermute x4, waiting for transfers between devices: 10.4 us -> 0.01 us  [along_z(): return lax.ppermute(piece, 'ctx', pairs)]
    pallas_call x1, Pallas kernels: 16.4 us -> 13.5 us  [attention(): pl.pallas_call(attention_kernel, name='attention', grid_spec=pltpu.Prefet...]
  transfers between devices with their start and end apart: 16 -> 16, of which waited for: 5 -> 6; matrix products, arithmetic and copies ran while one was open for 3% -> 3% of each run, Pallas kernels for 25% -> 21%
where the time goes in v7:
time: 145 us; the launch traced here: 147 us
  waiting for transfers between devices  53.9 us (37%)
  starting transfers between devices  53.5 us (37%)
  Pallas kernels  35 us (24%)
  local copies, waits for them, and re-layouts  3.13 us (2%)
    all_to_all x3, waiting for transfers between devices, exchanged(): lax.all_to_all(x, 'ctx', split_axis=0, concat_axis=0, tiled=True, axis_in...  32.9 us
    all_to_all x3, starting transfers between devices, exchanged(): lax.all_to_all(x, 'ctx', split_axis=0, concat_axis=0, tiled=True, axis_in...  27.5 us
    ppermute x9, waiting for transfers between devices, along_x(): return lax.ppermute(piece, 'ctx', pairs)  21 us
    pallas_call x1, Pallas kernels, attention(): pl.pallas_call(attention_kernel, name='attention', grid_spec=pltpu.Prefet...  13.5 us
    ppermute x9, starting transfers between devices, along_x(): return lax.ppermute(piece, 'ctx', pairs)  13.1 us
    ppermute x4, starting transfers between devices, along_z(): return lax.ppermute(piece, 'ctx', pairs)  12.9 us
    pallas_call x1, Pallas kernels, convolve(): pl.pallas_call(conv_kernel, name='convolution', grid=(channels // (2 * PA...  7.9 us
    pallas_call x1, Pallas kernels, transform_taps(): pl.pallas_call(taps_kernel, name='taps_spectrum', grid=(channels // (2 *...  4.98 us
  transfers between devices with their start and end apart: 16, of which 6 were waited for; matrix products, arithmetic and copies ran while one was open for 3% of the time, Pallas kernels for 21%

profile of v7, /device:TPU:16, one launch (start us, length us, event | category | flops | bytes accessed | tf_op | source)
XLA Modules:
  0.0 147.4 jit_solution(2903061691988770604)
XLA Ops:
  0.7 2.4 %pieces.2 = (bf16[2,768,128]{2,1,0:T(8,128)(2,1)}, bf16[2,768,128]{2,1,0:T(8,128)(2,1)}, bf16[2,768,128]{2,1,0:T(8,128)(2,1)}, bf16[2,768,128]{2,1,0:T(8,128)(2,1)}) custom-call(s32[1]{0:T(128)} %bitcast.x_ref, bf16[768,512]{1,0:T(8,128)(2,1)} %first_ref.1, bf16[768,512]{1,0:T(8,128)(2,1)} %second_ref.1), custom_call_target="tpu_custom_call" | custom-call | tf_op jit(solution)/shard_map/pieces/pallas_call | solution.py:53
  3.1 1.6 %collective-permute-start = (bf16[2,768,128]{2,1,0:T(8,128)(2,1)}, bf16[2,768,128]{2,1,0:T(8,128)(2,1)S(1)}, u32[]{:S(2)}, u32[]{:S(2)}) collective-permute-start(bf16[2,768,128]{2,1,0:T(8,128)(2,1)} %get-tuple-element.36), channel_id=1, source_target_pairs={{0,8},{8,16},{16,24},{24,0},{32,40},{40,48},{48,56},{56,32},{64,72... | collective-permute-start | bytes 1179656 | tf_op jit(solution)/shard_map/ppermute | solution.py:444
  4.7 2.7 %collective-permute-start.1 = (bf16[2,768,128]{2,1,0:T(8,128)(2,1)}, bf16[2,768,128]{2,1,0:T(8,128)(2,1)S(1)}, u32[]{:S(2)}, u32[]{:S(2)}) collective-permute-start(bf16[2,768,128]{2,1,0:T(8,128)(2,1)} %get-tuple-element.37), channel_id=1, source_target_pairs={{0,16},{8,24},{16,0},{24,8},{32,48},{40,56},{48,32},{56,40},{64,80... | collective-permute-start | bytes 1179656 | tf_op jit(solution)/shard_map/ppermute | solution.py:444
  7.4 1.4 collective-permute-start.2
  8.8 0.7 collective-permute-start.3
  9.5 6.1 %collective-permute-done.rest_1_ = bf16[2,768,128]{2,1,0:T(8,128)(2,1)S(1)} collective-permute-done((bf16[2,768,128]{2,1,0:T(8,128)(2,1)}, bf16[2,768,128]{2,1,0:T(8,128)(2,1)S(1)}, u32[]{:S(2)}, u32[]{:S(2)}) %collective-permute-start) | collective-permute-done | bytes 393248 | tf_op jit(solution)/shard_map/ppermute | solution.py:444
  15.6 3.8 %collective-permute-start.4 = (bf16[2,768,128]{2,1,0:T(8,128)(2,1)S(1)}, bf16[2,768,128]{2,1,0:T(8,128)(2,1)S(1)}, u32[]{:S(2)}, u32[]{:S(2)}) collective-permute-start(bf16[2,768,128]{2,1,0:T(8,128)(2,1)S(1)} %collective-permute-done.rest_1_), channel_id=1, source_target_pairs={{0,32},{16,48},{24,56},{32,64},{48,80},{56,88},{64,96},{80,112},{8... | collective-permute-start | bytes 1179656 | tf_op jit(solution)/shard_map/ppermute | solution.py:448
  19.5 2.3 %pieces.3 = (bf16[2,768,128]{2,1,0:T(8,128)(2,1)}, bf16[2,768,128]{2,1,0:T(8,128)(2,1)}, bf16[2,768,128]{2,1,0:T(8,128)(2,1)}, bf16[2,768,128]{2,1,0:T(8,128)(2,1)}) custom-call(s32[1]{0:T(128)} %bitcast.x_ref, bf16[768,512]{1,0:T(8,128)(2,1)} %first_ref.2, bf16[768,512]{1,0:T(8,128)(2,1)} %second_ref.2), custom_call_target="tpu_custom_call" | custom-call | tf_op jit(solution)/shard_map/pieces/pallas_call | solution.py:53
  21.8 0.1 select_reduce_fusion.1
  21.9 0.2 select_reduce_fusion
  22.1 2.7 %collective-permute-done.1.rest_2_ = bf16[2,768,128]{2,1,0:T(8,128)(2,1)S(1)} collective-permute-done((bf16[2,768,128]{2,1,0:T(8,128)(2,1)}, bf16[2,768,128]{2,1,0:T(8,128)(2,1)S(1)}, u32[]{:S(2)}, u32[]{:S(2)}) %collective-permute-start.1) | collective-permute-done | bytes 393248 | tf_op jit(solution)/shard_map/ppermute | solution.py:444
  24.9 4.6 %collective-permute-start.5 = (bf16[2,768,128]{2,1,0:T(8,128)(2,1)S(1)}, bf16[2,768,128]{2,1,0:T(8,128)(2,1)}, u32[]{:S(2)}, u32[]{:S(2)}) collective-permute-start(bf16[2,768,128]{2,1,0:T(8,128)(2,1)S(1)} %collective-permute-done.1.rest_2_), channel_id=1, source_target_pairs={{0,32},{8,40},{24,56},{32,64},{40,72},{56,88},{64,96},{72,104},{88... | collective-permute-start | bytes 1179656 | tf_op jit(solution)/shard_map/ppermute | solution.py:448
  29.4 0.0 collective-permute-done.2.rest_3_
  29.4 3.8 %collective-permute-start.6 = (bf16[2,768,128]{2,1,0:T(8,128)(2,1)}, bf16[2,768,128]{2,1,0:T(8,128)(2,1)}, u32[]{:S(2)}, u32[]{:S(2)}) collective-permute-start(bf16[2,768,128]{2,1,0:T(8,128)(2,1)} %collective-permute-done.2.rest_3_), channel_id=1, source_target_pairs={{0,32},{8,40},{16,48},{32,64},{40,72},{48,80},{64,96},{72,104},{80... | collective-permute-start | bytes 1179656 | tf_op jit(solution)/shard_map/ppermute | solution.py:448
  33.3 0.0 collective-permute-done.3.rest_4_
  33.3 0.0 collective-permute-done.4.rest_5_
  33.3 0.1 collective-permute-start.7
  33.4 0.1 collective-permute-start.8
  33.5 3.1 %collective-permute-start.9 = (bf16[2,768,128]{2,1,0:T(8,128)(2,1)}, bf16[2,768,128]{2,1,0:T(8,128)(2,1)}, u32[]{:S(2)}, u32[]{:S(2)}) collective-permute-start(bf16[2,768,128]{2,1,0:T(8,128)(2,1)} %get-tuple-element.55), channel_id=1, source_target_pairs={{0,24},{8,0},{16,8},{24,16},{32,56},{40,32},{48,40},{56,48},{64,88... | collective-permute-start | bytes 1179656 | tf_op jit(solution)/shard_map/ppermute | solution.py:444
  36.6 0.1 slice.19
  36.7 0.1 slice.18
  36.8 0.1 convert_element_type.3
  36.9 1.0 copy.16
  37.9 8.7 %all-to-all-start = ((bf16[32,16,768]{2,1,0:T(8,128)(2,1)}), bf16[32,16,768]{2,1,0:T(8,128)(2,1)S(1)}, u32[]{:S(2)}, u32[]{:S(2)}) async-start(bf16[32,16,768]{2,1,0:T(8,128)(2,1)} %bitcast.4), calls=%async_computation | async-start | bytes 1572864 | tf_op jit(solution)/shard_map/all_to_all | solution.py:440
  46.5 0.6 and_select_fusion.1
  47.2 0.0 collective-permute-done.5.rest_6_
  47.2 0.0 collective-permute-done.6.rest_7_
  47.2 8.8 %collective-permute-done.7.rest_9_ = bf16[2,768,128]{2,1,0:T(8,128)(2,1)} collective-permute-done((bf16[2,768,128]{2,1,0:T(8,128)(2,1)}, bf16[2,768,128]{2,1,0:T(8,128)(2,1)}, u32[]{:S(2)}, u32[]{:S(2)}) %collective-permute-start.7) | collective-permute-done | bytes 393248 | tf_op jit(solution)/shard_map/ppermute | solution.py:444
  56.0 0.0 collective-permute-done.8.rest_10_
  56.0 3.3 %collective-permute-done.9.rest_11_ = bf16[2,768,128]{2,1,0:T(8,128)(2,1)} collective-permute-done((bf16[2,768,128]{2,1,0:T(8,128)(2,1)}, bf16[2,768,128]{2,1,0:T(8,128)(2,1)}, u32[]{:S(2)}, u32[]{:S(2)}) %collective-permute-start.9) | collective-permute-done | bytes 393248 | tf_op jit(solution)/shard_map/ppermute | solution.py:444
  59.3 13.5 %attention.1 = (bf16[4,768,128]{2,1,0:T(8,128)(2,1)}, bf16[128,3072]{1,0:T(8,128)(2,1)}) custom-call(s32[4]{0:T(128)} %get-tuple-element.72.lo_ref, s32[4]{0:T(128)} %get-tuple-element.73.mid_ref, s32[1]{0:T(128)} %bitcast.x_ref, s32[4,1,768]{2,1,0:T(1,128)} %bitcast.19, bf16[2,768,128]{2,1,0:T(8,128)(2,1)} %get-tuple-element.45.rest_0_, ...), custom_call_target="tpu_custom_call" | custom-call | flops 16000000000 | bytes 3932160 | tf_op jit(solution)/shard_map/attention/pallas_call | solution.py:166
  72.8 0.0 all-to-all-done.taps_ref
  72.9 13.0 %all-to-all-start.1 = ((bf16[8,16,3072]{2,1,0:T(8,128)(2,1)}), bf16[8,16,3072]{2,1,0:T(8,128)(2,1)}, u32[]{:S(2)}, u32[]{:S(2)}) async-start(bf16[8,16,3072]{2,1,0:T(8,128)(2,1)} %bitcast.18), calls=%async_computation.1 | async-start | bytes 1572864 | tf_op jit(solution)/shard_map/all_to_all | solution.py:440
  85.9 5.0 %taps_spectrum.1.taps_ref = f32[3072,256]{1,0:T(8,128)} custom-call(bf16[32,16,768]{2,1,0:T(8,128)(2,1)} %copy-done.2, bf16[2,384,192]{2,1,0:T(8,128)(2,1)} %constant.53.clone.outer_ref, f32[2,192,128]{2,1,0:T(8,128)} %constant.54.clone.twist_ref, bf16[2,256,256]{2,1,0:T(8,128)(2,1)} %constant.55.clone.inner_ref), custom_call_target="tpu_custom_call" | custom-call | flops 5000000000 | bytes 4194304 | tf_op jit(solution)/shard_map/taps_spectrum/pallas_call | solution.py:338
  90.8 1.9 %slice_bitcast_fusion = (bf16[768,128]{1,0:T(8,128)(2,1)S(1)}, bf16[768,128]{1,0:T(8,128)(2,1)S(1)}, bf16[768,128]{1,0:T(8,128)(2,1)S(1)}, bf16[768,128]{1,0:T(8,128)(2,1)}) fusion(bf16[4,768,128]{2,1,0:T(8,128)(2,1)} %get-tuple-element.62), kind=kLoop, calls=%fused_computation.1 | loop fusion | bytes 1572864 | tf_op jit(solution)/shard_map/squeeze | solution.py:478
  92.8 3.2 %collective-permute-start.12 = (bf16[768,128]{1,0:T(8,128)(2,1)S(1)}, bf16[768,128]{1,0:T(8,128)(2,1)S(1)}, u32[]{:S(2)}, u32[]{:S(2)}) collective-permute-start(bf16[768,128]{1,0:T(8,128)(2,1)S(1)} %get-tuple-element.68), channel_id=1, source_target_pairs={{0,24},{8,0},{16,8},{24,16},{32,56},{40,32},{48,40},{56,48},{64,88... | collective-permute-start | bytes 589832 | tf_op jit(solution)/shard_map/ppermute | solution.py:444
  96.0 0.0 collective-permute-start.11
  96.0 0.9 collective-permute-start.10
  96.8 11.7 %all-to-all-done.1.signal_ref = bf16[8,16,3072]{2,1,0:T(8,128)(2,1)} async-done(((bf16[8,16,3072]{2,1,0:T(8,128)(2,1)}), bf16[8,16,3072]{2,1,0:T(8,128)(2,1)}, u32[]{:S(2)}, u32[]{:S(2)}) %all-to-all-start.1) | async-done | bytes 786464 | tf_op jit(solution)/shard_map/all_to_all | solution.py:440
  108.5 7.9 %convolution.1 = bf16[32,16,768]{2,1,0:T(8,128)(2,1)} custom-call(bf16[8,16,3072]{2,1,0:T(8,128)(2,1)} %all-to-all-done.1.signal_ref, f32[3072,256]{1,0:T(8,128)} %taps_spectrum.1.taps_ref, bf16[2,384,192]{2,1,0:T(8,128)(2,1)} %constant.56.clone.outer_ref, f32[2,192,128]{2,1,0:T(8,128)} %constant.54.clone.twist_ref, ...), custom_call_target="tpu_custom_call" | custom-call | flops 7000000000 | bytes 5242880 | tf_op jit(solution)/shard_map/convolution/pallas_call | solution.py:356
  116.4 0.0 collective-permute-done.12.rest_3_
  116.4 0.0 collective-permute-done.11.rest_2_
  116.5 0.0 collective-permute-done.10.rest_1_
  116.5 5.8 %all-to-all-start.2 = ((bf16[32,16,768]{2,1,0:T(8,128)(2,1)}), bf16[32,16,768]{2,1,0:T(8,128)(2,1)S(1)}, u32[]{:S(2)}, u32[]{:S(2)}) async-start(bf16[32,16,768]{2,1,0:T(8,128)(2,1)} %convolution.1), calls=%async_computation.2 | async-start | bytes 1572864 | tf_op jit(solution)/shard_map/all_to_all | solution.py:440
  122.3 0.0 copy-start
  122.3 2.0 %assemble.1 = bf16[768,512]{1,0:T(8,128)(2,1)} custom-call(s32[1]{0:T(128)} %bitcast.x_ref, bf16[768,128]{1,0:T(8,128)(2,1)} %get-tuple-element.63.rest_0_, bf16[768,128]{1,0:T(8,128)(2,1)} %collective-permute-done.10.rest_1_, bf16[768,128]{1,0:T(8,128)(2,1)} %copy-done.9, bf16[768,128]{1,0:T(8,128)(2,1)} %copy-done.8), custom_call_target="tpu_custom_call" | custom-call | flops 2000000000 | bytes 1048576 | tf_op jit(solution)/shard_map/assemble/pallas_call | solution.py:392
  124.4 21.2 %all-to-all-done.2 = bf16[32,16,768]{2,1,0:T(8,128)(2,1)S(1)} async-done(((bf16[32,16,768]{2,1,0:T(8,128)(2,1)}), bf16[32,16,768]{2,1,0:T(8,128)(2,1)S(1)}, u32[]{:S(2)}, u32[]{:S(2)}) %all-to-all-start.2) | async-done | bytes 786464 | tf_op jit(solution)/shard_map/all_to_all | solution.py:440
  145.6 1.9 %finish.1 = bf16[768,512]{1,0:T(8,128)(2,1)} custom-call(bf16[8,4,16,768]{3,2,1,0:T(8,128)(2,1)S(1)} %bitcast.16, bf16[768,512]{1,0:T(8,128)(2,1)S(1)} %copy-done), custom_call_target="tpu_custom_call" | custom-call | tf_op jit(solution)/shard_map/finish/pallas_call | solution.py:417
  (23 shorter events, 0.1 us)
Async XLA Ops:
  0.6 21.2 %copy-start.10 = (s32[64]{0:T(128)S(1)}, s32[64]{0:T(128)}, u32[]{:S(2)}) copy-start(s32[64]{0:T(128)} %param.16) | copy-start | bytes 772
  0.6 36.2 %copy-start.1 = (f32[512,768]{1,0:T(8,128)S(1)}, f32[512,768]{1,0:T(8,128)}, u32[]{:S(2)}) copy-start(f32[512,768]{1,0:T(8,128)} %param.19) | copy-start | bytes 4718596
  3.1 12.5 %collective-permute-start = (bf16[2,768,128]{2,1,0:T(8,128)(2,1)}, bf16[2,768,128]{2,1,0:T(8,128)(2,1)S(1)}, u32[]{:S(2)}, u32[]{:S(2)}) collective-permute-start(bf16[2,768,128]{2,1,0:T(8,128)(2,1)} %get-tuple-element.36), channel_id=1, source_target_pairs={{0,8},{8,16},{16,24},{24,0},{32,40},{40,48},{48,56},{56,32},{64,72... | collective-permute-start | bytes 1179656 | tf_op jit(solution)/shard_map/ppermute | solution.py:444
  4.7 20.2 %collective-permute-start.1 = (bf16[2,768,128]{2,1,0:T(8,128)(2,1)}, bf16[2,768,128]{2,1,0:T(8,128)(2,1)S(1)}, u32[]{:S(2)}, u32[]{:S(2)}) collective-permute-start(bf16[2,768,128]{2,1,0:T(8,128)(2,1)} %get-tuple-element.37), channel_id=1, source_target_pairs={{0,16},{8,24},{16,0},{24,8},{32,48},{40,56},{48,32},{56,40},{64,80... | collective-permute-start | bytes 1179656 | tf_op jit(solution)/shard_map/ppermute | solution.py:444
  7.4 22.1 %collective-permute-start.2 = (bf16[2,768,128]{2,1,0:T(8,128)(2,1)}, bf16[2,768,128]{2,1,0:T(8,128)(2,1)}, u32[]{:S(2)}, u32[]{:S(2)}) collective-permute-start(bf16[2,768,128]{2,1,0:T(8,128)(2,1)} %get-tuple-element.38), channel_id=1, source_target_pairs={{0,24},{8,0},{16,8},{24,16},{32,56},{40,32},{48,40},{56,48},{64,88... | collective-permute-start | bytes 1179656 | tf_op jit(solution)/shard_map/ppermute | solution.py:444
  8.8 24.5 %collective-permute-start.3 = (bf16[2,768,128]{2,1,0:T(8,128)(2,1)}, bf16[2,768,128]{2,1,0:T(8,128)(2,1)S(1)}, u32[]{:S(2)}, u32[]{:S(2)}) collective-permute-start(bf16[2,768,128]{2,1,0:T(8,128)(2,1)} %get-tuple-element.45.rest_0_), channel_id=1, source_target_pairs={{8,40},{16,48},{24,56},{40,72},{48,80},{56,88},{72,104},{80,112},{... | collective-permute-start | bytes 1179656 | tf_op jit(solution)/shard_map/ppermute | solution.py:448
  15.6 21.0 %copy-start.4 = (bf16[2,768,128]{2,1,0:T(8,128)(2,1)}, bf16[2,768,128]{2,1,0:T(8,128)(2,1)S(1)}, u32[]{:S(2)}) copy-start(bf16[2,768,128]{2,1,0:T(8,128)(2,1)S(1)} %collective-permute-done.rest_1_) | copy-start | bytes 1179652
  15.6 17.7 %collective-permute-start.4 = (bf16[2,768,128]{2,1,0:T(8,128)(2,1)S(1)}, bf16[2,768,128]{2,1,0:T(8,128)(2,1)S(1)}, u32[]{:S(2)}, u32[]{:S(2)}) collective-permute-start(bf16[2,768,128]{2,1,0:T(8,128)(2,1)S(1)} %collective-permute-done.rest_1_), channel_id=1, source_target_pairs={{0,32},{16,48},{24,56},{32,64},{48,80},{56,88},{64,96},{80,112},{8... | collective-permute-start | bytes 1179656 | tf_op jit(solution)/shard_map/ppermute | solution.py:448
  24.8 22.3 %copy-start.5 = (bf16[2,768,128]{2,1,0:T(8,128)(2,1)}, bf16[2,768,128]{2,1,0:T(8,128)(2,1)S(1)}, u32[]{:S(2)}) copy-start(bf16[2,768,128]{2,1,0:T(8,128)(2,1)S(1)} %collective-permute-done.1.rest_2_) | copy-start | bytes 1179652
  24.9 22.3 %collective-permute-start.5 = (bf16[2,768,128]{2,1,0:T(8,128)(2,1)S(1)}, bf16[2,768,128]{2,1,0:T(8,128)(2,1)}, u32[]{:S(2)}, u32[]{:S(2)}) collective-permute-start(bf16[2,768,128]{2,1,0:T(8,128)(2,1)S(1)} %collective-permute-done.1.rest_2_), channel_id=1, source_target_pairs={{0,32},{8,40},{24,56},{32,64},{40,72},{56,88},{64,96},{72,104},{88... | collective-permute-start | bytes 1179656 | tf_op jit(solution)/shard_map/ppermute | solution.py:448
  29.4 17.7 %collective-permute-start.6 = (bf16[2,768,128]{2,1,0:T(8,128)(2,1)}, bf16[2,768,128]{2,1,0:T(8,128)(2,1)}, u32[]{:S(2)}, u32[]{:S(2)}) collective-permute-start(bf16[2,768,128]{2,1,0:T(8,128)(2,1)} %collective-permute-done.2.rest_3_), channel_id=1, source_target_pairs={{0,32},{8,40},{16,48},{32,64},{40,72},{48,80},{64,96},{72,104},{80... | collective-permute-start | bytes 1179656 | tf_op jit(solution)/shard_map/ppermute | solution.py:448
  33.3 4.6 %copy-start.6 = (bf16[2,768,128]{2,1,0:T(8,128)(2,1)}, bf16[2,768,128]{2,1,0:T(8,128)(2,1)S(1)}, u32[]{:S(2)}) copy-start(bf16[2,768,128]{2,1,0:T(8,128)(2,1)S(1)} %collective-permute-done.3.rest_4_) | copy-start | bytes 1179652
  33.3 4.6 %copy-start.7 = (bf16[2,768,128]{2,1,0:T(8,128)(2,1)}, bf16[2,768,128]{2,1,0:T(8,128)(2,1)S(1)}, u32[]{:S(2)}) copy-start(bf16[2,768,128]{2,1,0:T(8,128)(2,1)S(1)} %collective-permute-done.4.rest_5_) | copy-start | bytes 1179652
  33.3 22.7 %collective-permute-start.7 = (bf16[2,768,128]{2,1,0:T(8,128)(2,1)}, bf16[2,768,128]{2,1,0:T(8,128)(2,1)}, u32[]{:S(2)}, u32[]{:S(2)}) collective-permute-start(bf16[2,768,128]{2,1,0:T(8,128)(2,1)} %get-tuple-element.53), channel_id=1, source_target_pairs={{0,8},{8,16},{16,24},{24,0},{32,40},{40,48},{48,56},{56,32},{64,72... | collective-permute-start | bytes 1179656 | tf_op jit(solution)/shard_map/ppermute | solution.py:444
  33.4 22.6 %collective-permute-start.8 = (bf16[2,768,128]{2,1,0:T(8,128)(2,1)}, bf16[2,768,128]{2,1,0:T(8,128)(2,1)}, u32[]{:S(2)}, u32[]{:S(2)}) collective-permute-start(bf16[2,768,128]{2,1,0:T(8,128)(2,1)} %get-tuple-element.54), channel_id=1, source_target_pairs={{0,16},{8,24},{16,0},{24,8},{32,48},{40,56},{48,32},{56,40},{64,80... | collective-permute-start | bytes 1179656 | tf_op jit(solution)/shard_map/ppermute | solution.py:444
  33.5 25.8 %collective-permute-start.9 = (bf16[2,768,128]{2,1,0:T(8,128)(2,1)}, bf16[2,768,128]{2,1,0:T(8,128)(2,1)}, u32[]{:S(2)}, u32[]{:S(2)}) collective-permute-start(bf16[2,768,128]{2,1,0:T(8,128)(2,1)} %get-tuple-element.55), channel_id=1, source_target_pairs={{0,24},{8,0},{16,8},{24,16},{32,56},{40,32},{48,40},{56,48},{64,88... | collective-permute-start | bytes 1179656 | tf_op jit(solution)/shard_map/ppermute | solution.py:444
  36.6 22.7 %copy-start.3 = (s32[3072]{0:T(1024)}, s32[3072]{0:T(1024)S(1)}, u32[]{:S(2)}) copy-start(s32[3072]{0:T(1024)S(1)} %broadcast_subtract_fusion) | copy-start | bytes 36868
  37.9 35.0 %all-to-all-start = ((bf16[32,16,768]{2,1,0:T(8,128)(2,1)}), bf16[32,16,768]{2,1,0:T(8,128)(2,1)S(1)}, u32[]{:S(2)}, u32[]{:S(2)}) async-start(bf16[32,16,768]{2,1,0:T(8,128)(2,1)} %bitcast.4), calls=%async_computation | async-start | bytes 1572864 | tf_op jit(solution)/shard_map/all_to_all | solution.py:440
  72.9 13.0 %copy-start.2 = (bf16[32,16,768]{2,1,0:T(8,128)(2,1)}, bf16[32,16,768]{2,1,0:T(8,128)(2,1)S(1)}, u32[]{:S(2)}) copy-start(bf16[32,16,768]{2,1,0:T(8,128)(2,1)S(1)} %all-to-all-done.taps_ref) | copy-start | bytes 2359300
  72.9 35.7 %all-to-all-start.1 = ((bf16[8,16,3072]{2,1,0:T(8,128)(2,1)}), bf16[8,16,3072]{2,1,0:T(8,128)(2,1)}, u32[]{:S(2)}, u32[]{:S(2)}) async-start(bf16[8,16,3072]{2,1,0:T(8,128)(2,1)} %bitcast.18), calls=%async_computation.1 | async-start | bytes 1572864 | tf_op jit(solution)/shard_map/all_to_all | solution.py:440
  92.8 23.6 %collective-permute-start.12 = (bf16[768,128]{1,0:T(8,128)(2,1)S(1)}, bf16[768,128]{1,0:T(8,128)(2,1)S(1)}, u32[]{:S(2)}, u32[]{:S(2)}) collective-permute-start(bf16[768,128]{1,0:T(8,128)(2,1)S(1)} %get-tuple-element.68), channel_id=1, source_target_pairs={{0,24},{8,0},{16,8},{24,16},{32,56},{40,32},{48,40},{56,48},{64,88... | collective-permute-start | bytes 589832 | tf_op jit(solution)/shard_map/ppermute | solution.py:444
  96.0 20.5 %collective-permute-start.11 = (bf16[768,128]{1,0:T(8,128)(2,1)S(1)}, bf16[768,128]{1,0:T(8,128)(2,1)S(1)}, u32[]{:S(2)}, u32[]{:S(2)}) collective-permute-start(bf16[768,128]{1,0:T(8,128)(2,1)S(1)} %get-tuple-element.69), channel_id=1, source_target_pairs={{0,16},{8,24},{16,0},{24,8},{32,48},{40,56},{48,32},{56,40},{64,80... | collective-permute-start | bytes 589832 | tf_op jit(solution)/shard_map/ppermute | solution.py:444
  96.0 20.5 %collective-permute-start.10 = (bf16[768,128]{1,0:T(8,128)(2,1)S(1)}, bf16[768,128]{1,0:T(8,128)(2,1)}, u32[]{:S(2)}, u32[]{:S(2)}) collective-permute-start(bf16[768,128]{1,0:T(8,128)(2,1)S(1)} %get-tuple-element.70), channel_id=1, source_target_pairs={{0,8},{8,16},{16,24},{24,0},{32,40},{40,48},{48,56},{56,32},{64,72... | collective-permute-start | bytes 589832 | tf_op jit(solution)/shard_map/ppermute | solution.py:444
  116.4 5.9 %copy-start.8 = (bf16[768,128]{1,0:T(8,128)(2,1)}, bf16[768,128]{1,0:T(8,128)(2,1)S(1)}, u32[]{:S(2)}) copy-start(bf16[768,128]{1,0:T(8,128)(2,1)S(1)} %collective-permute-done.12.rest_3_) | copy-start | bytes 589828
  116.4 5.9 %copy-start.9 = (bf16[768,128]{1,0:T(8,128)(2,1)}, bf16[768,128]{1,0:T(8,128)(2,1)S(1)}, u32[]{:S(2)}) copy-start(bf16[768,128]{1,0:T(8,128)(2,1)S(1)} %collective-permute-done.11.rest_2_) | copy-start | bytes 589828
  116.5 29.1 %all-to-all-start.2 = ((bf16[32,16,768]{2,1,0:T(8,128)(2,1)}), bf16[32,16,768]{2,1,0:T(8,128)(2,1)S(1)}, u32[]{:S(2)}, u32[]{:S(2)}) async-start(bf16[32,16,768]{2,1,0:T(8,128)(2,1)} %convolution.1), calls=%async_computation.2 | async-start | bytes 1572864 | tf_op jit(solution)/shard_map/all_to_all | solution.py:440
  122.3 23.2 %copy-start = (bf16[768,512]{1,0:T(8,128)(2,1)S(1)}, bf16[768,512]{1,0:T(8,128)(2,1)}, u32[]{:S(2)}) copy-start(bf16[768,512]{1,0:T(8,128)(2,1)} %gate_ref.1) | copy-start | bytes 2359300

commit v8 on v6

--- a/solution.py
+++ b/solution.py
@@ -12,7 +12,6 @@
 
 HEAD_DIM = 128
 X_SIZE = 4
-NEAR_FIRST = (0, 1, 3, 2)
 Q_BLOCK = 768
 K_BLOCK = 384
 LANES = 128
@@ -448,20 +447,15 @@
         return lax.ppermute(piece, "ctx", pairs)
 
     def arrived(pieces):
-        moved = {k: along_x(pieces[k], k) for k in NEAR_FIRST[1:]}
-        return [pieces[0]] + [moved[k] for k in range(1, X_SIZE)]
+        return [pieces[0]] + [along_x(pieces[k], k) for k in range(1, X_SIZE)]
 
     taps = filter_taps.astype(jnp.bfloat16).reshape(X_SIZE, z_size, per_device, row_count)
     taps = taps.transpose(1, 0, 2, 3).reshape(ctx, per_device, row_count)
-    pieces = pieces_of(x_index, key_rows, values)
-    own = arrived(pieces)
-    moved = {k: along_z(own[k], k) for k in NEAR_FIRST}
-    before = [moved[k] for k in range(X_SIZE)]
-    _, queries, in_gate = lax.optimization_barrier((pieces[0], queries, in_gate))
+    own = arrived(pieces_of(x_index, key_rows, values))
+    before = [along_z(own[k], k) for k in range(X_SIZE)]
+    own[1], queries, in_gate = lax.optimization_barrier((own[1], queries, in_gate))
     asked = pieces_of(x_index, queries, in_gate)
-    both = lax.optimization_barrier((*own, *asked))
-    own, asked = list(both[:X_SIZE]), list(both[X_SIZE:])
-    taps, asked[0] = lax.optimization_barrier((taps, asked[0]))
+    taps, *_ = lax.optimization_barrier((taps, *own, *asked))
     asked = arrived(asked)
     taps = exchanged(taps)
 

time: 137 us -> 133 us (0.971)
  starting transfers between devices: 52.1 us -> 47.6 us
  Pallas kernels: 37.9 us -> 35.8 us
  waiting for transfers between devices: 40.5 us -> 42.3 us
    all_to_all x3, starting transfers between devices: 26.1 us -> 20.8 us  [exchanged(): lax.all_to_all(x, 'ctx', split_axis=0, concat_axis=0, tiled=True, axis_in...]
    all_to_all x3, waiting for transfers between devices: 21.2 us -> 24.1 us  [exchanged(): lax.all_to_all(x, 'ctx', split_axis=0, concat_axis=0, tiled=True, axis_in...]
    pallas_call x1, Pallas kernels: 16.4 us -> 14.3 us  [attention(): pl.pallas_call(attention_kernel, name='attention', grid_spec=pltpu.Prefet...]
  transfers between devices with their start and end apart: 16 -> 16, of which waited for: 5 -> 6; matrix products, arithmetic and copies ran while one was open for 3% -> 4% of each run, Pallas kernels for 25% -> 24%
where the time goes in v8:
time: 133 us; the launch traced here: 131 us
  starting transfers between devices  47.6 us (36%)
  waiting for transfers between devices  42.3 us (32%)
  Pallas kernels  35.8 us (27%)
  local copies, waits for them, and re-layouts  3.14 us (2%)
  other arithmetic  1.64 us (1%)
    all_to_all x3, waiting for transfers between devices, exchanged(): lax.all_to_all(x, 'ctx', split_axis=0, concat_axis=0, tiled=True, axis_in...  24.1 us
    all_to_all x3, starting transfers between devices, exchanged(): lax.all_to_all(x, 'ctx', split_axis=0, concat_axis=0, tiled=True, axis_in...  20.8 us
    pallas_call x1, Pallas kernels, attention(): pl.pallas_call(attention_kernel, name='attention', grid_spec=pltpu.Prefet...  14.3 us
    ppermute x9, starting transfers between devices, along_x(): return lax.ppermute(piece, 'ctx', pairs)  13.9 us
    ppermute x4, starting transfers between devices, along_z(): return lax.ppermute(piece, 'ctx', pairs)  12.9 us
    ppermute x4, waiting for transfers between devices, along_z(): return lax.ppermute(piece, 'ctx', pairs)  10.1 us
    ppermute x9, waiting for transfers between devices, along_x(): return lax.ppermute(piece, 'ctx', pairs)  8.11 us
    pallas_call x1, Pallas kernels, convolve(): pl.pallas_call(conv_kernel, name='convolution', grid=(channels // (2 * PA...  7.9 us
  transfers between devices with their start and end apart: 16, of which 6 were waited for; matrix products, arithmetic and copies ran while one was open for 4% of the time, Pallas kernels for 24%

profile of v8, /device:TPU:16, one launch (start us, length us, event | category | flops | bytes accessed | tf_op | source)
XLA Modules:
  0.0 131.3 jit_solution(5890873642282530538)
XLA Ops:
  0.6 2.4 %pieces.2 = (bf16[2,768,128]{2,1,0:T(8,128)(2,1)}, bf16[2,768,128]{2,1,0:T(8,128)(2,1)}, bf16[2,768,128]{2,1,0:T(8,128)(2,1)}, bf16[2,768,128]{2,1,0:T(8,128)(2,1)}) custom-call(s32[1]{0:T(128)} %bitcast.x_ref, bf16[768,512]{1,0:T(8,128)(2,1)} %first_ref.1, bf16[768,512]{1,0:T(8,128)(2,1)} %second_ref.1), custom_call_target="tpu_custom_call" | custom-call | tf_op jit(solution)/shard_map/pieces/pallas_call | solution.py:52
  3.1 1.6 %collective-permute-start = (bf16[2,768,128]{2,1,0:T(8,128)(2,1)}, bf16[2,768,128]{2,1,0:T(8,128)(2,1)S(1)}, u32[]{:S(2)}, u32[]{:S(2)}) collective-permute-start(bf16[2,768,128]{2,1,0:T(8,128)(2,1)} %get-tuple-element.26), channel_id=1, source_target_pairs={{0,8},{8,16},{16,24},{24,0},{32,40},{40,48},{48,56},{56,32},{64,72... | collective-permute-start | bytes 1179656 | tf_op jit(solution)/shard_map/ppermute | solution.py:443
  4.6 2.7 %collective-permute-start.1 = (bf16[2,768,128]{2,1,0:T(8,128)(2,1)}, bf16[2,768,128]{2,1,0:T(8,128)(2,1)S(1)}, u32[]{:S(2)}, u32[]{:S(2)}) collective-permute-start(bf16[2,768,128]{2,1,0:T(8,128)(2,1)} %get-tuple-element.28), channel_id=1, source_target_pairs={{0,16},{8,24},{16,0},{24,8},{32,48},{40,56},{48,32},{56,40},{64,80... | collective-permute-start | bytes 1179656 | tf_op jit(solution)/shard_map/ppermute | solution.py:443
  7.4 1.4 %collective-permute-start.2 = (bf16[2,768,128]{2,1,0:T(8,128)(2,1)}, bf16[2,768,128]{2,1,0:T(8,128)(2,1)}, u32[]{:S(2)}, u32[]{:S(2)}) collective-permute-start(bf16[2,768,128]{2,1,0:T(8,128)(2,1)} %get-tuple-element.29), channel_id=1, source_target_pairs={{0,24},{8,0},{16,8},{24,16},{32,56},{40,32},{48,40},{56,48},{64,88... | collective-permute-start | bytes 1179656 | tf_op jit(solution)/shard_map/ppermute | solution.py:443
  8.8 0.7 collective-permute-start.3
  9.5 6.1 %collective-permute-done.rest_1_ = bf16[2,768,128]{2,1,0:T(8,128)(2,1)S(1)} collective-permute-done((bf16[2,768,128]{2,1,0:T(8,128)(2,1)}, bf16[2,768,128]{2,1,0:T(8,128)(2,1)S(1)}, u32[]{:S(2)}, u32[]{:S(2)}) %collective-permute-start) | collective-permute-done | bytes 393248 | tf_op jit(solution)/shard_map/ppermute | solution.py:443
  15.6 3.8 %collective-permute-start.4 = (bf16[2,768,128]{2,1,0:T(8,128)(2,1)S(1)}, bf16[2,768,128]{2,1,0:T(8,128)(2,1)S(1)}, u32[]{:S(2)}, u32[]{:S(2)}) collective-permute-start(bf16[2,768,128]{2,1,0:T(8,128)(2,1)S(1)} %collective-permute-done.rest_1_), channel_id=1, source_target_pairs={{0,32},{16,48},{24,56},{32,64},{48,80},{56,88},{64,96},{80,112},{8... | collective-permute-start | bytes 1179656 | tf_op jit(solution)/shard_map/ppermute | solution.py:447
  19.5 0.7 select_reduce_fusion.1
  20.2 0.2 select_reduce_fusion
  20.4 2.3 %pieces.3 = (bf16[2,768,128]{2,1,0:T(8,128)(2,1)}, bf16[2,768,128]{2,1,0:T(8,128)(2,1)}, bf16[2,768,128]{2,1,0:T(8,128)(2,1)}, bf16[2,768,128]{2,1,0:T(8,128)(2,1)}) custom-call(s32[1]{0:T(128)} %bitcast.x_ref, bf16[768,512]{1,0:T(8,128)(2,1)} %first_ref.2, bf16[768,512]{1,0:T(8,128)(2,1)} %second_ref.2), custom_call_target="tpu_custom_call" | custom-call | tf_op jit(solution)/shard_map/pieces/pallas_call | solution.py:52
  22.8 0.1 collective-permute-start.7
  22.9 2.0 %collective-permute-done.1.rest_2_ = bf16[2,768,128]{2,1,0:T(8,128)(2,1)S(1)} collective-permute-done((bf16[2,768,128]{2,1,0:T(8,128)(2,1)}, bf16[2,768,128]{2,1,0:T(8,128)(2,1)S(1)}, u32[]{:S(2)}, u32[]{:S(2)}) %collective-permute-start.1) | collective-permute-done | bytes 393248 | tf_op jit(solution)/shard_map/ppermute | solution.py:443
  24.8 2.0 %collective-permute-start.8 = (bf16[2,768,128]{2,1,0:T(8,128)(2,1)}, bf16[2,768,128]{2,1,0:T(8,128)(2,1)}, u32[]{:S(2)}, u32[]{:S(2)}) collective-permute-start(bf16[2,768,128]{2,1,0:T(8,128)(2,1)} %get-tuple-element.34), channel_id=1, source_target_pairs={{0,16},{8,24},{16,0},{24,8},{32,48},{40,56},{48,32},{56,40},{64,80... | collective-permute-start | bytes 1179656 | tf_op jit(solution)/shard_map/ppermute | solution.py:443
  26.8 0.0 collective-permute-done.2.rest_3_
  26.8 1.4 %collective-permute-start.9 = (bf16[2,768,128]{2,1,0:T(8,128)(2,1)}, bf16[2,768,128]{2,1,0:T(8,128)(2,1)}, u32[]{:S(2)}, u32[]{:S(2)}) collective-permute-start(bf16[2,768,128]{2,1,0:T(8,128)(2,1)} %get-tuple-element.35), channel_id=1, source_target_pairs={{0,24},{8,0},{16,8},{24,16},{32,56},{40,32},{48,40},{56,48},{64,88... | collective-permute-start | bytes 1179656 | tf_op jit(solution)/shard_map/ppermute | solution.py:443
  28.3 0.0 collective-permute-done.3.rest_4_
  28.3 4.6 %collective-permute-start.5 = (bf16[2,768,128]{2,1,0:T(8,128)(2,1)S(1)}, bf16[2,768,128]{2,1,0:T(8,128)(2,1)}, u32[]{:S(2)}, u32[]{:S(2)}) collective-permute-start(bf16[2,768,128]{2,1,0:T(8,128)(2,1)S(1)} %collective-permute-done.1.rest_2_), channel_id=1, source_target_pairs={{0,32},{8,40},{24,56},{32,64},{40,72},{56,88},{64,96},{72,104},{88... | collective-permute-start | bytes 1179656 | tf_op jit(solution)/shard_map/ppermute | solution.py:447
  32.9 0.0 collective-permute-done.4.rest_5_
  32.9 3.8 %collective-permute-start.6 = (bf16[2,768,128]{2,1,0:T(8,128)(2,1)}, bf16[2,768,128]{2,1,0:T(8,128)(2,1)}, u32[]{:S(2)}, u32[]{:S(2)}) collective-permute-start(bf16[2,768,128]{2,1,0:T(8,128)(2,1)} %collective-permute-done.2.rest_3_), channel_id=1, source_target_pairs={{0,32},{8,40},{16,48},{32,64},{40,72},{48,80},{64,96},{72,104},{80... | collective-permute-start | bytes 1179656 | tf_op jit(solution)/shard_map/ppermute | solution.py:447
  36.7 0.1 slice.19
  36.8 0.1 slice.18
  36.9 0.1 convert_element_type.3
  37.0 1.0 copy.16
  38.0 5.9 %all-to-all-start = ((bf16[32,16,768]{2,1,0:T(8,128)(2,1)}), bf16[32,16,768]{2,1,0:T(8,128)(2,1)S(1)}, u32[]{:S(2)}, u32[]{:S(2)}) async-start(bf16[32,16,768]{2,1,0:T(8,128)(2,1)} %bitcast.4), calls=%async_computation | async-start | bytes 1572864 | tf_op jit(solution)/shard_map/all_to_all | solution.py:439
  43.8 0.6 and_select_fusion.1
  44.5 0.0 collective-permute-done.5.rest_6_
  44.5 10.1 %collective-permute-done.6.rest_7_ = bf16[2,768,128]{2,1,0:T(8,128)(2,1)} collective-permute-done((bf16[2,768,128]{2,1,0:T(8,128)(2,1)}, bf16[2,768,128]{2,1,0:T(8,128)(2,1)}, u32[]{:S(2)}, u32[]{:S(2)}) %collective-permute-start.6) | collective-permute-done | bytes 393248 | tf_op jit(solution)/shard_map/ppermute | solution.py:447
  54.5 0.0 collective-permute-done.7.rest_9_
  54.5 0.0 collective-permute-done.8.rest_10_
  54.5 0.0 collective-permute-done.9.rest_11_
  54.5 14.3 %attention.1 = (bf16[4,768,128]{2,1,0:T(8,128)(2,1)}, bf16[128,3072]{1,0:T(8,128)(2,1)}) custom-call(s32[4]{0:T(128)} %get-tuple-element.52.lo_ref, s32[4]{0:T(128)} %get-tuple-element.53.mid_ref, s32[1]{0:T(128)} %bitcast.x_ref, s32[4,1,768]{2,1,0:T(1,128)} %bitcast.19, bf16[2,768,128]{2,1,0:T(8,128)(2,1)} %get-tuple-element.25.rest_0_, ...), custom_call_target="tpu_custom_call" | custom-call | flops 16000000000 | bytes 3932160 | tf_op jit(solution)/shard_map/attention/pallas_call | solution.py:165
  68.8 1.9 %all-to-all-done.taps_ref = bf16[32,16,768]{2,1,0:T(8,128)(2,1)S(1)} async-done(((bf16[32,16,768]{2,1,0:T(8,128)(2,1)}), bf16[32,16,768]{2,1,0:T(8,128)(2,1)S(1)}, u32[]{:S(2)}, u32[]{:S(2)}) %all-to-all-start) | async-done | bytes 786464 | tf_op jit(solution)/shard_map/all_to_all | solution.py:439
  70.8 11.0 %all-to-all-start.1 = ((bf16[8,16,3072]{2,1,0:T(8,128)(2,1)}), bf16[8,16,3072]{2,1,0:T(8,128)(2,1)}, u32[]{:S(2)}, u32[]{:S(2)}) async-start(bf16[8,16,3072]{2,1,0:T(8,128)(2,1)} %bitcast.18), calls=%async_computation.1 | async-start | bytes 1572864 | tf_op jit(solution)/shard_map/all_to_all | solution.py:439
  81.7 5.0 %taps_spectrum.1.taps_ref = f32[3072,256]{1,0:T(8,128)} custom-call(bf16[32,16,768]{2,1,0:T(8,128)(2,1)} %copy-done.2, bf16[2,384,192]{2,1,0:T(8,128)(2,1)} %constant.53.clone.outer_ref, f32[2,192,128]{2,1,0:T(8,128)} %constant.54.clone.twist_ref, bf16[2,256,256]{2,1,0:T(8,128)(2,1)} %constant.55.clone.inner_ref), custom_call_target="tpu_custom_call" | custom-call | flops 5000000000 | bytes 4194304 | tf_op jit(solution)/shard_map/taps_spectrum/pallas_call | solution.py:337
  86.7 1.9 %slice_bitcast_fusion = (bf16[768,128]{1,0:T(8,128)(2,1)S(1)}, bf16[768,128]{1,0:T(8,128)(2,1)S(1)}, bf16[768,128]{1,0:T(8,128)(2,1)S(1)}, bf16[768,128]{1,0:T(8,128)(2,1)}) fusion(bf16[4,768,128]{2,1,0:T(8,128)(2,1)} %get-tuple-element.42), kind=kLoop, calls=%fused_computation.1 | loop fusion | bytes 1572864 | tf_op jit(solution)/shard_map/squeeze | solution.py:471
  88.7 0.0 collective-permute-start.12
  88.7 4.7 %collective-permute-start.11 = (bf16[768,128]{1,0:T(8,128)(2,1)S(1)}, bf16[768,128]{1,0:T(8,128)(2,1)S(1)}, u32[]{:S(2)}, u32[]{:S(2)}) collective-permute-start(bf16[768,128]{1,0:T(8,128)(2,1)S(1)} %get-tuple-element.49), channel_id=1, source_target_pairs={{0,16},{8,24},{16,0},{24,8},{32,48},{40,56},{48,32},{56,40},{64,80... | collective-permute-start | bytes 589832 | tf_op jit(solution)/shard_map/ppermute | solution.py:443
  93.3 0.0 collective-permute-start.10
  93.3 6.4 %all-to-all-done.1.signal_ref = bf16[8,16,3072]{2,1,0:T(8,128)(2,1)} async-done(((bf16[8,16,3072]{2,1,0:T(8,128)(2,1)}), bf16[8,16,3072]{2,1,0:T(8,128)(2,1)}, u32[]{:S(2)}, u32[]{:S(2)}) %all-to-all-start.1) | async-done | bytes 786464 | tf_op jit(solution)/shard_map/all_to_all | solution.py:439
  99.7 7.9 %convolution.1 = bf16[32,16,768]{2,1,0:T(8,128)(2,1)} custom-call(bf16[8,16,3072]{2,1,0:T(8,128)(2,1)} %all-to-all-done.1.signal_ref, f32[3072,256]{1,0:T(8,128)} %taps_spectrum.1.taps_ref, bf16[2,384,192]{2,1,0:T(8,128)(2,1)} %constant.56.clone.outer_ref, f32[2,192,128]{2,1,0:T(8,128)} %constant.54.clone.twist_ref, ...), custom_call_target="tpu_custom_call" | custom-call | flops 7000000000 | bytes 5242880 | tf_op jit(solution)/shard_map/convolution/pallas_call | solution.py:355
  107.7 0.0 collective-permute-done.12.rest_3_
  107.7 0.0 collective-permute-done.11.rest_2_
  107.7 0.0 collective-permute-done.10.rest_1_
  107.7 3.9 %all-to-all-start.2 = ((bf16[32,16,768]{2,1,0:T(8,128)(2,1)}), bf16[32,16,768]{2,1,0:T(8,128)(2,1)S(1)}, u32[]{:S(2)}, u32[]{:S(2)}) async-start(bf16[32,16,768]{2,1,0:T(8,128)(2,1)} %convolution.1), calls=%async_computation.2 | async-start | bytes 1572864 | tf_op jit(solution)/shard_map/all_to_all | solution.py:439
  111.6 0.0 copy-start
  111.7 2.0 %assemble.1 = bf16[768,512]{1,0:T(8,128)(2,1)} custom-call(s32[1]{0:T(128)} %bitcast.x_ref, bf16[768,128]{1,0:T(8,128)(2,1)} %get-tuple-element.43.rest_0_, bf16[768,128]{1,0:T(8,128)(2,1)} %collective-permute-done.10.rest_1_, bf16[768,128]{1,0:T(8,128)(2,1)} %copy-done.9, bf16[768,128]{1,0:T(8,128)(2,1)} %copy-done.8), custom_call_target="tpu_custom_call" | custom-call | flops 2000000000 | bytes 1048576 | tf_op jit(solution)/shard_map/assemble/pallas_call | solution.py:391
  113.7 15.8 %all-to-all-done.2 = bf16[32,16,768]{2,1,0:T(8,128)(2,1)S(1)} async-done(((bf16[32,16,768]{2,1,0:T(8,128)(2,1)}), bf16[32,16,768]{2,1,0:T(8,128)(2,1)S(1)}, u32[]{:S(2)}, u32[]{:S(2)}) %all-to-all-start.2) | async-done | bytes 786464 | tf_op jit(solution)/shard_map/all_to_all | solution.py:439
  129.5 1.9 %finish.1 = bf16[768,512]{1,0:T(8,128)(2,1)} custom-call(bf16[8,4,16,768]{3,2,1,0:T(8,128)(2,1)S(1)} %bitcast.16, bf16[768,512]{1,0:T(8,128)(2,1)S(1)} %copy-done), custom_call_target="tpu_custom_call" | custom-call | tf_op jit(solution)/shard_map/finish/pallas_call | solution.py:416
  (21 shorter events, 0.0 us)
Async XLA Ops:
  0.6 36.3 %copy-start.1 = (f32[512,768]{1,0:T(8,128)S(1)}, f32[512,768]{1,0:T(8,128)}, u32[]{:S(2)}) copy-start(f32[512,768]{1,0:T(8,128)} %param.19) | copy-start | bytes 4718596
  3.1 12.5 %collective-permute-start = (bf16[2,768,128]{2,1,0:T(8,128)(2,1)}, bf16[2,768,128]{2,1,0:T(8,128)(2,1)S(1)}, u32[]{:S(2)}, u32[]{:S(2)}) collective-permute-start(bf16[2,768,128]{2,1,0:T(8,128)(2,1)} %get-tuple-element.26), channel_id=1, source_target_pairs={{0,8},{8,16},{16,24},{24,0},{32,40},{40,48},{48,56},{56,32},{64,72... | collective-permute-start | bytes 1179656 | tf_op jit(solution)/shard_map/ppermute | solution.py:443
  4.6 20.2 %collective-permute-start.1 = (bf16[2,768,128]{2,1,0:T(8,128)(2,1)}, bf16[2,768,128]{2,1,0:T(8,128)(2,1)S(1)}, u32[]{:S(2)}, u32[]{:S(2)}) collective-permute-start(bf16[2,768,128]{2,1,0:T(8,128)(2,1)} %get-tuple-element.28), channel_id=1, source_target_pairs={{0,16},{8,24},{16,0},{24,8},{32,48},{40,56},{48,32},{56,40},{64,80... | collective-permute-start | bytes 1179656 | tf_op jit(solution)/shard_map/ppermute | solution.py:443
  7.4 19.5 %collective-permute-start.2 = (bf16[2,768,128]{2,1,0:T(8,128)(2,1)}, bf16[2,768,128]{2,1,0:T(8,128)(2,1)}, u32[]{:S(2)}, u32[]{:S(2)}) collective-permute-start(bf16[2,768,128]{2,1,0:T(8,128)(2,1)} %get-tuple-element.29), channel_id=1, source_target_pairs={{0,24},{8,0},{16,8},{24,16},{32,56},{40,32},{48,40},{56,48},{64,88... | collective-permute-start | bytes 1179656 | tf_op jit(solution)/shard_map/ppermute | solution.py:443
  8.8 19.5 %collective-permute-start.3 = (bf16[2,768,128]{2,1,0:T(8,128)(2,1)}, bf16[2,768,128]{2,1,0:T(8,128)(2,1)S(1)}, u32[]{:S(2)}, u32[]{:S(2)}) collective-permute-start(bf16[2,768,128]{2,1,0:T(8,128)(2,1)} %get-tuple-element.25.rest_0_), channel_id=1, source_target_pairs={{8,40},{16,48},{24,56},{40,72},{48,80},{56,88},{72,104},{80,112},{... | collective-permute-start | bytes 1179656 | tf_op jit(solution)/shard_map/ppermute | solution.py:447
  15.6 22.4 %copy-start.4 = (bf16[2,768,128]{2,1,0:T(8,128)(2,1)}, bf16[2,768,128]{2,1,0:T(8,128)(2,1)S(1)}, u32[]{:S(2)}) copy-start(bf16[2,768,128]{2,1,0:T(8,128)(2,1)S(1)} %collective-permute-done.rest_1_) | copy-start | bytes 1179652
  15.6 17.3 %collective-permute-start.4 = (bf16[2,768,128]{2,1,0:T(8,128)(2,1)S(1)}, bf16[2,768,128]{2,1,0:T(8,128)(2,1)S(1)}, u32[]{:S(2)}, u32[]{:S(2)}) collective-permute-start(bf16[2,768,128]{2,1,0:T(8,128)(2,1)S(1)} %collective-permute-done.rest_1_), channel_id=1, source_target_pairs={{0,32},{16,48},{24,56},{32,64},{48,80},{56,88},{64,96},{80,112},{8... | collective-permute-start | bytes 1179656 | tf_op jit(solution)/shard_map/ppermute | solution.py:447
  22.8 31.8 %collective-permute-start.7 = (bf16[2,768,128]{2,1,0:T(8,128)(2,1)}, bf16[2,768,128]{2,1,0:T(8,128)(2,1)}, u32[]{:S(2)}, u32[]{:S(2)}) collective-permute-start(bf16[2,768,128]{2,1,0:T(8,128)(2,1)} %get-tuple-element.33), channel_id=1, source_target_pairs={{0,8},{8,16},{16,24},{24,0},{32,40},{40,48},{48,56},{56,32},{64,72... | collective-permute-start | bytes 1179656 | tf_op jit(solution)/shard_map/ppermute | solution.py:443
  24.8 19.6 %copy-start.5 = (bf16[2,768,128]{2,1,0:T(8,128)(2,1)}, bf16[2,768,128]{2,1,0:T(8,128)(2,1)S(1)}, u32[]{:S(2)}) copy-start(bf16[2,768,128]{2,1,0:T(8,128)(2,1)S(1)} %collective-permute-done.1.rest_2_) | copy-start | bytes 1179652
  24.8 29.7 %collective-permute-start.8 = (bf16[2,768,128]{2,1,0:T(8,128)(2,1)}, bf16[2,768,128]{2,1,0:T(8,128)(2,1)}, u32[]{:S(2)}, u32[]{:S(2)}) collective-permute-start(bf16[2,768,128]{2,1,0:T(8,128)(2,1)} %get-tuple-element.34), channel_id=1, source_target_pairs={{0,16},{8,24},{16,0},{24,8},{32,48},{40,56},{48,32},{56,40},{64,80... | collective-permute-start | bytes 1179656 | tf_op jit(solution)/shard_map/ppermute | solution.py:443
  26.8 27.7 %collective-permute-start.9 = (bf16[2,768,128]{2,1,0:T(8,128)(2,1)}, bf16[2,768,128]{2,1,0:T(8,128)(2,1)}, u32[]{:S(2)}, u32[]{:S(2)}) collective-permute-start(bf16[2,768,128]{2,1,0:T(8,128)(2,1)} %get-tuple-element.35), channel_id=1, source_target_pairs={{0,24},{8,0},{16,8},{24,16},{32,56},{40,32},{48,40},{56,48},{64,88... | collective-permute-start | bytes 1179656 | tf_op jit(solution)/shard_map/ppermute | solution.py:443
  28.3 9.7 %copy-start.6 = (bf16[2,768,128]{2,1,0:T(8,128)(2,1)}, bf16[2,768,128]{2,1,0:T(8,128)(2,1)S(1)}, u32[]{:S(2)}) copy-start(bf16[2,768,128]{2,1,0:T(8,128)(2,1)S(1)} %collective-permute-done.3.rest_4_) | copy-start | bytes 1179652
  28.3 16.2 %collective-permute-start.5 = (bf16[2,768,128]{2,1,0:T(8,128)(2,1)S(1)}, bf16[2,768,128]{2,1,0:T(8,128)(2,1)}, u32[]{:S(2)}, u32[]{:S(2)}) collective-permute-start(bf16[2,768,128]{2,1,0:T(8,128)(2,1)S(1)} %collective-permute-done.1.rest_2_), channel_id=1, source_target_pairs={{0,32},{8,40},{24,56},{32,64},{40,72},{56,88},{64,96},{72,104},{88... | collective-permute-start | bytes 1179656 | tf_op jit(solution)/shard_map/ppermute | solution.py:447
  32.9 5.1 %copy-start.7 = (bf16[2,768,128]{2,1,0:T(8,128)(2,1)}, bf16[2,768,128]{2,1,0:T(8,128)(2,1)S(1)}, u32[]{:S(2)}) copy-start(bf16[2,768,128]{2,1,0:T(8,128)(2,1)S(1)} %collective-permute-done.4.rest_5_) | copy-start | bytes 1179652
  32.9 21.6 %collective-permute-start.6 = (bf16[2,768,128]{2,1,0:T(8,128)(2,1)}, bf16[2,768,128]{2,1,0:T(8,128)(2,1)}, u32[]{:S(2)}, u32[]{:S(2)}) collective-permute-start(bf16[2,768,128]{2,1,0:T(8,128)(2,1)} %collective-permute-done.2.rest_3_), channel_id=1, source_target_pairs={{0,32},{8,40},{16,48},{32,64},{40,72},{48,80},{64,96},{72,104},{80... | collective-permute-start | bytes 1179656 | tf_op jit(solution)/shard_map/ppermute | solution.py:447
  36.7 17.8 %copy-start.3 = (s32[3072]{0:T(1024)}, s32[3072]{0:T(1024)S(1)}, u32[]{:S(2)}) copy-start(s32[3072]{0:T(1024)S(1)} %broadcast_subtract_fusion) | copy-start | bytes 36868
  38.0 32.8 %all-to-all-start = ((bf16[32,16,768]{2,1,0:T(8,128)(2,1)}), bf16[32,16,768]{2,1,0:T(8,128)(2,1)S(1)}, u32[]{:S(2)}, u32[]{:S(2)}) async-start(bf16[32,16,768]{2,1,0:T(8,128)(2,1)} %bitcast.4), calls=%async_computation | async-start | bytes 1572864 | tf_op jit(solution)/shard_map/all_to_all | solution.py:439
  70.8 11.0 %copy-start.2 = (bf16[32,16,768]{2,1,0:T(8,128)(2,1)}, bf16[32,16,768]{2,1,0:T(8,128)(2,1)S(1)}, u32[]{:S(2)}) copy-start(bf16[32,16,768]{2,1,0:T(8,128)(2,1)S(1)} %all-to-all-done.taps_ref) | copy-start | bytes 2359300
  70.8 29.0 %all-to-all-start.1 = ((bf16[8,16,3072]{2,1,0:T(8,128)(2,1)}), bf16[8,16,3072]{2,1,0:T(8,128)(2,1)}, u32[]{:S(2)}, u32[]{:S(2)}) async-start(bf16[8,16,3072]{2,1,0:T(8,128)(2,1)} %bitcast.18), calls=%async_computation.1 | async-start | bytes 1572864 | tf_op jit(solution)/shard_map/all_to_all | solution.py:439
  88.7 19.0 %collective-permute-start.12 = (bf16[768,128]{1,0:T(8,128)(2,1)S(1)}, bf16[768,128]{1,0:T(8,128)(2,1)S(1)}, u32[]{:S(2)}, u32[]{:S(2)}) collective-permute-start(bf16[768,128]{1,0:T(8,128)(2,1)S(1)} %get-tuple-element.48), channel_id=1, source_target_pairs={{0,24},{8,0},{16,8},{24,16},{32,56},{40,32},{48,40},{56,48},{64,88... | collective-permute-start | bytes 589832 | tf_op jit(solution)/shard_map/ppermute | solution.py:443
  88.7 19.0 %collective-permute-start.11 = (bf16[768,128]{1,0:T(8,128)(2,1)S(1)}, bf16[768,128]{1,0:T(8,128)(2,1)S(1)}, u32[]{:S(2)}, u32[]{:S(2)}) collective-permute-start(bf16[768,128]{1,0:T(8,128)(2,1)S(1)} %get-tuple-element.49), channel_id=1, source_target_pairs={{0,16},{8,24},{16,0},{24,8},{32,48},{40,56},{48,32},{56,40},{64,80... | collective-permute-start | bytes 589832 | tf_op jit(solution)/shard_map/ppermute | solution.py:443
  93.3 14.4 %collective-permute-start.10 = (bf16[768,128]{1,0:T(8,128)(2,1)S(1)}, bf16[768,128]{1,0:T(8,128)(2,1)}, u32[]{:S(2)}, u32[]{:S(2)}) collective-permute-start(bf16[768,128]{1,0:T(8,128)(2,1)S(1)} %get-tuple-element.50), channel_id=1, source_target_pairs={{0,8},{8,16},{16,24},{24,0},{32,40},{40,48},{48,56},{56,32},{64,72... | collective-permute-start | bytes 589832 | tf_op jit(solution)/shard_map/ppermute | solution.py:443
  107.7 4.0 %copy-start.8 = (bf16[768,128]{1,0:T(8,128)(2,1)}, bf16[768,128]{1,0:T(8,128)(2,1)S(1)}, u32[]{:S(2)}) copy-start(bf16[768,128]{1,0:T(8,128)(2,1)S(1)} %collective-permute-done.12.rest_3_) | copy-start | bytes 589828
  107.7 4.0 %copy-start.9 = (bf16[768,128]{1,0:T(8,128)(2,1)}, bf16[768,128]{1,0:T(8,128)(2,1)S(1)}, u32[]{:S(2)}) copy-start(bf16[768,128]{1,0:T(8,128)(2,1)S(1)} %collective-permute-done.11.rest_2_) | copy-start | bytes 589828
  107.7 21.8 %all-to-all-start.2 = ((bf16[32,16,768]{2,1,0:T(8,128)(2,1)}), bf16[32,16,768]{2,1,0:T(8,128)(2,1)S(1)}, u32[]{:S(2)}, u32[]{:S(2)}) async-start(bf16[32,16,768]{2,1,0:T(8,128)(2,1)} %convolution.1), calls=%async_computation.2 | async-start | bytes 1572864 | tf_op jit(solution)/shard_map/all_to_all | solution.py:439
  111.6 17.8 %copy-start = (bf16[768,512]{1,0:T(8,128)(2,1)S(1)}, bf16[768,512]{1,0:T(8,128)(2,1)}, u32[]{:S(2)}) copy-start(bf16[768,512]{1,0:T(8,128)(2,1)} %gate_ref.1) | copy-start | bytes 2359300

commit v9 on v8

--- a/solution.py
+++ b/solution.py
@@ -455,8 +455,9 @@
     before = [along_z(own[k], k) for k in range(X_SIZE)]
     own[1], queries, in_gate = lax.optimization_barrier((own[1], queries, in_gate))
     asked = pieces_of(x_index, queries, in_gate)
-    taps, *_ = lax.optimization_barrier((taps, *own, *asked))
     asked = arrived(asked)
+    taps, *here = lax.optimization_barrier((taps, *before, *asked))
+    before, asked = here[:X_SIZE], here[X_SIZE:]
     taps = exchanged(taps)
 
     group_first = (me // X_SIZE) * group_rows

time: 133 us -> 145 us (1.090); the launches traced: 131 us -> 147 us
  waiting for transfers between devices: 42.3 us -> 60.3 us
  starting transfers between devices: 47.6 us -> 45.8 us
    all_to_all x3, waiting for transfers between devices: 24.1 us -> 42.2 us  [exchanged(): lax.all_to_all(x, 'ctx', split_axis=0, concat_axis=0, tiled=True, axis_in...]
  transfers between devices with their start and end apart: 16 -> 16, of which waited for: 6 -> 7; matrix products, arithmetic and copies ran while one was open for 4% -> 3% of each run, Pallas kernels for 24% -> 21%
where the time goes in v9:
time: 145 us; the launch traced here: 147 us
  waiting for transfers between devices  60.3 us (42%)
  starting transfers between devices  45.8 us (32%)
  Pallas kernels  35.1 us (24%)
  local copies, waits for them, and re-layouts  3.13 us (2%)
  other arithmetic  1.59 us (1%)
    all_to_all x3, waiting for transfers between devices, exchanged(): lax.all_to_all(x, 'ctx', split_axis=0, concat_axis=0, tiled=True, axis_in...  42.2 us
    all_to_all x3, starting transfers between devices, exchanged(): lax.all_to_all(x, 'ctx', split_axis=0, concat_axis=0, tiled=True, axis_in...  19.6 us
    pallas_call x1, Pallas kernels, attention(): pl.pallas_call(attention_kernel, name='attention', grid_spec=pltpu.Prefet...  13.5 us
    ppermute x9, starting transfers between devices, along_x(): return lax.ppermute(piece, 'ctx', pairs)  13.4 us
    ppermute x4, starting transfers between devices, along_z(): return lax.ppermute(piece, 'ctx', pairs)  12.9 us
    ppermute x4, waiting for transfers between devices, along_z(): return lax.ppermute(piece, 'ctx', pairs)  9.7 us
    ppermute x9, waiting for transfers between devices, along_x(): return lax.ppermute(piece, 'ctx', pairs)  8.34 us
    pallas_call x1, Pallas kernels, convolve(): pl.pallas_call(conv_kernel, name='convolution', grid=(channels // (2 * PA...  7.9 us
  transfers between devices with their start and end apart: 16, of which 7 were waited for; matrix products, arithmetic and copies ran while one was open for 3% of the time, Pallas kernels for 21%

profile of v9, /device:TPU:16, one launch (start us, length us, event | category | flops | bytes accessed | tf_op | source)
XLA Modules:
  0.0 146.7 jit_solution(11321159437173982741)
XLA Ops:
  0.6 2.4 %pieces.2 = (bf16[2,768,128]{2,1,0:T(8,128)(2,1)}, bf16[2,768,128]{2,1,0:T(8,128)(2,1)}, bf16[2,768,128]{2,1,0:T(8,128)(2,1)}, bf16[2,768,128]{2,1,0:T(8,128)(2,1)}) custom-call(s32[1]{0:T(128)} %bitcast.x_ref, bf16[768,512]{1,0:T(8,128)(2,1)} %first_ref.1, bf16[768,512]{1,0:T(8,128)(2,1)} %second_ref.1), custom_call_target="tpu_custom_call" | custom-call | tf_op jit(solution)/shard_map/pieces/pallas_call | solution.py:52
  3.1 1.6 %collective-permute-start = (bf16[2,768,128]{2,1,0:T(8,128)(2,1)}, bf16[2,768,128]{2,1,0:T(8,128)(2,1)S(1)}, u32[]{:S(2)}, u32[]{:S(2)}) collective-permute-start(bf16[2,768,128]{2,1,0:T(8,128)(2,1)} %get-tuple-element.34), channel_id=1, source_target_pairs={{0,8},{8,16},{16,24},{24,0},{32,40},{40,48},{48,56},{56,32},{64,72... | collective-permute-start | bytes 1179656 | tf_op jit(solution)/shard_map/ppermute | solution.py:443
  4.6 2.7 %collective-permute-start.1 = (bf16[2,768,128]{2,1,0:T(8,128)(2,1)}, bf16[2,768,128]{2,1,0:T(8,128)(2,1)S(1)}, u32[]{:S(2)}, u32[]{:S(2)}) collective-permute-start(bf16[2,768,128]{2,1,0:T(8,128)(2,1)} %get-tuple-element.36), channel_id=1, source_target_pairs={{0,16},{8,24},{16,0},{24,8},{32,48},{40,56},{48,32},{56,40},{64,80... | collective-permute-start | bytes 1179656 | tf_op jit(solution)/shard_map/ppermute | solution.py:443
  7.4 1.4 collective-permute-start.2
  8.8 0.7 collective-permute-start.3
  9.5 6.1 %collective-permute-done.rest_1_ = bf16[2,768,128]{2,1,0:T(8,128)(2,1)S(1)} collective-permute-done((bf16[2,768,128]{2,1,0:T(8,128)(2,1)}, bf16[2,768,128]{2,1,0:T(8,128)(2,1)S(1)}, u32[]{:S(2)}, u32[]{:S(2)}) %collective-permute-start) | collective-permute-done | bytes 393248 | tf_op jit(solution)/shard_map/ppermute | solution.py:443
  15.6 3.8 %collective-permute-start.4 = (bf16[2,768,128]{2,1,0:T(8,128)(2,1)S(1)}, bf16[2,768,128]{2,1,0:T(8,128)(2,1)S(1)}, u32[]{:S(2)}, u32[]{:S(2)}) collective-permute-start(bf16[2,768,128]{2,1,0:T(8,128)(2,1)S(1)} %collective-permute-done.rest_1_), channel_id=1, source_target_pairs={{0,32},{16,48},{24,56},{32,64},{48,80},{56,88},{64,96},{80,112},{8... | collective-permute-start | bytes 1179656 | tf_op jit(solution)/shard_map/ppermute | solution.py:447
  19.4 0.7 select_reduce_fusion.1
  20.2 2.3 %pieces.3 = (bf16[2,768,128]{2,1,0:T(8,128)(2,1)}, bf16[2,768,128]{2,1,0:T(8,128)(2,1)}, bf16[2,768,128]{2,1,0:T(8,128)(2,1)}, bf16[2,768,128]{2,1,0:T(8,128)(2,1)}) custom-call(s32[1]{0:T(128)} %bitcast.x_ref, bf16[768,512]{1,0:T(8,128)(2,1)} %first_ref.2, bf16[768,512]{1,0:T(8,128)(2,1)} %second_ref.2), custom_call_target="tpu_custom_call" | custom-call | tf_op jit(solution)/shard_map/pieces/pallas_call | solution.py:52
  22.5 0.1 collective-permute-start.7
  22.6 2.2 %collective-permute-done.1.rest_2_ = bf16[2,768,128]{2,1,0:T(8,128)(2,1)S(1)} collective-permute-done((bf16[2,768,128]{2,1,0:T(8,128)(2,1)}, bf16[2,768,128]{2,1,0:T(8,128)(2,1)S(1)}, u32[]{:S(2)}, u32[]{:S(2)}) %collective-permute-start.1) | collective-permute-done | bytes 393248 | tf_op jit(solution)/shard_map/ppermute | solution.py:443
  24.8 1.8 %collective-permute-start.8 = (bf16[2,768,128]{2,1,0:T(8,128)(2,1)}, bf16[2,768,128]{2,1,0:T(8,128)(2,1)}, u32[]{:S(2)}, u32[]{:S(2)}) collective-permute-start(bf16[2,768,128]{2,1,0:T(8,128)(2,1)} %get-tuple-element.42), channel_id=1, source_target_pairs={{0,16},{8,24},{16,0},{24,8},{32,48},{40,56},{48,32},{56,40},{64,80... | collective-permute-start | bytes 1179656 | tf_op jit(solution)/shard_map/ppermute | solution.py:443
  26.6 0.0 collective-permute-done.2.rest_3_
  26.6 1.4 collective-permute-start.9
  28.1 0.0 collective-permute-done.3.rest_4_
  28.1 4.6 %collective-permute-start.5 = (bf16[2,768,128]{2,1,0:T(8,128)(2,1)S(1)}, bf16[2,768,128]{2,1,0:T(8,128)(2,1)}, u32[]{:S(2)}, u32[]{:S(2)}) collective-permute-start(bf16[2,768,128]{2,1,0:T(8,128)(2,1)S(1)} %collective-permute-done.1.rest_2_), channel_id=1, source_target_pairs={{0,32},{8,40},{24,56},{32,64},{40,72},{56,88},{64,96},{72,104},{88... | collective-permute-start | bytes 1179656 | tf_op jit(solution)/shard_map/ppermute | solution.py:447
  32.6 0.0 collective-permute-done.4.rest_5_
  32.6 3.8 %collective-permute-start.6 = (bf16[2,768,128]{2,1,0:T(8,128)(2,1)S(1)}, bf16[2,768,128]{2,1,0:T(8,128)(2,1)}, u32[]{:S(2)}, u32[]{:S(2)}) collective-permute-start(bf16[2,768,128]{2,1,0:T(8,128)(2,1)S(1)} %collective-permute-done.2.rest_3_), channel_id=1, source_target_pairs={{0,32},{8,40},{16,48},{32,64},{40,72},{48,80},{64,96},{72,104},{80... | collective-permute-start | bytes 1179656 | tf_op jit(solution)/shard_map/ppermute | solution.py:447
  36.5 0.2 select_reduce_fusion
  36.7 0.1 slice.19
  36.8 0.1 slice.18
  36.9 0.1 convert_element_type.3
  37.0 1.0 copy.16
  37.9 3.5 %collective-permute-done.5.rest_6_ = bf16[2,768,128]{2,1,0:T(8,128)(2,1)} collective-permute-done((bf16[2,768,128]{2,1,0:T(8,128)(2,1)S(1)}, bf16[2,768,128]{2,1,0:T(8,128)(2,1)}, u32[]{:S(2)}, u32[]{:S(2)}) %collective-permute-start.5) | collective-permute-done | bytes 393248 | tf_op jit(solution)/shard_map/ppermute | solution.py:447
  41.4 6.2 %collective-permute-done.6.rest_7_ = bf16[2,768,128]{2,1,0:T(8,128)(2,1)} collective-permute-done((bf16[2,768,128]{2,1,0:T(8,128)(2,1)S(1)}, bf16[2,768,128]{2,1,0:T(8,128)(2,1)}, u32[]{:S(2)}, u32[]{:S(2)}) %collective-permute-start.6) | collective-permute-done | bytes 393248 | tf_op jit(solution)/shard_map/ppermute | solution.py:447
  47.6 0.0 collective-permute-done.7.rest_9_
  47.6 0.0 collective-permute-done.8.rest_10_
  47.6 0.0 collective-permute-done.9.rest_11_
  47.7 10.7 %all-to-all-start = ((bf16[32,16,768]{2,1,0:T(8,128)(2,1)}), bf16[32,16,768]{2,1,0:T(8,128)(2,1)S(1)}, u32[]{:S(2)}, u32[]{:S(2)}) async-start(bf16[32,16,768]{2,1,0:T(8,128)(2,1)} %bitcast.4), calls=%async_computation | async-start | bytes 1572864 | tf_op jit(solution)/shard_map/all_to_all | solution.py:439
  58.4 0.6 and_select_fusion.1
  59.0 13.5 %attention.1 = (bf16[4,768,128]{2,1,0:T(8,128)(2,1)}, bf16[128,3072]{1,0:T(8,128)(2,1)}) custom-call(s32[4]{0:T(128)} %get-tuple-element.68.lo_ref, s32[4]{0:T(128)} %get-tuple-element.69.mid_ref, s32[1]{0:T(128)} %bitcast.x_ref, s32[4,1,768]{2,1,0:T(1,128)} %bitcast.19, bf16[2,768,128]{2,1,0:T(8,128)(2,1)} %get-tuple-element.33.rest_0_, ...), custom_call_target="tpu_custom_call" | custom-call | flops 16000000000 | bytes 3932160 | tf_op jit(solution)/shard_map/attention/pallas_call | solution.py:165
  72.5 7.7 %all-to-all-done.taps_ref = bf16[32,16,768]{2,1,0:T(8,128)(2,1)S(1)} async-done(((bf16[32,16,768]{2,1,0:T(8,128)(2,1)}), bf16[32,16,768]{2,1,0:T(8,128)(2,1)S(1)}, u32[]{:S(2)}, u32[]{:S(2)}) %all-to-all-start) | async-done | bytes 786464 | tf_op jit(solution)/shard_map/all_to_all | solution.py:439
  80.2 4.2 %all-to-all-start.1 = ((bf16[8,16,3072]{2,1,0:T(8,128)(2,1)}), bf16[8,16,3072]{2,1,0:T(8,128)(2,1)}, u32[]{:S(2)}, u32[]{:S(2)}) async-start(bf16[8,16,3072]{2,1,0:T(8,128)(2,1)} %bitcast.18), calls=%async_computation.1 | async-start | bytes 1572864 | tf_op jit(solution)/shard_map/all_to_all | solution.py:439
  84.4 5.0 %taps_spectrum.1.taps_ref = f32[3072,256]{1,0:T(8,128)} custom-call(bf16[32,16,768]{2,1,0:T(8,128)(2,1)} %copy-done.2, bf16[2,384,192]{2,1,0:T(8,128)(2,1)} %constant.53.clone.outer_ref, f32[2,192,128]{2,1,0:T(8,128)} %constant.54.clone.twist_ref, bf16[2,256,256]{2,1,0:T(8,128)(2,1)} %constant.55.clone.inner_ref), custom_call_target="tpu_custom_call" | custom-call | flops 5000000000 | bytes 4194304 | tf_op jit(solution)/shard_map/taps_spectrum/pallas_call | solution.py:337
  89.4 1.9 %slice_bitcast_fusion = (bf16[768,128]{1,0:T(8,128)(2,1)S(1)}, bf16[768,128]{1,0:T(8,128)(2,1)S(1)}, bf16[768,128]{1,0:T(8,128)(2,1)S(1)}, bf16[768,128]{1,0:T(8,128)(2,1)}) fusion(bf16[4,768,128]{2,1,0:T(8,128)(2,1)} %get-tuple-element.58), kind=kLoop, calls=%fused_computation.1 | loop fusion | bytes 1572864 | tf_op jit(solution)/shard_map/squeeze | solution.py:472
  91.4 2.6 %collective-permute-start.12 = (bf16[768,128]{1,0:T(8,128)(2,1)S(1)}, bf16[768,128]{1,0:T(8,128)(2,1)S(1)}, u32[]{:S(2)}, u32[]{:S(2)}) collective-permute-start(bf16[768,128]{1,0:T(8,128)(2,1)S(1)} %get-tuple-element.64), channel_id=1, source_target_pairs={{0,24},{8,0},{16,8},{24,16},{32,56},{40,32},{48,40},{56,48},{64,88... | collective-permute-start | bytes 589832 | tf_op jit(solution)/shard_map/ppermute | solution.py:443
  94.0 0.9 collective-permute-start.11
  94.8 0.9 collective-permute-start.10
  95.7 13.2 %all-to-all-done.1.signal_ref = bf16[8,16,3072]{2,1,0:T(8,128)(2,1)} async-done(((bf16[8,16,3072]{2,1,0:T(8,128)(2,1)}), bf16[8,16,3072]{2,1,0:T(8,128)(2,1)}, u32[]{:S(2)}, u32[]{:S(2)}) %all-to-all-start.1) | async-done | bytes 786464 | tf_op jit(solution)/shard_map/all_to_all | solution.py:439
  109.0 7.9 %convolution.1 = bf16[32,16,768]{2,1,0:T(8,128)(2,1)} custom-call(bf16[8,16,3072]{2,1,0:T(8,128)(2,1)} %all-to-all-done.1.signal_ref, f32[3072,256]{1,0:T(8,128)} %taps_spectrum.1.taps_ref, bf16[2,384,192]{2,1,0:T(8,128)(2,1)} %constant.56.clone.outer_ref, f32[2,192,128]{2,1,0:T(8,128)} %constant.54.clone.twist_ref, ...), custom_call_target="tpu_custom_call" | custom-call | flops 7000000000 | bytes 5242880 | tf_op jit(solution)/shard_map/convolution/pallas_call | solution.py:355
  116.9 0.0 collective-permute-done.12.rest_3_
  116.9 0.0 collective-permute-done.11.rest_2_
  116.9 0.0 collective-permute-done.10.rest_1_
  116.9 4.6 %all-to-all-start.2 = ((bf16[32,16,768]{2,1,0:T(8,128)(2,1)}), bf16[32,16,768]{2,1,0:T(8,128)(2,1)S(1)}, u32[]{:S(2)}, u32[]{:S(2)}) async-start(bf16[32,16,768]{2,1,0:T(8,128)(2,1)} %convolution.1), calls=%async_computation.2 | async-start | bytes 1572864 | tf_op jit(solution)/shard_map/all_to_all | solution.py:439
  121.5 0.0 copy-start
  121.6 2.0 %assemble.1 = bf16[768,512]{1,0:T(8,128)(2,1)} custom-call(s32[1]{0:T(128)} %bitcast.x_ref, bf16[768,128]{1,0:T(8,128)(2,1)} %get-tuple-element.59.rest_0_, bf16[768,128]{1,0:T(8,128)(2,1)} %collective-permute-done.10.rest_1_, bf16[768,128]{1,0:T(8,128)(2,1)} %copy-done.10, bf16[768,128]{1,0:T(8,128)(2,1)} %copy-done.9), custom_call_target="tpu_custom_call" | custom-call | flops 2000000000 | bytes 1048576 | tf_op jit(solution)/shard_map/assemble/pallas_call | solution.py:391
  123.6 21.3 %all-to-all-done.2 = bf16[32,16,768]{2,1,0:T(8,128)(2,1)S(1)} async-done(((bf16[32,16,768]{2,1,0:T(8,128)(2,1)}), bf16[32,16,768]{2,1,0:T(8,128)(2,1)S(1)}, u32[]{:S(2)}, u32[]{:S(2)}) %all-to-all-start.2) | async-done | bytes 786464 | tf_op jit(solution)/shard_map/all_to_all | solution.py:439
  144.9 1.9 %finish.1 = bf16[768,512]{1,0:T(8,128)(2,1)} custom-call(bf16[8,4,16,768]{3,2,1,0:T(8,128)(2,1)S(1)} %bitcast.16, bf16[768,512]{1,0:T(8,128)(2,1)S(1)} %copy-done), custom_call_target="tpu_custom_call" | custom-call | tf_op jit(solution)/shard_map/finish/pallas_call | solution.py:416
  (23 shorter events, 0.0 us)
Async XLA Ops:
  0.6 36.2 %copy-start.1 = (f32[512,768]{1,0:T(8,128)S(1)}, f32[512,768]{1,0:T(8,128)}, u32[]{:S(2)}) copy-start(f32[512,768]{1,0:T(8,128)} %param.19) | copy-start | bytes 4718596
  3.1 12.5 %collective-permute-start = (bf16[2,768,128]{2,1,0:T(8,128)(2,1)}, bf16[2,768,128]{2,1,0:T(8,128)(2,1)S(1)}, u32[]{:S(2)}, u32[]{:S(2)}) collective-permute-start(bf16[2,768,128]{2,1,0:T(8,128)(2,1)} %get-tuple-element.34), channel_id=1, source_target_pairs={{0,8},{8,16},{16,24},{24,0},{32,40},{40,48},{48,56},{56,32},{64,72... | collective-permute-start | bytes 1179656 | tf_op jit(solution)/shard_map/ppermute | solution.py:443
  4.6 20.2 %collective-permute-start.1 = (bf16[2,768,128]{2,1,0:T(8,128)(2,1)}, bf16[2,768,128]{2,1,0:T(8,128)(2,1)S(1)}, u32[]{:S(2)}, u32[]{:S(2)}) collective-permute-start(bf16[2,768,128]{2,1,0:T(8,128)(2,1)} %get-tuple-element.36), channel_id=1, source_target_pairs={{0,16},{8,24},{16,0},{24,8},{32,48},{40,56},{48,32},{56,40},{64,80... | collective-permute-start | bytes 1179656 | tf_op jit(solution)/shard_map/ppermute | solution.py:443
  7.4 19.2 %collective-permute-start.2 = (bf16[2,768,128]{2,1,0:T(8,128)(2,1)}, bf16[2,768,128]{2,1,0:T(8,128)(2,1)S(1)}, u32[]{:S(2)}, u32[]{:S(2)}) collective-permute-start(bf16[2,768,128]{2,1,0:T(8,128)(2,1)} %get-tuple-element.37), channel_id=1, source_target_pairs={{0,24},{8,0},{16,8},{24,16},{32,56},{40,32},{48,40},{56,48},{64,88... | collective-permute-start | bytes 1179656 | tf_op jit(solution)/shard_map/ppermute | solution.py:443
  8.8 19.2 %collective-permute-start.3 = (bf16[2,768,128]{2,1,0:T(8,128)(2,1)}, bf16[2,768,128]{2,1,0:T(8,128)(2,1)S(1)}, u32[]{:S(2)}, u32[]{:S(2)}) collective-permute-start(bf16[2,768,128]{2,1,0:T(8,128)(2,1)} %get-tuple-element.33.rest_0_), channel_id=1, source_target_pairs={{8,40},{16,48},{24,56},{40,72},{48,80},{56,88},{72,104},{80,112},{... | collective-permute-start | bytes 1179656 | tf_op jit(solution)/shard_map/ppermute | solution.py:447
  15.6 32.1 %copy-start.4 = (bf16[2,768,128]{2,1,0:T(8,128)(2,1)}, bf16[2,768,128]{2,1,0:T(8,128)(2,1)S(1)}, u32[]{:S(2)}) copy-start(bf16[2,768,128]{2,1,0:T(8,128)(2,1)S(1)} %collective-permute-done.rest_1_) | copy-start | bytes 1179652
  15.6 17.0 %collective-permute-start.4 = (bf16[2,768,128]{2,1,0:T(8,128)(2,1)S(1)}, bf16[2,768,128]{2,1,0:T(8,128)(2,1)S(1)}, u32[]{:S(2)}, u32[]{:S(2)}) collective-permute-start(bf16[2,768,128]{2,1,0:T(8,128)(2,1)S(1)} %collective-permute-done.rest_1_), channel_id=1, source_target_pairs={{0,32},{16,48},{24,56},{32,64},{48,80},{56,88},{64,96},{80,112},{8... | collective-permute-start | bytes 1179656 | tf_op jit(solution)/shard_map/ppermute | solution.py:447
  22.5 25.1 %collective-permute-start.7 = (bf16[2,768,128]{2,1,0:T(8,128)(2,1)}, bf16[2,768,128]{2,1,0:T(8,128)(2,1)}, u32[]{:S(2)}, u32[]{:S(2)}) collective-permute-start(bf16[2,768,128]{2,1,0:T(8,128)(2,1)} %get-tuple-element.41), channel_id=1, source_target_pairs={{0,8},{8,16},{16,24},{24,0},{32,40},{40,48},{48,56},{56,32},{64,72... | collective-permute-start | bytes 1179656 | tf_op jit(solution)/shard_map/ppermute | solution.py:443
  24.8 34.1 %copy-start.5 = (bf16[2,768,128]{2,1,0:T(8,128)(2,1)}, bf16[2,768,128]{2,1,0:T(8,128)(2,1)S(1)}, u32[]{:S(2)}) copy-start(bf16[2,768,128]{2,1,0:T(8,128)(2,1)S(1)} %collective-permute-done.1.rest_2_) | copy-start | bytes 1179652
  24.8 22.8 %collective-permute-start.8 = (bf16[2,768,128]{2,1,0:T(8,128)(2,1)}, bf16[2,768,128]{2,1,0:T(8,128)(2,1)}, u32[]{:S(2)}, u32[]{:S(2)}) collective-permute-start(bf16[2,768,128]{2,1,0:T(8,128)(2,1)} %get-tuple-element.42), channel_id=1, source_target_pairs={{0,16},{8,24},{16,0},{24,8},{32,48},{40,56},{48,32},{56,40},{64,80... | collective-permute-start | bytes 1179656 | tf_op jit(solution)/shard_map/ppermute | solution.py:443
  26.6 21.0 %copy-start.6 = (bf16[2,768,128]{2,1,0:T(8,128)(2,1)}, bf16[2,768,128]{2,1,0:T(8,128)(2,1)S(1)}, u32[]{:S(2)}) copy-start(bf16[2,768,128]{2,1,0:T(8,128)(2,1)S(1)} %collective-permute-done.2.rest_3_) | copy-start | bytes 1179652
  26.6 21.0 %collective-permute-start.9 = (bf16[2,768,128]{2,1,0:T(8,128)(2,1)}, bf16[2,768,128]{2,1,0:T(8,128)(2,1)}, u32[]{:S(2)}, u32[]{:S(2)}) collective-permute-start(bf16[2,768,128]{2,1,0:T(8,128)(2,1)} %get-tuple-element.43), channel_id=1, source_target_pairs={{0,24},{8,0},{16,8},{24,16},{32,56},{40,32},{48,40},{56,48},{64,88... | collective-permute-start | bytes 1179656 | tf_op jit(solution)/shard_map/ppermute | solution.py:443
  28.1 19.6 %copy-start.7 = (bf16[2,768,128]{2,1,0:T(8,128)(2,1)}, bf16[2,768,128]{2,1,0:T(8,128)(2,1)S(1)}, u32[]{:S(2)}) copy-start(bf16[2,768,128]{2,1,0:T(8,128)(2,1)S(1)} %collective-permute-done.3.rest_4_) | copy-start | bytes 1179652
  28.1 13.3 %collective-permute-start.5 = (bf16[2,768,128]{2,1,0:T(8,128)(2,1)S(1)}, bf16[2,768,128]{2,1,0:T(8,128)(2,1)}, u32[]{:S(2)}, u32[]{:S(2)}) collective-permute-start(bf16[2,768,128]{2,1,0:T(8,128)(2,1)S(1)} %collective-permute-done.1.rest_2_), channel_id=1, source_target_pairs={{0,32},{8,40},{24,56},{32,64},{40,72},{56,88},{64,96},{72,104},{88... | collective-permute-start | bytes 1179656 | tf_op jit(solution)/shard_map/ppermute | solution.py:447
  32.6 3.8 %copy-start.8 = (bf16[2,768,128]{2,1,0:T(8,128)(2,1)}, bf16[2,768,128]{2,1,0:T(8,128)(2,1)S(1)}, u32[]{:S(2)}) copy-start(bf16[2,768,128]{2,1,0:T(8,128)(2,1)S(1)} %collective-permute-done.4.rest_5_) | copy-start | bytes 1179652
  32.6 15.0 %collective-permute-start.6 = (bf16[2,768,128]{2,1,0:T(8,128)(2,1)S(1)}, bf16[2,768,128]{2,1,0:T(8,128)(2,1)}, u32[]{:S(2)}, u32[]{:S(2)}) collective-permute-start(bf16[2,768,128]{2,1,0:T(8,128)(2,1)S(1)} %collective-permute-done.2.rest_3_), channel_id=1, source_target_pairs={{0,32},{8,40},{16,48},{32,64},{40,72},{48,80},{64,96},{72,104},{80... | collective-permute-start | bytes 1179656 | tf_op jit(solution)/shard_map/ppermute | solution.py:447
  36.7 22.3 %copy-start.3 = (s32[3072]{0:T(1024)}, s32[3072]{0:T(1024)S(1)}, u32[]{:S(2)}) copy-start(s32[3072]{0:T(1024)S(1)} %broadcast_subtract_fusion) | copy-start | bytes 36868
  47.7 32.6 %all-to-all-start = ((bf16[32,16,768]{2,1,0:T(8,128)(2,1)}), bf16[32,16,768]{2,1,0:T(8,128)(2,1)S(1)}, u32[]{:S(2)}, u32[]{:S(2)}) async-start(bf16[32,16,768]{2,1,0:T(8,128)(2,1)} %bitcast.4), calls=%async_computation | async-start | bytes 1572864 | tf_op jit(solution)/shard_map/all_to_all | solution.py:439
  80.2 4.2 %copy-start.2 = (bf16[32,16,768]{2,1,0:T(8,128)(2,1)}, bf16[32,16,768]{2,1,0:T(8,128)(2,1)S(1)}, u32[]{:S(2)}) copy-start(bf16[32,16,768]{2,1,0:T(8,128)(2,1)S(1)} %all-to-all-done.taps_ref) | copy-start | bytes 2359300
  80.2 28.7 %all-to-all-start.1 = ((bf16[8,16,3072]{2,1,0:T(8,128)(2,1)}), bf16[8,16,3072]{2,1,0:T(8,128)(2,1)}, u32[]{:S(2)}, u32[]{:S(2)}) async-start(bf16[8,16,3072]{2,1,0:T(8,128)(2,1)} %bitcast.18), calls=%async_computation.1 | async-start | bytes 1572864 | tf_op jit(solution)/shard_map/all_to_all | solution.py:439
  91.4 25.5 %collective-permute-start.12 = (bf16[768,128]{1,0:T(8,128)(2,1)S(1)}, bf16[768,128]{1,0:T(8,128)(2,1)S(1)}, u32[]{:S(2)}, u32[]{:S(2)}) collective-permute-start(bf16[768,128]{1,0:T(8,128)(2,1)S(1)} %get-tuple-element.64), channel_id=1, source_target_pairs={{0,24},{8,0},{16,8},{24,16},{32,56},{40,32},{48,40},{56,48},{64,88... | collective-permute-start | bytes 589832 | tf_op jit(solution)/shard_map/ppermute | solution.py:443
  94.0 22.9 %collective-permute-start.11 = (bf16[768,128]{1,0:T(8,128)(2,1)S(1)}, bf16[768,128]{1,0:T(8,128)(2,1)S(1)}, u32[]{:S(2)}, u32[]{:S(2)}) collective-permute-start(bf16[768,128]{1,0:T(8,128)(2,1)S(1)} %get-tuple-element.65), channel_id=1, source_target_pairs={{0,16},{8,24},{16,0},{24,8},{32,48},{40,56},{48,32},{56,40},{64,80... | collective-permute-start | bytes 589832 | tf_op jit(solution)/shard_map/ppermute | solution.py:443
  94.8 22.0 %collective-permute-start.10 = (bf16[768,128]{1,0:T(8,128)(2,1)S(1)}, bf16[768,128]{1,0:T(8,128)(2,1)}, u32[]{:S(2)}, u32[]{:S(2)}) collective-permute-start(bf16[768,128]{1,0:T(8,128)(2,1)S(1)} %get-tuple-element.66), channel_id=1, source_target_pairs={{0,8},{8,16},{16,24},{24,0},{32,40},{40,48},{48,56},{56,32},{64,72... | collective-permute-start | bytes 589832 | tf_op jit(solution)/shard_map/ppermute | solution.py:443
  116.9 4.7 %copy-start.9 = (bf16[768,128]{1,0:T(8,128)(2,1)}, bf16[768,128]{1,0:T(8,128)(2,1)S(1)}, u32[]{:S(2)}) copy-start(bf16[768,128]{1,0:T(8,128)(2,1)S(1)} %collective-permute-done.12.rest_3_) | copy-start | bytes 589828
  116.9 4.7 %copy-start.10 = (bf16[768,128]{1,0:T(8,128)(2,1)}, bf16[768,128]{1,0:T(8,128)(2,1)S(1)}, u32[]{:S(2)}) copy-start(bf16[768,128]{1,0:T(8,128)(2,1)S(1)} %collective-permute-done.11.rest_2_) | copy-start | bytes 589828
  116.9 28.0 %all-to-all-start.2 = ((bf16[32,16,768]{2,1,0:T(8,128)(2,1)}), bf16[32,16,768]{2,1,0:T(8,128)(2,1)S(1)}, u32[]{:S(2)}, u32[]{:S(2)}) async-start(bf16[32,16,768]{2,1,0:T(8,128)(2,1)} %convolution.1), calls=%async_computation.2 | async-start | bytes 1572864 | tf_op jit(solution)/shard_map/all_to_all | solution.py:439
  121.5 23.3 %copy-start = (bf16[768,512]{1,0:T(8,128)(2,1)S(1)}, bf16[768,512]{1,0:T(8,128)(2,1)}, u32[]{:S(2)}) copy-start(bf16[768,512]{1,0:T(8,128)(2,1)} %gate_ref.1) | copy-start | bytes 2359300

commit v10 on v8

--- a/solution.py
+++ b/solution.py
@@ -455,6 +455,8 @@
     before = [along_z(own[k], k) for k in range(X_SIZE)]
     own[1], queries, in_gate = lax.optimization_barrier((own[1], queries, in_gate))
     asked = pieces_of(x_index, queries, in_gate)
+    asked = list(asked)
+    before[0], before[1], asked[2], asked[3] = lax.optimization_barrier((before[0], before[1], asked[2], asked[3]))
     taps, *_ = lax.optimization_barrier((taps, *own, *asked))
     asked = arrived(asked)
     taps = exchanged(taps)

time: 133 us -> 139 us (1.045)
  starting transfers between devices: 47.6 us -> 58.1 us
  waiting for transfers between devices: 42.3 us -> 37 us
  Pallas kernels: 35.8 us -> 37.8 us
    all_to_all x3, starting transfers between devices: 20.8 us -> 30.8 us  [exchanged(): lax.all_to_all(x, 'ctx', split_axis=0, concat_axis=0, tiled=True, axis_in...]
    ppermute x4, waiting for transfers between devices: 10.1 us -> 3.38 us  [along_z(): return lax.ppermute(piece, 'ctx', pairs)]
    ppermute x9, waiting for transfers between devices: 8.11 us -> 10.5 us  [along_x(): return lax.ppermute(piece, 'ctx', pairs)]
    pallas_call x1, Pallas kernels: 14.3 us -> 16.2 us  [attention(): pl.pallas_call(attention_kernel, name='attention', grid_spec=pltpu.Prefet...]
  transfers between devices with their start and end apart: 16 -> 16, of which waited for: 6 -> 6; matrix products, arithmetic and copies ran while one was open for 4% -> 3% of each run, Pallas kernels for 24% -> 24%
where the time goes in v10:
time: 139 us
  starting transfers between devices  58.1 us (42%)
  Pallas kernels  37.8 us (27%)
  waiting for transfers between devices  37 us (27%)
  local copies, waits for them, and re-layouts  3.14 us (2%)
  other arithmetic  1.64 us (1%)
    all_to_all x3, starting transfers between devices, exchanged(): lax.all_to_all(x, 'ctx', split_axis=0, concat_axis=0, tiled=True, axis_in...  30.8 us
    all_to_all x3, waiting for transfers between devices, exchanged(): lax.all_to_all(x, 'ctx', split_axis=0, concat_axis=0, tiled=True, axis_in...  23.1 us
    pallas_call x1, Pallas kernels, attention(): pl.pallas_call(attention_kernel, name='attention', grid_spec=pltpu.Prefet...  16.2 us
    ppermute x9, starting transfers between devices, along_x(): return lax.ppermute(piece, 'ctx', pairs)  14.4 us
    ppermute x4, starting transfers between devices, along_z(): return lax.ppermute(piece, 'ctx', pairs)  12.9 us
    ppermute x9, waiting for transfers between devices, along_x(): return lax.ppermute(piece, 'ctx', pairs)  10.5 us
    pallas_call x1, Pallas kernels, convolve(): pl.pallas_call(conv_kernel, name='convolution', grid=(channels // (2 * PA...  7.91 us
    pallas_call x1, Pallas kernels, transform_taps(): pl.pallas_call(taps_kernel, name='taps_spectrum', grid=(channels // (2 *...  4.98 us
  transfers between devices with their start and end apart: 16, of which 6 were waited for; matrix products, arithmetic and copies ran while one was open for 3% of the time, Pallas kernels for 24%

profile of v10, /device:TPU:16, one launch (start us, length us, event | category | flops | bytes accessed | tf_op | source)
XLA Modules:
  0.0 138.6 jit_solution(1926896892724187073)
XLA Ops:
  0.6 2.4 %pieces.2 = (bf16[2,768,128]{2,1,0:T(8,128)(2,1)}, bf16[2,768,128]{2,1,0:T(8,128)(2,1)}, bf16[2,768,128]{2,1,0:T(8,128)(2,1)}, bf16[2,768,128]{2,1,0:T(8,128)(2,1)}) custom-call(s32[1]{0:T(128)} %bitcast.x_ref, bf16[768,512]{1,0:T(8,128)(2,1)} %first_ref.1, bf16[768,512]{1,0:T(8,128)(2,1)} %second_ref.1), custom_call_target="tpu_custom_call" | custom-call | tf_op jit(solution)/shard_map/pieces/pallas_call | solution.py:52
  3.1 1.6 %collective-permute-start = (bf16[2,768,128]{2,1,0:T(8,128)(2,1)}, bf16[2,768,128]{2,1,0:T(8,128)(2,1)S(1)}, u32[]{:S(2)}, u32[]{:S(2)}) collective-permute-start(bf16[2,768,128]{2,1,0:T(8,128)(2,1)} %get-tuple-element.30), channel_id=1, source_target_pairs={{0,8},{8,16},{16,24},{24,0},{32,40},{40,48},{48,56},{56,32},{64,72... | collective-permute-start | bytes 1179656 | tf_op jit(solution)/shard_map/ppermute | solution.py:443
  4.6 2.7 %collective-permute-start.1 = (bf16[2,768,128]{2,1,0:T(8,128)(2,1)}, bf16[2,768,128]{2,1,0:T(8,128)(2,1)S(1)}, u32[]{:S(2)}, u32[]{:S(2)}) collective-permute-start(bf16[2,768,128]{2,1,0:T(8,128)(2,1)} %get-tuple-element.32), channel_id=1, source_target_pairs={{0,16},{8,24},{16,0},{24,8},{32,48},{40,56},{48,32},{56,40},{64,80... | collective-permute-start | bytes 1179656 | tf_op jit(solution)/shard_map/ppermute | solution.py:443
  7.4 1.4 %collective-permute-start.2 = (bf16[2,768,128]{2,1,0:T(8,128)(2,1)}, bf16[2,768,128]{2,1,0:T(8,128)(2,1)}, u32[]{:S(2)}, u32[]{:S(2)}) collective-permute-start(bf16[2,768,128]{2,1,0:T(8,128)(2,1)} %get-tuple-element.33), channel_id=1, source_target_pairs={{0,24},{8,0},{16,8},{24,16},{32,56},{40,32},{48,40},{56,48},{64,88... | collective-permute-start | bytes 1179656 | tf_op jit(solution)/shard_map/ppermute | solution.py:443
  8.8 0.7 collective-permute-start.3
  9.5 6.1 %collective-permute-done.rest_1_ = bf16[2,768,128]{2,1,0:T(8,128)(2,1)S(1)} collective-permute-done((bf16[2,768,128]{2,1,0:T(8,128)(2,1)}, bf16[2,768,128]{2,1,0:T(8,128)(2,1)S(1)}, u32[]{:S(2)}, u32[]{:S(2)}) %collective-permute-start) | collective-permute-done | bytes 393248 | tf_op jit(solution)/shard_map/ppermute | solution.py:443
  15.6 3.8 %collective-permute-start.4 = (bf16[2,768,128]{2,1,0:T(8,128)(2,1)S(1)}, bf16[2,768,128]{2,1,0:T(8,128)(2,1)S(1)}, u32[]{:S(2)}, u32[]{:S(2)}) collective-permute-start(bf16[2,768,128]{2,1,0:T(8,128)(2,1)S(1)} %collective-permute-done.rest_1_), channel_id=1, source_target_pairs={{0,32},{16,48},{24,56},{32,64},{48,80},{56,88},{64,96},{80,112},{8... | collective-permute-start | bytes 1179656 | tf_op jit(solution)/shard_map/ppermute | solution.py:447
  19.5 0.7 select_reduce_fusion.1
  20.2 0.2 select_reduce_fusion
  20.4 2.3 %pieces.3 = (bf16[2,768,128]{2,1,0:T(8,128)(2,1)}, bf16[2,768,128]{2,1,0:T(8,128)(2,1)}, bf16[2,768,128]{2,1,0:T(8,128)(2,1)}, bf16[2,768,128]{2,1,0:T(8,128)(2,1)}) custom-call(s32[1]{0:T(128)} %bitcast.x_ref, bf16[768,512]{1,0:T(8,128)(2,1)} %first_ref.2, bf16[768,512]{1,0:T(8,128)(2,1)} %second_ref.2), custom_call_target="tpu_custom_call" | custom-call | tf_op jit(solution)/shard_map/pieces/pallas_call | solution.py:52
  22.8 0.1 collective-permute-start.7
  22.9 2.0 %collective-permute-done.1.rest_2_ = bf16[2,768,128]{2,1,0:T(8,128)(2,1)S(1)} collective-permute-done((bf16[2,768,128]{2,1,0:T(8,128)(2,1)}, bf16[2,768,128]{2,1,0:T(8,128)(2,1)S(1)}, u32[]{:S(2)}, u32[]{:S(2)}) %collective-permute-start.1) | collective-permute-done | bytes 393248 | tf_op jit(solution)/shard_map/ppermute | solution.py:443
  24.8 4.6 %collective-permute-start.5 = (bf16[2,768,128]{2,1,0:T(8,128)(2,1)S(1)}, bf16[2,768,128]{2,1,0:T(8,128)(2,1)}, u32[]{:S(2)}, u32[]{:S(2)}) collective-permute-start(bf16[2,768,128]{2,1,0:T(8,128)(2,1)S(1)} %collective-permute-done.1.rest_2_), channel_id=1, source_target_pairs={{0,32},{8,40},{24,56},{32,64},{40,72},{56,88},{64,96},{72,104},{88... | collective-permute-start | bytes 1179656 | tf_op jit(solution)/shard_map/ppermute | solution.py:447
  29.4 0.0 collective-permute-done.2.rest_3_
  29.4 3.8 %collective-permute-start.6 = (bf16[2,768,128]{2,1,0:T(8,128)(2,1)}, bf16[2,768,128]{2,1,0:T(8,128)(2,1)}, u32[]{:S(2)}, u32[]{:S(2)}) collective-permute-start(bf16[2,768,128]{2,1,0:T(8,128)(2,1)} %collective-permute-done.2.rest_3_), channel_id=1, source_target_pairs={{0,32},{8,40},{16,48},{32,64},{40,72},{48,80},{64,96},{72,104},{80... | collective-permute-start | bytes 1179656 | tf_op jit(solution)/shard_map/ppermute | solution.py:447
  33.3 0.0 collective-permute-done.3.rest_4_
  33.3 0.0 collective-permute-done.4.rest_5_
  33.3 0.1 collective-permute-start.8
  33.4 3.4 %collective-permute-start.9 = (bf16[2,768,128]{2,1,0:T(8,128)(2,1)}, bf16[2,768,128]{2,1,0:T(8,128)(2,1)}, u32[]{:S(2)}, u32[]{:S(2)}) collective-permute-start(bf16[2,768,128]{2,1,0:T(8,128)(2,1)} %get-tuple-element.43), channel_id=1, source_target_pairs={{0,24},{8,0},{16,8},{24,16},{32,56},{40,32},{48,40},{56,48},{64,88... | collective-permute-start | bytes 1179656 | tf_op jit(solution)/shard_map/ppermute | solution.py:443
  36.8 0.1 slice.19
  36.9 0.1 slice.18
  37.0 0.1 convert_element_type.3
  37.1 1.0 copy.16
  38.1 7.1 %all-to-all-start = ((bf16[32,16,768]{2,1,0:T(8,128)(2,1)}), bf16[32,16,768]{2,1,0:T(8,128)(2,1)S(1)}, u32[]{:S(2)}, u32[]{:S(2)}) async-start(bf16[32,16,768]{2,1,0:T(8,128)(2,1)} %bitcast.4), calls=%async_computation | async-start | bytes 1572864 | tf_op jit(solution)/shard_map/all_to_all | solution.py:439
  45.2 0.6 and_select_fusion.1
  45.8 0.0 collective-permute-done.5.rest_6_
  45.8 3.4 %collective-permute-done.6.rest_7_ = bf16[2,768,128]{2,1,0:T(8,128)(2,1)} collective-permute-done((bf16[2,768,128]{2,1,0:T(8,128)(2,1)}, bf16[2,768,128]{2,1,0:T(8,128)(2,1)}, u32[]{:S(2)}, u32[]{:S(2)}) %collective-permute-start.6) | collective-permute-done | bytes 393248 | tf_op jit(solution)/shard_map/ppermute | solution.py:447
  49.2 0.0 collective-permute-done.7.rest_9_
  49.2 0.0 collective-permute-done.8.rest_10_
  49.2 2.4 %collective-permute-done.9.rest_11_ = bf16[2,768,128]{2,1,0:T(8,128)(2,1)} collective-permute-done((bf16[2,768,128]{2,1,0:T(8,128)(2,1)}, bf16[2,768,128]{2,1,0:T(8,128)(2,1)}, u32[]{:S(2)}, u32[]{:S(2)}) %collective-permute-start.9) | collective-permute-done | bytes 393248 | tf_op jit(solution)/shard_map/ppermute | solution.py:443
  51.6 16.2 %attention.1 = (bf16[4,768,128]{2,1,0:T(8,128)(2,1)}, bf16[128,3072]{1,0:T(8,128)(2,1)}) custom-call(s32[4]{0:T(128)} %get-tuple-element.60.lo_ref, s32[4]{0:T(128)} %get-tuple-element.61.mid_ref, s32[1]{0:T(128)} %bitcast.x_ref, s32[4,1,768]{2,1,0:T(1,128)} %bitcast.19, bf16[2,768,128]{2,1,0:T(8,128)(2,1)} %get-tuple-element.29.rest_0_, ...), custom_call_target="tpu_custom_call" | custom-call | flops 16000000000 | bytes 3932160 | tf_op jit(solution)/shard_map/attention/pallas_call | solution.py:165
  67.9 0.0 all-to-all-done.taps_ref
  67.9 17.7 %all-to-all-start.1 = ((bf16[8,16,3072]{2,1,0:T(8,128)(2,1)}), bf16[8,16,3072]{2,1,0:T(8,128)(2,1)}, u32[]{:S(2)}, u32[]{:S(2)}) async-start(bf16[8,16,3072]{2,1,0:T(8,128)(2,1)} %bitcast.18), calls=%async_computation.1 | async-start | bytes 1572864 | tf_op jit(solution)/shard_map/all_to_all | solution.py:439
  85.6 5.0 %taps_spectrum.1.taps_ref = f32[3072,256]{1,0:T(8,128)} custom-call(bf16[32,16,768]{2,1,0:T(8,128)(2,1)} %copy-done.2, bf16[2,384,192]{2,1,0:T(8,128)(2,1)} %constant.53.clone.outer_ref, f32[2,192,128]{2,1,0:T(8,128)} %constant.54.clone.twist_ref, bf16[2,256,256]{2,1,0:T(8,128)(2,1)} %constant.55.clone.inner_ref), custom_call_target="tpu_custom_call" | custom-call | flops 5000000000 | bytes 4194304 | tf_op jit(solution)/shard_map/taps_spectrum/pallas_call | solution.py:337
  90.5 1.9 %slice_bitcast_fusion = (bf16[768,128]{1,0:T(8,128)(2,1)S(1)}, bf16[768,128]{1,0:T(8,128)(2,1)S(1)}, bf16[768,128]{1,0:T(8,128)(2,1)S(1)}, bf16[768,128]{1,0:T(8,128)(2,1)}) fusion(bf16[4,768,128]{2,1,0:T(8,128)(2,1)} %get-tuple-element.50), kind=kLoop, calls=%fused_computation.1 | loop fusion | bytes 1572864 | tf_op jit(solution)/shard_map/squeeze | solution.py:473
  92.5 1.9 %collective-permute-start.12 = (bf16[768,128]{1,0:T(8,128)(2,1)S(1)}, bf16[768,128]{1,0:T(8,128)(2,1)S(1)}, u32[]{:S(2)}, u32[]{:S(2)}) collective-permute-start(bf16[768,128]{1,0:T(8,128)(2,1)S(1)} %get-tuple-element.56), channel_id=1, source_target_pairs={{0,24},{8,0},{16,8},{24,16},{32,56},{40,32},{48,40},{56,48},{64,88... | collective-permute-start | bytes 589832 | tf_op jit(solution)/shard_map/ppermute | solution.py:443
  94.4 3.2 %collective-permute-start.11 = (bf16[768,128]{1,0:T(8,128)(2,1)S(1)}, bf16[768,128]{1,0:T(8,128)(2,1)S(1)}, u32[]{:S(2)}, u32[]{:S(2)}) collective-permute-start(bf16[768,128]{1,0:T(8,128)(2,1)S(1)} %get-tuple-element.57), channel_id=1, source_target_pairs={{0,16},{8,24},{16,0},{24,8},{32,48},{40,56},{48,32},{56,40},{64,80... | collective-permute-start | bytes 589832 | tf_op jit(solution)/shard_map/ppermute | solution.py:443
  97.6 0.0 collective-permute-start.10
  97.6 5.2 %all-to-all-done.1.signal_ref = bf16[8,16,3072]{2,1,0:T(8,128)(2,1)} async-done(((bf16[8,16,3072]{2,1,0:T(8,128)(2,1)}), bf16[8,16,3072]{2,1,0:T(8,128)(2,1)}, u32[]{:S(2)}, u32[]{:S(2)}) %all-to-all-start.1) | async-done | bytes 786464 | tf_op jit(solution)/shard_map/all_to_all | solution.py:439
  102.8 7.9 %convolution.1 = bf16[32,16,768]{2,1,0:T(8,128)(2,1)} custom-call(bf16[8,16,3072]{2,1,0:T(8,128)(2,1)} %all-to-all-done.1.signal_ref, f32[3072,256]{1,0:T(8,128)} %taps_spectrum.1.taps_ref, bf16[2,384,192]{2,1,0:T(8,128)(2,1)} %constant.56.clone.outer_ref, f32[2,192,128]{2,1,0:T(8,128)} %constant.54.clone.twist_ref, ...), custom_call_target="tpu_custom_call" | custom-call | flops 7000000000 | bytes 5242880 | tf_op jit(solution)/shard_map/convolution/pallas_call | solution.py:355
  110.7 0.0 collective-permute-done.12.rest_3_
  110.7 0.0 collective-permute-done.11.rest_2_
  110.7 0.0 collective-permute-done.10.rest_1_
  110.8 6.0 %all-to-all-start.2 = ((bf16[32,16,768]{2,1,0:T(8,128)(2,1)}), bf16[32,16,768]{2,1,0:T(8,128)(2,1)S(1)}, u32[]{:S(2)}, u32[]{:S(2)}) async-start(bf16[32,16,768]{2,1,0:T(8,128)(2,1)} %convolution.1), calls=%async_computation.2 | async-start | bytes 1572864 | tf_op jit(solution)/shard_map/all_to_all | solution.py:439
  116.8 0.0 copy-start
  116.8 2.0 %assemble.1 = bf16[768,512]{1,0:T(8,128)(2,1)} custom-call(s32[1]{0:T(128)} %bitcast.x_ref, bf16[768,128]{1,0:T(8,128)(2,1)} %get-tuple-element.51.rest_0_, bf16[768,128]{1,0:T(8,128)(2,1)} %collective-permute-done.10.rest_1_, bf16[768,128]{1,0:T(8,128)(2,1)} %copy-done.9, bf16[768,128]{1,0:T(8,128)(2,1)} %copy-done.8), custom_call_target="tpu_custom_call" | custom-call | flops 2000000000 | bytes 1048576 | tf_op jit(solution)/shard_map/assemble/pallas_call | solution.py:391
  118.8 17.9 %all-to-all-done.2 = bf16[32,16,768]{2,1,0:T(8,128)(2,1)S(1)} async-done(((bf16[32,16,768]{2,1,0:T(8,128)(2,1)}), bf16[32,16,768]{2,1,0:T(8,128)(2,1)S(1)}, u32[]{:S(2)}, u32[]{:S(2)}) %all-to-all-start.2) | async-done | bytes 786464 | tf_op jit(solution)/shard_map/all_to_all | solution.py:439
  136.7 1.9 %finish.1 = bf16[768,512]{1,0:T(8,128)(2,1)} custom-call(bf16[8,4,16,768]{3,2,1,0:T(8,128)(2,1)S(1)} %bitcast.16, bf16[768,512]{1,0:T(8,128)(2,1)S(1)} %copy-done), custom_call_target="tpu_custom_call" | custom-call | tf_op jit(solution)/shard_map/finish/pallas_call | solution.py:416
  (21 shorter events, 0.0 us)
Async XLA Ops:
  0.6 36.4 %copy-start.1 = (f32[512,768]{1,0:T(8,128)S(1)}, f32[512,768]{1,0:T(8,128)}, u32[]{:S(2)}) copy-start(f32[512,768]{1,0:T(8,128)} %param.19) | copy-start | bytes 4718596
  3.1 12.5 %collective-permute-start = (bf16[2,768,128]{2,1,0:T(8,128)(2,1)}, bf16[2,768,128]{2,1,0:T(8,128)(2,1)S(1)}, u32[]{:S(2)}, u32[]{:S(2)}) collective-permute-start(bf16[2,768,128]{2,1,0:T(8,128)(2,1)} %get-tuple-element.30), channel_id=1, source_target_pairs={{0,8},{8,16},{16,24},{24,0},{32,40},{40,48},{48,56},{56,32},{64,72... | collective-permute-start | bytes 1179656 | tf_op jit(solution)/shard_map/ppermute | solution.py:443
  4.6 20.2 %collective-permute-start.1 = (bf16[2,768,128]{2,1,0:T(8,128)(2,1)}, bf16[2,768,128]{2,1,0:T(8,128)(2,1)S(1)}, u32[]{:S(2)}, u32[]{:S(2)}) collective-permute-start(bf16[2,768,128]{2,1,0:T(8,128)(2,1)} %get-tuple-element.32), channel_id=1, source_target_pairs={{0,16},{8,24},{16,0},{24,8},{32,48},{40,56},{48,32},{56,40},{64,80... | collective-permute-start | bytes 1179656 | tf_op jit(solution)/shard_map/ppermute | solution.py:443
  7.4 22.1 %collective-permute-start.2 = (bf16[2,768,128]{2,1,0:T(8,128)(2,1)}, bf16[2,768,128]{2,1,0:T(8,128)(2,1)}, u32[]{:S(2)}, u32[]{:S(2)}) collective-permute-start(bf16[2,768,128]{2,1,0:T(8,128)(2,1)} %get-tuple-element.33), channel_id=1, source_target_pairs={{0,24},{8,0},{16,8},{24,16},{32,56},{40,32},{48,40},{56,48},{64,88... | collective-permute-start | bytes 1179656 | tf_op jit(solution)/shard_map/ppermute | solution.py:443
  8.8 24.5 %collective-permute-start.3 = (bf16[2,768,128]{2,1,0:T(8,128)(2,1)}, bf16[2,768,128]{2,1,0:T(8,128)(2,1)S(1)}, u32[]{:S(2)}, u32[]{:S(2)}) collective-permute-start(bf16[2,768,128]{2,1,0:T(8,128)(2,1)} %get-tuple-element.29.rest_0_), channel_id=1, source_target_pairs={{8,40},{16,48},{24,56},{40,72},{48,80},{56,88},{72,104},{80,112},{... | collective-permute-start | bytes 1179656 | tf_op jit(solution)/shard_map/ppermute | solution.py:447
  15.6 22.5 %copy-start.4 = (bf16[2,768,128]{2,1,0:T(8,128)(2,1)}, bf16[2,768,128]{2,1,0:T(8,128)(2,1)S(1)}, u32[]{:S(2)}) copy-start(bf16[2,768,128]{2,1,0:T(8,128)(2,1)S(1)} %collective-permute-done.rest_1_) | copy-start | bytes 1179652
  15.6 17.7 %collective-permute-start.4 = (bf16[2,768,128]{2,1,0:T(8,128)(2,1)S(1)}, bf16[2,768,128]{2,1,0:T(8,128)(2,1)S(1)}, u32[]{:S(2)}, u32[]{:S(2)}) collective-permute-start(bf16[2,768,128]{2,1,0:T(8,128)(2,1)S(1)} %collective-permute-done.rest_1_), channel_id=1, source_target_pairs={{0,32},{16,48},{24,56},{32,64},{48,80},{56,88},{64,96},{80,112},{8... | collective-permute-start | bytes 1179656 | tf_op jit(solution)/shard_map/ppermute | solution.py:447
  22.8 26.4 %collective-permute-start.7 = (bf16[2,768,128]{2,1,0:T(8,128)(2,1)}, bf16[2,768,128]{2,1,0:T(8,128)(2,1)}, u32[]{:S(2)}, u32[]{:S(2)}) collective-permute-start(bf16[2,768,128]{2,1,0:T(8,128)(2,1)} %get-tuple-element.41), channel_id=1, source_target_pairs={{0,8},{8,16},{16,24},{24,0},{32,40},{40,48},{48,56},{56,32},{64,72... | collective-permute-start | bytes 1179656 | tf_op jit(solution)/shard_map/ppermute | solution.py:443
  24.8 21.0 %copy-start.5 = (bf16[2,768,128]{2,1,0:T(8,128)(2,1)}, bf16[2,768,128]{2,1,0:T(8,128)(2,1)S(1)}, u32[]{:S(2)}) copy-start(bf16[2,768,128]{2,1,0:T(8,128)(2,1)S(1)} %collective-permute-done.1.rest_2_) | copy-start | bytes 1179652
  24.8 21.0 %collective-permute-start.5 = (bf16[2,768,128]{2,1,0:T(8,128)(2,1)S(1)}, bf16[2,768,128]{2,1,0:T(8,128)(2,1)}, u32[]{:S(2)}, u32[]{:S(2)}) collective-permute-start(bf16[2,768,128]{2,1,0:T(8,128)(2,1)S(1)} %collective-permute-done.1.rest_2_), channel_id=1, source_target_pairs={{0,32},{8,40},{24,56},{32,64},{40,72},{56,88},{64,96},{72,104},{88... | collective-permute-start | bytes 1179656 | tf_op jit(solution)/shard_map/ppermute | solution.py:447
  29.4 19.7 %collective-permute-start.6 = (bf16[2,768,128]{2,1,0:T(8,128)(2,1)}, bf16[2,768,128]{2,1,0:T(8,128)(2,1)}, u32[]{:S(2)}, u32[]{:S(2)}) collective-permute-start(bf16[2,768,128]{2,1,0:T(8,128)(2,1)} %collective-permute-done.2.rest_3_), channel_id=1, source_target_pairs={{0,32},{8,40},{16,48},{32,64},{40,72},{48,80},{64,96},{72,104},{80... | collective-permute-start | bytes 1179656 | tf_op jit(solution)/shard_map/ppermute | solution.py:447
  33.3 4.8 %copy-start.6 = (bf16[2,768,128]{2,1,0:T(8,128)(2,1)}, bf16[2,768,128]{2,1,0:T(8,128)(2,1)S(1)}, u32[]{:S(2)}) copy-start(bf16[2,768,128]{2,1,0:T(8,128)(2,1)S(1)} %collective-permute-done.3.rest_4_) | copy-start | bytes 1179652
  33.3 4.8 %copy-start.7 = (bf16[2,768,128]{2,1,0:T(8,128)(2,1)}, bf16[2,768,128]{2,1,0:T(8,128)(2,1)S(1)}, u32[]{:S(2)}) copy-start(bf16[2,768,128]{2,1,0:T(8,128)(2,1)S(1)} %collective-permute-done.4.rest_5_) | copy-start | bytes 1179652
  33.3 15.9 %collective-permute-start.8 = (bf16[2,768,128]{2,1,0:T(8,128)(2,1)}, bf16[2,768,128]{2,1,0:T(8,128)(2,1)}, u32[]{:S(2)}, u32[]{:S(2)}) collective-permute-start(bf16[2,768,128]{2,1,0:T(8,128)(2,1)} %get-tuple-element.42), channel_id=1, source_target_pairs={{0,16},{8,24},{16,0},{24,8},{32,48},{40,56},{48,32},{56,40},{64,80... | collective-permute-start | bytes 1179656 | tf_op jit(solution)/shard_map/ppermute | solution.py:443
  33.4 18.2 %collective-permute-start.9 = (bf16[2,768,128]{2,1,0:T(8,128)(2,1)}, bf16[2,768,128]{2,1,0:T(8,128)(2,1)}, u32[]{:S(2)}, u32[]{:S(2)}) collective-permute-start(bf16[2,768,128]{2,1,0:T(8,128)(2,1)} %get-tuple-element.43), channel_id=1, source_target_pairs={{0,24},{8,0},{16,8},{24,16},{32,56},{40,32},{48,40},{56,48},{64,88... | collective-permute-start | bytes 1179656 | tf_op jit(solution)/shard_map/ppermute | solution.py:443
  36.8 14.8 %copy-start.3 = (s32[3072]{0:T(1024)}, s32[3072]{0:T(1024)S(1)}, u32[]{:S(2)}) copy-start(s32[3072]{0:T(1024)S(1)} %broadcast_subtract_fusion) | copy-start | bytes 36868
  38.1 29.8 %all-to-all-start = ((bf16[32,16,768]{2,1,0:T(8,128)(2,1)}), bf16[32,16,768]{2,1,0:T(8,128)(2,1)S(1)}, u32[]{:S(2)}, u32[]{:S(2)}) async-start(bf16[32,16,768]{2,1,0:T(8,128)(2,1)} %bitcast.4), calls=%async_computation | async-start | bytes 1572864 | tf_op jit(solution)/shard_map/all_to_all | solution.py:439
  67.9 17.7 %copy-start.2 = (bf16[32,16,768]{2,1,0:T(8,128)(2,1)}, bf16[32,16,768]{2,1,0:T(8,128)(2,1)S(1)}, u32[]{:S(2)}) copy-start(bf16[32,16,768]{2,1,0:T(8,128)(2,1)S(1)} %all-to-all-done.taps_ref) | copy-start | bytes 2359300
  67.9 34.9 %all-to-all-start.1 = ((bf16[8,16,3072]{2,1,0:T(8,128)(2,1)}), bf16[8,16,3072]{2,1,0:T(8,128)(2,1)}, u32[]{:S(2)}, u32[]{:S(2)}) async-start(bf16[8,16,3072]{2,1,0:T(8,128)(2,1)} %bitcast.18), calls=%async_computation.1 | async-start | bytes 1572864 | tf_op jit(solution)/shard_map/all_to_all | solution.py:439
  92.5 18.2 %collective-permute-start.12 = (bf16[768,128]{1,0:T(8,128)(2,1)S(1)}, bf16[768,128]{1,0:T(8,128)(2,1)S(1)}, u32[]{:S(2)}, u32[]{:S(2)}) collective-permute-start(bf16[768,128]{1,0:T(8,128)(2,1)S(1)} %get-tuple-element.56), channel_id=1, source_target_pairs={{0,24},{8,0},{16,8},{24,16},{32,56},{40,32},{48,40},{56,48},{64,88... | collective-permute-start | bytes 589832 | tf_op jit(solution)/shard_map/ppermute | solution.py:443
  94.4 16.3 %collective-permute-start.11 = (bf16[768,128]{1,0:T(8,128)(2,1)S(1)}, bf16[768,128]{1,0:T(8,128)(2,1)S(1)}, u32[]{:S(2)}, u32[]{:S(2)}) collective-permute-start(bf16[768,128]{1,0:T(8,128)(2,1)S(1)} %get-tuple-element.57), channel_id=1, source_target_pairs={{0,16},{8,24},{16,0},{24,8},{32,48},{40,56},{48,32},{56,40},{64,80... | collective-permute-start | bytes 589832 | tf_op jit(solution)/shard_map/ppermute | solution.py:443
  97.6 13.1 %collective-permute-start.10 = (bf16[768,128]{1,0:T(8,128)(2,1)S(1)}, bf16[768,128]{1,0:T(8,128)(2,1)}, u32[]{:S(2)}, u32[]{:S(2)}) collective-permute-start(bf16[768,128]{1,0:T(8,128)(2,1)S(1)} %get-tuple-element.58), channel_id=1, source_target_pairs={{0,8},{8,16},{16,24},{24,0},{32,40},{40,48},{48,56},{56,32},{64,72... | collective-permute-start | bytes 589832 | tf_op jit(solution)/shard_map/ppermute | solution.py:443
  110.7 6.0 %copy-start.8 = (bf16[768,128]{1,0:T(8,128)(2,1)}, bf16[768,128]{1,0:T(8,128)(2,1)S(1)}, u32[]{:S(2)}) copy-start(bf16[768,128]{1,0:T(8,128)(2,1)S(1)} %collective-permute-done.12.rest_3_) | copy-start | bytes 589828
  110.7 6.0 %copy-start.9 = (bf16[768,128]{1,0:T(8,128)(2,1)}, bf16[768,128]{1,0:T(8,128)(2,1)S(1)}, u32[]{:S(2)}) copy-start(bf16[768,128]{1,0:T(8,128)(2,1)S(1)} %collective-permute-done.11.rest_2_) | copy-start | bytes 589828
  110.8 26.0 %all-to-all-start.2 = ((bf16[32,16,768]{2,1,0:T(8,128)(2,1)}), bf16[32,16,768]{2,1,0:T(8,128)(2,1)S(1)}, u32[]{:S(2)}, u32[]{:S(2)}) async-start(bf16[32,16,768]{2,1,0:T(8,128)(2,1)} %convolution.1), calls=%async_computation.2 | async-start | bytes 1572864 | tf_op jit(solution)/shard_map/all_to_all | solution.py:439
  116.8 20.0 %copy-start = (bf16[768,512]{1,0:T(8,128)(2,1)S(1)}, bf16[768,512]{1,0:T(8,128)(2,1)}, u32[]{:S(2)}) copy-start(bf16[768,512]{1,0:T(8,128)(2,1)} %gate_ref.1) | copy-start | bytes 2359300

commit v11 on v8

--- a/solution.py
+++ b/solution.py
@@ -455,8 +455,10 @@
     before = [along_z(own[k], k) for k in range(X_SIZE)]
     own[1], queries, in_gate = lax.optimization_barrier((own[1], queries, in_gate))
     asked = pieces_of(x_index, queries, in_gate)
-    taps, *_ = lax.optimization_barrier((taps, *own, *asked))
     asked = arrived(asked)
+    taps, asked[1], asked[3], before[0], before[1] = lax.optimization_barrier(
+        (taps, asked[1], asked[3], before[0], before[1])
+    )
     taps = exchanged(taps)
 
     group_first = (me // X_SIZE) * group_rows

time: 133 us -> 135 us (1.015); the launches traced: 131 us -> 135 us
  Pallas kernels: 35.8 us -> 37.2 us
  starting transfers between devices: 47.6 us -> 49 us
    ppermute x4, waiting for transfers between devices: 10.1 us -> 1.88 us  [along_z(): return lax.ppermute(piece, 'ctx', pairs)]
    ppermute x9, waiting for transfers between devices: 8.11 us -> 13 us  [along_x(): return lax.ppermute(piece, 'ctx', pairs)]
    all_to_all x3, starting transfers between devices: 20.8 us -> 25.5 us  [exchanged(): lax.all_to_all(x, 'ctx', split_axis=0, concat_axis=0, tiled=True, axis_in...]
    all_to_all x3, waiting for transfers between devices: 24.1 us -> 28.7 us  [exchanged(): lax.all_to_all(x, 'ctx', split_axis=0, concat_axis=0, tiled=True, axis_in...]
    ppermute x9, starting transfers between devices: 13.9 us -> 10.5 us  [along_x(): return lax.ppermute(piece, 'ctx', pairs)]
    pallas_call x1, Pallas kernels: 14.3 us -> 15.7 us  [attention(): pl.pallas_call(attention_kernel, name='attention', grid_spec=pltpu.Prefet...]
  transfers between devices with their start and end apart: 16 -> 16, of which waited for: 6 -> 7; matrix products, arithmetic and copies ran while one was open for 4% -> 3% of each run, Pallas kernels for 24% -> 24%
where the time goes in v11:
time: 135 us
  starting transfers between devices  49 us (36%)
  waiting for transfers between devices  43.6 us (32%)
  Pallas kernels  37.2 us (28%)
  local copies, waits for them, and re-layouts  3.14 us (2%)
  other arithmetic  1.64 us (1%)
    all_to_all x3, waiting for transfers between devices, exchanged(): lax.all_to_all(x, 'ctx', split_axis=0, concat_axis=0, tiled=True, axis_in...  28.7 us
    all_to_all x3, starting transfers between devices, exchanged(): lax.all_to_all(x, 'ctx', split_axis=0, concat_axis=0, tiled=True, axis_in...  25.5 us
    pallas_call x1, Pallas kernels, attention(): pl.pallas_call(attention_kernel, name='attention', grid_spec=pltpu.Prefet...  15.7 us
    ppermute x9, waiting for transfers between devices, along_x(): return lax.ppermute(piece, 'ctx', pairs)  13 us
    ppermute x4, starting transfers between devices, along_z(): return lax.ppermute(piece, 'ctx', pairs)  12.9 us
    ppermute x9, starting transfers between devices, along_x(): return lax.ppermute(piece, 'ctx', pairs)  10.5 us
    pallas_call x1, Pallas kernels, convolve(): pl.pallas_call(conv_kernel, name='convolution', grid=(channels // (2 * PA...  7.9 us
    pallas_call x1, Pallas kernels, transform_taps(): pl.pallas_call(taps_kernel, name='taps_spectrum', grid=(channels // (2 *...  4.98 us
  transfers between devices with their start and end apart: 16, of which 7 were waited for; matrix products, arithmetic and copies ran while one was open for 3% of the time, Pallas kernels for 24%

profile of v11, /device:TPU:16, one launch (start us, length us, event | category | flops | bytes accessed | tf_op | source)
XLA Modules:
  0.0 135.4 jit_solution(2698735741539903307)
XLA Ops:
  0.6 2.4 %pieces.2 = (bf16[2,768,128]{2,1,0:T(8,128)(2,1)}, bf16[2,768,128]{2,1,0:T(8,128)(2,1)}, bf16[2,768,128]{2,1,0:T(8,128)(2,1)}, bf16[2,768,128]{2,1,0:T(8,128)(2,1)}) custom-call(s32[1]{0:T(128)} %bitcast.x_ref, bf16[768,512]{1,0:T(8,128)(2,1)} %first_ref.1, bf16[768,512]{1,0:T(8,128)(2,1)} %second_ref.1), custom_call_target="tpu_custom_call" | custom-call | tf_op jit(solution)/shard_map/pieces/pallas_call | solution.py:52
  3.1 1.6 %collective-permute-start = (bf16[2,768,128]{2,1,0:T(8,128)(2,1)}, bf16[2,768,128]{2,1,0:T(8,128)(2,1)S(1)}, u32[]{:S(2)}, u32[]{:S(2)}) collective-permute-start(bf16[2,768,128]{2,1,0:T(8,128)(2,1)} %get-tuple-element.30), channel_id=1, source_target_pairs={{0,8},{8,16},{16,24},{24,0},{32,40},{40,48},{48,56},{56,32},{64,72... | collective-permute-start | bytes 1179656 | tf_op jit(solution)/shard_map/ppermute | solution.py:443
  4.6 2.7 %collective-permute-start.1 = (bf16[2,768,128]{2,1,0:T(8,128)(2,1)}, bf16[2,768,128]{2,1,0:T(8,128)(2,1)S(1)}, u32[]{:S(2)}, u32[]{:S(2)}) collective-permute-start(bf16[2,768,128]{2,1,0:T(8,128)(2,1)} %get-tuple-element.32), channel_id=1, source_target_pairs={{0,16},{8,24},{16,0},{24,8},{32,48},{40,56},{48,32},{56,40},{64,80... | collective-permute-start | bytes 1179656 | tf_op jit(solution)/shard_map/ppermute | solution.py:443
  7.4 1.4 %collective-permute-start.2 = (bf16[2,768,128]{2,1,0:T(8,128)(2,1)}, bf16[2,768,128]{2,1,0:T(8,128)(2,1)}, u32[]{:S(2)}, u32[]{:S(2)}) collective-permute-start(bf16[2,768,128]{2,1,0:T(8,128)(2,1)} %get-tuple-element.33), channel_id=1, source_target_pairs={{0,24},{8,0},{16,8},{24,16},{32,56},{40,32},{48,40},{56,48},{64,88... | collective-permute-start | bytes 1179656 | tf_op jit(solution)/shard_map/ppermute | solution.py:443
  8.8 0.7 collective-permute-start.5
  9.5 6.1 %collective-permute-done.rest_1_ = bf16[2,768,128]{2,1,0:T(8,128)(2,1)S(1)} collective-permute-done((bf16[2,768,128]{2,1,0:T(8,128)(2,1)}, bf16[2,768,128]{2,1,0:T(8,128)(2,1)S(1)}, u32[]{:S(2)}, u32[]{:S(2)}) %collective-permute-start) | collective-permute-done | bytes 393248 | tf_op jit(solution)/shard_map/ppermute | solution.py:443
  15.6 3.8 %collective-permute-start.6 = (bf16[2,768,128]{2,1,0:T(8,128)(2,1)S(1)}, bf16[2,768,128]{2,1,0:T(8,128)(2,1)S(1)}, u32[]{:S(2)}, u32[]{:S(2)}) collective-permute-start(bf16[2,768,128]{2,1,0:T(8,128)(2,1)S(1)} %collective-permute-done.rest_1_), channel_id=1, source_target_pairs={{0,32},{16,48},{24,56},{32,64},{48,80},{56,88},{64,96},{80,112},{8... | collective-permute-start | bytes 1179656 | tf_op jit(solution)/shard_map/ppermute | solution.py:447
  19.5 0.7 select_reduce_fusion.1
  20.2 2.3 %pieces.3 = (bf16[2,768,128]{2,1,0:T(8,128)(2,1)}, bf16[2,768,128]{2,1,0:T(8,128)(2,1)}, bf16[2,768,128]{2,1,0:T(8,128)(2,1)}, bf16[2,768,128]{2,1,0:T(8,128)(2,1)}) custom-call(s32[1]{0:T(128)} %bitcast.x_ref, bf16[768,512]{1,0:T(8,128)(2,1)} %first_ref.2, bf16[768,512]{1,0:T(8,128)(2,1)} %second_ref.2), custom_call_target="tpu_custom_call" | custom-call | tf_op jit(solution)/shard_map/pieces/pallas_call | solution.py:52
  22.5 0.1 collective-permute-start.3
  22.6 2.2 %collective-permute-done.1.rest_2_ = bf16[2,768,128]{2,1,0:T(8,128)(2,1)S(1)} collective-permute-done((bf16[2,768,128]{2,1,0:T(8,128)(2,1)}, bf16[2,768,128]{2,1,0:T(8,128)(2,1)S(1)}, u32[]{:S(2)}, u32[]{:S(2)}) %collective-permute-start.1) | collective-permute-done | bytes 393248 | tf_op jit(solution)/shard_map/ppermute | solution.py:443
  24.8 1.0 collective-permute-start.4
  25.9 0.2 select_reduce_fusion
  26.1 0.0 collective-permute-done.2.rest_3_
  26.1 1.7 %collective-permute-start.9 = (bf16[2,768,128]{2,1,0:T(8,128)(2,1)}, bf16[2,768,128]{2,1,0:T(8,128)(2,1)}, u32[]{:S(2)}, u32[]{:S(2)}) collective-permute-start(bf16[2,768,128]{2,1,0:T(8,128)(2,1)} %get-tuple-element.42), channel_id=1, source_target_pairs={{0,16},{8,24},{16,0},{24,8},{32,48},{40,56},{48,32},{56,40},{64,80... | collective-permute-start | bytes 1179656 | tf_op jit(solution)/shard_map/ppermute | solution.py:443
  27.8 0.0 collective-permute-done.5.rest_4_
  27.8 4.6 %collective-permute-start.7 = (bf16[2,768,128]{2,1,0:T(8,128)(2,1)S(1)}, bf16[2,768,128]{2,1,0:T(8,128)(2,1)}, u32[]{:S(2)}, u32[]{:S(2)}) collective-permute-start(bf16[2,768,128]{2,1,0:T(8,128)(2,1)S(1)} %collective-permute-done.1.rest_2_), channel_id=1, source_target_pairs={{0,32},{8,40},{24,56},{32,64},{40,72},{56,88},{64,96},{72,104},{88... | collective-permute-start | bytes 1179656 | tf_op jit(solution)/shard_map/ppermute | solution.py:447
  32.3 0.0 collective-permute-done.6.rest_5_
  32.3 3.8 %collective-permute-start.8 = (bf16[2,768,128]{2,1,0:T(8,128)(2,1)}, bf16[2,768,128]{2,1,0:T(8,128)(2,1)}, u32[]{:S(2)}, u32[]{:S(2)}) collective-permute-start(bf16[2,768,128]{2,1,0:T(8,128)(2,1)} %collective-permute-done.2.rest_3_), channel_id=1, source_target_pairs={{0,32},{8,40},{16,48},{32,64},{40,72},{48,80},{64,96},{72,104},{80... | collective-permute-start | bytes 1179656 | tf_op jit(solution)/shard_map/ppermute | solution.py:447
  36.2 0.1 slice.19
  36.3 0.1 slice.18
  36.4 0.1 convert_element_type.3
  36.4 1.0 copy.16
  37.4 4.7 %collective-permute-done.3.rest_9_ = bf16[2,768,128]{2,1,0:T(8,128)(2,1)} collective-permute-done((bf16[2,768,128]{2,1,0:T(8,128)(2,1)}, bf16[2,768,128]{2,1,0:T(8,128)(2,1)}, u32[]{:S(2)}, u32[]{:S(2)}) %collective-permute-start.3) | collective-permute-done | bytes 393248 | tf_op jit(solution)/shard_map/ppermute | solution.py:443
  42.1 0.0 collective-permute-done.4.rest_11_
  42.1 7.5 %all-to-all-start = ((bf16[32,16,768]{2,1,0:T(8,128)(2,1)}), bf16[32,16,768]{2,1,0:T(8,128)(2,1)S(1)}, u32[]{:S(2)}, u32[]{:S(2)}) async-start(bf16[32,16,768]{2,1,0:T(8,128)(2,1)} %bitcast.4), calls=%async_computation | async-start | bytes 1572864 | tf_op jit(solution)/shard_map/all_to_all | solution.py:439
  49.6 0.6 and_select_fusion.1
  50.2 0.0 collective-permute-done.7.rest_6_
  50.2 1.9 %collective-permute-done.8.rest_7_ = bf16[2,768,128]{2,1,0:T(8,128)(2,1)} collective-permute-done((bf16[2,768,128]{2,1,0:T(8,128)(2,1)}, bf16[2,768,128]{2,1,0:T(8,128)(2,1)}, u32[]{:S(2)}, u32[]{:S(2)}) %collective-permute-start.8) | collective-permute-done | bytes 393248 | tf_op jit(solution)/shard_map/ppermute | solution.py:447
  52.1 0.0 collective-permute-done.9.rest_10_
  52.1 15.7 %attention.1 = (bf16[4,768,128]{2,1,0:T(8,128)(2,1)}, bf16[128,3072]{1,0:T(8,128)(2,1)}) custom-call(s32[4]{0:T(128)} %get-tuple-element.60.lo_ref, s32[4]{0:T(128)} %get-tuple-element.61.mid_ref, s32[1]{0:T(128)} %bitcast.x_ref, s32[4,1,768]{2,1,0:T(1,128)} %bitcast.19, bf16[2,768,128]{2,1,0:T(8,128)(2,1)} %get-tuple-element.29.rest_0_, ...), custom_call_target="tpu_custom_call" | custom-call | flops 16000000000 | bytes 3932160 | tf_op jit(solution)/shard_map/attention/pallas_call | solution.py:165
  67.8 1.5 %all-to-all-done.taps_ref = bf16[32,16,768]{2,1,0:T(8,128)(2,1)S(1)} async-done(((bf16[32,16,768]{2,1,0:T(8,128)(2,1)}), bf16[32,16,768]{2,1,0:T(8,128)(2,1)S(1)}, u32[]{:S(2)}, u32[]{:S(2)}) %all-to-all-start) | async-done | bytes 786464 | tf_op jit(solution)/shard_map/all_to_all | solution.py:439
  69.2 13.1 %all-to-all-start.1 = ((bf16[8,16,3072]{2,1,0:T(8,128)(2,1)}), bf16[8,16,3072]{2,1,0:T(8,128)(2,1)}, u32[]{:S(2)}, u32[]{:S(2)}) async-start(bf16[8,16,3072]{2,1,0:T(8,128)(2,1)} %bitcast.18), calls=%async_computation.1 | async-start | bytes 1572864 | tf_op jit(solution)/shard_map/all_to_all | solution.py:439
  82.4 5.0 %taps_spectrum.1.taps_ref = f32[3072,256]{1,0:T(8,128)} custom-call(bf16[32,16,768]{2,1,0:T(8,128)(2,1)} %copy-done.2, bf16[2,384,192]{2,1,0:T(8,128)(2,1)} %constant.53.clone.outer_ref, f32[2,192,128]{2,1,0:T(8,128)} %constant.54.clone.twist_ref, bf16[2,256,256]{2,1,0:T(8,128)(2,1)} %constant.55.clone.inner_ref), custom_call_target="tpu_custom_call" | custom-call | flops 5000000000 | bytes 4194304 | tf_op jit(solution)/shard_map/taps_spectrum/pallas_call | solution.py:337
  87.4 1.9 %slice_bitcast_fusion = (bf16[768,128]{1,0:T(8,128)(2,1)S(1)}, bf16[768,128]{1,0:T(8,128)(2,1)S(1)}, bf16[768,128]{1,0:T(8,128)(2,1)S(1)}, bf16[768,128]{1,0:T(8,128)(2,1)}) fusion(bf16[4,768,128]{2,1,0:T(8,128)(2,1)} %get-tuple-element.50), kind=kLoop, calls=%fused_computation.1 | loop fusion | bytes 1572864 | tf_op jit(solution)/shard_map/squeeze | solution.py:473
  89.3 0.0 collective-permute-start.12
  89.3 0.8 collective-permute-start.11
  90.1 1.2 collective-permute-start.10
  91.3 7.8 %all-to-all-done.1.signal_ref = bf16[8,16,3072]{2,1,0:T(8,128)(2,1)} async-done(((bf16[8,16,3072]{2,1,0:T(8,128)(2,1)}), bf16[8,16,3072]{2,1,0:T(8,128)(2,1)}, u32[]{:S(2)}, u32[]{:S(2)}) %all-to-all-start.1) | async-done | bytes 786464 | tf_op jit(solution)/shard_map/all_to_all | solution.py:439
  99.1 7.9 %convolution.1 = bf16[32,16,768]{2,1,0:T(8,128)(2,1)} custom-call(bf16[8,16,3072]{2,1,0:T(8,128)(2,1)} %all-to-all-done.1.signal_ref, f32[3072,256]{1,0:T(8,128)} %taps_spectrum.1.taps_ref, bf16[2,384,192]{2,1,0:T(8,128)(2,1)} %constant.56.clone.outer_ref, f32[2,192,128]{2,1,0:T(8,128)} %constant.54.clone.twist_ref, ...), custom_call_target="tpu_custom_call" | custom-call | flops 7000000000 | bytes 5242880 | tf_op jit(solution)/shard_map/convolution/pallas_call | solution.py:355
  107.0 0.0 collective-permute-done.12.rest_3_
  107.0 0.0 collective-permute-done.11.rest_2_
  107.1 0.0 collective-permute-done.10.rest_1_
  107.1 4.9 %all-to-all-start.2 = ((bf16[32,16,768]{2,1,0:T(8,128)(2,1)}), bf16[32,16,768]{2,1,0:T(8,128)(2,1)S(1)}, u32[]{:S(2)}, u32[]{:S(2)}) async-start(bf16[32,16,768]{2,1,0:T(8,128)(2,1)} %convolution.1), calls=%async_computation.2 | async-start | bytes 1572864 | tf_op jit(solution)/shard_map/all_to_all | solution.py:439
  112.0 0.0 copy-start
  112.0 2.0 %assemble.1 = bf16[768,512]{1,0:T(8,128)(2,1)} custom-call(s32[1]{0:T(128)} %bitcast.x_ref, bf16[768,128]{1,0:T(8,128)(2,1)} %get-tuple-element.51.rest_0_, bf16[768,128]{1,0:T(8,128)(2,1)} %collective-permute-done.10.rest_1_, bf16[768,128]{1,0:T(8,128)(2,1)} %copy-done.9, bf16[768,128]{1,0:T(8,128)(2,1)} %copy-done.8), custom_call_target="tpu_custom_call" | custom-call | flops 2000000000 | bytes 1048576 | tf_op jit(solution)/shard_map/assemble/pallas_call | solution.py:391
  114.1 19.4 %all-to-all-done.2 = bf16[32,16,768]{2,1,0:T(8,128)(2,1)S(1)} async-done(((bf16[32,16,768]{2,1,0:T(8,128)(2,1)}), bf16[32,16,768]{2,1,0:T(8,128)(2,1)S(1)}, u32[]{:S(2)}, u32[]{:S(2)}) %all-to-all-start.2) | async-done | bytes 786464 | tf_op jit(solution)/shard_map/all_to_all | solution.py:439
  133.5 1.9 %finish.1 = bf16[768,512]{1,0:T(8,128)(2,1)} custom-call(bf16[8,4,16,768]{3,2,1,0:T(8,128)(2,1)S(1)} %bitcast.16, bf16[768,512]{1,0:T(8,128)(2,1)S(1)} %copy-done), custom_call_target="tpu_custom_call" | custom-call | tf_op jit(solution)/shard_map/finish/pallas_call | solution.py:416
  (21 shorter events, 0.0 us)
Async XLA Ops:
  0.6 35.7 %copy-start.1 = (f32[512,768]{1,0:T(8,128)S(1)}, f32[512,768]{1,0:T(8,128)}, u32[]{:S(2)}) copy-start(f32[512,768]{1,0:T(8,128)} %param.19) | copy-start | bytes 4718596
  3.1 12.5 %collective-permute-start = (bf16[2,768,128]{2,1,0:T(8,128)(2,1)}, bf16[2,768,128]{2,1,0:T(8,128)(2,1)S(1)}, u32[]{:S(2)}, u32[]{:S(2)}) collective-permute-start(bf16[2,768,128]{2,1,0:T(8,128)(2,1)} %get-tuple-element.30), channel_id=1, source_target_pairs={{0,8},{8,16},{16,24},{24,0},{32,40},{40,48},{48,56},{56,32},{64,72... | collective-permute-start | bytes 1179656 | tf_op jit(solution)/shard_map/ppermute | solution.py:443
  4.6 20.2 %collective-permute-start.1 = (bf16[2,768,128]{2,1,0:T(8,128)(2,1)}, bf16[2,768,128]{2,1,0:T(8,128)(2,1)S(1)}, u32[]{:S(2)}, u32[]{:S(2)}) collective-permute-start(bf16[2,768,128]{2,1,0:T(8,128)(2,1)} %get-tuple-element.32), channel_id=1, source_target_pairs={{0,16},{8,24},{16,0},{24,8},{32,48},{40,56},{48,32},{56,40},{64,80... | collective-permute-start | bytes 1179656 | tf_op jit(solution)/shard_map/ppermute | solution.py:443
  7.4 18.7 %collective-permute-start.2 = (bf16[2,768,128]{2,1,0:T(8,128)(2,1)}, bf16[2,768,128]{2,1,0:T(8,128)(2,1)}, u32[]{:S(2)}, u32[]{:S(2)}) collective-permute-start(bf16[2,768,128]{2,1,0:T(8,128)(2,1)} %get-tuple-element.33), channel_id=1, source_target_pairs={{0,24},{8,0},{16,8},{24,16},{32,56},{40,32},{48,40},{56,48},{64,88... | collective-permute-start | bytes 1179656 | tf_op jit(solution)/shard_map/ppermute | solution.py:443
  8.8 19.0 %collective-permute-start.5 = (bf16[2,768,128]{2,1,0:T(8,128)(2,1)}, bf16[2,768,128]{2,1,0:T(8,128)(2,1)S(1)}, u32[]{:S(2)}, u32[]{:S(2)}) collective-permute-start(bf16[2,768,128]{2,1,0:T(8,128)(2,1)} %get-tuple-element.29.rest_0_), channel_id=1, source_target_pairs={{8,40},{16,48},{24,56},{40,72},{48,80},{56,88},{72,104},{80,112},{... | collective-permute-start | bytes 1179656 | tf_op jit(solution)/shard_map/ppermute | solution.py:447
  15.6 26.5 %copy-start.4 = (bf16[2,768,128]{2,1,0:T(8,128)(2,1)}, bf16[2,768,128]{2,1,0:T(8,128)(2,1)S(1)}, u32[]{:S(2)}) copy-start(bf16[2,768,128]{2,1,0:T(8,128)(2,1)S(1)} %collective-permute-done.rest_1_) | copy-start | bytes 1179652
  15.6 16.8 %collective-permute-start.6 = (bf16[2,768,128]{2,1,0:T(8,128)(2,1)S(1)}, bf16[2,768,128]{2,1,0:T(8,128)(2,1)S(1)}, u32[]{:S(2)}, u32[]{:S(2)}) collective-permute-start(bf16[2,768,128]{2,1,0:T(8,128)(2,1)S(1)} %collective-permute-done.rest_1_), channel_id=1, source_target_pairs={{0,32},{16,48},{24,56},{32,64},{48,80},{56,88},{64,96},{80,112},{8... | collective-permute-start | bytes 1179656 | tf_op jit(solution)/shard_map/ppermute | solution.py:447
  22.5 19.6 %collective-permute-start.3 = (bf16[2,768,128]{2,1,0:T(8,128)(2,1)}, bf16[2,768,128]{2,1,0:T(8,128)(2,1)}, u32[]{:S(2)}, u32[]{:S(2)}) collective-permute-start(bf16[2,768,128]{2,1,0:T(8,128)(2,1)} %get-tuple-element.36), channel_id=1, source_target_pairs={{0,8},{8,16},{16,24},{24,0},{32,40},{40,48},{48,56},{56,32},{64,72... | collective-permute-start | bytes 1179656 | tf_op jit(solution)/shard_map/ppermute | solution.py:443
  24.8 25.4 %copy-start.5 = (bf16[2,768,128]{2,1,0:T(8,128)(2,1)}, bf16[2,768,128]{2,1,0:T(8,128)(2,1)S(1)}, u32[]{:S(2)}) copy-start(bf16[2,768,128]{2,1,0:T(8,128)(2,1)S(1)} %collective-permute-done.1.rest_2_) | copy-start | bytes 1179652
  24.8 17.3 %collective-permute-start.4 = (bf16[2,768,128]{2,1,0:T(8,128)(2,1)}, bf16[2,768,128]{2,1,0:T(8,128)(2,1)}, u32[]{:S(2)}, u32[]{:S(2)}) collective-permute-start(bf16[2,768,128]{2,1,0:T(8,128)(2,1)} %get-tuple-element.37), channel_id=1, source_target_pairs={{0,24},{8,0},{16,8},{24,16},{32,56},{40,32},{48,40},{56,48},{64,88... | collective-permute-start | bytes 1179656 | tf_op jit(solution)/shard_map/ppermute | solution.py:443
  26.1 26.0 %collective-permute-start.9 = (bf16[2,768,128]{2,1,0:T(8,128)(2,1)}, bf16[2,768,128]{2,1,0:T(8,128)(2,1)}, u32[]{:S(2)}, u32[]{:S(2)}) collective-permute-start(bf16[2,768,128]{2,1,0:T(8,128)(2,1)} %get-tuple-element.42), channel_id=1, source_target_pairs={{0,16},{8,24},{16,0},{24,8},{32,48},{40,56},{48,32},{56,40},{64,80... | collective-permute-start | bytes 1179656 | tf_op jit(solution)/shard_map/ppermute | solution.py:443
  27.8 14.3 %copy-start.6 = (bf16[2,768,128]{2,1,0:T(8,128)(2,1)}, bf16[2,768,128]{2,1,0:T(8,128)(2,1)S(1)}, u32[]{:S(2)}) copy-start(bf16[2,768,128]{2,1,0:T(8,128)(2,1)S(1)} %collective-permute-done.5.rest_4_) | copy-start | bytes 1179652
  27.8 22.5 %collective-permute-start.7 = (bf16[2,768,128]{2,1,0:T(8,128)(2,1)S(1)}, bf16[2,768,128]{2,1,0:T(8,128)(2,1)}, u32[]{:S(2)}, u32[]{:S(2)}) collective-permute-start(bf16[2,768,128]{2,1,0:T(8,128)(2,1)S(1)} %collective-permute-done.1.rest_2_), channel_id=1, source_target_pairs={{0,32},{8,40},{24,56},{32,64},{40,72},{56,88},{64,96},{72,104},{88... | collective-permute-start | bytes 1179656 | tf_op jit(solution)/shard_map/ppermute | solution.py:447
  32.3 9.8 %copy-start.7 = (bf16[2,768,128]{2,1,0:T(8,128)(2,1)}, bf16[2,768,128]{2,1,0:T(8,128)(2,1)S(1)}, u32[]{:S(2)}) copy-start(bf16[2,768,128]{2,1,0:T(8,128)(2,1)S(1)} %collective-permute-done.6.rest_5_) | copy-start | bytes 1179652
  32.3 19.8 %collective-permute-start.8 = (bf16[2,768,128]{2,1,0:T(8,128)(2,1)}, bf16[2,768,128]{2,1,0:T(8,128)(2,1)}, u32[]{:S(2)}, u32[]{:S(2)}) collective-permute-start(bf16[2,768,128]{2,1,0:T(8,128)(2,1)} %collective-permute-done.2.rest_3_), channel_id=1, source_target_pairs={{0,32},{8,40},{16,48},{32,64},{40,72},{48,80},{64,96},{72,104},{80... | collective-permute-start | bytes 1179656 | tf_op jit(solution)/shard_map/ppermute | solution.py:447
  36.2 15.9 %copy-start.3 = (s32[3072]{0:T(1024)}, s32[3072]{0:T(1024)S(1)}, u32[]{:S(2)}) copy-start(s32[3072]{0:T(1024)S(1)} %broadcast_subtract_fusion) | copy-start | bytes 36868
  42.1 27.1 %all-to-all-start = ((bf16[32,16,768]{2,1,0:T(8,128)(2,1)}), bf16[32,16,768]{2,1,0:T(8,128)(2,1)S(1)}, u32[]{:S(2)}, u32[]{:S(2)}) async-start(bf16[32,16,768]{2,1,0:T(8,128)(2,1)} %bitcast.4), calls=%async_computation | async-start | bytes 1572864 | tf_op jit(solution)/shard_map/all_to_all | solution.py:439
  69.2 13.1 %copy-start.2 = (bf16[32,16,768]{2,1,0:T(8,128)(2,1)}, bf16[32,16,768]{2,1,0:T(8,128)(2,1)S(1)}, u32[]{:S(2)}) copy-start(bf16[32,16,768]{2,1,0:T(8,128)(2,1)S(1)} %all-to-all-done.taps_ref) | copy-start | bytes 2359300
  69.2 29.9 %all-to-all-start.1 = ((bf16[8,16,3072]{2,1,0:T(8,128)(2,1)}), bf16[8,16,3072]{2,1,0:T(8,128)(2,1)}, u32[]{:S(2)}, u32[]{:S(2)}) async-start(bf16[8,16,3072]{2,1,0:T(8,128)(2,1)} %bitcast.18), calls=%async_computation.1 | async-start | bytes 1572864 | tf_op jit(solution)/shard_map/all_to_all | solution.py:439
  89.3 17.7 %collective-permute-start.12 = (bf16[768,128]{1,0:T(8,128)(2,1)S(1)}, bf16[768,128]{1,0:T(8,128)(2,1)S(1)}, u32[]{:S(2)}, u32[]{:S(2)}) collective-permute-start(bf16[768,128]{1,0:T(8,128)(2,1)S(1)} %get-tuple-element.56), channel_id=1, source_target_pairs={{0,24},{8,0},{16,8},{24,16},{32,56},{40,32},{48,40},{56,48},{64,88... | collective-permute-start | bytes 589832 | tf_op jit(solution)/shard_map/ppermute | solution.py:443
  89.3 17.7 %collective-permute-start.11 = (bf16[768,128]{1,0:T(8,128)(2,1)S(1)}, bf16[768,128]{1,0:T(8,128)(2,1)S(1)}, u32[]{:S(2)}, u32[]{:S(2)}) collective-permute-start(bf16[768,128]{1,0:T(8,128)(2,1)S(1)} %get-tuple-element.57), channel_id=1, source_target_pairs={{0,16},{8,24},{16,0},{24,8},{32,48},{40,56},{48,32},{56,40},{64,80... | collective-permute-start | bytes 589832 | tf_op jit(solution)/shard_map/ppermute | solution.py:443
  90.1 16.9 %collective-permute-start.10 = (bf16[768,128]{1,0:T(8,128)(2,1)S(1)}, bf16[768,128]{1,0:T(8,128)(2,1)}, u32[]{:S(2)}, u32[]{:S(2)}) collective-permute-start(bf16[768,128]{1,0:T(8,128)(2,1)S(1)} %get-tuple-element.58), channel_id=1, source_target_pairs={{0,8},{8,16},{16,24},{24,0},{32,40},{40,48},{48,56},{56,32},{64,72... | collective-permute-start | bytes 589832 | tf_op jit(solution)/shard_map/ppermute | solution.py:443
  107.0 5.0 %copy-start.8 = (bf16[768,128]{1,0:T(8,128)(2,1)}, bf16[768,128]{1,0:T(8,128)(2,1)S(1)}, u32[]{:S(2)}) copy-start(bf16[768,128]{1,0:T(8,128)(2,1)S(1)} %collective-permute-done.12.rest_3_) | copy-start | bytes 589828
  107.1 4.9 %copy-start.9 = (bf16[768,128]{1,0:T(8,128)(2,1)}, bf16[768,128]{1,0:T(8,128)(2,1)S(1)}, u32[]{:S(2)}) copy-start(bf16[768,128]{1,0:T(8,128)(2,1)S(1)} %collective-permute-done.11.rest_2_) | copy-start | bytes 589828
  107.1 26.4 %all-to-all-start.2 = ((bf16[32,16,768]{2,1,0:T(8,128)(2,1)}), bf16[32,16,768]{2,1,0:T(8,128)(2,1)S(1)}, u32[]{:S(2)}, u32[]{:S(2)}) async-start(bf16[32,16,768]{2,1,0:T(8,128)(2,1)} %convolution.1), calls=%async_computation.2 | async-start | bytes 1572864 | tf_op jit(solution)/shard_map/all_to_all | solution.py:439
  112.0 21.5 %copy-start = (bf16[768,512]{1,0:T(8,128)(2,1)S(1)}, bf16[768,512]{1,0:T(8,128)(2,1)}, u32[]{:S(2)}) copy-start(bf16[768,512]{1,0:T(8,128)(2,1)} %gate_ref.1) | copy-start | bytes 2359300
